TPU v7x, 256 devices: a whole 4x4x8 slice. The times are simulated.
256 devices in a mesh: mol: 8 (over x, core), task: 32 (over z, y).
Axes of the slice: x: 4, y: 4, z: 8, core: 2. Of those that a mesh axis runs over, the one named last changes fastest.
Arguments:
- node_embed: bfloat16 [12288, 6272], P(('mol', 'task')), may hold values from -6 to 6
- wigner: bfloat16 [256, 29, 49], replicated, as said below
- source: int32 [49152], P(('mol', 'task')), may hold values from 0 to 47
- target: int32 [49152], P(('mol', 'task')), may hold values from 0 to 47
- rotation: int32 [49152], P(('mol', 'task')), may hold values from 0 to 255
- edge_filter: bfloat16 [49152, 128], P(('mol', 'task')), may hold values from -6 to 6
- edge_count: int32 [256], P(('mol', 'task')), may hold values from 1 to 192, as said below
- w_zero: bfloat16 [1792, 896], P('task'), may hold values from -0.125 to 0.125
- w_one_real: bfloat16 [1536, 768], P('task'), may hold values from -0.109375 to 0.109375
- w_one_imag: bfloat16 [1536, 768], P('task'), may hold values from -0.109375 to 0.109375
- w_two_real: bfloat16 [1280, 640], P('task'), may hold values from -0.125 to 0.125
- w_two_imag: bfloat16 [1280, 640], P('task'), may hold values from -0.125 to 0.125
- atom_struct: int32 [12288], P(('mol', 'task')), may hold values from 0 to 3
- struct_task: int32 [1024], P(('mol', 'task')), may hold values from 0 to 4
- task_head: float32 [5, 128], replicated, may hold values from -0.5 to 0.5
Outputs:
- update: bfloat16 [12288, 6272], P(('mol', 'task'))
- energy: float32 [1024], P(('mol', 'task'))
Inputs may be any that keep to these rules, and one draw needn't show every extreme that they name: Each device has ceil(edge_count / 64) live blocks; for every task index and every mol index i below 4, the live blocks of mol index i and of mol index i + 4 sum to at most 4. `wigner`: entry (r, j) is zero unless edge-frame row r and coefficient j have the same degree.
All inputs are finite; a program needn't handle non-finite values.
Results may differ from a plain program's by a relative error of at most 0.0057.
Values may be sent and summed in bfloat16 or wider, within the bound.
No kernel may reach another device: no remote copies, remote signals or barrier semaphores. Data moves between devices by JAX's collectives and lax.ppermute only.
A program may use at most 128 MiB of HBM per device.

v0:
```python
import jax
import jax.numpy as jnp
from jax import lax
from jax.sharding import PartitionSpec as P

C = 128
COEF = 49
MROWS = 29
BLK = 64


def shifted(value, axis, steps):
    count = lax.axis_size(axis)
    pairs = [(source, (source + steps) % count) for source in range(count)]
    return lax.ppermute(value, axis, pairs)


def product_bf(left_side, right_side):
    return jnp.dot(left_side, right_side, preferred_element_type=jnp.float32)


def convolve(features, filters, weights):
    w_zero, w_one_real, w_one_imag, w_two_real, w_two_imag = weights
    number = features.shape[0]
    doubled = features.shape[2]
    channels = doubled // 2

    def section(first_row, final_row):
        return features[:, first_row:final_row, :].reshape(
            number, (final_row - first_row) * doubled
        )

    order_zero = section(0, 7)
    plus_one = section(7, 13)
    minus_one = section(13, 19)
    plus_two = section(19, 24)
    minus_two = section(24, 29)
    pieces = [
        product_bf(order_zero, w_zero).reshape(number, 7, channels),
        (product_bf(plus_one, w_one_real) - product_bf(minus_one, w_one_imag)).reshape(
            number, 6, channels
        ),
        (product_bf(minus_one, w_one_real) + product_bf(plus_one, w_one_imag)).reshape(
            number, 6, channels
        ),
        (product_bf(plus_two, w_two_real) - product_bf(minus_two, w_two_imag)).reshape(
            number, 5, channels
        ),
        (product_bf(minus_two, w_two_real) + product_bf(plus_two, w_two_imag)).reshape(
            number, 5, channels
        ),
    ]
    joined = jnp.concatenate(pieces, axis=1)
    return (joined * filters[:, None, :].astype(jnp.float32)).astype(jnp.bfloat16)


def turn_in(matrices, pairs):
    return jnp.einsum("nij,njc->nic", matrices, pairs, preferred_element_type=jnp.float32).astype(
        jnp.bfloat16
    )


def turn_back(message, matrices, targets, num_atoms):
    back = jnp.einsum("nij,nic->njc", matrices, message, preferred_element_type=jnp.float32)
    flat = back.reshape(back.shape[0], back.shape[1] * back.shape[2])
    return jax.ops.segment_sum(flat, targets, num_segments=num_atoms)


def body(
    node_embed,
    wigner,
    source,
    target,
    rotation,
    edge_filter,
    edge_count,
    w_zero,
    w_one_real,
    w_one_imag,
    w_two_real,
    w_two_imag,
    atom_struct,
    struct_task,
    task_head,
):
    weights = (
        lax.all_gather(w_zero, "task", axis=0, tiled=True),
        lax.all_gather(w_one_real, "task", axis=0, tiled=True),
        lax.all_gather(w_one_imag, "task", axis=0, tiled=True),
        lax.all_gather(w_two_real, "task", axis=0, tiled=True),
        lax.all_gather(w_two_imag, "task", axis=0, tiled=True),
    )
    num_atoms = node_embed.shape[0]
    slots_all = source.shape[0]
    per_block = BLK
    blocks_all = slots_all // per_block
    channels = C
    cube = node_embed.reshape(num_atoms, COEF, channels)
    limit = edge_count[0]
    live = (jnp.arange(slots_all, dtype=jnp.int32) < limit)[:, None]
    filters = jnp.where(live, edge_filter, jnp.zeros_like(edge_filter))

    def endpoints(first_row, final_row):
        return jnp.concatenate(
            (
                jnp.take(cube, source[first_row:final_row], axis=0),
                jnp.take(cube, target[first_row:final_row], axis=0),
            ),
            axis=2,
        )

    def wigner_rows(first_row, final_row):
        return jnp.take(wigner, rotation[first_row:final_row], axis=0)

    partner = lax.axis_size("mol") // 2
    keep_blocks = (blocks_all + 1) // 2
    spare_blocks = blocks_all - keep_blocks
    split_row = keep_blocks * per_block
    live_blocks = (limit + per_block - 1) // per_block
    tail_target = target[split_row:]
    tail_rotation = rotation[split_row:]
    tail_filters = filters[split_row:]
    tail_matrices = wigner_rows(split_row, slots_all)
    got_pairs, got_rotation, got_target, got_filters = shifted(
        (endpoints(split_row, slots_all), tail_rotation, tail_target, tail_filters), "mol", partner
    )
    got_matrices = jnp.take(wigner, got_rotation, axis=0)
    got_features = turn_in(got_matrices, got_pairs)
    head_matrices = wigner_rows(0, split_row)
    head_features = turn_in(head_matrices, endpoints(0, split_row))
    pool_features = jnp.concatenate((head_features, got_features), axis=0).reshape(
        blocks_all, per_block, MROWS, 2 * channels
    )
    pool_filters = jnp.concatenate((filters[:split_row], got_filters), axis=0).reshape(
        blocks_all, per_block, channels
    )
    slot_ids = jnp.arange(keep_blocks, dtype=jnp.int32)
    borrowed = slot_ids >= live_blocks
    offset = slot_ids - live_blocks
    picks = jnp.where(borrowed, keep_blocks + jnp.clip(offset, 0, spare_blocks - 1), slot_ids)
    usable = jnp.logical_or(jnp.logical_not(borrowed), offset < spare_blocks)
    chosen_features = jnp.take(pool_features, picks, axis=0).reshape(split_row, MROWS, 2 * channels)
    picked_filters = jnp.take(pool_filters, picks, axis=0)
    chosen_filters = jnp.where(
        usable[:, None, None], picked_filters, jnp.zeros_like(picked_filters)
    ).reshape(split_row, channels)
    messages = convolve(chosen_features, chosen_filters, weights).reshape(
        keep_blocks, per_block, MROWS, channels
    )
    own_messages = jnp.where(
        borrowed[:, None, None, None], jnp.zeros_like(messages), messages
    ).reshape(split_row, MROWS, channels)
    summed = turn_back(own_messages, head_matrices, target[:split_row], num_atoms)
    back_ids = live_blocks + jnp.arange(spare_blocks, dtype=jnp.int32)
    picked_back = jnp.take(messages, jnp.clip(back_ids, 0, keep_blocks - 1), axis=0)
    reply = jnp.where(
        (back_ids < keep_blocks)[:, None, None, None], picked_back, jnp.zeros_like(picked_back)
    )
    returned = shifted(reply, "mol", partner)
    summed = summed + turn_back(
        returned.reshape(slots_all - split_row, MROWS, channels),
        tail_matrices,
        target[split_row:],
        num_atoms,
    )
    update = summed.astype(jnp.bfloat16)
    struct_number = struct_task.shape[0]
    task_match = (
        struct_task[:, None] == jnp.arange(task_head.shape[0], dtype=jnp.int32)[None, :]
    ).astype(jnp.float32)
    struct_head = jnp.sum(task_match[:, :, None] * task_head[None, :, :], axis=1)
    member = (atom_struct[:, None] == jnp.arange(struct_number, dtype=jnp.int32)[None, :]).astype(
        jnp.float32
    )
    atom_head = jnp.sum(member[:, :, None] * struct_head[None, :, :], axis=1)
    scalar_part = node_embed[:, :channels].astype(jnp.float32) + summed[:, :channels]
    per_atom = jnp.sum(scalar_part * atom_head, axis=1)
    energy = jnp.sum(member * per_atom[:, None], axis=0)
    return (update, energy)


def solution(mesh):
    in_specs = (
        P(("mol", "task"), None),
        P(),
        P(("mol", "task")),
        P(("mol", "task")),
        P(("mol", "task")),
        P(("mol", "task"), None),
        P(("mol", "task")),
        P("task", None),
        P("task", None),
        P("task", None),
        P("task", None),
        P("task", None),
        P(("mol", "task")),
        P(("mol", "task")),
        P(),
    )
    out_specs = (P(("mol", "task"), None), P(("mol", "task")))
    return jax.shard_map(body, mesh=mesh, in_specs=in_specs, out_specs=out_specs, check_vma=False)
```

profile of v0, /device:TPU:1, one launch (start us, length us, event | category | flops | bytes accessed | tf_op | source)
XLA Modules:
  0.0 462.2 jit_solution(877452829610913151)
XLA Ops:
  10.0 1.4 reshape.267
  11.4 0.7 compare_and_fusion.1
  12.1 0.7 gather_fusion.6
  12.9 0.7 gather_fusion.7
  14.2 1.6 copy.116
  15.8 3.6 collective-permute-start.1
  20.3 3.0 collective-permute-start.2
  23.4 0.9 gather_fusion.4
  24.4 2.1 gather_fusion.3
  27.4 1.5 broadcast_select_fusion
  28.9 1.5 broadcast_select_fusion.1
  30.9 3.7 copy.114
  34.8 0.8 gather_fusion
  35.6 1.4 gather_fusion.8
  37.0 4.4 fusion.4
  41.7 11.8 %collective-permute-done = s32[64]{0:T(128)S(1)} collective-permute-done((s32[64]{0:T(128)S(1)}, s32[64]{0:T(128)S(1)}, u32[]{:S(2)}, u32[]{:S(2)}) %collective-permute-start) | collective-permute-done | bytes 288 | tf_op jit(solution)/shard_map/ppermute | solution.py:15
  55.4 0.7 fusion.33
  56.2 2.9 fusion.12
  59.4 1.7 copy.118
  61.1 2.0 gather_fusion.1
  63.1 1.7 copy.119
  65.6 0.8 fusion.46
  66.5 1.9 copy.124
  68.4 0.9 copy.123
  69.3 1.0 copy.120
  70.3 17.3 %all-gather.12.cloned.1.call-done = bf16[1280,640]{1,0:T(8,128)(2,1)} async-done(((bf16[40,640]{1,0:T(8,128)(2,1)}), bf16[1280,640]{1,0:T(8,128)(2,1)}) %all-gather.12.cloned.1.call-update) | async-done | bytes 1638416 | tf_op jit(solution)/shard_map/all_gather | solution.py:90
  87.5 1.9 fusion.50
  89.4 75.6 %all-gather.14.cloned.1.call-done = bf16[1280,640]{1,0:T(8,128)(2,1)} async-done(((bf16[40,640]{1,0:T(8,128)(2,1)}), bf16[1280,640]{1,0:T(8,128)(2,1)}) %all-gather.14.cloned.1.call-update) | async-done | bytes 1638416 | tf_op jit(solution)/shard_map/all_gather | solution.py:91
  165.0 2.7 convolution_add_fusion.1
  167.7 1.9 concatenate.50
  169.7 1.8 copy.130
  171.5 1.5 fusion.49
  173.5 0.9 concatenate.49
  174.6 0.9 copy.134
  175.5 0.9 copy.133
  176.4 67.8 %all-gather.8.cloned.1.call-done = bf16[1536,768]{1,0:T(8,128)(2,1)} async-done(((bf16[48,768]{1,0:T(8,128)(2,1)}), bf16[1536,768]{1,0:T(8,128)(2,1)}) %all-gather.8.cloned.1.call-update) | async-done | bytes 2359312 | tf_op jit(solution)/shard_map/all_gather | solution.py:88
  244.2 2.9 fusion.48
  247.1 75.1 %all-gather.10.cloned.1.call-done = bf16[1536,768]{1,0:T(8,128)(2,1)} async-done(((bf16[48,768]{1,0:T(8,128)(2,1)}), bf16[1536,768]{1,0:T(8,128)(2,1)}) %all-gather.10.cloned.1.call-update) | async-done | bytes 2359312 | tf_op jit(solution)/shard_map/all_gather | solution.py:89
  322.2 2.4 convolution_add_fusion
  324.6 0.8 concatenate.48
  325.5 0.9 copy.126
  326.9 1.1 copy-done.1
  328.6 0.9 concatenate.47
  329.6 0.9 copy.132
  330.5 0.9 copy.131
  331.5 70.3 %all-gather.6.cloned.1.call-done = bf16[1792,896]{1,0:T(8,128)(2,1)} async-done(((bf16[56,896]{1,0:T(8,128)(2,1)}), bf16[1792,896]{1,0:T(8,128)(2,1)}) %all-gather.6.cloned.1.call-update) | async-done | bytes 3211280 | tf_op jit(solution)/shard_map/all_gather | solution.py:87
  401.8 4.5 copy.121
  406.3 2.9 constant_dynamic-update-slice_fusion.4
  409.5 10.6 %concatenate.51 = f32[2,64,29,128]{3,2,1,0:T(8,128)S(1)} concatenate(f32[2,64,7,128]{3,2,1,0:T(8,128)S(1)} %copy.139, f32[2,64,6,128]{3,2,1,0:T(8,128)} %concatenate.47, f32[2,64,6,128]{3,2,1,0:T(8,128)} %concatenate.48, f32[2,64,5,128]{3,2,1,0:T(8,128)} %concatenate.49, f32[2,64,5,128]{3,2,1,0:T(8,128)} %concatenate.50), dimensions={2} | concatenate | bytes 3801088 | tf_op jit(solution)/shard_map/concatenate | solution.py:53
  420.1 0.9 fusion.23
  421.0 2.7 collective-permute-start.3
  423.7 0.8 constant_dynamic-update-slice_fusion.3
  424.5 0.8 constant_dynamic-update-slice_fusion.2
  425.3 0.8 constant_dynamic-update-slice_fusion.1
  426.1 0.8 constant_dynamic-update-slice_fusion
  426.8 1.9 fusion.18
  428.7 3.9 fusion.16
  432.6 3.7 copy.136
  436.3 3.1 copy.137
  439.4 6.9 %scatter_custom_fusion = f32[48,6272]{1,0:T(8,128)} fusion(s32[128]{0:T(128)S(1)} %slice-done.1, f32[128,6272]{1,0:T(8,128)} %copy.137, f32[]{:T(128)} %constant.91.clone.1), kind=kCustom, calls=%fused_computation.41 | custom fusion | flops 802816 | bytes 1204736 | tf_op jit(solution)/shard_map/scatter-add | solution.py:66
  446.3 2.4 fusion.24
  448.7 3.2 scatter_custom_fusion.1
  452.0 2.2 fusion.44
  454.2 0.8 fusion.35
  (131 shorter events, 11.3 us)
Async XLA Ops:
  7.2 80.4 %all-gather.12.cloned.1.call-start = ((), (), s32[]{:S(2)}) async-start(), calls=%async_computation.3 | async-start | bytes 1689600 | tf_op jit(solution)/shard_map/all_gather | solution.py:90
  7.9 157.1 %all-gather.14.cloned.1.call-start = ((), (), s32[]{:S(2)}) async-start(), calls=%async_computation.4 | async-start | bytes 1689600 | tf_op jit(solution)/shard_map/all_gather | solution.py:91
  8.6 235.5 %all-gather.8.cloned.1.call-start = ((), (), s32[]{:S(2)}) async-start(), calls=%async_computation.1 | async-start | bytes 2433024 | tf_op jit(solution)/shard_map/all_gather | solution.py:88
  9.4 312.9 %all-gather.10.cloned.1.call-start = ((), (), s32[]{:S(2)}) async-start(), calls=%async_computation.2 | async-start | bytes 2433024 | tf_op jit(solution)/shard_map/all_gather | solution.py:89
  10.0 391.8 %all-gather.6.cloned.1.call-start = ((), (), s32[]{:S(2)}) async-start(), calls=%async_computation | async-start | bytes 3311616 | tf_op jit(solution)/shard_map/all_gather | solution.py:87
  14.2 5.2 %copy-start.30 = (s32[192]{0:T(256)S(1)}, s32[192]{0:T(256)}, u32[]{:S(2)}) copy-start(s32[192]{0:T(256)} %param.25) | copy-start | bytes 2308
  14.2 5.9 %copy-start.24 = (bf16[192,128]{1,0:T(8,128)(2,1)S(1)}, bf16[192,128]{1,0:T(8,128)(2,1)}, u32[]{:S(2)}) copy-start(bf16[192,128]{1,0:T(8,128)(2,1)} %param.26) | copy-start | bytes 147460
  14.2 9.1 %copy-start.26 = (s32[192]{0:T(256)S(1)}, s32[192]{0:T(256)}, u32[]{:S(2)}) copy-start(s32[192]{0:T(256)} %param.23) | copy-start | bytes 2308
  14.2 9.1 %copy-start.27 = (s32[192]{0:T(256)S(1)}, s32[192]{0:T(256)}, u32[]{:S(2)}) copy-start(s32[192]{0:T(256)} %param.24) | copy-start | bytes 2308
  15.8 40.4 %collective-permute-start.1 = (bf16[64,49,256]{2,0,1:T(8,128)(2,1)}, bf16[64,49,256]{2,0,1:T(8,128)(2,1)}, u32[]{:S(2)}, u32[]{:S(2)}) collective-permute-start(bf16[64,49,256]{2,0,1:T(8,128)(2,1)} %copy.116), channel_id=1, source_target_pairs={{0,128},{32,160},{64,192},{96,224},{128,0},{160,32},{192,64},{224,... | collective-permute-start | bytes 4816904 | tf_op jit(solution)/shard_map/ppermute | solution.py:15
  19.4 34.1 %collective-permute-start = (s32[64]{0:T(128)S(1)}, s32[64]{0:T(128)S(1)}, u32[]{:S(2)}, u32[]{:S(2)}) collective-permute-start(s32[64]{0:T(128)S(1)} %slice.51), channel_id=1, source_target_pairs={{0,128},{32,160},{64,192},{96,224},{128,0},{160,32},{192,64},{224,... | collective-permute-start | bytes 776 | tf_op jit(solution)/shard_map/ppermute | solution.py:15
  20.2 10.2 %copy-start.21 = (bf16[192,128]{1,0:T(8,128)(2,1)}, bf16[192,128]{1,0:T(8,128)(2,1)S(1)}, u32[]{:S(2)}) copy-start(bf16[192,128]{1,0:T(8,128)(2,1)S(1)} %broadcast_select_fusion.7) | copy-start | bytes 147460
  20.3 33.9 %collective-permute-start.2 = (bf16[64,128]{1,0:T(8,128)(2,1)S(1)}, bf16[64,128]{1,0:T(8,128)(2,1)S(1)}, u32[]{:S(2)}, u32[]{:S(2)}) collective-permute-start(bf16[64,128]{1,0:T(8,128)(2,1)S(1)} %slice.98), channel_id=1, source_target_pairs={{0,128},{32,160},{64,192},{96,224},{128,0},{160,32},{192,64},{224,... | collective-permute-start | bytes 49160 | tf_op jit(solution)/shard_map/ppermute | solution.py:15
  24.3 2.2 copy-start.28
  24.4 2.2 copy-start.29
  24.4 2.2 copy-start.25
  26.5 2.4 copy-start.2
  28.9 2.1 copy-start.19
  35.6 5.8 %copy-start.5 = (bf16[128,29,49]{2,1,0:T(8,128)(2,1)}, bf16[128,29,49]{2,1,0:T(8,128)(2,1)S(1)}, u32[]{:S(2)}) copy-start(bf16[128,29,49]{2,1,0:T(8,128)(2,1)S(1)} %gather_fusion) | copy-start | bytes 1091332
  37.0 17.2 %slice-start = ((bf16[192,128]{1,0:T(8,128)(2,1)}), bf16[128,128]{1,0:T(8,128)(2,1)S(1)}, s32[]{:S(2)}) async-start(bf16[192,128]{1,0:T(8,128)(2,1)} %copy-done.21), calls=%async_computation.5 | async-start | bytes 65536 | tf_op jit(solution)/shard_map/slice | solution.py:134
  54.1 4.9 %copy-start.12 = (bf16[128,29,256]{2,1,0:T(8,128)(2,1)S(1)}, bf16[128,29,256]{2,1,0:T(8,128)(2,1)}, u32[]{:S(2)}) copy-start(bf16[128,29,256]{2,1,0:T(8,128)(2,1)} %fusion.4) | copy-start | bytes 5701636
  65.4 22.2 %copy-start.9 = (bf16[128,5,256]{0,2,1:T(8,128)(2,1)}, bf16[128,5,256]{0,2,1:T(8,128)(2,1)S(1)}, u32[]{:S(2)}) copy-start(bf16[128,5,256]{0,2,1:T(8,128)(2,1)S(1)} %copy.128) | copy-start | bytes 983044
  65.6 99.4 %copy-start.11 = (bf16[128,5,256]{0,2,1:T(8,128)(2,1)}, bf16[128,5,256]{0,2,1:T(8,128)(2,1)S(1)}, u32[]{:S(2)}) copy-start(bf16[128,5,256]{0,2,1:T(8,128)(2,1)S(1)} %copy.127) | copy-start | bytes 983044
  165.0 6.5 %copy-start.3 = (bf16[1280,640]{1,0:T(8,128)(2,1)S(1)}, bf16[1280,640]{1,0:T(8,128)(2,1)}, u32[]{:S(2)}) copy-start(bf16[1280,640]{1,0:T(8,128)(2,1)} %all-gather.12.cloned.1.call-done) | copy-start | bytes 4915204
  167.7 5.3 %copy-start.4 = (bf16[1280,640]{1,0:T(8,128)(2,1)S(1)}, bf16[1280,640]{1,0:T(8,128)(2,1)}, u32[]{:S(2)}) copy-start(bf16[1280,640]{1,0:T(8,128)(2,1)} %all-gather.14.cloned.1.call-done) | copy-start | bytes 4915204
  171.5 1.5 copy-start.10
  173.0 1.5 copy-start.18
  173.5 70.6 %copy-start.7 = (bf16[128,6,256]{0,2,1:T(8,128)(2,1)S(1)}, bf16[128,6,256]{0,2,1:T(8,128)(2,1)}, u32[]{:S(2)}) copy-start(bf16[128,6,256]{0,2,1:T(8,128)(2,1)} %copy.124) | copy-start | bytes 1179652
  175.5 146.8 %copy-start.8 = (bf16[128,6,256]{0,2,1:T(8,128)(2,1)S(1)}, bf16[128,6,256]{0,2,1:T(8,128)(2,1)}, u32[]{:S(2)}) copy-start(bf16[128,6,256]{0,2,1:T(8,128)(2,1)} %copy.123) | copy-start | bytes 1179652
  322.2 4.2 copy-start
  326.4 1.7 copy-start.1
  328.1 1.5 copy-start.15
  409.5 10.6 %copy-start.22 = (f32[1,64,128]{2,1,0:T(8,128)S(1)}, f32[1,64,128]{2,1,0:T(8,128)}, u32[]{:S(2)}) copy-start(f32[1,64,128]{2,1,0:T(8,128)} %constant_dynamic-slice_fusion) | copy-start | bytes 98308
  409.5 14.2 %copy-start.14 = (f32[128,6,128]{2,0,1:T(8,128)S(1)}, f32[128,6,128]{2,0,1:T(8,128)}, u32[]{:S(2)}) copy-start(f32[128,6,128]{2,0,1:T(8,128)} %copy.131) | copy-start | bytes 1179652
  420.1 4.4 copy-start.13
  420.1 5.2 %copy-start.17 = (f32[128,5,128]{2,0,1:T(8,128)S(1)}, f32[128,5,128]{2,0,1:T(8,128)}, u32[]{:S(2)}) copy-start(f32[128,5,128]{2,0,1:T(8,128)} %copy.133) | copy-start | bytes 983044
  420.1 5.9 %copy-start.16 = (f32[128,5,128]{2,0,1:T(8,128)S(1)}, f32[128,5,128]{2,0,1:T(8,128)}, u32[]{:S(2)}) copy-start(f32[128,5,128]{2,0,1:T(8,128)} %copy.134) | copy-start | bytes 983044
  420.1 6.7 %copy-start.20 = (f32[128,128]{1,0:T(8,128)S(1)}, f32[128,128]{1,0:T(8,128)}, u32[]{:S(2)}) copy-start(f32[128,128]{1,0:T(8,128)} %fusion.33) | copy-start | bytes 196612
  421.0 25.3 %collective-permute-start.3 = (bf16[1,64,29,128]{3,2,1,0:T(8,128)(2,1)}, bf16[1,64,29,128]{3,2,1,0:T(8,128)(2,1)}, u32[]{:S(2)}, u32[]{:S(2)}) collective-permute-start(bf16[1,64,29,128]{3,2,1,0:T(8,128)(2,1)} %fusion.23), channel_id=1, source_target_pairs={{0,128},{32,160},{64,192},{96,224},{128,0},{160,32},{192,64},{224,... | collective-permute-start | bytes 1425416 | tf_op jit(solution)/shard_map/ppermute | solution.py:15
  426.1 2.6 copy-start.6
  436.3 3.2 slice-start.1
  452.0 2.3 copy-start.23
Sparse Core Ops, SparseCore 0:
  10.6 76.8 all-gather.11
  90.1 74.8 all-gather.13
  167.6 76.5 all-gather.7
  246.6 75.5 all-gather.9
  324.7 77.0 all-gather.5
where the time goes:
time: 466 us; the launch traced here: 462 us
  waiting for transfers between devices  320 us (69%)
  local copies, waits for them, and re-layouts  64.6 us (14%)
  matrix products  29.3 us (6%)
  other arithmetic  23.2 us (5%)
  between operations  15.1 us (3%)
  starting transfers between devices  9.53 us (2%)
    all_gather x1, waiting for transfers between devices, body(): lax.all_gather(w_two_imag, 'task', axis=0, tiled=True)  75.6 us
    all_gather x1, waiting for transfers between devices, body(): lax.all_gather(w_one_imag, 'task', axis=0, tiled=True)  75.1 us
    all_gather x1, waiting for transfers between devices, body(): lax.all_gather(w_zero, 'task', axis=0, tiled=True)  70.3 us
    all_gather x1, waiting for transfers between devices, body(): lax.all_gather(w_one_real, 'task', axis=0, tiled=True)  67.8 us
    concatenate x11, local copies, waits for them, and re-layouts, convolve(): joined = jnp.concatenate(pieces, axis=1)  19.7 us
    all_gather x1, waiting for transfers between devices, body(): lax.all_gather(w_two_real, 'task', axis=0, tiled=True)  17.3 us
    dot_general x9, matrix products, product_bf(): return jnp.dot(left_side, right_side, preferred_element_type=jnp.float32)  15.8 us
    ppermute x4, waiting for transfers between devices, shifted(): return lax.ppermute(value, axis, pairs)  11.8 us
  transfers between devices with their start and end apart: 9, of which 6 were waited for; matrix products, arithmetic and copies ran while one was open for 19% of the time, Pallas kernels for 0%

commit v1 on v0

v1 whole, which is shorter than its diff:
```python
import jax
import jax.numpy as jnp
from jax import lax
from jax.experimental import pallas as pl
from jax.experimental.pallas import tpu as pltpu
from jax.sharding import PartitionSpec as P

C = 128
COEF = 49
MROWS = 29
EDGES = 192
ATOMS = 48
NROT = 256
FLAT = MROWS * COEF
TILES = 86
VMEM = pltpu.VMEM
SMEM = pltpu.SMEM
BF = jnp.bfloat16
F32 = jnp.float32

ROWS = [[degree] for degree in range(7)]
for degree in range(1, 7):
    ROWS[degree] += [6 + degree, 12 + degree]
for degree in range(2, 7):
    ROWS[degree] += [17 + degree, 22 + degree]

MADE = (
    tuple(range(7, 19)) + (0, 1, 29),
    tuple(range(19, 29)) + (2, 3, 4, 5, 6),
)

H0 = ((0, 0), (0, -1))
H1 = ((0, 1), (0, 2))
U = (
    ((0, 0), (-1, 0)),
    ((1, 0), (4, 0)),
    ((-2, 0), (3, 0)),
    ((2, 0), (-3, 0)),
)


def moved(blocks, z, y):
    return [(a + z, b + y) for a, b in blocks]


def block_offsets():
    first = moved(H0, 0, 0) + moved(H1, 0, 0)
    for step in (1, 2, 3):
        for half in (H0, H1):
            first += moved(half, -step, 0) + moved(half, step, 0)
    first += moved(H0, -4, 0) + moved(H1, 4, 0)
    second = moved(U[0], 0, 0) + moved(U[1], 0, 0) + moved(U[2], 0, 0) + moved(U[3], 0, 0)
    for part in U:
        second += moved(part, 0, -1) + moved(part, 0, 1)
    second += moved(U[0], 0, -2) + moved(U[2], 0, 2)
    second += moved(U[1], 0, -2) + moved(U[3], 0, 2)
    return first, second


def feature_kernel(
    core, node, wig, source, target, rotation, filt, own, send, d_out, xs, xt, fz, fa, ff, sem
):
    hot_s = (source[...] == lax.broadcasted_iota(jnp.int32, (EDGES, ATOMS), 1)).astype(BF)
    hot_t = (target[...] == lax.broadcasted_iota(jnp.int32, (EDGES, ATOMS), 1)).astype(BF)
    hot_r = (rotation[...] == lax.broadcasted_iota(jnp.int32, (EDGES, NROT), 1)).astype(BF)
    d_out[...] = jnp.dot(hot_r, wig[...], preferred_element_type=F32)
    for part in range(7):
        cols = pl.ds(part * 896, 896)
        xs[:, cols] = jnp.dot(hot_s, node[:, cols], preferred_element_type=F32)
        xt[:, cols] = jnp.dot(hot_t, node[:, cols], preferred_element_type=F32)
    ff[:, :C] = filt[...]
    ff[:, C:] = filt[...]
    is_second = core[0]
    base_one = is_second * 12
    base_two = (1 - is_second) * 12

    def one_block(block, carry):
        rows = pl.ds(pl.multiple_of(block * 16, 16), 16)
        for degree in range(7):
            sums = {}
            for j in range(degree * degree, (degree + 1) * (degree + 1)):
                a = xs[rows, j * C : (j + 1) * C]
                b = xt[rows, j * C : (j + 1) * C]
                for r in ROWS[degree]:
                    k = r * COEF + j
                    d = jnp.broadcast_to(d_out[rows, k : k + 1], (16, C))
                    if r in sums:
                        sums[r] = (sums[r][0] + d * a, sums[r][1] + d * b)
                    else:
                        sums[r] = (d * a, d * b)
            for r in ROWS[degree]:
                one, two = (v.astype(BF) for v in sums[r])
                if r < 7:
                    ref, plane = fz, r
                elif r < 19:
                    ref, plane = fa, base_one + (r - 7)
                else:
                    q = r - 19
                    ref, plane = fa, base_two + (q // 5) * 6 + q % 5
                ref[plane, rows, :C] = one
                ref[plane, rows, C:] = two
        return carry

    lax.fori_loop(0, EDGES // 16, one_block, 0)
    copies = []
    for place, out in ((0, own), (12, send)):
        copies += [
            pltpu.make_async_copy(fz, out.at[pl.ds(0, 7)], sem.at[len(copies)]),
            pltpu.make_async_copy(
                fa.at[pl.ds(place, 12)], out.at[pl.ds(7, 12)], sem.at[len(copies) + 1]
            ),
            pltpu.make_async_copy(ff, out.at[19], sem.at[len(copies) + 2]),
        ]
    for copy in copies:
        copy.start()
    for copy in copies:
        copy.wait()


def features(core, node, wig, source, target, rotation, filt):
    vm = pl.BlockSpec(memory_space=VMEM)
    anywhere = pl.BlockSpec(memory_space=pl.ANY)
    return pl.pallas_call(
        feature_kernel,
        out_shape=(
            jax.ShapeDtypeStruct((20, EDGES, 2 * C), BF),
            jax.ShapeDtypeStruct((20, EDGES, 2 * C), BF),
            jax.ShapeDtypeStruct((EDGES, FLAT), F32),
        ),
        in_specs=[pl.BlockSpec(memory_space=SMEM)] + [vm] * 6,
        out_specs=(anywhere, anywhere, vm),
        scratch_shapes=[
            VMEM((EDGES, COEF * C), F32),
            VMEM((EDGES, COEF * C), F32),
            VMEM((7, EDGES, 2 * C), BF),
            VMEM((24, EDGES, 2 * C), BF),
            VMEM((EDGES, 2 * C), BF),
            pltpu.SemaphoreType.DMA((6,)),
        ],
        compiler_params=pltpu.CompilerParams(vmem_limit_bytes=40 * 2**20),
        cost_estimate=pl.CostEstimate(flops=6 * 10**9, bytes_accessed=8 * 10**6, transcendentals=0),
        name="features",
    )(core, node, wig, source, target, rotation, filt)


def weight_rows(ref, groups, first, count, g):
    per_tile = ref.at[pl.ds(first * groups, count * groups)].reshape(count, groups, 8, C)
    return per_tile[:, g].reshape(count * 8, C)


def conv_kernel(core, shard, *refs):
    blocks = refs[:18]
    own, got, mine, other, wa, wb, wc, xz, xa, fl, wsem, fsem = refs[18:]

    def fetch(per_shard):
        copies = []
        index = 0
        for block in blocks:
            for part in range(block.shape[0] // TILES):
                t = shard[index]
                first = part * TILES
                for dst, count in zip((wa, wb, wc), per_shard):
                    copies.append(
                        pltpu.make_async_copy(
                            block.at[pl.ds(first, count)],
                            dst.at[pl.ds(t * count, count)],
                            wsem.at[len(copies)],
                        )
                    )
                    first += count
                index += 1
        return copies

    def fetch_features(pieces):
        copies = []
        for who, src in enumerate((own, got)):
            for k in range(7):
                copies.append(
                    pltpu.make_async_copy(
                        src.at[k], xz.at[k, pl.ds(who * EDGES, EDGES)], fsem.at[len(copies)]
                    )
                )
            for sign in range(2):
                for k in range(pieces):
                    copies.append(
                        pltpu.make_async_copy(
                            src.at[7 + sign * 6 + k],
                            xa.at[k, pl.ds((sign * 2 + who) * EDGES, EDGES)],
                            fsem.at[len(copies)],
                        )
                    )
            copies.append(
                pltpu.make_async_copy(
                    src.at[19], fl.at[pl.ds(who * EDGES, EDGES)], fsem.at[len(copies)]
                )
            )
        return copies

    def finish(plane, value, filters):
        message = (value * filters).astype(BF)
        mine[plane] = message[:EDGES]
        other[plane] = message[EDGES:]

    def run(pieces, zero_groups, per_shard):
        waits = fetch_features(pieces) + fetch(per_shard)
        for copy in waits:
            copy.start()
        for copy in waits:
            copy.wait()
        filters = fl[:, :C].astype(F32)

        def column(g, carry):
            real = jnp.zeros((4 * EDGES, C), F32)
            imag = jnp.zeros((4 * EDGES, C), F32)
            for k in range(pieces):
                x = xa[k]
                real += jnp.dot(x, weight_rows(wa, pieces, k * 32, 32, g), preferred_element_type=F32)
                imag += jnp.dot(x, weight_rows(wb, pieces, k * 32, 32, g), preferred_element_type=F32)
            half = 2 * EDGES
            finish(g, real[:half] - imag[half:], filters)
            finish(pieces + g, real[half:] + imag[:half], filters)
            return carry

        lax.fori_loop(0, pieces, column, 0)

        def zero_column(g, carry):
            total = jnp.zeros((2 * EDGES, C), F32)
            for k in range(7):
                total += jnp.dot(
                    xz[k], weight_rows(wc, zero_groups, k * 32, 32, g), preferred_element_type=F32
                )
            finish(2 * pieces + g, total, filters)
            return carry

        lax.fori_loop(0, zero_groups, zero_column, 0)

    @pl.when(core[0] == 0)
    def _():
        run(6, 2, (36, 36, 14))

    @pl.when(core[0] == 1)
    def _():
        run(5, 5, (25, 25, 35))


def convolve(core, shard, blocks, own, got):
    vm = pl.BlockSpec(memory_space=VMEM)
    anywhere = pl.BlockSpec(memory_space=pl.ANY)
    smem = pl.BlockSpec(memory_space=SMEM)
    out = jax.ShapeDtypeStruct((15, EDGES, C), BF)
    return pl.pallas_call(
        conv_kernel,
        out_shape=(out, out),
        in_specs=[smem, smem] + [anywhere] * 20,
        out_specs=(vm, vm),
        scratch_shapes=[
            VMEM((32 * 36, 8, C), BF),
            VMEM((32 * 36, 8, C), BF),
            VMEM((32 * 35, 8, C), BF),
            VMEM((7, 2 * EDGES, 2 * C), BF),
            VMEM((6, 4 * EDGES, 2 * C), BF),
            VMEM((2 * EDGES, 2 * C), BF),
            pltpu.SemaphoreType.DMA((96,)),
            pltpu.SemaphoreType.DMA((40,)),
        ],
        compiler_params=pltpu.CompilerParams(vmem_limit_bytes=40 * 2**20),
        cost_estimate=pl.CostEstimate(flops=4 * 10**9, bytes_accessed=12 * 10**6, transcendentals=0),
        name="convolve",
    )(core, shard, *blocks, own, got)


def back_kernel(
    place_mine, place_got, task, mine, got, d, target, node, struct, head, update, energy, m, hi, lo, sem
):
    copies = []
    for i in range(15):
        copies.append(pltpu.make_async_copy(mine.at[i], m.at[place_mine[i]], sem.at[2 * i]))
        copies.append(pltpu.make_async_copy(got.at[i], m.at[place_got[i]], sem.at[2 * i + 1]))
    for copy in copies:
        copy.start()
    for copy in copies:
        copy.wait()

    def one_block(block, carry):
        rows = pl.ds(pl.multiple_of(block * 16, 16), 16)
        for degree in range(7):
            parts = {r: m[r, rows, :].astype(F32) for r in ROWS[degree]}
            for j in range(degree * degree, (degree + 1) * (degree + 1)):
                total = None
                for r in ROWS[degree]:
                    k = r * COEF + j
                    term = jnp.broadcast_to(d[rows, k : k + 1], (16, C)) * parts[r]
                    total = term if total is None else total + term
                top = total.astype(BF)
                hi[rows, j * C : (j + 1) * C] = top
                lo[rows, j * C : (j + 1) * C] = (total - top.astype(F32)).astype(BF)
        return carry

    lax.fori_loop(0, EDGES // 16, one_block, 0)
    hot = (target[...] == lax.broadcasted_iota(jnp.int32, (ATOMS, EDGES), 0)).astype(BF)
    for part in range(7):
        cols = pl.ds(part * 896, 896)
        total = jnp.dot(hot, hi[:, cols], preferred_element_type=F32) + jnp.dot(
            hot, lo[:, cols], preferred_element_type=F32
        )
        update[:, cols] = total.astype(BF)
        if part == 0:
            scalar_part = node[:, :C].astype(F32) + total[:, :C]
    lane = lax.broadcasted_iota(jnp.int32, (1, C), 1)
    result = jnp.zeros((1, C), F32)
    for s in range(4):
        member = jnp.where(struct[...] == s, scalar_part, 0.0) * head[pl.ds(task[s], 1), :]
        value = jnp.sum(jnp.sum(member, axis=0, keepdims=True), axis=1, keepdims=True)
        result = jnp.where(lane == s, value, result)
    energy[...] = result


def turn_back(place_mine, place_got, task, mine, got, d, target, node, struct, head):
    vm = pl.BlockSpec(memory_space=VMEM)
    anywhere = pl.BlockSpec(memory_space=pl.ANY)
    smem = pl.BlockSpec(memory_space=SMEM)
    return pl.pallas_call(
        back_kernel,
        out_shape=(
            jax.ShapeDtypeStruct((ATOMS, COEF * C), BF),
            jax.ShapeDtypeStruct((1, C), F32),
        ),
        in_specs=[smem] * 3 + [anywhere] * 2 + [vm] * 5,
        out_specs=(vm, vm),
        scratch_shapes=[
            VMEM((30, EDGES, C), BF),
            VMEM((EDGES, COEF * C), BF),
            VMEM((EDGES, COEF * C), BF),
            pltpu.SemaphoreType.DMA((30,)),
        ],
        compiler_params=pltpu.CompilerParams(vmem_limit_bytes=40 * 2**20),
        cost_estimate=pl.CostEstimate(flops=10**9, bytes_accessed=4 * 10**6, transcendentals=0),
        name="turn_back",
    )(place_mine, place_got, task, mine, got, d, target, node, struct, head)


def exchange(value, sizes, steps_first, steps_second):
    mol, nz, ny = sizes
    pairs = []
    for device in range(mol * nz * ny):
        m, t = divmod(device, nz * ny)
        z, y = divmod(t, ny)
        dz, dy = steps_first if m % 2 == 0 else steps_second
        to = ((z + dz) % nz) * ny + (y + dy) % ny
        pairs.append((device, m * nz * ny + to))
    return lax.ppermute(value, ("mol", "task"), pairs)


def tiles_of(w):
    rows, cols = w.shape
    return w.reshape(rows // 8, 8, cols // C, C).transpose(0, 2, 1, 3).reshape(-1, 8, C)


def body(
    node_embed,
    wigner,
    source,
    target,
    rotation,
    edge_filter,
    edge_count,
    w_zero,
    w_one_real,
    w_one_imag,
    w_two_real,
    w_two_imag,
    atom_struct,
    struct_task,
    task_head,
):
    sizes = (8, 8, 4)
    core = lax.axis_index("mol") % 2
    task = lax.axis_index("task")
    z, y = task // 4, task % 4
    first = core == 0

    def pick(a, b):
        return jnp.where(first, a, b)

    zero_tiles = w_zero
    pack_first = jnp.concatenate(
        (tiles_of(w_one_real), tiles_of(w_one_imag), tiles_of(zero_tiles[:, : 2 * C]))
    )
    pack_second = jnp.concatenate(
        (
            tiles_of(w_two_real),
            tiles_of(w_two_imag),
            tiles_of(zero_tiles[:, 2 * C :]),
            jnp.zeros((1, 8, C), BF),
        )
    )
    b0 = pick(pack_first, pack_second)
    a1 = exchange(b0, sizes, (0, 1), (1, 0))
    a2 = exchange(b0, sizes, (0, -1), (-1, 0))
    a3 = exchange(b0, sizes, (0, 2), (4, 0))
    h0 = jnp.concatenate((b0, a1))
    h1 = jnp.concatenate((a2, a3))

    def forth(value, second=(0, 1)):
        return exchange(value, sizes, (1, 0), second)

    def aft(value, second=(0, -1)):
        return exchange(value, sizes, (-1, 0), second)

    p1p = forth(pick(h0, jnp.concatenate((a1, a3))), (1, 0))
    p1m = aft(pick(h0, h1), (-1, 0))
    s2 = pick(h1, h0)
    p2p, p2m = forth(s2), aft(s2)
    p3p, p3m = forth(pick(p1p, h1)), aft(pick(p1m, h1))
    p4p, p4m = forth(pick(p2p, p1p)), aft(pick(p2m, p1p))
    p5p, p5m = forth(pick(p3p, p1m)), aft(pick(p3m, p1m))
    p6p, p6m = forth(pick(p4p, p2p)), aft(p4m)
    p7p, p7m = forth(pick(p5p, p3p)), aft(pick(p6m, p5m))

    blocks = (b0, a1, a2, a3, p1p, p1m, p2p, p2m, p3p, p3m, p4p, p4m, p5p, p5m, p6p, p6m, p7p, p7m)
    offsets_first, offsets_second = block_offsets()
    table = jnp.asarray((offsets_first, offsets_second), jnp.int32)[core]
    shard = ((z + table[:, 0]) % 8) * 4 + (y + table[:, 1]) % 4

    live = (jnp.arange(EDGES, dtype=jnp.int32) < edge_count[0])[:, None]
    filters = jnp.where(live, edge_filter, jnp.zeros_like(edge_filter))
    core_vec = core.reshape(1).astype(jnp.int32)
    own, send, d = features(
        core_vec,
        node_embed,
        wigner.reshape(NROT, FLAT),
        source.reshape(EDGES, 1),
        target.reshape(EDGES, 1),
        rotation.reshape(EDGES, 1),
        filters,
    )
    swap = [(i, i ^ 1) for i in range(8)]
    got = lax.ppermute(send, "mol", swap)
    mine, other = convolve(core_vec, shard, blocks, own, got)
    back = lax.ppermute(other, "mol", swap)
    places = jnp.asarray(MADE, jnp.int32)
    update, energy = turn_back(
        places[core],
        places[1 - core],
        struct_task,
        mine,
        back,
        d,
        target.reshape(1, EDGES),
        node_embed,
        atom_struct.reshape(ATOMS, 1),
        task_head,
    )
    return update, energy[0, :4]


def solution(mesh):
    both = P(("mol", "task"))
    wide = P(("mol", "task"), None)
    rows = P("task", None)
    in_specs = (wide, P(), both, both, both, wide, both, rows, rows, rows, rows, rows, both, both, P())
    return jax.shard_map(
        body, mesh=mesh, in_specs=in_specs, out_specs=(wide, both), check_vma=False
    )
```

time: 466 us -> 129 us (0.28)
  waiting for transfers between devices: 320 us -> 19.5 us
  Pallas kernels: 0 us -> 51.8 us
  local copies, waits for them, and re-layouts: 64.6 us -> 17.7 us
  matrix products: 29.3 us -> 0 us
  starting transfers between devices: 9.53 us -> 32.7 us
  other arithmetic: 23.2 us -> 4.63 us
  between operations: 15.1 us -> 1.58 us
    all_gather x5 -> x0, waiting for transfers between devices: 306 us -> none  [the longest x1 75.6 us: body(): lax.all_gather(w_two_imag, 'task', axis=0, tiled=True)]
    pallas_call x0 -> x3, Pallas kernels: none -> 51.8 us  [the longest x1 22.6 us: convolve(): pl.pallas_call(conv_kernel, out_shape=(out, out), in_specs=[smem, smem] +...]
    dot_general x13 -> x0, matrix products: 29.3 us -> none  [the longest x9 15.8 us: product_bf(): return jnp.dot(left_side, right_side, preferred_element_type=jnp.float32)]
    ppermute x4 -> x19, starting transfers between devices: 9.34 us -> 32.7 us  [the longest x17 28.2 us: exchange(): return lax.ppermute(value, ('mol', 'task'), pairs)]
    concatenate x12 -> x2, local copies, waits for them, and re-layouts: 21.3 us -> 0.1 us  [the longest x1 0.07 us: body(): jnp.concatenate((tiles_of(w_two_real), tiles_of(w_two_imag), tiles_of(zer...]
    gather x11 -> x0, local copies, waits for them, and re-layouts: 12.2 us -> none  [the longest x2 3.68 us: body(): jnp.take(pool_features, picks, axis=0)]
    scatter-add x2 -> x0, other arithmetic: 10.1 us -> none  [turn_back(): return jax.ops.segment_sum(flat, targets, num_segments=num_atoms)]
    dot_general x2 -> x0, local copies, waits for them, and re-layouts: 8.2 us -> none  [the longest x1 4.55 us: product_bf(): return jnp.dot(left_side, right_side, preferred_element_type=jnp.float32)]
  transfers between devices with their start and end apart: 9 -> 19, of which waited for: 6 -> 9; matrix products, arithmetic and copies ran while one was open for 19% -> 5% of each run, Pallas kernels for 0% -> 11%
where the time goes in v1:
time: 129 us; the launch traced here: 128 us
  Pallas kernels  51.8 us (40%)
  starting transfers between devices  32.7 us (25%)
  waiting for transfers between devices  19.5 us (15%)
  local copies, waits for them, and re-layouts  17.7 us (14%)
  other arithmetic  4.63 us (4%)
  between operations  1.58 us (1%)
    ppermute x17, starting transfers between devices, exchange(): return lax.ppermute(value, ('mol', 'task'), pairs)  28.2 us
    pallas_call x1, Pallas kernels, convolve(): pl.pallas_call(conv_kernel, out_shape=(out, out), in_specs=[smem, smem] +...  22.6 us
    ppermute x17, waiting for transfers between devices, exchange(): return lax.ppermute(value, ('mol', 'task'), pairs)  17.5 us
    pallas_call x1, Pallas kernels, turn_back(): pl.pallas_call(back_kernel, out_shape=(jax.ShapeDtypeStruct((ATOMS, COEF...  15 us
    unnamed x50, local copies, waits for them, and re-layouts  14.5 us
    pallas_call x1, Pallas kernels, features(): pl.pallas_call(feature_kernel, out_shape=(jax.ShapeDtypeStruct((20, EDGES...  14.2 us
    select_n x7, other arithmetic, pick(): return jnp.where(first, a, b)  3.72 us
    ppermute x1, starting transfers between devices, body(): back = lax.ppermute(other, 'mol', swap)  3.52 us
  transfers between devices with their start and end apart: 19, of which 9 were waited for; matrix products, arithmetic and copies ran while one was open for 5% of the time, Pallas kernels for 11%

profile of v1, /device:TPU:1, one launch (start us, length us, event | category | flops | bytes accessed | tf_op | source)
XLA Modules:
  0.0 127.9 jit_solution(763357644196551554)
XLA Ops:
  0.6 0.9 slice.18
  1.5 0.8 slice.17
  2.3 0.1 pad.7.clone
  2.4 1.1 maximum_select_fusion.1.refs_0_
  3.4 7.8 %collective-permute-start.2 = (bf16[86,8,128]{2,1,0:T(8,128)(2,1)S(1)}, bf16[86,8,128]{2,1,0:T(8,128)(2,1)S(1)}, u32[]{:S(2)}, u32[]{:S(2)}) collective-permute-start(bf16[86,8,128]{2,1,0:T(8,128)(2,1)S(1)} %maximum_select_fusion.1.refs_0_), channel_id=1, source_target_pairs={{0,2},{1,3},{2,0},{3,1},{4,6},{5,7},{6,4},{7,5},{8,10},{9,11},{10,... | collective-permute-start | bytes 528392 | tf_op jit(solution)/shard_map/ppermute | solution.py:351
  11.3 0.0 collective-permute-start.1
  11.3 1.5 %collective-permute-start = (bf16[86,8,128]{2,1,0:T(8,128)(2,1)S(1)}, bf16[86,8,128]{2,1,0:T(8,128)(2,1)S(1)}, u32[]{:S(2)}, u32[]{:S(2)}) collective-permute-start(bf16[86,8,128]{2,1,0:T(8,128)(2,1)S(1)} %maximum_select_fusion.1.refs_0_), channel_id=1, source_target_pairs={{0,1},{1,2},{2,3},{3,0},{4,5},{5,6},{6,7},{7,4},{8,9},{9,10},{10,1... | collective-permute-start | bytes 528392 | tf_op jit(solution)/shard_map/ppermute | solution.py:351
  13.4 0.9 broadcast_select_fusion.11.filt
  14.3 0.0 copy-start.19
  14.3 1.6 %copy.21 = bf16[256,29,49]{0,2,1:T(8,128)(2,1)S(1)} copy(bf16[256,29,49]{0,1,2:T(8,128)(2,1)} %param.18) | data formatting | bytes 1455104 | tf_op args[1]
  15.9 0.0 copy-start.6
  15.9 0.0 copy-start.20
  15.9 0.2 reshape.82
  16.1 0.3 copy.22.wig
  16.4 0.1 copy.23.source
  16.6 0.1 copy.24.target
  16.7 0.1 copy.25.rotation
  16.8 1.8 %collective-permute-done.1.refs_2_ = bf16[86,8,128]{2,1,0:T(8,128)(2,1)S(1)} collective-permute-done((bf16[86,8,128]{2,1,0:T(8,128)(2,1)S(1)}, bf16[86,8,128]{2,1,0:T(8,128)(2,1)S(1)}, u32[]{:S(2)}, u32[]{:S(2)}) %collective-permute-start.1) | collective-permute-done | bytes 176160 | tf_op jit(solution)/shard_map/ppermute | solution.py:351
  18.7 0.0 collective-permute-done.2.refs_3_
  18.7 0.1 broadcast_select_fusion.9
  18.9 0.6 copy-done.4
  19.4 1.3 %collective-permute-start.5 = (bf16[172,8,128]{2,1,0:T(8,128)(2,1)S(1)}, bf16[172,8,128]{2,1,0:T(8,128)(2,1)S(1)}, u32[]{:S(2)}, u32[]{:S(2)}) collective-permute-start(bf16[172,8,128]{2,1,0:T(8,128)(2,1)S(1)} %get-tuple-element.16), channel_id=1, source_target_pairs={{0,4},{1,5},{2,6},{3,7},{4,8},{5,9},{6,10},{7,11},{8,12},{9,13},{1... | collective-permute-start | bytes 1056776 | tf_op jit(solution)/shard_map/ppermute | solution.py:351
  20.7 1.4 %collective-permute-start.6 = (bf16[172,8,128]{2,1,0:T(8,128)(2,1)S(1)}, bf16[172,8,128]{2,1,0:T(8,128)(2,1)S(1)}, u32[]{:S(2)}, u32[]{:S(2)}) collective-permute-start(bf16[172,8,128]{2,1,0:T(8,128)(2,1)S(1)} %get-tuple-element.16), channel_id=1, source_target_pairs={{0,28},{1,29},{2,30},{3,31},{4,0},{5,1},{6,2},{7,3},{8,4},{9,5},{1... | collective-permute-start | bytes 1056776 | tf_op jit(solution)/shard_map/ppermute | solution.py:351
  22.2 2.7 %collective-permute-start.4 = (bf16[172,8,128]{2,1,0:T(8,128)(2,1)S(1)}, bf16[172,8,128]{2,1,0:T(8,128)(2,1)S(1)}, u32[]{:S(2)}, u32[]{:S(2)}) collective-permute-start(bf16[172,8,128]{2,1,0:T(8,128)(2,1)S(1)} %get-tuple-element.17), channel_id=1, source_target_pairs={{0,28},{1,29},{2,30},{3,31},{4,0},{5,1},{6,2},{7,3},{8,4},{9,5},{1... | collective-permute-start | bytes 1056776 | tf_op jit(solution)/shard_map/ppermute | solution.py:351
  24.8 1.1 copy-done.7
  25.9 14.2 %features.1 = (bf16[20,192,256]{2,1,0:T(8,128)(2,1)S(1)}, bf16[20,192,256]{2,1,0:T(8,128)(2,1)}, f32[192,1421]{1,0:T(8,128)S(1)}) custom-call(s32[1]{0:T(128)} %bitcast.2.core, bf16[48,6272]{1,0:T(8,128)(2,1)S(1)} %copy-done.7, bf16[256,1421]{1,0:T(8,128)(2,1)S(1)} %copy.22.wig, s32[192,1]{1,0:T(8,128)S(1)} %copy.23.source, s32[192,1]{1,0:T(8,128)S(1)} %copy.24.target, ...), custom_call_target="tpu_custom_call" | custom-call | flops 6000000000 | bytes 8000000 | tf_op jit(solution)/shard_map/features/pallas_call | solution.py:123
  40.1 1.0 collective-permute-start.17
  41.1 0.1 broadcast_select_fusion.5
  41.2 0.1 collective-permute-start.7
  41.3 2.7 %collective-permute-start.8 = (bf16[172,8,128]{2,1,0:T(8,128)(2,1)S(1)}, bf16[172,8,128]{2,1,0:T(8,128)(2,1)S(1)}, u32[]{:S(2)}, u32[]{:S(2)}) collective-permute-start(bf16[172,8,128]{2,1,0:T(8,128)(2,1)S(1)} %get-tuple-element.23), channel_id=1, source_target_pairs={{0,28},{1,29},{2,30},{3,31},{4,0},{5,1},{6,2},{7,3},{8,4},{9,5},{1... | collective-permute-start | bytes 1056776 | tf_op jit(solution)/shard_map/ppermute | solution.py:351
  44.0 0.0 collective-permute-start.10
  44.0 1.4 %collective-permute-start.9 = (bf16[172,8,128]{2,1,0:T(8,128)(2,1)S(1)}, bf16[172,8,128]{2,1,0:T(8,128)(2,1)S(1)}, u32[]{:S(2)}, u32[]{:S(2)}) collective-permute-start(bf16[172,8,128]{2,1,0:T(8,128)(2,1)S(1)} %get-tuple-element.21), channel_id=1, source_target_pairs={{0,4},{1,5},{2,6},{3,7},{4,8},{5,9},{6,10},{7,11},{8,12},{9,13},{1... | collective-permute-start | bytes 1056776 | tf_op jit(solution)/shard_map/ppermute | solution.py:351
  45.4 3.5 %collective-permute-done.7.refs_8_ = bf16[172,8,128]{2,1,0:T(8,128)(2,1)S(1)} collective-permute-done((bf16[172,8,128]{2,1,0:T(8,128)(2,1)S(1)}, bf16[172,8,128]{2,1,0:T(8,128)(2,1)S(1)}, u32[]{:S(2)}, u32[]{:S(2)}) %collective-permute-start.7) | collective-permute-done | bytes 352288 | tf_op jit(solution)/shard_map/ppermute | solution.py:351
  49.0 0.1 broadcast_select_fusion.3
  49.1 0.0 copy-start.23
  49.1 2.8 %collective-permute-start.12 = (bf16[172,8,128]{2,1,0:T(8,128)(2,1)S(1)}, bf16[172,8,128]{2,1,0:T(8,128)(2,1)S(1)}, u32[]{:S(2)}, u32[]{:S(2)}) collective-permute-start(bf16[172,8,128]{2,1,0:T(8,128)(2,1)S(1)} %get-tuple-element.18), channel_id=1, source_target_pairs={{0,28},{1,29},{2,30},{3,31},{4,0},{5,1},{6,2},{7,3},{8,4},{9,5},{1... | collective-permute-start | bytes 1056776 | tf_op jit(solution)/shard_map/ppermute | solution.py:351
  51.8 0.2 collective-permute-done.10.refs_11_
  52.0 3.1 %collective-permute-start.14 = (bf16[172,8,128]{2,1,0:T(8,128)(2,1)S(1)}, bf16[172,8,128]{2,1,0:T(8,128)(2,1)S(1)}, u32[]{:S(2)}, u32[]{:S(2)}) collective-permute-start(bf16[172,8,128]{2,1,0:T(8,128)(2,1)S(1)} %collective-permute-done.10.refs_11_), channel_id=1, source_target_pairs={{0,28},{1,29},{2,30},{3,31},{4,0},{5,1},{6,2},{7,3},{8,4},{9,5},{1... | collective-permute-start | bytes 1056776 | tf_op jit(solution)/shard_map/ppermute | solution.py:351
  55.1 0.8 broadcast_select_fusion.2
  55.9 0.2 collective-permute-done.12.refs_13_
  56.1 3.8 %collective-permute-done.14.refs_15_ = bf16[172,8,128]{2,1,0:T(8,128)(2,1)S(1)} collective-permute-done((bf16[172,8,128]{2,1,0:T(8,128)(2,1)S(1)}, bf16[172,8,128]{2,1,0:T(8,128)(2,1)S(1)}, u32[]{:S(2)}, u32[]{:S(2)}) %collective-permute-start.14) | collective-permute-done | bytes 352288 | tf_op jit(solution)/shard_map/ppermute | solution.py:351
  59.9 0.8 broadcast_select_fusion
  60.7 0.8 copy-done
  61.4 3.4 %collective-permute-start.16 = (bf16[172,8,128]{2,1,0:T(8,128)(2,1)}, bf16[172,8,128]{2,1,0:T(8,128)(2,1)}, u32[]{:S(2)}, u32[]{:S(2)}) collective-permute-start(bf16[172,8,128]{2,1,0:T(8,128)(2,1)} %broadcast_select_fusion), channel_id=1, source_target_pairs={{0,28},{1,29},{2,30},{3,31},{4,0},{5,1},{6,2},{7,3},{8,4},{9,5},{1... | collective-permute-start | bytes 1056776 | tf_op jit(solution)/shard_map/ppermute | solution.py:351
  64.9 0.8 broadcast_select_fusion.1
  65.6 0.7 copy-done.2
  66.4 0.3 collective-permute-done.13.refs_14_
  66.7 2.7 %collective-permute-done.16.refs_17_ = bf16[172,8,128]{2,1,0:T(8,128)(2,1)} collective-permute-done((bf16[172,8,128]{2,1,0:T(8,128)(2,1)}, bf16[172,8,128]{2,1,0:T(8,128)(2,1)}, u32[]{:S(2)}, u32[]{:S(2)}) %collective-permute-start.16) | collective-permute-done | bytes 352288 | tf_op jit(solution)/shard_map/ppermute | solution.py:351
  69.5 5.0 %collective-permute-done.15.refs_16_ = bf16[172,8,128]{2,1,0:T(8,128)(2,1)} collective-permute-done((bf16[172,8,128]{2,1,0:T(8,128)(2,1)}, bf16[172,8,128]{2,1,0:T(8,128)(2,1)}, u32[]{:S(2)}, u32[]{:S(2)}) %collective-permute-start.15) | collective-permute-done | bytes 352288 | tf_op jit(solution)/shard_map/ppermute | solution.py:351
  74.4 1.0 copy-done.1
  75.4 1.0 copy-done.3
  76.4 0.9 copy-done.5
  77.3 1.0 copy-done.10
  78.3 1.5 %copy-done.18 = bf16[20,192,256]{2,1,0:T(8,128)(2,1)S(1)} copy-done((bf16[20,192,256]{2,1,0:T(8,128)(2,1)S(1)}, bf16[20,192,256]{2,1,0:T(8,128)(2,1)}, u32[]{:S(2)}) %copy-start.18) | copy-done | bytes 1966104
  79.8 22.6 %convolve.1 = (bf16[15,192,128]{2,1,0:T(8,128)(2,1)S(1)}, bf16[15,192,128]{2,1,0:T(8,128)(2,1)}) custom-call(s32[1]{0:T(128)} %bitcast.2.core, s32[32]{0:T(128)S(1)} %fusion.shard, bf16[86,8,128]{2,1,0:T(8,128)(2,1)S(1)} %maximum_select_fusion.1.refs_0_, bf16[86,8,128]{2,1,0:T(8,128)(2,1)S(1)} %copy-done.5, ...), custom_call_target="tpu_custom_call" | custom-call | flops 4000000000 | bytes 12000000 | tf_op jit(solution)/shard_map/convolve/pallas_call | solution.py:251
  102.4 0.9 copy-done.15
  103.3 3.5 %collective-permute-start.18 = (bf16[15,192,128]{2,1,0:T(8,128)(2,1)}, bf16[15,192,128]{2,1,0:T(8,128)(2,1)S(1)}, u32[]{:S(2)}, u32[]{:S(2)}) collective-permute-start(bf16[15,192,128]{2,1,0:T(8,128)(2,1)} %get-tuple-element.12), channel_id=1, source_target_pairs={{0,32},{32,0},{64,96},{96,64},{128,160},{160,128},{192,224},{224,1... | collective-permute-start | bytes 2211848 | tf_op jit(solution)/shard_map/ppermute | solution.py:440
  106.8 0.1 copy.26.struct
  106.9 1.9 %collective-permute-done.18.got = bf16[15,192,128]{2,1,0:T(8,128)(2,1)S(1)} collective-permute-done((bf16[15,192,128]{2,1,0:T(8,128)(2,1)}, bf16[15,192,128]{2,1,0:T(8,128)(2,1)S(1)}, u32[]{:S(2)}, u32[]{:S(2)}) %collective-permute-start.18) | collective-permute-done | bytes 737312 | tf_op jit(solution)/shard_map/ppermute | solution.py:440
  108.9 1.1 copy-done.8
  109.9 1.3 copy-done.14
  111.2 1.1 copy-done.16
  112.3 15.0 %turn_back.1 = (bf16[48,6272]{1,0:T(8,128)(2,1)}, f32[1,128]{1,0:T(1,128)S(1)}) custom-call(s32[15]{0:T(128)S(1)} %get-tuple-element.26.place_mine, s32[15]{0:T(128)S(1)} %get-tuple-element.25.place_got, s32[4]{0:T(128)S(1)} %copy-done.12, bf16[15,192,128]{2,1,0:T(8,128)(2,1)S(1)} %copy-done.16, bf16[15,192,128]{2,1,0:T(8,128)(2,1)S(1)} %collective-permute-done.18.got, ...), custom_call_target="tpu_custom_call" | custom-call | flops 1000000000 | bytes 4000000 | tf_op jit(solution)/shard_map/turn_back/pallas_call | solution.py:322
  127.3 0.5 slice_bitcast_fusion
  (50 shorter events, 0.2 us)
Async XLA Ops:
  3.4 15.2 %collective-permute-start.2 = (bf16[86,8,128]{2,1,0:T(8,128)(2,1)S(1)}, bf16[86,8,128]{2,1,0:T(8,128)(2,1)S(1)}, u32[]{:S(2)}, u32[]{:S(2)}) collective-permute-start(bf16[86,8,128]{2,1,0:T(8,128)(2,1)S(1)} %maximum_select_fusion.1.refs_0_), channel_id=1, source_target_pairs={{0,2},{1,3},{2,0},{3,1},{4,6},{5,7},{6,4},{7,5},{8,10},{9,11},{10,... | collective-permute-start | bytes 528392 | tf_op jit(solution)/shard_map/ppermute | solution.py:351
  11.3 7.4 %collective-permute-start.1 = (bf16[86,8,128]{2,1,0:T(8,128)(2,1)S(1)}, bf16[86,8,128]{2,1,0:T(8,128)(2,1)S(1)}, u32[]{:S(2)}, u32[]{:S(2)}) collective-permute-start(bf16[86,8,128]{2,1,0:T(8,128)(2,1)S(1)} %maximum_select_fusion.1.refs_0_), channel_id=1, source_target_pairs={{0,3},{1,0},{2,1},{3,2},{4,7},{5,4},{6,5},{7,6},{8,11},{9,8},{10,9... | collective-permute-start | bytes 528392 | tf_op jit(solution)/shard_map/ppermute | solution.py:351
  11.3 7.5 %collective-permute-start = (bf16[86,8,128]{2,1,0:T(8,128)(2,1)S(1)}, bf16[86,8,128]{2,1,0:T(8,128)(2,1)S(1)}, u32[]{:S(2)}, u32[]{:S(2)}) collective-permute-start(bf16[86,8,128]{2,1,0:T(8,128)(2,1)S(1)} %maximum_select_fusion.1.refs_0_), channel_id=1, source_target_pairs={{0,1},{1,2},{2,3},{3,0},{4,5},{5,6},{6,7},{7,4},{8,9},{9,10},{10,1... | collective-permute-start | bytes 528392 | tf_op jit(solution)/shard_map/ppermute | solution.py:351
  14.3 2.1 %copy-start.19 = (s32[192]{0:T(256)S(1)}, s32[192]{0:T(256)}, u32[]{:S(2)}) copy-start(s32[192]{0:T(256)} %param.19) | copy-start | bytes 2308
  15.9 0.7 copy-start.6
  15.9 0.8 copy-start.20
  18.7 0.7 copy-start.4
  19.4 21.7 %collective-permute-start.5 = (bf16[172,8,128]{2,1,0:T(8,128)(2,1)S(1)}, bf16[172,8,128]{2,1,0:T(8,128)(2,1)S(1)}, u32[]{:S(2)}, u32[]{:S(2)}) collective-permute-start(bf16[172,8,128]{2,1,0:T(8,128)(2,1)S(1)} %get-tuple-element.16), channel_id=1, source_target_pairs={{0,4},{1,5},{2,6},{3,7},{4,8},{5,9},{6,10},{7,11},{8,12},{9,13},{1... | collective-permute-start | bytes 1056776 | tf_op jit(solution)/shard_map/ppermute | solution.py:351
  20.7 20.4 %collective-permute-start.6 = (bf16[172,8,128]{2,1,0:T(8,128)(2,1)S(1)}, bf16[172,8,128]{2,1,0:T(8,128)(2,1)S(1)}, u32[]{:S(2)}, u32[]{:S(2)}) collective-permute-start(bf16[172,8,128]{2,1,0:T(8,128)(2,1)S(1)} %get-tuple-element.16), channel_id=1, source_target_pairs={{0,28},{1,29},{2,30},{3,31},{4,0},{5,1},{6,2},{7,3},{8,4},{9,5},{1... | collective-permute-start | bytes 1056776 | tf_op jit(solution)/shard_map/ppermute | solution.py:351
  22.1 18.9 %collective-permute-start.3 = (bf16[172,8,128]{2,1,0:T(8,128)(2,1)S(1)}, bf16[172,8,128]{2,1,0:T(8,128)(2,1)S(1)}, u32[]{:S(2)}, u32[]{:S(2)}) collective-permute-start(bf16[172,8,128]{2,1,0:T(8,128)(2,1)S(1)} %get-tuple-element.24), channel_id=1, source_target_pairs={{0,4},{1,5},{2,6},{3,7},{4,8},{5,9},{6,10},{7,11},{8,12},{9,13},{1... | collective-permute-start | bytes 1056776 | tf_op jit(solution)/shard_map/ppermute | solution.py:351
  22.2 18.9 %collective-permute-start.4 = (bf16[172,8,128]{2,1,0:T(8,128)(2,1)S(1)}, bf16[172,8,128]{2,1,0:T(8,128)(2,1)S(1)}, u32[]{:S(2)}, u32[]{:S(2)}) collective-permute-start(bf16[172,8,128]{2,1,0:T(8,128)(2,1)S(1)} %get-tuple-element.17), channel_id=1, source_target_pairs={{0,28},{1,29},{2,30},{3,31},{4,0},{5,1},{6,2},{7,3},{8,4},{9,5},{1... | collective-permute-start | bytes 1056776 | tf_op jit(solution)/shard_map/ppermute | solution.py:351
  24.8 1.1 copy-start.7
  40.1 9.0 %copy-start.13 = (f32[192,1421]{1,0:T(8,128)}, f32[192,1421]{1,0:T(8,128)S(1)}, u32[]{:S(2)}) copy-start(f32[192,1421]{1,0:T(8,128)S(1)} %get-tuple-element.13.d) | copy-start | bytes 3273988
  40.1 9.0 %copy-start.17 = (bf16[20,192,256]{2,1,0:T(8,128)(2,1)}, bf16[20,192,256]{2,1,0:T(8,128)(2,1)S(1)}, u32[]{:S(2)}) copy-start(bf16[20,192,256]{2,1,0:T(8,128)(2,1)S(1)} %get-tuple-element.9.refs_18_) | copy-start | bytes 5898244
  40.1 34.3 %collective-permute-start.17 = (bf16[20,192,256]{2,1,0:T(8,128)(2,1)}, bf16[20,192,256]{2,1,0:T(8,128)(2,1)}, u32[]{:S(2)}, u32[]{:S(2)}) collective-permute-start(bf16[20,192,256]{2,1,0:T(8,128)(2,1)} %get-tuple-element.10), channel_id=1, source_target_pairs={{0,32},{32,0},{64,96},{96,64},{128,160},{160,128},{192,224},{224,1... | collective-permute-start | bytes 5898248 | tf_op jit(solution)/shard_map/ppermute | solution.py:438
  41.2 7.8 %collective-permute-start.7 = (bf16[172,8,128]{2,1,0:T(8,128)(2,1)S(1)}, bf16[172,8,128]{2,1,0:T(8,128)(2,1)S(1)}, u32[]{:S(2)}, u32[]{:S(2)}) collective-permute-start(bf16[172,8,128]{2,1,0:T(8,128)(2,1)S(1)} %get-tuple-element.22), channel_id=1, source_target_pairs={{0,4},{1,5},{2,6},{3,7},{4,8},{5,9},{6,10},{7,11},{8,12},{9,13},{1... | collective-permute-start | bytes 1056776 | tf_op jit(solution)/shard_map/ppermute | solution.py:351
  41.3 7.7 %collective-permute-start.8 = (bf16[172,8,128]{2,1,0:T(8,128)(2,1)S(1)}, bf16[172,8,128]{2,1,0:T(8,128)(2,1)S(1)}, u32[]{:S(2)}, u32[]{:S(2)}) collective-permute-start(bf16[172,8,128]{2,1,0:T(8,128)(2,1)S(1)} %get-tuple-element.23), channel_id=1, source_target_pairs={{0,28},{1,29},{2,30},{3,31},{4,0},{5,1},{6,2},{7,3},{8,4},{9,5},{1... | collective-permute-start | bytes 1056776 | tf_op jit(solution)/shard_map/ppermute | solution.py:351
  44.0 8.1 %collective-permute-start.10 = (bf16[172,8,128]{2,1,0:T(8,128)(2,1)S(1)}, bf16[172,8,128]{2,1,0:T(8,128)(2,1)S(1)}, u32[]{:S(2)}, u32[]{:S(2)}) collective-permute-start(bf16[172,8,128]{2,1,0:T(8,128)(2,1)S(1)} %get-tuple-element.20), channel_id=1, source_target_pairs={{0,28},{1,29},{2,30},{3,31},{4,0},{5,1},{6,2},{7,3},{8,4},{9,5},{1... | collective-permute-start | bytes 1056776 | tf_op jit(solution)/shard_map/ppermute | solution.py:351
  44.0 11.1 %collective-permute-start.9 = (bf16[172,8,128]{2,1,0:T(8,128)(2,1)S(1)}, bf16[172,8,128]{2,1,0:T(8,128)(2,1)S(1)}, u32[]{:S(2)}, u32[]{:S(2)}) collective-permute-start(bf16[172,8,128]{2,1,0:T(8,128)(2,1)S(1)} %get-tuple-element.21), channel_id=1, source_target_pairs={{0,4},{1,5},{2,6},{3,7},{4,8},{5,9},{6,10},{7,11},{8,12},{9,13},{1... | collective-permute-start | bytes 1056776 | tf_op jit(solution)/shard_map/ppermute | solution.py:351
  49.1 17.3 %copy-start.23 = (s32[2,32,2]{1,2,0:T(2,128)S(1)}, s32[2,32,2]{1,2,0:T(2,128)}, u32[]{:S(2)}) copy-start(s32[2,32,2]{1,2,0:T(2,128)} %constant.73.clone) | copy-start | bytes 1540
  49.1 7.0 %collective-permute-start.12 = (bf16[172,8,128]{2,1,0:T(8,128)(2,1)S(1)}, bf16[172,8,128]{2,1,0:T(8,128)(2,1)S(1)}, u32[]{:S(2)}, u32[]{:S(2)}) collective-permute-start(bf16[172,8,128]{2,1,0:T(8,128)(2,1)S(1)} %get-tuple-element.18), channel_id=1, source_target_pairs={{0,28},{1,29},{2,30},{3,31},{4,0},{5,1},{6,2},{7,3},{8,4},{9,5},{1... | collective-permute-start | bytes 1056776 | tf_op jit(solution)/shard_map/ppermute | solution.py:351
  52.0 13.6 %copy-start.9 = (bf16[172,8,128]{2,1,0:T(8,128)(2,1)}, bf16[172,8,128]{2,1,0:T(8,128)(2,1)S(1)}, u32[]{:S(2)}) copy-start(bf16[172,8,128]{2,1,0:T(8,128)(2,1)S(1)} %collective-permute-done.10.refs_11_) | copy-start | bytes 1056772
  52.0 7.9 %collective-permute-start.14 = (bf16[172,8,128]{2,1,0:T(8,128)(2,1)S(1)}, bf16[172,8,128]{2,1,0:T(8,128)(2,1)S(1)}, u32[]{:S(2)}, u32[]{:S(2)}) collective-permute-start(bf16[172,8,128]{2,1,0:T(8,128)(2,1)S(1)} %collective-permute-done.10.refs_11_), channel_id=1, source_target_pairs={{0,28},{1,29},{2,30},{3,31},{4,0},{5,1},{6,2},{7,3},{8,4},{9,5},{1... | collective-permute-start | bytes 1056776 | tf_op jit(solution)/shard_map/ppermute | solution.py:351
  55.1 9.7 %collective-permute-start.11 = (bf16[172,8,128]{2,1,0:T(8,128)(2,1)S(1)}, bf16[172,8,128]{2,1,0:T(8,128)(2,1)S(1)}, u32[]{:S(2)}, u32[]{:S(2)}) collective-permute-start(bf16[172,8,128]{2,1,0:T(8,128)(2,1)S(1)} %get-tuple-element.19), channel_id=1, source_target_pairs={{0,4},{1,5},{2,6},{3,7},{4,8},{5,9},{6,10},{7,11},{8,12},{9,13},{1... | collective-permute-start | bytes 1056776 | tf_op jit(solution)/shard_map/ppermute | solution.py:351
  55.9 10.8 %collective-permute-start.13 = (bf16[172,8,128]{2,1,0:T(8,128)(2,1)}, bf16[172,8,128]{2,1,0:T(8,128)(2,1)}, u32[]{:S(2)}, u32[]{:S(2)}) collective-permute-start(bf16[172,8,128]{2,1,0:T(8,128)(2,1)} %broadcast_select_fusion.2), channel_id=1, source_target_pairs={{0,4},{1,5},{2,6},{3,7},{4,8},{5,9},{6,10},{7,11},{8,12},{9,13},{1... | collective-permute-start | bytes 1056776 | tf_op jit(solution)/shard_map/ppermute | solution.py:351
  60.7 0.8 copy-start
  61.4 8.0 %collective-permute-start.16 = (bf16[172,8,128]{2,1,0:T(8,128)(2,1)}, bf16[172,8,128]{2,1,0:T(8,128)(2,1)}, u32[]{:S(2)}, u32[]{:S(2)}) collective-permute-start(bf16[172,8,128]{2,1,0:T(8,128)(2,1)} %broadcast_select_fusion), channel_id=1, source_target_pairs={{0,28},{1,29},{2,30},{3,31},{4,0},{5,1},{6,2},{7,3},{8,4},{9,5},{1... | collective-permute-start | bytes 1056776 | tf_op jit(solution)/shard_map/ppermute | solution.py:351
  65.6 0.7 copy-start.2
  66.4 8.0 %collective-permute-start.15 = (bf16[172,8,128]{2,1,0:T(8,128)(2,1)}, bf16[172,8,128]{2,1,0:T(8,128)(2,1)}, u32[]{:S(2)}, u32[]{:S(2)}) collective-permute-start(bf16[172,8,128]{2,1,0:T(8,128)(2,1)} %broadcast_select_fusion.1), channel_id=1, source_target_pairs={{0,4},{1,5},{2,6},{3,7},{4,8},{5,9},{6,10},{7,11},{8,12},{9,13},{1... | collective-permute-start | bytes 1056776 | tf_op jit(solution)/shard_map/ppermute | solution.py:351
  74.4 1.0 copy-start.1
  75.4 1.0 copy-start.3
  76.4 0.9 copy-start.5
  77.3 1.0 copy-start.10
  78.3 1.5 %copy-start.18 = (bf16[20,192,256]{2,1,0:T(8,128)(2,1)S(1)}, bf16[20,192,256]{2,1,0:T(8,128)(2,1)}, u32[]{:S(2)}) copy-start(bf16[20,192,256]{2,1,0:T(8,128)(2,1)} %copy-done.17) | copy-start | bytes 5898244
  79.8 27.0 %copy-start.22 = (s32[48]{0:T(128)S(1)}, s32[48]{0:T(128)}, u32[]{:S(2)}) copy-start(s32[48]{0:T(128)} %param.29) | copy-start | bytes 580
  79.8 27.1 %copy-start.21 = (s32[2,15]{1,0:T(2,128)S(1)}, s32[2,15]{1,0:T(2,128)}, u32[]{:S(2)}) copy-start(s32[2,15]{1,0:T(2,128)} %constant.74.clone) | copy-start | bytes 364
  79.8 29.0 %copy-start.11 = (f32[5,128]{1,0:T(8,128)S(1)}, f32[5,128]{1,0:T(8,128)}, u32[]{:S(2)}) copy-start(f32[5,128]{1,0:T(8,128)} %head.1) | copy-start | bytes 7684
  79.8 29.0 %copy-start.12 = (s32[4]{0:T(128)S(1)}, s32[4]{0:T(128)}, u32[]{:S(2)}) copy-start(s32[4]{0:T(128)} %task.1) | copy-start | bytes 52
  102.4 0.9 copy-start.15
  103.3 5.6 %collective-permute-start.18 = (bf16[15,192,128]{2,1,0:T(8,128)(2,1)}, bf16[15,192,128]{2,1,0:T(8,128)(2,1)S(1)}, u32[]{:S(2)}, u32[]{:S(2)}) collective-permute-start(bf16[15,192,128]{2,1,0:T(8,128)(2,1)} %get-tuple-element.12), channel_id=1, source_target_pairs={{0,32},{32,0},{64,96},{96,64},{128,160},{160,128},{192,224},{224,1... | collective-permute-start | bytes 2211848 | tf_op jit(solution)/shard_map/ppermute | solution.py:440
  108.9 1.1 copy-start.8
  109.9 1.3 copy-start.14
  111.2 1.1 copy-start.16

commit v2 on v1

v2 whole, which is shorter than its diff:
```python
import jax
import jax.numpy as jnp
from jax import lax
from jax.experimental import pallas as pl
from jax.experimental.pallas import tpu as pltpu
from jax.sharding import PartitionSpec as P

C = 128
COEF = 49
MROWS = 29
EDGES = 192
ATOMS = 48
NROT = 256
TILES = 86
VMEM = pltpu.VMEM
SMEM = pltpu.SMEM
BF = jnp.bfloat16
F32 = jnp.float32

ROWS = [[degree] for degree in range(7)]
for degree in range(1, 7):
    ROWS[degree] += [6 + degree, 12 + degree]
for degree in range(2, 7):
    ROWS[degree] += [17 + degree, 22 + degree]

MADE = (
    tuple(range(7, 19)) + (0, 1, 29),
    tuple(range(19, 29)) + (2, 3, 4, 5, 6),
)

H0 = ((0, 0), (0, -1))
H1 = ((0, 1), (0, 2))
U = (
    ((0, 0), (-1, 0)),
    ((1, 0), (4, 0)),
    ((-2, 0), (3, 0)),
    ((2, 0), (-3, 0)),
)


def moved(blocks, z, y):
    return [(a + z, b + y) for a, b in blocks]


def block_offsets():
    first = moved(H0, 0, 0) + moved(H1, 0, 0) + moved(H0, -1, 0) + moved(H1, 1, 0)
    for step in (1, 2, 3):
        first += moved(H1, -step, 0) + moved(H0, -step - 1, 0)
        first += moved(H0, step, 0) + moved(H1, step + 1, 0)
    second = [block for part in U for block in part]
    for part in (0, 2):
        for y in (-1, 1):
            second += moved(U[part], 0, y) + moved(U[part + 1], 0, y)
    for part in (0, 2):
        second += moved(U[part], 0, 2) + moved(U[part + 1], 0, 2)
    return first, second


def feature_kernel(
    core, node, wig, source, target, rotation, filt, own, send, wc_out, x, xs, xt, wc, fz, fa, ff, sem
):
    wc[...] = jnp.zeros_like(wc)
    for degree in range(7):
        at = degree * degree
        for r in ROWS[degree]:
            wc[r * 16 : r * 16 + 2 * degree + 1, :] = wig[r, at : at + 2 * degree + 1, :].astype(F32)
    entries = wc[...].astype(BF)
    wc_out[...] = entries
    for j in range(COEF):
        x[j * ATOMS : (j + 1) * ATOMS, :] = node[:, j * C : (j + 1) * C]
    width = 13 * ATOMS
    lane = lax.broadcasted_iota(jnp.int32, (1, width), 1)
    atom = lane % ATOMS
    xs[...] = (source[...] == atom).astype(F32).astype(BF)
    xt[...] = (target[...] == atom).astype(F32).astype(BF)
    hot_r = (rotation[...] == lax.broadcasted_iota(jnp.int32, (1, NROT), 1)).astype(F32).astype(BF)
    d_all = lax.dot_general(
        hot_r, entries, (((1,), (1,)), ((), ())), preferred_element_type=F32
    ).astype(BF)
    ff[:, :C] = filt[...]
    ff[:, C:] = filt[...]
    is_second = core[0]
    base_one = is_second * 12
    base_two = (1 - is_second) * 12
    for degree in range(7):
        wide = (2 * degree + 1) * ATOMS
        at = degree * degree
        which = lax.broadcasted_iota(jnp.int32, (C, wide), 0)
        which = which - lax.broadcasted_iota(jnp.int32, (C, wide), 1) // ATOMS
        coefs = x[at * ATOMS : at * ATOMS + wide, :]
        for r in ROWS[degree]:
            part, offset = divmod(r, 8)
            spread = (which == offset * 16).astype(F32).astype(BF)
            d = d_all[:, part * C : (part + 1) * C]
            d = jnp.dot(d, spread, preferred_element_type=F32).astype(BF)
            one = jnp.dot(d * xs[:, :wide], coefs, preferred_element_type=F32).astype(BF)
            two = jnp.dot(d * xt[:, :wide], coefs, preferred_element_type=F32).astype(BF)
            if r < 7:
                ref, plane = fz, r
            elif r < 19:
                ref, plane = fa, base_one + (r - 7)
            else:
                q = r - 19
                ref, plane = fa, base_two + (q // 5) * 6 + q % 5
            ref[plane, :, :C] = one
            ref[plane, :, C:] = two
    copies = []
    for place, out in ((0, own), (12, send)):
        copies += [
            pltpu.make_async_copy(fz, out.at[pl.ds(0, 7)], sem.at[len(copies)]),
            pltpu.make_async_copy(
                fa.at[pl.ds(place, 12)], out.at[pl.ds(7, 12)], sem.at[len(copies) + 1]
            ),
            pltpu.make_async_copy(ff, out.at[19], sem.at[len(copies) + 2]),
        ]
    for copy in copies:
        copy.start()
    for copy in copies:
        copy.wait()


def features(core, node, wig, source, target, rotation, filt):
    vm = pl.BlockSpec(memory_space=VMEM)
    anywhere = pl.BlockSpec(memory_space=pl.ANY)
    return pl.pallas_call(
        feature_kernel,
        out_shape=(
            jax.ShapeDtypeStruct((20, EDGES, 2 * C), BF),
            jax.ShapeDtypeStruct((20, EDGES, 2 * C), BF),
            jax.ShapeDtypeStruct((4 * C, NROT), BF),
        ),
        in_specs=[pl.BlockSpec(memory_space=SMEM)] + [vm] * 6,
        out_specs=(anywhere, anywhere, vm),
        scratch_shapes=[
            VMEM((COEF * ATOMS, C), BF),
            VMEM((EDGES, 13 * ATOMS), BF),
            VMEM((EDGES, 13 * ATOMS), BF),
            VMEM((4 * C, NROT), F32),
            VMEM((7, EDGES, 2 * C), BF),
            VMEM((24, EDGES, 2 * C), BF),
            VMEM((EDGES, 2 * C), BF),
            pltpu.SemaphoreType.DMA((6,)),
        ],
        compiler_params=pltpu.CompilerParams(vmem_limit_bytes=16 * 2**20),
        cost_estimate=pl.CostEstimate(flops=6 * 10**9, bytes_accessed=8 * 10**6, transcendentals=0),
        name="features",
    )(core, node, wig, source, target, rotation, filt)


def conv_kernel(core, shard, *refs):
    blocks = refs[:12]
    own, got, mine, other, w_all, xz, xa, fl, fsem = refs[12:]

    def place_blocks():
        index = 0
        for block in blocks:
            for part in range(block.shape[0] // TILES):
                w_all[shard[index]] = block[part * TILES : (part + 1) * TILES]
                index += 1

    def rows_of(first, count, g):
        tiles = w_all[:, pl.ds(first + g * count, count)]
        return tiles.reshape(32 * count * 8, C)

    def fetch_features(pieces):
        copies = []

        def add(src, dst):
            copies.append(pltpu.make_async_copy(src, dst, fsem.at[len(copies)]))

        for who, src in enumerate((own, got)):
            for k in range(7):
                add(src.at[k], xz.at[pl.ds(who * EDGES, EDGES), pl.ds(k * 2 * C, 2 * C)])
            for sign in range(2):
                for k in range(pieces):
                    add(
                        src.at[7 + sign * 6 + k],
                        xa.at[pl.ds((sign * 2 + who) * EDGES, EDGES), pl.ds(k * 2 * C, 2 * C)],
                    )
            add(src.at[19], fl.at[pl.ds(who * EDGES, EDGES)])
        return copies

    def finish(plane, value, filters):
        message = (value * filters).astype(BF)
        mine[plane] = message[:EDGES]
        other[plane] = message[EDGES:]

    def run(pieces, tiles, zero_groups):
        waits = fetch_features(pieces)
        for copy in waits:
            copy.start()
        place_blocks()
        for copy in waits:
            copy.wait()
        filters = fl[:, :C].astype(F32)
        deep = pieces * 2 * C
        half = 2 * EDGES
        size = pieces * tiles

        def column(g, carry):
            w = jnp.concatenate(
                (rows_of(0, tiles, g), rows_of(size, tiles, g)), axis=1
            )
            both = jnp.dot(xa[:, :deep], w, preferred_element_type=F32)
            finish(g, both[:half, :C] - both[half:, C:], filters)
            finish(pieces + g, both[half:, :C] + both[:half, C:], filters)
            return carry

        lax.fori_loop(0, pieces, column, 0)
        for g in range(0, zero_groups, 2):
            count = min(2, zero_groups - g)
            w = jnp.concatenate(
                [rows_of(2 * size, 7, g + i) for i in range(count)], axis=1
            )
            total = jnp.dot(xz[...], w, preferred_element_type=F32)
            for i in range(count):
                finish(2 * pieces + g + i, total[:, i * C : (i + 1) * C], filters)

    @pl.when(core[0] == 0)
    def _():
        run(6, 6, 2)

    @pl.when(core[0] == 1)
    def _():
        run(5, 5, 5)


def convolve(core, shard, blocks, own, got):
    vm = pl.BlockSpec(memory_space=VMEM)
    anywhere = pl.BlockSpec(memory_space=pl.ANY)
    smem = pl.BlockSpec(memory_space=SMEM)
    out = jax.ShapeDtypeStruct((15, EDGES, C), BF)
    return pl.pallas_call(
        conv_kernel,
        out_shape=(out, out),
        in_specs=[smem, smem] + [vm] * 12 + [anywhere] * 2,
        out_specs=(vm, vm),
        scratch_shapes=[
            VMEM((32, TILES, 8, C), BF),
            VMEM((2 * EDGES, 14 * C), BF),
            VMEM((4 * EDGES, 12 * C), BF),
            VMEM((2 * EDGES, 2 * C), BF),
            pltpu.SemaphoreType.DMA((40,)),
        ],
        compiler_params=pltpu.CompilerParams(vmem_limit_bytes=24 * 2**20),
        cost_estimate=pl.CostEstimate(flops=4 * 10**9, bytes_accessed=12 * 10**6, transcendentals=0),
        name="convolve",
    )(core, shard, *blocks, own, got)


def back_kernel(
    place_mine, place_got, task, mine, got, wig, rotation, target, node, struct, head, update, energy, m, d, sem
):
    copies = []
    for i in range(15):
        copies.append(
            pltpu.make_async_copy(mine.at[i], m.at[place_mine[i], pl.ds(0, EDGES)], sem.at[2 * i])
        )
        copies.append(
            pltpu.make_async_copy(got.at[i], m.at[place_got[i], pl.ds(0, EDGES)], sem.at[2 * i + 1])
        )
    for copy in copies:
        copy.start()
    hot_r = lax.broadcasted_iota(jnp.int32, (NROT, EDGES), 0) == rotation[...]
    hot_r = hot_r.astype(F32).astype(BF)
    d[...] = jnp.dot(wig[...], hot_r, preferred_element_type=F32)
    ends = lax.broadcasted_iota(jnp.int32, (ATOMS, EDGES), 0) == target[...]
    for copy in copies:
        copy.wait()
    for degree in range(7):
        span = range(degree * degree, (degree + 1) * (degree + 1))
        total = None
        for r in ROWS[degree]:
            hot = jnp.concatenate(
                [jnp.where(ends, d[r * 16 + j : r * 16 + j + 1, :], 0.0).astype(BF) for j in range(len(span))],
                axis=0,
            )
            term = jnp.dot(hot, m[r], preferred_element_type=F32)
            total = term if total is None else total + term
        for place, j in enumerate(span):
            value = total[place * ATOMS : (place + 1) * ATOMS]
            update[:, j * C : (j + 1) * C] = value.astype(BF)
            if j == 0:
                scalar_part = node[:, :C].astype(F32) + value
    lane = lax.broadcasted_iota(jnp.int32, (1, C), 1)
    result = jnp.zeros((1, C), F32)
    for s in range(4):
        member = jnp.where(struct[...] == s, scalar_part, 0.0) * head[pl.ds(task[s], 1), :]
        value = jnp.sum(jnp.sum(member, axis=0, keepdims=True), axis=1, keepdims=True)
        result = jnp.where(lane == s, value, result)
    energy[...] = result


def turn_back(place_mine, place_got, task, mine, got, wig, rotation, target, node, struct, head):
    vm = pl.BlockSpec(memory_space=VMEM)
    anywhere = pl.BlockSpec(memory_space=pl.ANY)
    smem = pl.BlockSpec(memory_space=SMEM)
    return pl.pallas_call(
        back_kernel,
        out_shape=(
            jax.ShapeDtypeStruct((ATOMS, COEF * C), BF),
            jax.ShapeDtypeStruct((1, C), F32),
        ),
        in_specs=[smem] * 3 + [anywhere] * 2 + [vm] * 6,
        out_specs=(vm, vm),
        scratch_shapes=[
            VMEM((30, EDGES, C), BF),
            VMEM((4 * C, EDGES), F32),
            pltpu.SemaphoreType.DMA((30,)),
        ],
        compiler_params=pltpu.CompilerParams(vmem_limit_bytes=16 * 2**20),
        cost_estimate=pl.CostEstimate(flops=10**9, bytes_accessed=4 * 10**6, transcendentals=0),
        name="turn_back",
    )(place_mine, place_got, task, mine, got, wig, rotation, target, node, struct, head)


def exchange(value, sizes, steps_first, steps_second):
    mol, nz, ny = sizes
    pairs = []
    for device in range(mol * nz * ny):
        m, t = divmod(device, nz * ny)
        z, y = divmod(t, ny)
        dz, dy = steps_first if m % 2 == 0 else steps_second
        to = ((z + dz) % nz) * ny + (y + dy) % ny
        pairs.append((device, m * nz * ny + to))
    return lax.ppermute(value, ("mol", "task"), pairs)


def tiles_of(w):
    rows, cols = w.shape
    return w.reshape(rows // 8, 8, cols // C, C).transpose(2, 0, 1, 3).reshape(-1, 8, C)


def body(
    node_embed,
    wigner,
    source,
    target,
    rotation,
    edge_filter,
    edge_count,
    w_zero,
    w_one_real,
    w_one_imag,
    w_two_real,
    w_two_imag,
    atom_struct,
    struct_task,
    task_head,
):
    sizes = (8, 8, 4)
    core = lax.axis_index("mol") % 2
    task = lax.axis_index("task")
    z, y = task // 4, task % 4
    first = core == 0

    def pick(a, b):
        return jnp.where(first, a, b)

    zero_tiles = w_zero
    pack_first = jnp.concatenate(
        (tiles_of(w_one_real), tiles_of(w_one_imag), tiles_of(zero_tiles[:, : 2 * C]))
    )
    pack_second = jnp.concatenate(
        (
            tiles_of(w_two_real),
            tiles_of(w_two_imag),
            tiles_of(zero_tiles[:, 2 * C :]),
            jnp.zeros((1, 8, C), BF),
        )
    )
    b0 = pick(pack_first, pack_second)
    a1 = exchange(b0, sizes, (0, 1), (1, 0))
    a2 = exchange(b0, sizes, (0, -1), (-1, 0))
    a3 = exchange(b0, sizes, (0, 2), (4, 0))
    h0 = jnp.concatenate((b0, a1))
    h1 = jnp.concatenate((a2, a3))

    def forth(value, second=(0, 1)):
        return exchange(value, sizes, (1, 0), second)

    def aft(value, second=(0, -1)):
        return exchange(value, sizes, (-1, 0), second)

    p1p = forth(pick(h0, jnp.concatenate((a1, a3))), (1, 0))
    p1m = aft(h1, (-1, 0))
    s1p = forth(jnp.concatenate((pick(h1, h0), pick(p1p, h1))))
    s1m = aft(jnp.concatenate((h0, pick(p1m, h1))))
    p1 = jnp.concatenate((p1p, p1m))
    s2p, s2m = forth(pick(s1p, p1)), aft(pick(s1m, p1))
    s3p, s3m = forth(pick(s2p, s1p)), aft(s2m)

    blocks = (b0, a1, a2, a3, p1p, p1m, s1p, s1m, s2p, s2m, s3p, s3m)
    offsets_first, offsets_second = block_offsets()
    table = jnp.asarray((offsets_first, offsets_second), jnp.int32)[core]
    shard = ((z + table[:, 0]) % 8) * 4 + (y + table[:, 1]) % 4

    live = (jnp.arange(EDGES, dtype=jnp.int32) < edge_count[0])[:, None]
    filters = jnp.where(live, edge_filter, jnp.zeros_like(edge_filter))
    core_vec = core.reshape(1).astype(jnp.int32)
    own, send, entries = features(
        core_vec,
        node_embed,
        wigner.transpose(1, 2, 0),
        source.reshape(EDGES, 1),
        target.reshape(EDGES, 1),
        rotation.reshape(EDGES, 1),
        filters,
    )
    swap = [(i, i ^ 1) for i in range(8)]
    got = lax.ppermute(send, "mol", swap)
    mine, other = convolve(core_vec, shard, blocks, own, got)
    back = lax.ppermute(other, "mol", swap)
    places = jnp.asarray(MADE, jnp.int32)
    update, energy = turn_back(
        places[core],
        places[1 - core],
        struct_task,
        mine,
        back,
        entries,
        rotation.reshape(1, EDGES),
        target.reshape(1, EDGES),
        node_embed,
        atom_struct.reshape(ATOMS, 1),
        task_head,
    )
    return update, energy[0, :4]


def solution(mesh):
    both = P(("mol", "task"))
    wide = P(("mol", "task"), None)
    rows = P("task", None)
    in_specs = (wide, P(), both, both, both, wide, both, rows, rows, rows, rows, rows, both, both, P())
    return jax.shard_map(
        body, mesh=mesh, in_specs=in_specs, out_specs=(wide, both), check_vma=False
    )
```

time: 129 us -> 102 us (0.79)
  Pallas kernels: 51.8 us -> 24.6 us
  waiting for transfers between devices: 19.5 us -> 27.7 us
  starting transfers between devices: 32.7 us -> 27.4 us
  other arithmetic: 4.63 us -> 1.96 us
    pallas_call x1, Pallas kernels: 22.6 us -> 9.68 us  [convolve(): pl.pallas_call(conv_kernel, out_shape=(out, out), in_specs=[smem, smem] +...]
    pallas_call x1, Pallas kernels: 15 us -> 5.69 us  [turn_back(): pl.pallas_call(back_kernel, out_shape=(jax.ShapeDtypeStruct((ATOMS, COEF...]
    ppermute x17 -> x11, waiting for transfers between devices: 17.5 us -> 25.7 us  [exchange(): return lax.ppermute(value, ('mol', 'task'), pairs)]
    ppermute x17 -> x11, starting transfers between devices: 28.2 us -> 22.9 us  [exchange(): return lax.ppermute(value, ('mol', 'task'), pairs)]
    pallas_call x1, Pallas kernels: 14.2 us -> 9.19 us  [features(): pl.pallas_call(feature_kernel, out_shape=(jax.ShapeDtypeStruct((20, EDGES...]
    unnamed x50 -> x49, local copies, waits for them, and re-layouts: 14.5 us -> 9.58 us
    reshape x2 -> x8, local copies, waits for them, and re-layouts: 0.51 us -> 5.17 us  [tiles_of(): w.reshape(rows // 8, 8, cols // C, C).transpose(2, 0, 1, 3)]
    select_n x7 -> x4, other arithmetic: 3.72 us -> 1.43 us  [pick(): return jnp.where(first, a, b)]
  transfers between devices with their start and end apart: 19 -> 13, of which waited for: 9 -> 7; matrix products, arithmetic and copies ran while one was open for 5% -> 4% of each run, Pallas kernels for 11% -> 9%
where the time goes in v2:
time: 102 us; the launch traced here: 101 us
  waiting for transfers between devices  27.7 us (27%)
  starting transfers between devices  27.4 us (27%)
  Pallas kernels  24.6 us (24%)
  local copies, waits for them, and re-layouts  17.8 us (17%)
  other arithmetic  1.96 us (2%)
  between operations  1.58 us (2%)
    ppermute x11, waiting for transfers between devices, exchange(): return lax.ppermute(value, ('mol', 'task'), pairs)  25.7 us
    ppermute x11, starting transfers between devices, exchange(): return lax.ppermute(value, ('mol', 'task'), pairs)  22.9 us
    pallas_call x1, Pallas kernels, convolve(): pl.pallas_call(conv_kernel, out_shape=(out, out), in_specs=[smem, smem] +...  9.68 us
    unnamed x49, local copies, waits for them, and re-layouts  9.58 us
    pallas_call x1, Pallas kernels, features(): pl.pallas_call(feature_kernel, out_shape=(jax.ShapeDtypeStruct((20, EDGES...  9.19 us
    pallas_call x1, Pallas kernels, turn_back(): pl.pallas_call(back_kernel, out_shape=(jax.ShapeDtypeStruct((ATOMS, COEF...  5.69 us
    reshape x8, local copies, waits for them, and re-layouts, tiles_of(): w.reshape(rows // 8, 8, cols // C, C).transpose(2, 0, 1, 3)  5.17 us
    ppermute x1, starting transfers between devices, body(): back = lax.ppermute(other, 'mol', swap)  3.29 us
  transfers between devices with their start and end apart: 13, of which 7 were waited for; matrix products, arithmetic and copies ran while one was open for 4% of the time, Pallas kernels for 9%

profile of v2, /device:TPU:1, one launch (start us, length us, event | category | flops | bytes accessed | tf_op | source)
XLA Modules:
  0.0 101.0 jit_solution(2529994794446846968)
XLA Ops:
  0.6 0.9 slice_bitcast_fusion
  1.5 0.8 slice_bitcast_fusion.1
  2.3 1.0 copy.28
  3.3 0.9 copy.27
  4.2 0.0 copy-start.19
  4.2 0.8 copy.30
  5.0 0.0 copy-start.5
  5.0 0.8 copy.31
  5.9 0.1 pad.12.clone
  5.9 0.2 maximum_select_fusion.1.refs_0_
  6.1 7.8 %collective-permute-start.2 = (bf16[86,8,128]{2,1,0:T(8,128)(2,1)S(1)}, bf16[86,8,128]{2,1,0:T(8,128)(2,1)S(1)}, u32[]{:S(2)}, u32[]{:S(2)}) collective-permute-start(bf16[86,8,128]{2,1,0:T(8,128)(2,1)S(1)} %maximum_select_fusion.1.refs_0_), channel_id=1, source_target_pairs={{0,2},{1,3},{2,0},{3,1},{4,6},{5,7},{6,4},{7,5},{8,10},{9,11},{10,... | collective-permute-start | bytes 528392 | tf_op jit(solution)/shard_map/ppermute | solution.py:326
  13.9 0.7 collective-permute-start
  14.7 1.9 %collective-permute-start.1 = (bf16[86,8,128]{2,1,0:T(8,128)(2,1)S(1)}, bf16[86,8,128]{2,1,0:T(8,128)(2,1)S(1)}, u32[]{:S(2)}, u32[]{:S(2)}) collective-permute-start(bf16[86,8,128]{2,1,0:T(8,128)(2,1)S(1)} %maximum_select_fusion.1.refs_0_), channel_id=1, source_target_pairs={{0,3},{1,0},{2,1},{3,2},{4,7},{5,4},{6,5},{7,6},{8,11},{9,8},{10,9... | collective-permute-start | bytes 528392 | tf_op jit(solution)/shard_map/ppermute | solution.py:326
  16.6 0.3 collective-permute-done.2.refs_3_
  16.9 3.0 %collective-permute-done.refs_1_ = bf16[86,8,128]{2,1,0:T(8,128)(2,1)S(1)} collective-permute-done((bf16[86,8,128]{2,1,0:T(8,128)(2,1)S(1)}, bf16[86,8,128]{2,1,0:T(8,128)(2,1)S(1)}, u32[]{:S(2)}, u32[]{:S(2)}) %collective-permute-start) | collective-permute-done | bytes 176160 | tf_op jit(solution)/shard_map/ppermute | solution.py:326
  19.9 0.1 maximum_select_fusion
  20.0 1.5 %collective-permute-start.3 = (bf16[172,8,128]{2,1,0:T(8,128)(2,1)S(1)}, bf16[172,8,128]{2,1,0:T(8,128)(2,1)S(1)}, u32[]{:S(2)}, u32[]{:S(2)}) collective-permute-start(bf16[172,8,128]{2,1,0:T(8,128)(2,1)S(1)} %maximum_select_fusion), channel_id=1, source_target_pairs={{0,4},{1,5},{2,6},{3,7},{4,8},{5,9},{6,10},{7,11},{8,12},{9,13},{1... | collective-permute-start | bytes 1056776 | tf_op jit(solution)/shard_map/ppermute | solution.py:326
  21.5 0.0 collective-permute-done.1.refs_2_
  21.5 0.6 copy-done
  22.1 2.2 %collective-permute-start.4 = (bf16[172,8,128]{2,1,0:T(8,128)(2,1)S(1)}, bf16[172,8,128]{2,1,0:T(8,128)(2,1)S(1)}, u32[]{:S(2)}, u32[]{:S(2)}) collective-permute-start(bf16[172,8,128]{2,1,0:T(8,128)(2,1)S(1)} %constant_dynamic-update-slice_fusion), channel_id=1, source_target_pairs={{0,28},{1,29},{2,30},{3,31},{4,0},{5,1},{6,2},{7,3},{8,4},{9,5},{1... | collective-permute-start | bytes 1056776 | tf_op jit(solution)/shard_map/ppermute | solution.py:326
  24.4 0.4 copy.39
  24.8 0.8 copy.34.source
  25.6 0.8 copy.35.target
  26.3 0.8 copy.36.rotation
  27.7 3.1 %collective-permute-done.3.refs_4_ = bf16[172,8,128]{2,1,0:T(8,128)(2,1)S(1)} collective-permute-done((bf16[172,8,128]{2,1,0:T(8,128)(2,1)S(1)}, bf16[172,8,128]{2,1,0:T(8,128)(2,1)S(1)}, u32[]{:S(2)}, u32[]{:S(2)}) %collective-permute-start.3) | collective-permute-done | bytes 352288 | tf_op jit(solution)/shard_map/ppermute | solution.py:326
  30.9 1.5 %collective-permute-done.4.refs_5_ = bf16[172,8,128]{2,1,0:T(8,128)(2,1)S(1)} collective-permute-done((bf16[172,8,128]{2,1,0:T(8,128)(2,1)S(1)}, bf16[172,8,128]{2,1,0:T(8,128)(2,1)S(1)}, u32[]{:S(2)}, u32[]{:S(2)}) %collective-permute-start.4) | collective-permute-done | bytes 352288 | tf_op jit(solution)/shard_map/ppermute | solution.py:326
  32.3 0.3 constant_dynamic-update-slice_fusion.2
  32.6 0.0 copy-start.18
  32.6 0.0 copy-start.2
  32.7 0.0 copy-start.7
  32.7 0.1 pad_maximum_fusion.1
  32.8 3.0 %collective-permute-start.6 = (bf16[344,8,128]{2,1,0:T(8,128)(2,1)S(1)}, bf16[344,8,128]{2,1,0:T(8,128)(2,1)S(1)}, u32[]{:S(2)}, u32[]{:S(2)}) collective-permute-start(bf16[344,8,128]{2,1,0:T(8,128)(2,1)S(1)} %pad_maximum_fusion.1), channel_id=1, source_target_pairs={{0,28},{1,29},{2,30},{3,31},{4,0},{5,1},{6,2},{7,3},{8,4},{9,5},{1... | collective-permute-start | bytes 2113544 | tf_op jit(solution)/shard_map/ppermute | solution.py:326
  35.8 0.1 pad_maximum_fusion
  35.9 0.3 collective-permute-start.5
  36.1 0.1 broadcast_select_fusion.6.filt
  36.3 9.2 %features.1 = (bf16[20,192,256]{2,1,0:T(8,128)(2,1)S(1)}, bf16[20,192,256]{2,1,0:T(8,128)(2,1)}, bf16[512,256]{1,0:T(8,128)(2,1)S(1)}) custom-call(s32[1]{0:T(128)} %bitcast.2.core, bf16[48,6272]{1,0:T(8,128)(2,1)S(1)} %copy-done.7, bf16[29,49,256]{2,1,0:T(8,128)(2,1)S(1)} %bitcast.51, s32[192,1]{1,0:T(8,128)S(1)} %copy-done.2, s32[192,1]{1,0:T(8,128)S(1)} %copy-done.3, ...), custom_call_target="tpu_custom_call" | custom-call | flops 6000000000 | bytes 8000000 | tf_op jit(solution)/shard_map/features/pallas_call | solution.py:125
  45.5 0.0 copy-start.13
  45.5 0.7 copy-done.13
  46.2 1.3 %copy-done.15 = bf16[20,192,256]{2,1,0:T(8,128)(2,1)} copy-done((bf16[20,192,256]{2,1,0:T(8,128)(2,1)}, bf16[20,192,256]{2,1,0:T(8,128)(2,1)S(1)}, u32[]{:S(2)}) %copy-start.15) | copy-done | bytes 1966104
  47.4 1.2 %collective-permute-start.11 = (bf16[20,192,256]{2,1,0:T(8,128)(2,1)}, bf16[20,192,256]{2,1,0:T(8,128)(2,1)}, u32[]{:S(2)}, u32[]{:S(2)}) collective-permute-start(bf16[20,192,256]{2,1,0:T(8,128)(2,1)} %get-tuple-element.10), channel_id=1, source_target_pairs={{0,32},{32,0},{64,96},{96,64},{128,160},{160,128},{192,224},{224,1... | collective-permute-start | bytes 5898248 | tf_op jit(solution)/shard_map/ppermute | solution.py:411
  48.7 0.0 collective-permute-done.6.refs_7_
  48.7 0.0 collective-permute-done.5.refs_6_
  48.7 0.2 broadcast_select_fusion.1
  48.9 0.1 collective-permute-start.7
  49.0 2.7 %collective-permute-start.8 = (bf16[344,8,128]{2,1,0:T(8,128)(2,1)S(1)}, bf16[344,8,128]{2,1,0:T(8,128)(2,1)}, u32[]{:S(2)}, u32[]{:S(2)}) collective-permute-start(bf16[344,8,128]{2,1,0:T(8,128)(2,1)S(1)} %get-tuple-element.16), channel_id=1, source_target_pairs={{0,28},{1,29},{2,30},{3,31},{4,0},{5,1},{6,2},{7,3},{8,4},{9,5},{1... | collective-permute-start | bytes 2113544 | tf_op jit(solution)/shard_map/ppermute | solution.py:326
  51.6 8.8 %collective-permute-done.7.refs_8_ = bf16[344,8,128]{2,1,0:T(8,128)(2,1)S(1)} collective-permute-done((bf16[344,8,128]{2,1,0:T(8,128)(2,1)S(1)}, bf16[344,8,128]{2,1,0:T(8,128)(2,1)S(1)}, u32[]{:S(2)}, u32[]{:S(2)}) %collective-permute-start.7) | collective-permute-done | bytes 704544 | tf_op jit(solution)/shard_map/ppermute | solution.py:326
  60.4 1.0 %broadcast_select_fusion = bf16[344,8,128]{2,1,0:T(8,128)(2,1)} fusion(bf16[344,8,128]{2,1,0:T(8,128)(2,1)S(1)} %collective-permute-done.7.refs_8_, bf16[344,8,128]{2,1,0:T(8,128)(2,1)S(1)} %collective-permute-done.5.refs_6_, pred[]{:T(512)S(6)} %eq.9), kind=kLoop, calls=%fused_computation.3 | loop fusion | flops 352256 | bytes 2113537 | tf_op jit(solution)/shard_map/jit(_where)/select_n | solution.py:358
  61.4 0.0 collective-permute-start.9
  61.4 0.0 collective-permute-done.8.refs_9_
  61.4 2.7 %collective-permute-start.10 = (bf16[344,8,128]{2,1,0:T(8,128)(2,1)}, bf16[344,8,128]{2,1,0:T(8,128)(2,1)}, u32[]{:S(2)}, u32[]{:S(2)}) collective-permute-start(bf16[344,8,128]{2,1,0:T(8,128)(2,1)} %collective-permute-done.8.refs_9_), channel_id=1, source_target_pairs={{0,28},{1,29},{2,30},{3,31},{4,0},{5,1},{6,2},{7,3},{8,4},{9,5},{1... | collective-permute-start | bytes 2113544 | tf_op jit(solution)/shard_map/ppermute | solution.py:326
  64.1 0.0 collective-permute-done.11.refs_13_
  64.1 9.1 %collective-permute-done.9.refs_10_ = bf16[344,8,128]{2,1,0:T(8,128)(2,1)} collective-permute-done((bf16[344,8,128]{2,1,0:T(8,128)(2,1)}, bf16[344,8,128]{2,1,0:T(8,128)(2,1)}, u32[]{:S(2)}, u32[]{:S(2)}) %collective-permute-start.9) | collective-permute-done | bytes 704544 | tf_op jit(solution)/shard_map/ppermute | solution.py:326
  73.2 0.9 copy-done.1
  74.1 1.5 %copy-done.16 = bf16[20,192,256]{2,1,0:T(8,128)(2,1)S(1)} copy-done((bf16[20,192,256]{2,1,0:T(8,128)(2,1)S(1)}, bf16[20,192,256]{2,1,0:T(8,128)(2,1)}, u32[]{:S(2)}) %copy-start.16) | copy-done | bytes 1966104
  75.7 9.7 %convolve.1 = (bf16[15,192,128]{2,1,0:T(8,128)(2,1)S(1)}, bf16[15,192,128]{2,1,0:T(8,128)(2,1)}) custom-call(s32[1]{0:T(128)} %bitcast.2.core, s32[32]{0:T(128)S(1)} %fusion.shard, bf16[86,8,128]{2,1,0:T(8,128)(2,1)S(1)} %maximum_select_fusion.1.refs_0_, bf16[86,8,128]{2,1,0:T(8,128)(2,1)S(1)} %collective-permute-done.refs_1_, ...), custom_call_target="tpu_custom_call" | custom-call | flops 4000000000 | bytes 12000000 | tf_op jit(solution)/shard_map/convolve/pallas_call | solution.py:233
  85.4 0.9 copy-done.11
  86.3 3.3 %collective-permute-start.12 = (bf16[15,192,128]{2,1,0:T(8,128)(2,1)}, bf16[15,192,128]{2,1,0:T(8,128)(2,1)S(1)}, u32[]{:S(2)}, u32[]{:S(2)}) collective-permute-start(bf16[15,192,128]{2,1,0:T(8,128)(2,1)} %get-tuple-element.12), channel_id=1, source_target_pairs={{0,32},{32,0},{64,96},{96,64},{128,160},{160,128},{192,224},{224,1... | collective-permute-start | bytes 2211848 | tf_op jit(solution)/shard_map/ppermute | solution.py:413
  89.6 0.1 copy.37.struct
  89.7 1.9 %collective-permute-done.12.got = bf16[15,192,128]{2,1,0:T(8,128)(2,1)S(1)} collective-permute-done((bf16[15,192,128]{2,1,0:T(8,128)(2,1)}, bf16[15,192,128]{2,1,0:T(8,128)(2,1)S(1)}, u32[]{:S(2)}, u32[]{:S(2)}) %collective-permute-start.12) | collective-permute-done | bytes 737312 | tf_op jit(solution)/shard_map/ppermute | solution.py:413
  91.6 1.1 %copy-done.8 = bf16[48,6272]{1,0:T(8,128)(2,1)S(1)} copy-done((bf16[48,6272]{1,0:T(8,128)(2,1)S(1)}, bf16[48,6272]{1,0:T(8,128)(2,1)}, u32[]{:S(2)}) %copy-start.8) | copy-done | bytes 602136
  92.7 1.1 %copy-done.12 = bf16[15,192,128]{2,1,0:T(8,128)(2,1)S(1)} copy-done((bf16[15,192,128]{2,1,0:T(8,128)(2,1)S(1)}, bf16[15,192,128]{2,1,0:T(8,128)(2,1)}, u32[]{:S(2)}) %copy-start.12) | copy-done | bytes 737304
  93.8 0.9 copy-done.14
  94.7 5.7 %turn_back.1 = (bf16[48,6272]{1,0:T(8,128)(2,1)}, f32[1,128]{1,0:T(1,128)S(1)}) custom-call(s32[15]{0:T(128)S(1)} %get-tuple-element.23.place_mine, s32[15]{0:T(128)S(1)} %get-tuple-element.22.place_got, s32[4]{0:T(128)S(1)} %copy-done.10, bf16[15,192,128]{2,1,0:T(8,128)(2,1)S(1)} %copy-done.12, bf16[15,192,128]{2,1,0:T(8,128)(2,1)S(1)} %collective-permute-done.12.got, ...), custom_call_target="tpu_custom_call" | custom-call | flops 1000000000 | bytes 4000000 | tf_op jit(solution)/shard_map/turn_back/pallas_call | solution.py:298
  100.4 0.5 slice_bitcast_fusion.2
  (41 shorter events, 0.2 us)
Async XLA Ops:
  2.3 22.1 %copy-start.17 = (bf16[256,29,49]{0,1,2:T(8,128)(2,1)S(1)}, bf16[256,29,49]{0,1,2:T(8,128)(2,1)}, u32[]{:S(2)}) copy-start(bf16[256,29,49]{0,1,2:T(8,128)(2,1)} %param.18) | copy-start | bytes 2182660
  4.2 20.6 %copy-start.19 = (s32[192]{0:T(256)S(1)}, s32[192]{0:T(256)}, u32[]{:S(2)}) copy-start(s32[192]{0:T(256)} %param.19) | copy-start | bytes 2308
  5.0 20.5 %copy-start.5 = (s32[192]{0:T(256)S(1)}, s32[192]{0:T(256)}, u32[]{:S(2)}) copy-start(s32[192]{0:T(256)} %param.20) | copy-start | bytes 2308
  5.9 20.4 %copy-start.6 = (s32[192]{0:T(256)S(1)}, s32[192]{0:T(256)}, u32[]{:S(2)}) copy-start(s32[192]{0:T(256)} %param.21) | copy-start | bytes 2308
  6.1 10.8 %collective-permute-start.2 = (bf16[86,8,128]{2,1,0:T(8,128)(2,1)S(1)}, bf16[86,8,128]{2,1,0:T(8,128)(2,1)S(1)}, u32[]{:S(2)}, u32[]{:S(2)}) collective-permute-start(bf16[86,8,128]{2,1,0:T(8,128)(2,1)S(1)} %maximum_select_fusion.1.refs_0_), channel_id=1, source_target_pairs={{0,2},{1,3},{2,0},{3,1},{4,6},{5,7},{6,4},{7,5},{8,10},{9,11},{10,... | collective-permute-start | bytes 528392 | tf_op jit(solution)/shard_map/ppermute | solution.py:326
  13.9 6.0 %collective-permute-start = (bf16[86,8,128]{2,1,0:T(8,128)(2,1)S(1)}, bf16[86,8,128]{2,1,0:T(8,128)(2,1)S(1)}, u32[]{:S(2)}, u32[]{:S(2)}) collective-permute-start(bf16[86,8,128]{2,1,0:T(8,128)(2,1)S(1)} %maximum_select_fusion.1.refs_0_), channel_id=1, source_target_pairs={{0,1},{1,2},{2,3},{3,0},{4,5},{5,6},{6,7},{7,4},{8,9},{9,10},{10,1... | collective-permute-start | bytes 528392 | tf_op jit(solution)/shard_map/ppermute | solution.py:326
  14.7 6.8 %collective-permute-start.1 = (bf16[86,8,128]{2,1,0:T(8,128)(2,1)S(1)}, bf16[86,8,128]{2,1,0:T(8,128)(2,1)S(1)}, u32[]{:S(2)}, u32[]{:S(2)}) collective-permute-start(bf16[86,8,128]{2,1,0:T(8,128)(2,1)S(1)} %maximum_select_fusion.1.refs_0_), channel_id=1, source_target_pairs={{0,3},{1,0},{2,1},{3,2},{4,7},{5,4},{6,5},{7,6},{8,11},{9,8},{10,9... | collective-permute-start | bytes 528392 | tf_op jit(solution)/shard_map/ppermute | solution.py:326
  20.0 10.9 %collective-permute-start.3 = (bf16[172,8,128]{2,1,0:T(8,128)(2,1)S(1)}, bf16[172,8,128]{2,1,0:T(8,128)(2,1)S(1)}, u32[]{:S(2)}, u32[]{:S(2)}) collective-permute-start(bf16[172,8,128]{2,1,0:T(8,128)(2,1)S(1)} %maximum_select_fusion), channel_id=1, source_target_pairs={{0,4},{1,5},{2,6},{3,7},{4,8},{5,9},{6,10},{7,11},{8,12},{9,13},{1... | collective-permute-start | bytes 1056776 | tf_op jit(solution)/shard_map/ppermute | solution.py:326
  21.5 0.7 copy-start
  22.1 10.2 %collective-permute-start.4 = (bf16[172,8,128]{2,1,0:T(8,128)(2,1)S(1)}, bf16[172,8,128]{2,1,0:T(8,128)(2,1)S(1)}, u32[]{:S(2)}, u32[]{:S(2)}) collective-permute-start(bf16[172,8,128]{2,1,0:T(8,128)(2,1)S(1)} %constant_dynamic-update-slice_fusion), channel_id=1, source_target_pairs={{0,28},{1,29},{2,30},{3,31},{4,0},{5,1},{6,2},{7,3},{8,4},{9,5},{1... | collective-permute-start | bytes 1056776 | tf_op jit(solution)/shard_map/ppermute | solution.py:326
  32.6 3.5 %copy-start.18 = (bf16[192,128]{1,0:T(8,128)(2,1)S(1)}, bf16[192,128]{1,0:T(8,128)(2,1)}, u32[]{:S(2)}) copy-start(bf16[192,128]{1,0:T(8,128)(2,1)} %param.22) | copy-start | bytes 147460
  32.6 3.6 %copy-start.2 = (s32[192,1]{1,0:T(8,128)S(1)}, s32[192,1]{1,0:T(8,128)}, u32[]{:S(2)}) copy-start(s32[192,1]{1,0:T(8,128)} %copy.34.source) | copy-start | bytes 2308
  32.6 3.6 %copy-start.3 = (s32[192,1]{1,0:T(8,128)S(1)}, s32[192,1]{1,0:T(8,128)}, u32[]{:S(2)}) copy-start(s32[192,1]{1,0:T(8,128)} %copy.35.target) | copy-start | bytes 2308
  32.7 3.6 %copy-start.4 = (s32[192,1]{1,0:T(8,128)S(1)}, s32[192,1]{1,0:T(8,128)}, u32[]{:S(2)}) copy-start(s32[192,1]{1,0:T(8,128)} %copy.36.rotation) | copy-start | bytes 2308
  32.7 3.6 %copy-start.7 = (bf16[48,6272]{1,0:T(8,128)(2,1)S(1)}, bf16[48,6272]{1,0:T(8,128)(2,1)}, u32[]{:S(2)}) copy-start(bf16[48,6272]{1,0:T(8,128)(2,1)} %node.3) | copy-start | bytes 1806340
  32.8 15.9 %collective-permute-start.6 = (bf16[344,8,128]{2,1,0:T(8,128)(2,1)S(1)}, bf16[344,8,128]{2,1,0:T(8,128)(2,1)S(1)}, u32[]{:S(2)}, u32[]{:S(2)}) collective-permute-start(bf16[344,8,128]{2,1,0:T(8,128)(2,1)S(1)} %pad_maximum_fusion.1), channel_id=1, source_target_pairs={{0,28},{1,29},{2,30},{3,31},{4,0},{5,1},{6,2},{7,3},{8,4},{9,5},{1... | collective-permute-start | bytes 2113544 | tf_op jit(solution)/shard_map/ppermute | solution.py:326
  35.9 12.8 %collective-permute-start.5 = (bf16[344,8,128]{2,1,0:T(8,128)(2,1)S(1)}, bf16[344,8,128]{2,1,0:T(8,128)(2,1)S(1)}, u32[]{:S(2)}, u32[]{:S(2)}) collective-permute-start(bf16[344,8,128]{2,1,0:T(8,128)(2,1)S(1)} %pad_maximum_fusion), channel_id=1, source_target_pairs={{0,4},{1,5},{2,6},{3,7},{4,8},{5,9},{6,10},{7,11},{8,12},{9,13},{1... | collective-permute-start | bytes 2113544 | tf_op jit(solution)/shard_map/ppermute | solution.py:326
  45.5 0.7 copy-start.13
  46.2 1.3 %copy-start.15 = (bf16[20,192,256]{2,1,0:T(8,128)(2,1)}, bf16[20,192,256]{2,1,0:T(8,128)(2,1)S(1)}, u32[]{:S(2)}) copy-start(bf16[20,192,256]{2,1,0:T(8,128)(2,1)S(1)} %get-tuple-element.9.refs_12_) | copy-start | bytes 5898244
  47.4 16.7 %collective-permute-start.11 = (bf16[20,192,256]{2,1,0:T(8,128)(2,1)}, bf16[20,192,256]{2,1,0:T(8,128)(2,1)}, u32[]{:S(2)}, u32[]{:S(2)}) collective-permute-start(bf16[20,192,256]{2,1,0:T(8,128)(2,1)} %get-tuple-element.10), channel_id=1, source_target_pairs={{0,32},{32,0},{64,96},{96,64},{128,160},{160,128},{192,224},{224,1... | collective-permute-start | bytes 5898248 | tf_op jit(solution)/shard_map/ppermute | solution.py:411
  48.7 15.4 %copy-start.22 = (s32[2,32,2]{1,2,0:T(2,128)S(1)}, s32[2,32,2]{1,2,0:T(2,128)}, u32[]{:S(2)}) copy-start(s32[2,32,2]{1,2,0:T(2,128)} %constant.73.clone) | copy-start | bytes 1540
  48.9 11.5 %collective-permute-start.7 = (bf16[344,8,128]{2,1,0:T(8,128)(2,1)S(1)}, bf16[344,8,128]{2,1,0:T(8,128)(2,1)S(1)}, u32[]{:S(2)}, u32[]{:S(2)}) collective-permute-start(bf16[344,8,128]{2,1,0:T(8,128)(2,1)S(1)} %get-tuple-element.17), channel_id=1, source_target_pairs={{0,4},{1,5},{2,6},{3,7},{4,8},{5,9},{6,10},{7,11},{8,12},{9,13},{1... | collective-permute-start | bytes 2113544 | tf_op jit(solution)/shard_map/ppermute | solution.py:326
  49.0 12.5 %collective-permute-start.8 = (bf16[344,8,128]{2,1,0:T(8,128)(2,1)S(1)}, bf16[344,8,128]{2,1,0:T(8,128)(2,1)}, u32[]{:S(2)}, u32[]{:S(2)}) collective-permute-start(bf16[344,8,128]{2,1,0:T(8,128)(2,1)S(1)} %get-tuple-element.16), channel_id=1, source_target_pairs={{0,28},{1,29},{2,30},{3,31},{4,0},{5,1},{6,2},{7,3},{8,4},{9,5},{1... | collective-permute-start | bytes 2113544 | tf_op jit(solution)/shard_map/ppermute | solution.py:326
  61.4 11.8 %collective-permute-start.9 = (bf16[344,8,128]{2,1,0:T(8,128)(2,1)}, bf16[344,8,128]{2,1,0:T(8,128)(2,1)}, u32[]{:S(2)}, u32[]{:S(2)}) collective-permute-start(bf16[344,8,128]{2,1,0:T(8,128)(2,1)} %broadcast_select_fusion), channel_id=1, source_target_pairs={{0,4},{1,5},{2,6},{3,7},{4,8},{5,9},{6,10},{7,11},{8,12},{9,13},{1... | collective-permute-start | bytes 2113544 | tf_op jit(solution)/shard_map/ppermute | solution.py:326
  61.4 11.8 %collective-permute-start.10 = (bf16[344,8,128]{2,1,0:T(8,128)(2,1)}, bf16[344,8,128]{2,1,0:T(8,128)(2,1)}, u32[]{:S(2)}, u32[]{:S(2)}) collective-permute-start(bf16[344,8,128]{2,1,0:T(8,128)(2,1)} %collective-permute-done.8.refs_9_), channel_id=1, source_target_pairs={{0,28},{1,29},{2,30},{3,31},{4,0},{5,1},{6,2},{7,3},{8,4},{9,5},{1... | collective-permute-start | bytes 2113544 | tf_op jit(solution)/shard_map/ppermute | solution.py:326
  73.2 0.9 copy-start.1
  74.1 1.5 %copy-start.16 = (bf16[20,192,256]{2,1,0:T(8,128)(2,1)S(1)}, bf16[20,192,256]{2,1,0:T(8,128)(2,1)}, u32[]{:S(2)}) copy-start(bf16[20,192,256]{2,1,0:T(8,128)(2,1)} %copy-done.15) | copy-start | bytes 5898244
  75.7 13.9 %copy-start.21 = (s32[48]{0:T(128)S(1)}, s32[48]{0:T(128)}, u32[]{:S(2)}) copy-start(s32[48]{0:T(128)} %param.29) | copy-start | bytes 580
  75.7 14.0 %copy-start.20 = (s32[2,15]{1,0:T(2,128)S(1)}, s32[2,15]{1,0:T(2,128)}, u32[]{:S(2)}) copy-start(s32[2,15]{1,0:T(2,128)} %constant.74.clone) | copy-start | bytes 364
  75.7 15.9 %copy-start.9 = (f32[5,128]{1,0:T(8,128)S(1)}, f32[5,128]{1,0:T(8,128)}, u32[]{:S(2)}) copy-start(f32[5,128]{1,0:T(8,128)} %head.1) | copy-start | bytes 7684
  75.7 15.9 %copy-start.10 = (s32[4]{0:T(128)S(1)}, s32[4]{0:T(128)}, u32[]{:S(2)}) copy-start(s32[4]{0:T(128)} %task.1) | copy-start | bytes 52
  85.4 0.9 copy-start.11
  86.3 5.3 %collective-permute-start.12 = (bf16[15,192,128]{2,1,0:T(8,128)(2,1)}, bf16[15,192,128]{2,1,0:T(8,128)(2,1)S(1)}, u32[]{:S(2)}, u32[]{:S(2)}) collective-permute-start(bf16[15,192,128]{2,1,0:T(8,128)(2,1)} %get-tuple-element.12), channel_id=1, source_target_pairs={{0,32},{32,0},{64,96},{96,64},{128,160},{160,128},{192,224},{224,1... | collective-permute-start | bytes 2211848 | tf_op jit(solution)/shard_map/ppermute | solution.py:413
  91.6 1.1 %copy-start.8 = (bf16[48,6272]{1,0:T(8,128)(2,1)S(1)}, bf16[48,6272]{1,0:T(8,128)(2,1)}, u32[]{:S(2)}) copy-start(bf16[48,6272]{1,0:T(8,128)(2,1)} %node.3) | copy-start | bytes 1806340
  92.7 1.1 %copy-start.12 = (bf16[15,192,128]{2,1,0:T(8,128)(2,1)S(1)}, bf16[15,192,128]{2,1,0:T(8,128)(2,1)}, u32[]{:S(2)}) copy-start(bf16[15,192,128]{2,1,0:T(8,128)(2,1)} %copy-done.11) | copy-start | bytes 2211844
  93.8 0.9 copy-start.14

commit v3 on v2

--- a/solution.py
+++ b/solution.py
@@ -12,6 +12,7 @@
 ATOMS = 48
 NROT = 256
 TILES = 86
+LATE = 8
 VMEM = pltpu.VMEM
 SMEM = pltpu.SMEM
 BF = jnp.bfloat16
@@ -141,26 +142,62 @@
             VMEM((EDGES, 2 * C), BF),
             pltpu.SemaphoreType.DMA((6,)),
         ],
-        compiler_params=pltpu.CompilerParams(vmem_limit_bytes=16 * 2**20),
+        compiler_params=pltpu.CompilerParams(vmem_limit_bytes=8 * 2**20),
         cost_estimate=pl.CostEstimate(flops=6 * 10**9, bytes_accessed=8 * 10**6, transcendentals=0),
         name="features",
     )(core, node, wig, source, target, rotation, filt)
 
 
-def conv_kernel(core, shard, *refs):
-    blocks = refs[:12]
-    own, got, mine, other, w_all, xz, xa, fl, fsem = refs[12:]
-
-    def place_blocks():
-        index = 0
-        for block in blocks:
-            for part in range(block.shape[0] // TILES):
-                w_all[shard[index]] = block[part * TILES : (part + 1) * TILES]
-                index += 1
-
-    def rows_of(first, count, g):
-        tiles = w_all[:, pl.ds(first + g * count, count)]
-        return tiles.reshape(32 * count * 8, C)
+def pack_kernel(core, zero, one_real, one_imag, two_real, two_imag, out):
+    def run(parts):
+        at = 0
+        for ref, first, groups in parts:
+            tiles = ref.shape[0] // 8
+            for g in range(first, first + groups):
+                out[at : at + tiles] = ref[:, g * C : (g + 1) * C].reshape(tiles, 8, C)
+                at += tiles
+        if at < TILES:
+            out[at:] = jnp.zeros((TILES - at, 8, C), BF)
+
+    @pl.when(core[0] == 0)
+    def _():
+        run(((one_real, 0, 6), (one_imag, 0, 6), (zero, 0, 2)))
+
+    @pl.when(core[0] == 1)
+    def _():
+        run(((two_real, 0, 5), (two_imag, 0, 5), (zero, 2, 5)))
+
+
+def pack(core, zero, one_real, one_imag, two_real, two_imag):
+    vm = pl.BlockSpec(memory_space=VMEM)
+    return pl.pallas_call(
+        pack_kernel,
+        out_shape=jax.ShapeDtypeStruct((TILES, 8, C), BF),
+        in_specs=[pl.BlockSpec(memory_space=SMEM)] + [vm] * 5,
+        out_specs=vm,
+        compiler_params=pltpu.CompilerParams(vmem_limit_bytes=4 * 2**20),
+        name="pack",
+    )(core, zero, one_real, one_imag, two_real, two_imag)
+
+
+def by_core(core, run):
+    @pl.when(core[0] == 0)
+    def _():
+        run(6, 6, 2)
+
+    @pl.when(core[0] == 1)
+    def _():
+        run(5, 5, 5)
+
+
+def group_rows(held, first, count, g):
+    tiles = held[:, pl.ds(first + g * count, count)]
+    return tiles.reshape(held.shape[0] * count * 8, C)
+
+
+def early_kernel(core, shard, *refs):
+    blocks = refs[:10]
+    own, got, part, part_zero, late, late_zero, w_all, xz, xa, fsem = refs[10:]
 
     def fetch_features(pieces):
         copies = []
@@ -177,8 +214,102 @@
                         src.at[7 + sign * 6 + k],
                         xa.at[pl.ds((sign * 2 + who) * EDGES, EDGES), pl.ds(k * 2 * C, 2 * C)],
                     )
-            add(src.at[19], fl.at[pl.ds(who * EDGES, EDGES)])
         return copies
+
+    def chosen(rows, deep):
+        lane = lax.broadcasted_iota(jnp.int32, (1, LATE * rows), 1)
+        wanted = lane
+        for i in range(LATE):
+            here = jnp.logical_and(lane >= i * rows, lane < (i + 1) * rows)
+            wanted = jnp.where(here, lane + (shard[32 - LATE + i] - i) * rows, wanted)
+        return (lax.broadcasted_iota(jnp.int32, (deep, 1), 0) == wanted).astype(F32).astype(BF)
+
+    def run(pieces, tiles, zero_groups):
+        copies = fetch_features(pieces)
+        for copy in copies:
+            copy.start()
+        for copy in copies:
+            copy.wait()
+        deep = pieces * 2 * C
+        size = pieces * tiles
+
+        def column(g, carry):
+            w = jnp.concatenate(
+                (group_rows(w_all, 0, tiles, g), group_rows(w_all, size, tiles, g)), axis=1
+            )
+            part[g] = jnp.dot(xa[:, :deep], w, preferred_element_type=F32)
+            return carry
+
+        lax.fori_loop(0, pieces, column, 0)
+        for g in range(0, zero_groups, 2):
+            count = min(2, zero_groups - g)
+            w = jnp.concatenate(
+                [group_rows(w_all, 2 * size, 7, g + i) for i in range(count)], axis=1
+            )
+            part_zero[g // 2, :, : count * C] = jnp.dot(xz[...], w, preferred_element_type=F32)
+        rows = tiles * 8
+        late[:, : LATE * rows] = jnp.dot(
+            xa[:, :deep], chosen(rows, deep), preferred_element_type=F32
+        ).astype(BF)
+        late_zero[...] = jnp.dot(
+            xz[...], chosen(56, 14 * C), preferred_element_type=F32
+        ).astype(BF)
+
+    def place(block, index):
+        def one(i, carry):
+            w_all[shard[index + i]] = block[pl.ds(i * TILES, TILES)]
+            return carry
+
+        lax.fori_loop(0, block.shape[0] // TILES, one, 0)
+
+    index = 0
+    for block in blocks:
+        place(block, index)
+        index += block.shape[0] // TILES
+
+    def clear(i, carry):
+        w_all[shard[32 - LATE + i]] = jnp.zeros((TILES, 8, C), BF)
+        return carry
+
+    lax.fori_loop(0, LATE, clear, 0)
+    by_core(core, run)
+
+
+def mix_early(core, shard, blocks, own, got):
+    vm = pl.BlockSpec(memory_space=VMEM)
+    anywhere = pl.BlockSpec(memory_space=pl.ANY)
+    smem = pl.BlockSpec(memory_space=SMEM)
+    return pl.pallas_call(
+        early_kernel,
+        out_shape=(
+            jax.ShapeDtypeStruct((6, 4 * EDGES, 2 * C), F32),
+            jax.ShapeDtypeStruct((3, 2 * EDGES, 2 * C), F32),
+            jax.ShapeDtypeStruct((4 * EDGES, LATE * 48), BF),
+            jax.ShapeDtypeStruct((2 * EDGES, LATE * 56), BF),
+        ),
+        in_specs=[smem, smem] + [vm] * 10 + [anywhere] * 2,
+        out_specs=(vm,) * 4,
+        scratch_shapes=[
+            VMEM((32, TILES, 8, C), BF),
+            VMEM((2 * EDGES, 14 * C), BF),
+            VMEM((4 * EDGES, 12 * C), BF),
+            pltpu.SemaphoreType.DMA((38,)),
+        ],
+        compiler_params=pltpu.CompilerParams(vmem_limit_bytes=20 * 2**20),
+        cost_estimate=pl.CostEstimate(flops=4 * 10**9, bytes_accessed=12 * 10**6, transcendentals=0),
+        name="mix_early",
+    )(core, shard, *blocks, own, got)
+
+
+def late_kernel(core, up, down, part, part_zero, late, late_zero, own, got, mine, other, fl, fsem):
+    copies = [
+        pltpu.make_async_copy(src.at[19], fl.at[pl.ds(who * EDGES, EDGES)], fsem.at[who])
+        for who, src in enumerate((own, got))
+    ]
+    for copy in copies:
+        copy.start()
+    for copy in copies:
+        copy.wait()
 
     def finish(plane, value, filters):
         message = (value * filters).astype(BF)
@@ -186,22 +317,20 @@
         other[plane] = message[EDGES:]
 
     def run(pieces, tiles, zero_groups):
-        waits = fetch_features(pieces)
-        for copy in waits:
-            copy.start()
-        place_blocks()
-        for copy in waits:
-            copy.wait()
         filters = fl[:, :C].astype(F32)
-        deep = pieces * 2 * C
         half = 2 * EDGES
         size = pieces * tiles
 
+        def rows_of(first, count, g):
+            return jnp.concatenate(
+                (group_rows(up, first, count, g), group_rows(down, first, count, g)), axis=0
+            )
+
         def column(g, carry):
-            w = jnp.concatenate(
-                (rows_of(0, tiles, g), rows_of(size, tiles, g)), axis=1
+            w = jnp.concatenate((rows_of(0, tiles, g), rows_of(size, tiles, g)), axis=1)
+            both = part[g] + jnp.dot(
+                late[:, : LATE * tiles * 8], w, preferred_element_type=F32
             )
-            both = jnp.dot(xa[:, :deep], w, preferred_element_type=F32)
             finish(g, both[:half, :C] - both[half:, C:], filters)
             finish(pieces + g, both[half:, :C] + both[:half, C:], filters)
             return carry
@@ -209,89 +338,90 @@
         lax.fori_loop(0, pieces, column, 0)
         for g in range(0, zero_groups, 2):
             count = min(2, zero_groups - g)
-            w = jnp.concatenate(
-                [rows_of(2 * size, 7, g + i) for i in range(count)], axis=1
+            w = jnp.concatenate([rows_of(2 * size, 7, g + i) for i in range(count)], axis=1)
+            total = part_zero[g // 2, :, : count * C] + jnp.dot(
+                late_zero[...], w, preferred_element_type=F32
             )
-            total = jnp.dot(xz[...], w, preferred_element_type=F32)
             for i in range(count):
                 finish(2 * pieces + g + i, total[:, i * C : (i + 1) * C], filters)
 
-    @pl.when(core[0] == 0)
-    def _():
-        run(6, 6, 2)
-
-    @pl.when(core[0] == 1)
-    def _():
-        run(5, 5, 5)
-
-
-def convolve(core, shard, blocks, own, got):
+    by_core(core, run)
+
+
+def mix_late(core, up, down, part, part_zero, late, late_zero, own, got):
     vm = pl.BlockSpec(memory_space=VMEM)
     anywhere = pl.BlockSpec(memory_space=pl.ANY)
-    smem = pl.BlockSpec(memory_space=SMEM)
     out = jax.ShapeDtypeStruct((15, EDGES, C), BF)
     return pl.pallas_call(
-        conv_kernel,
+        late_kernel,
         out_shape=(out, out),
-        in_specs=[smem, smem] + [vm] * 12 + [anywhere] * 2,
+        in_specs=[pl.BlockSpec(memory_space=SMEM)] + [vm] * 6 + [anywhere] * 2,
         out_specs=(vm, vm),
-        scratch_shapes=[
-            VMEM((32, TILES, 8, C), BF),
-            VMEM((2 * EDGES, 14 * C), BF),
-            VMEM((4 * EDGES, 12 * C), BF),
-            VMEM((2 * EDGES, 2 * C), BF),
-            pltpu.SemaphoreType.DMA((40,)),
-        ],
-        compiler_params=pltpu.CompilerParams(vmem_limit_bytes=24 * 2**20),
-        cost_estimate=pl.CostEstimate(flops=4 * 10**9, bytes_accessed=12 * 10**6, transcendentals=0),
-        name="convolve",
-    )(core, shard, *blocks, own, got)
+        scratch_shapes=[VMEM((2 * EDGES, 2 * C), BF), pltpu.SemaphoreType.DMA((2,))],
+        compiler_params=pltpu.CompilerParams(vmem_limit_bytes=8 * 2**20),
+        cost_estimate=pl.CostEstimate(flops=10**9, bytes_accessed=8 * 10**6, transcendentals=0),
+        name="mix_late",
+    )(core, up, down, part, part_zero, late, late_zero, own, got)
+
+
+def ends_kernel(wig, rotation, target, after, out):
+    del after
+    hot_r = lax.broadcasted_iota(jnp.int32, (NROT, EDGES), 0) == rotation[...]
+    d = jnp.dot(wig[...], hot_r.astype(F32).astype(BF), preferred_element_type=F32)
+    ends = lax.broadcasted_iota(jnp.int32, (ATOMS, EDGES), 0) == target[...]
+    at = 0
+    for degree in range(7):
+        for r in ROWS[degree]:
+            for j in range(2 * degree + 1):
+                entry = d[r * 16 + j : r * 16 + j + 1, :]
+                out[at : at + ATOMS, :] = jnp.where(ends, entry, 0.0).astype(BF)
+                at += ATOMS
+
+
+def ends_of(wig, rotation, target, after):
+    vm = pl.BlockSpec(memory_space=VMEM)
+    return pl.pallas_call(
+        ends_kernel,
+        out_shape=jax.ShapeDtypeStruct((235 * ATOMS, EDGES), BF),
+        in_specs=[vm] * 3 + [pl.BlockSpec(memory_space=pl.ANY)],
+        out_specs=vm,
+        compiler_params=pltpu.CompilerParams(vmem_limit_bytes=4 * 2**20),
+        cost_estimate=pl.CostEstimate(flops=10**8, bytes_accessed=6 * 10**6, transcendentals=0),
+        name="ends_of",
+    )(wig, rotation, target, after)
 
 
 def back_kernel(
-    place_mine, place_got, task, mine, got, wig, rotation, target, node, struct, head, update, energy, m, d, sem
+    place_mine, place_got, task, mine, got, hot, node, struct, head, update, energy, m, first, sem
 ):
-    copies = []
+    copies = [pltpu.make_async_copy(node.at[:, pl.ds(0, C)], first, sem.at[30])]
     for i in range(15):
-        copies.append(
-            pltpu.make_async_copy(mine.at[i], m.at[place_mine[i], pl.ds(0, EDGES)], sem.at[2 * i])
-        )
-        copies.append(
-            pltpu.make_async_copy(got.at[i], m.at[place_got[i], pl.ds(0, EDGES)], sem.at[2 * i + 1])
-        )
+        copies.append(pltpu.make_async_copy(mine.at[i], m.at[place_mine[i]], sem.at[2 * i]))
+        copies.append(pltpu.make_async_copy(got.at[i], m.at[place_got[i]], sem.at[2 * i + 1]))
     for copy in copies:
         copy.start()
-    hot_r = lax.broadcasted_iota(jnp.int32, (NROT, EDGES), 0) == rotation[...]
-    hot_r = hot_r.astype(F32).astype(BF)
-    d[...] = jnp.dot(wig[...], hot_r, preferred_element_type=F32)
-    ends = lax.broadcasted_iota(jnp.int32, (ATOMS, EDGES), 0) == target[...]
     for copy in copies:
         copy.wait()
+    at = 0
     for degree in range(7):
-        span = range(degree * degree, (degree + 1) * (degree + 1))
+        span = 2 * degree + 1
         total = None
         for r in ROWS[degree]:
-            hot = jnp.concatenate(
-                [jnp.where(ends, d[r * 16 + j : r * 16 + j + 1, :], 0.0).astype(BF) for j in range(len(span))],
-                axis=0,
-            )
-            term = jnp.dot(hot, m[r], preferred_element_type=F32)
+            term = jnp.dot(hot[at : at + span * ATOMS, :], m[r], preferred_element_type=F32)
             total = term if total is None else total + term
-        for place, j in enumerate(span):
+            at += span * ATOMS
+        for place in range(span):
             value = total[place * ATOMS : (place + 1) * ATOMS]
+            j = degree * degree + place
             update[:, j * C : (j + 1) * C] = value.astype(BF)
             if j == 0:
-                scalar_part = node[:, :C].astype(F32) + value
-    lane = lax.broadcasted_iota(jnp.int32, (1, C), 1)
-    result = jnp.zeros((1, C), F32)
+                scalar_part = first[...].astype(F32) + value
     for s in range(4):
         member = jnp.where(struct[...] == s, scalar_part, 0.0) * head[pl.ds(task[s], 1), :]
-        value = jnp.sum(jnp.sum(member, axis=0, keepdims=True), axis=1, keepdims=True)
-        result = jnp.where(lane == s, value, result)
-    energy[...] = result
-
-
-def turn_back(place_mine, place_got, task, mine, got, wig, rotation, target, node, struct, head):
+        energy[s] = jnp.sum(member)
+
+
+def turn_back(place_mine, place_got, task, mine, got, hot, node, struct, head):
     vm = pl.BlockSpec(memory_space=VMEM)
     anywhere = pl.BlockSpec(memory_space=pl.ANY)
     smem = pl.BlockSpec(memory_space=SMEM)
@@ -299,19 +429,19 @@
         back_kernel,
         out_shape=(
             jax.ShapeDtypeStruct((ATOMS, COEF * C), BF),
-            jax.ShapeDtypeStruct((1, C), F32),
+            jax.ShapeDtypeStruct((4,), F32),
         ),
-        in_specs=[smem] * 3 + [anywhere] * 2 + [vm] * 6,
-        out_specs=(vm, vm),
+        in_specs=[smem] * 3 + [anywhere] * 2 + [vm, anywhere, vm, vm],
+        out_specs=(vm, smem),
         scratch_shapes=[
             VMEM((30, EDGES, C), BF),
-            VMEM((4 * C, EDGES), F32),
-            pltpu.SemaphoreType.DMA((30,)),
+            VMEM((ATOMS, C), BF),
+            pltpu.SemaphoreType.DMA((31,)),
         ],
-        compiler_params=pltpu.CompilerParams(vmem_limit_bytes=16 * 2**20),
+        compiler_params=pltpu.CompilerParams(vmem_limit_bytes=6 * 2**20),
         cost_estimate=pl.CostEstimate(flops=10**9, bytes_accessed=4 * 10**6, transcendentals=0),
         name="turn_back",
-    )(place_mine, place_got, task, mine, got, wig, rotation, target, node, struct, head)
+    )(place_mine, place_got, task, mine, got, hot, node, struct, head)
 
 
 def exchange(value, sizes, steps_first, steps_second):
@@ -324,11 +454,6 @@
         to = ((z + dz) % nz) * ny + (y + dy) % ny
         pairs.append((device, m * nz * ny + to))
     return lax.ppermute(value, ("mol", "task"), pairs)
-
-
-def tiles_of(w):
-    rows, cols = w.shape
-    return w.reshape(rows // 8, 8, cols // C, C).transpose(2, 0, 1, 3).reshape(-1, 8, C)
 
 
 def body(
@@ -354,22 +479,12 @@
     z, y = task // 4, task % 4
     first = core == 0
 
+    core_vec = core.reshape(1).astype(jnp.int32)
+
     def pick(a, b):
         return jnp.where(first, a, b)
 
-    zero_tiles = w_zero
-    pack_first = jnp.concatenate(
-        (tiles_of(w_one_real), tiles_of(w_one_imag), tiles_of(zero_tiles[:, : 2 * C]))
-    )
-    pack_second = jnp.concatenate(
-        (
-            tiles_of(w_two_real),
-            tiles_of(w_two_imag),
-            tiles_of(zero_tiles[:, 2 * C :]),
-            jnp.zeros((1, 8, C), BF),
-        )
-    )
-    b0 = pick(pack_first, pack_second)
+    b0 = pack(core_vec, w_zero, w_one_real, w_one_imag, w_two_real, w_two_imag)
     a1 = exchange(b0, sizes, (0, 1), (1, 0))
     a2 = exchange(b0, sizes, (0, -1), (-1, 0))
     a3 = exchange(b0, sizes, (0, 2), (4, 0))
@@ -388,16 +503,8 @@
     s1m = aft(jnp.concatenate((h0, pick(p1m, h1))))
     p1 = jnp.concatenate((p1p, p1m))
     s2p, s2m = forth(pick(s1p, p1)), aft(pick(s1m, p1))
-    s3p, s3m = forth(pick(s2p, s1p)), aft(s2m)
-
-    blocks = (b0, a1, a2, a3, p1p, p1m, s1p, s1m, s2p, s2m, s3p, s3m)
-    offsets_first, offsets_second = block_offsets()
-    table = jnp.asarray((offsets_first, offsets_second), jnp.int32)[core]
-    shard = ((z + table[:, 0]) % 8) * 4 + (y + table[:, 1]) % 4
-
     live = (jnp.arange(EDGES, dtype=jnp.int32) < edge_count[0])[:, None]
     filters = jnp.where(live, edge_filter, jnp.zeros_like(edge_filter))
-    core_vec = core.reshape(1).astype(jnp.int32)
     own, send, entries = features(
         core_vec,
         node_embed,
@@ -407,9 +514,20 @@
         rotation.reshape(EDGES, 1),
         filters,
     )
+    hot = ends_of(entries, rotation.reshape(1, EDGES), target.reshape(1, EDGES), s1m)
+    s2p, s2m, hot = lax.optimization_barrier((s2p, s2m, hot))
+    s3p, s3m = forth(pick(s2p, s1p)), aft(s2m)
+
+    blocks = (b0, a1, a2, a3, p1p, p1m, s1p, s1m, s2p, s2m)
+    offsets_first, offsets_second = block_offsets()
+    table = jnp.asarray((offsets_first, offsets_second), jnp.int32)[core]
+    shard = ((z + table[:, 0]) % 8) * 4 + (y + table[:, 1]) % 4
+
     swap = [(i, i ^ 1) for i in range(8)]
     got = lax.ppermute(send, "mol", swap)
-    mine, other = convolve(core_vec, shard, blocks, own, got)
+    parts = mix_early(core_vec, shard, blocks, own, got)
+    held = (4, TILES, 8, C)
+    mine, other = mix_late(core_vec, s3p.reshape(held), s3m.reshape(held), *parts, own, got)
     back = lax.ppermute(other, "mol", swap)
     places = jnp.asarray(MADE, jnp.int32)
     update, energy = turn_back(
@@ -418,14 +536,12 @@
         struct_task,
         mine,
         back,
-        entries,
-        rotation.reshape(1, EDGES),
-        target.reshape(1, EDGES),
+        hot,
         node_embed,
         atom_struct.reshape(ATOMS, 1),
         task_head,
     )
-    return update, energy[0, :4]
+    return update, energy
 
 
 def solution(mesh):

time: 102 us -> 94.5 us (0.926)
  waiting for transfers between devices: 27.7 us -> 14.9 us
  Pallas kernels: 24.6 us -> 30 us
    ppermute x11, waiting for transfers between devices: 25.7 us -> 13 us  [exchange(): return lax.ppermute(value, ('mol', 'task'), pairs)]
    pallas_call x1 -> x4, Pallas kernels: 9.68 us -> 15.4 us  [the longest x1 10.3 us: mix_early(): pl.pallas_call(early_kernel, out_shape=(jax.ShapeDtypeStruct((6, 4 * EDGE...]
    reshape x8 -> x0, local copies, waits for them, and re-layouts: 5.17 us -> none  [tiles_of(): w.reshape(rows // 8, 8, cols // C, C).transpose(2, 0, 1, 3)]
    unnamed x49 -> x76, local copies, waits for them, and re-layouts: 9.58 us -> 14.6 us
    ppermute x1, starting transfers between devices: 3.29 us -> 5.66 us  [body(): back = lax.ppermute(other, 'mol', swap)]
    ppermute x11, starting transfers between devices: 22.9 us -> 21 us  [exchange(): return lax.ppermute(value, ('mol', 'task'), pairs)]
  transfers between devices with their start and end apart: 13 -> 13, of which waited for: 7 -> 7; matrix products, arithmetic and copies ran while one was open for 4% -> 6% of each run, Pallas kernels for 9% -> 22%
where the time goes in v3:
time: 94.5 us; the launch traced here: 93.9 us
  Pallas kernels  30 us (32%)
  starting transfers between devices  28.1 us (30%)
  local copies, waits for them, and re-layouts  17.1 us (18%)
  waiting for transfers between devices  14.9 us (16%)
  other arithmetic  1.96 us (2%)
  between operations  1.89 us (2%)
    ppermute x11, starting transfers between devices, exchange(): return lax.ppermute(value, ('mol', 'task'), pairs)  21 us
    unnamed x76, local copies, waits for them, and re-layouts  14.6 us
    ppermute x11, waiting for transfers between devices, exchange(): return lax.ppermute(value, ('mol', 'task'), pairs)  13 us
    pallas_call x1, Pallas kernels, mix_early(): pl.pallas_call(early_kernel, out_shape=(jax.ShapeDtypeStruct((6, 4 * EDGE...  10.3 us
    pallas_call x1, Pallas kernels, features(): pl.pallas_call(feature_kernel, out_shape=(jax.ShapeDtypeStruct((20, EDGES...  9.2 us
    ppermute x1, starting transfers between devices, body(): back = lax.ppermute(other, 'mol', swap)  5.66 us
    pallas_call x1, Pallas kernels, turn_back(): pl.pallas_call(back_kernel, out_shape=(jax.ShapeDtypeStruct((ATOMS, COEF...  5.38 us
    pallas_call x1, Pallas kernels, mix_late(): pl.pallas_call(late_kernel, out_shape=(out, out), in_specs=[pl.BlockSpec(...  4.28 us
  transfers between devices with their start and end apart: 13, of which 7 were waited for; matrix products, arithmetic and copies ran while one was open for 6% of the time, Pallas kernels for 22%

profile of v3, /device:TPU:1, one launch (start us, length us, event | category | flops | bytes accessed | tf_op | source)
XLA Modules:
  0.0 93.9 jit_solution(16096062791014580793)
XLA Ops:
  0.7 0.9 copy-done.18
  1.6 0.9 copy-done.22
  2.4 0.9 copy-done.23
  3.3 0.8 copy-done.24
  4.1 0.8 copy-done.25
  5.0 2.5 %collective-permute-start.2 = (bf16[86,8,128]{2,1,0:T(8,128)(2,1)S(1)}, bf16[86,8,128]{2,1,0:T(8,128)(2,1)S(1)}, u32[]{:S(2)}, u32[]{:S(2)}) collective-permute-start(bf16[86,8,128]{2,1,0:T(8,128)(2,1)S(1)} %pack.1.refs_0_), channel_id=1, source_target_pairs={{0,1},{1,2},{2,3},{3,0},{4,5},{5,6},{6,7},{7,4},{8,9},{9,10},{10,1... | collective-permute-start | bytes 528392 | tf_op jit(solution)/shard_map/ppermute | solution.py:456
  7.5 6.0 %collective-permute-start.1 = (bf16[86,8,128]{2,1,0:T(8,128)(2,1)S(1)}, bf16[86,8,128]{2,1,0:T(8,128)(2,1)S(1)}, u32[]{:S(2)}, u32[]{:S(2)}) collective-permute-start(bf16[86,8,128]{2,1,0:T(8,128)(2,1)S(1)} %pack.1.refs_0_), channel_id=1, source_target_pairs={{0,2},{1,3},{2,0},{3,1},{4,6},{5,7},{6,4},{7,5},{8,10},{9,11},{10,... | collective-permute-start | bytes 528392 | tf_op jit(solution)/shard_map/ppermute | solution.py:456
  13.5 1.9 %collective-permute-start = (bf16[86,8,128]{2,1,0:T(8,128)(2,1)S(1)}, bf16[86,8,128]{2,1,0:T(8,128)(2,1)S(1)}, u32[]{:S(2)}, u32[]{:S(2)}) collective-permute-start(bf16[86,8,128]{2,1,0:T(8,128)(2,1)S(1)} %pack.1.refs_0_), channel_id=1, source_target_pairs={{0,3},{1,0},{2,1},{3,2},{4,7},{5,4},{6,5},{7,6},{8,11},{9,8},{10,9... | collective-permute-start | bytes 528392 | tf_op jit(solution)/shard_map/ppermute | solution.py:456
  15.5 0.0 collective-permute-done.2.refs_1_
  15.5 2.9 %collective-permute-done.1.refs_3_ = bf16[86,8,128]{2,1,0:T(8,128)(2,1)S(1)} collective-permute-done((bf16[86,8,128]{2,1,0:T(8,128)(2,1)S(1)}, bf16[86,8,128]{2,1,0:T(8,128)(2,1)S(1)}, u32[]{:S(2)}, u32[]{:S(2)}) %collective-permute-start.1) | collective-permute-done | bytes 176160 | tf_op jit(solution)/shard_map/ppermute | solution.py:456
  18.4 0.1 maximum_select_fusion
  18.4 0.1 collective-permute-start.3
  18.5 2.4 %collective-permute-done.refs_2_ = bf16[86,8,128]{2,1,0:T(8,128)(2,1)S(1)} collective-permute-done((bf16[86,8,128]{2,1,0:T(8,128)(2,1)S(1)}, bf16[86,8,128]{2,1,0:T(8,128)(2,1)S(1)}, u32[]{:S(2)}, u32[]{:S(2)}) %collective-permute-start) | collective-permute-done | bytes 176160 | tf_op jit(solution)/shard_map/ppermute | solution.py:456
  20.9 0.6 copy-done.16
  21.6 2.5 %collective-permute-start.5 = (bf16[172,8,128]{2,1,0:T(8,128)(2,1)S(1)}, bf16[172,8,128]{2,1,0:T(8,128)(2,1)S(1)}, u32[]{:S(2)}, u32[]{:S(2)}) collective-permute-start(bf16[172,8,128]{2,1,0:T(8,128)(2,1)S(1)} %constant_dynamic-update-slice_fusion), channel_id=1, source_target_pairs={{0,28},{1,29},{2,30},{3,31},{4,0},{5,1},{6,2},{7,3},{8,4},{9,5},{1... | collective-permute-start | bytes 1056776 | tf_op jit(solution)/shard_map/ppermute | solution.py:456
  24.1 1.3 %copy.27 = bf16[256,29,49]{0,2,1:T(8,128)(2,1)} copy(bf16[256,29,49]{0,1,2:T(8,128)(2,1)S(1)} %copy-done.31) | data formatting | bytes 1455104 | tf_op args[1]
  25.4 0.8 copy.22.source
  26.2 0.8 copy.23.target
  26.9 0.8 copy.24.rotation
  28.4 0.1 broadcast_select_fusion.6.filt
  28.5 1.6 %collective-permute-done.3.refs_4_ = bf16[172,8,128]{2,1,0:T(8,128)(2,1)S(1)} collective-permute-done((bf16[172,8,128]{2,1,0:T(8,128)(2,1)S(1)}, bf16[172,8,128]{2,1,0:T(8,128)(2,1)S(1)}, u32[]{:S(2)}, u32[]{:S(2)}) %collective-permute-start.3) | collective-permute-done | bytes 352288 | tf_op jit(solution)/shard_map/ppermute | solution.py:456
  30.1 1.3 %collective-permute-done.5.refs_5_ = bf16[172,8,128]{2,1,0:T(8,128)(2,1)S(1)} collective-permute-done((bf16[172,8,128]{2,1,0:T(8,128)(2,1)S(1)}, bf16[172,8,128]{2,1,0:T(8,128)(2,1)S(1)}, u32[]{:S(2)}, u32[]{:S(2)}) %collective-permute-start.5) | collective-permute-done | bytes 352288 | tf_op jit(solution)/shard_map/ppermute | solution.py:456
  31.4 0.3 broadcast_select_fusion.3
  31.6 0.0 copy-start.7
  31.7 0.0 copy-start.10
  31.7 0.4 copy-done.4
  32.1 0.1 pad_maximum_fusion.1
  32.2 2.3 %collective-permute-start.7 = (bf16[344,8,128]{2,1,0:T(8,128)(2,1)S(1)}, bf16[344,8,128]{2,1,0:T(8,128)(2,1)S(1)}, u32[]{:S(2)}, u32[]{:S(2)}) collective-permute-start(bf16[344,8,128]{2,1,0:T(8,128)(2,1)S(1)} %pad_maximum_fusion.1), channel_id=1, source_target_pairs={{0,28},{1,29},{2,30},{3,31},{4,0},{5,1},{6,2},{7,3},{8,4},{9,5},{1... | collective-permute-start | bytes 2113544 | tf_op jit(solution)/shard_map/ppermute | solution.py:456
  34.5 0.1 pad_maximum_fusion
  34.6 0.1 collective-permute-start.4
  34.7 0.0 copy-start.5
  34.7 9.2 %features.1 = (bf16[20,192,256]{2,1,0:T(8,128)(2,1)S(1)}, bf16[20,192,256]{2,1,0:T(8,128)(2,1)}, bf16[512,256]{1,0:T(8,128)(2,1)S(1)}) custom-call(s32[1]{0:T(128)} %bitcast.2.core, bf16[48,6272]{1,0:T(8,128)(2,1)S(1)} %copy-done.10, bf16[29,49,256]{2,1,0:T(8,128)(2,1)S(1)} %bitcast.24, s32[192,1]{1,0:T(8,128)S(1)} %copy-done.19, s32[192,1]{1,0:T(8,128)S(1)} %copy-done.20, ...), custom_call_target="tpu_custom_call" | custom-call | flops 6000000000 | bytes 8000000 | tf_op jit(solution)/shard_map/features/pallas_call | solution.py:126
  44.0 0.0 copy-start.14
  44.0 1.4 %collective-permute-start.11 = (bf16[20,192,256]{2,1,0:T(8,128)(2,1)}, bf16[20,192,256]{2,1,0:T(8,128)(2,1)}, u32[]{:S(2)}, u32[]{:S(2)}) collective-permute-start(bf16[20,192,256]{2,1,0:T(8,128)(2,1)} %get-tuple-element.18), channel_id=1, source_target_pairs={{0,32},{32,0},{64,96},{96,64},{128,160},{160,128},{192,224},{224,1... | collective-permute-start | bytes 5898248 | tf_op jit(solution)/shard_map/ppermute | solution.py:527
  45.4 0.0 copy-done.5
  45.4 0.0 collective-permute-done.7.after.refs_7_
  45.5 0.7 collective-permute-done.4.refs_6_
  46.1 1.3 %broadcast_select_fusion.1 = (bf16[344,8,128]{2,1,0:T(8,128)(2,1)}, bf16[344,8,128]{2,1,0:T(8,128)(2,1)}) fusion(bf16[344,8,128]{2,1,0:T(8,128)(2,1)S(1)} %collective-permute-done.7.after.refs_7_, bf16[344,8,128]{2,1,0:T(8,128)(2,1)S(1)} %constant_dynamic-update-slice_fusion.2, pred[]{:T(512)S(6)} %eq.9, ...), kind=kLoop, calls=%fused_computation.4 | loop fusion | flops 704512 | bytes 3522561 | tf_op jit(solution)/shard_map/jit(_where)/select_n | solution.py:485
  47.5 0.4 collective-permute-start.6
  47.9 2.3 %collective-permute-start.8 = (bf16[344,8,128]{2,1,0:T(8,128)(2,1)}, bf16[344,8,128]{2,1,0:T(8,128)(2,1)}, u32[]{:S(2)}, u32[]{:S(2)}) collective-permute-start(bf16[344,8,128]{2,1,0:T(8,128)(2,1)} %get-tuple-element.26), channel_id=1, source_target_pairs={{0,28},{1,29},{2,30},{3,31},{4,0},{5,1},{6,2},{7,3},{8,4},{9,5},{1... | collective-permute-start | bytes 2113544 | tf_op jit(solution)/shard_map/ppermute | solution.py:456
  50.1 0.9 %copy-done.15 = bf16[512,256]{1,0:T(8,128)(2,1)S(1)} copy-done((bf16[512,256]{1,0:T(8,128)(2,1)S(1)}, bf16[512,256]{1,0:T(8,128)(2,1)}, u32[]{:S(2)}) %copy-start.15) | copy-done | bytes 262168
  51.1 0.7 copy-done.29
  51.8 0.8 ends_of.1.hot
  52.6 2.5 %copy-done = bf16[11280,192]{1,0:T(8,128)(2,1)} copy-done((bf16[11280,192]{1,0:T(8,128)(2,1)}, bf16[11280,192]{1,0:T(8,128)(2,1)S(1)}, u32[]{:S(2)}) %copy-start) | copy-done | bytes 4331544
  55.1 4.1 %collective-permute-done.6.refs_8_ = bf16[344,8,128]{2,1,0:T(8,128)(2,1)} collective-permute-done((bf16[344,8,128]{2,1,0:T(8,128)(2,1)}, bf16[344,8,128]{2,1,0:T(8,128)(2,1)}, u32[]{:S(2)}, u32[]{:S(2)}) %collective-permute-start.6) | collective-permute-done | bytes 704544 | tf_op jit(solution)/shard_map/ppermute | solution.py:456
  59.2 0.0 collective-permute-done.8.refs_9_
  59.2 0.1 broadcast_select_fusion
  59.3 0.1 collective-permute-start.9
  59.4 2.7 %collective-permute-start.10 = (bf16[344,8,128]{2,1,0:T(8,128)(2,1)}, bf16[344,8,128]{2,1,0:T(8,128)(2,1)S(1)}, u32[]{:S(2)}, u32[]{:S(2)}) collective-permute-start(bf16[344,8,128]{2,1,0:T(8,128)(2,1)} %collective-permute-done.8.refs_9_), channel_id=1, source_target_pairs={{0,28},{1,29},{2,30},{3,31},{4,0},{5,1},{6,2},{7,3},{8,4},{9,5},{1... | collective-permute-start | bytes 2113544 | tf_op jit(solution)/shard_map/ppermute | solution.py:456
  62.2 0.0 collective-permute-done.11.refs_11_.got
  62.3 10.3 %mix_early.1 = (f32[6,768,256]{2,1,0:T(8,128)S(1)}, f32[3,384,256]{2,1,0:T(8,128)S(1)}, bf16[768,384]{1,0:T(8,128)(2,1)S(1)}, bf16[384,448]{1,0:T(8,128)(2,1)S(1)}) custom-call(s32[1]{0:T(128)} %bitcast.2.core, s32[32]{0:T(128)S(1)} %fusion.shard, bf16[86,8,128]{2,1,0:T(8,128)(2,1)S(1)} %pack.1.refs_0_, bf16[86,8,128]{2,1,0:T(8,128)(2,1)S(1)} %copy-done.3, ...), custom_call_target="tpu_custom_call" | custom-call | flops 4000000000 | bytes 12000000 | tf_op jit(solution)/shard_map/mix_early/pallas_call | solution.py:282
  72.6 0.0 collective-permute-done.9
  72.6 0.0 collective-permute-done.10
  72.6 0.0 copy-start.35
  72.6 0.0 copy-start.34
  72.6 0.0 copy-start.26
  72.6 0.0 copy-start.30
  72.7 4.3 %mix_late.1 = (bf16[15,192,128]{2,1,0:T(8,128)(2,1)S(1)}, bf16[15,192,128]{2,1,0:T(8,128)(2,1)}) custom-call(s32[1]{0:T(128)} %bitcast.2.core, bf16[4,86,8,128]{3,2,1,0:T(8,128)(2,1)S(1)} %bitcast.25, bf16[4,86,8,128]{3,2,1,0:T(8,128)(2,1)S(1)} %bitcast.26, f32[6,768,256]{2,1,0:T(8,128)S(1)} %get-tuple-element.19.part, ...), custom_call_target="tpu_custom_call" | custom-call | flops 1000000000 | bytes 8000000 | tf_op jit(solution)/shard_map/mix_late/pallas_call | solution.py:355
  76.9 5.7 %collective-permute-start.12 = (bf16[15,192,128]{2,1,0:T(8,128)(2,1)}, bf16[15,192,128]{2,1,0:T(8,128)(2,1)S(1)}, u32[]{:S(2)}, u32[]{:S(2)}) collective-permute-start(bf16[15,192,128]{2,1,0:T(8,128)(2,1)} %get-tuple-element.24), channel_id=1, source_target_pairs={{0,32},{32,0},{64,96},{96,64},{128,160},{160,128},{192,224},{224,1... | collective-permute-start | bytes 2211848 | tf_op jit(solution)/shard_map/ppermute | solution.py:531
  82.6 0.1 copy.25.struct
  82.7 1.9 %collective-permute-done.12.got = bf16[15,192,128]{2,1,0:T(8,128)(2,1)S(1)} collective-permute-done((bf16[15,192,128]{2,1,0:T(8,128)(2,1)}, bf16[15,192,128]{2,1,0:T(8,128)(2,1)S(1)}, u32[]{:S(2)}, u32[]{:S(2)}) %collective-permute-start.12) | collective-permute-done | bytes 737312 | tf_op jit(solution)/shard_map/ppermute | solution.py:531
  84.7 2.6 %copy-done.1 = bf16[11280,192]{1,0:T(8,128)(2,1)S(1)} copy-done((bf16[11280,192]{1,0:T(8,128)(2,1)S(1)}, bf16[11280,192]{1,0:T(8,128)(2,1)}, u32[]{:S(2)}) %copy-start.1) | copy-done | bytes 4331544
  87.3 1.1 %copy-done.11 = bf16[48,6272]{1,0:T(8,128)(2,1)S(1)} copy-done((bf16[48,6272]{1,0:T(8,128)(2,1)S(1)}, bf16[48,6272]{1,0:T(8,128)(2,1)}, u32[]{:S(2)}) %copy-start.11) | copy-done | bytes 602136
  88.4 5.4 %turn_back.1 = (bf16[48,6272]{1,0:T(8,128)(2,1)}, f32[4]{0:T(128)}) custom-call(s32[15]{0:T(128)S(1)} %get-tuple-element.33.place_mine, s32[15]{0:T(128)S(1)} %get-tuple-element.32.place_got, s32[4]{0:T(128)S(1)} %copy-done.30, bf16[15,192,128]{2,1,0:T(8,128)(2,1)S(1)} %get-tuple-element.23.mine, bf16[15,192,128]{2,1,0:T(8,128)(2,1)S(1)} %collective-permute-done.12.got, ...), custom_call_target="tpu_custom_call" | custom-call | flops 1000000000 | bytes 4000000 | tf_op jit(solution)/shard_map/turn_back/pallas_call | solution.py:428
  (61 shorter events, 0.2 us)
Async XLA Ops:
  0.6 24.8 %copy-start.33 = (s32[192]{0:T(256)S(1)}, s32[192]{0:T(256)}, u32[]{:S(2)}) copy-start(s32[192]{0:T(256)} %param.19) | copy-start | bytes 2308
  0.6 25.5 %copy-start.27 = (s32[192]{0:T(256)S(1)}, s32[192]{0:T(256)}, u32[]{:S(2)}) copy-start(s32[192]{0:T(256)} %param.20) | copy-start | bytes 2308
  0.7 0.9 copy-start.18
  1.6 0.9 copy-start.22
  2.4 0.9 copy-start.23
  3.3 0.8 copy-start.24
  4.1 0.8 copy-start.25
  4.9 19.1 %copy-start.31 = (bf16[256,29,49]{0,1,2:T(8,128)(2,1)S(1)}, bf16[256,29,49]{0,1,2:T(8,128)(2,1)}, u32[]{:S(2)}) copy-start(bf16[256,29,49]{0,1,2:T(8,128)(2,1)} %param.18) | copy-start | bytes 2182660
  4.9 22.0 %copy-start.28 = (s32[192]{0:T(256)S(1)}, s32[192]{0:T(256)}, u32[]{:S(2)}) copy-start(s32[192]{0:T(256)} %param.21) | copy-start | bytes 2308
  4.9 23.4 %copy-start.32 = (bf16[192,128]{1,0:T(8,128)(2,1)S(1)}, bf16[192,128]{1,0:T(8,128)(2,1)}, u32[]{:S(2)}) copy-start(bf16[192,128]{1,0:T(8,128)(2,1)} %param.22) | copy-start | bytes 147460
  5.0 10.5 %collective-permute-start.2 = (bf16[86,8,128]{2,1,0:T(8,128)(2,1)S(1)}, bf16[86,8,128]{2,1,0:T(8,128)(2,1)S(1)}, u32[]{:S(2)}, u32[]{:S(2)}) collective-permute-start(bf16[86,8,128]{2,1,0:T(8,128)(2,1)S(1)} %pack.1.refs_0_), channel_id=1, source_target_pairs={{0,1},{1,2},{2,3},{3,0},{4,5},{5,6},{6,7},{7,4},{8,9},{9,10},{10,1... | collective-permute-start | bytes 528392 | tf_op jit(solution)/shard_map/ppermute | solution.py:456
  7.5 10.8 %collective-permute-start.1 = (bf16[86,8,128]{2,1,0:T(8,128)(2,1)S(1)}, bf16[86,8,128]{2,1,0:T(8,128)(2,1)S(1)}, u32[]{:S(2)}, u32[]{:S(2)}) collective-permute-start(bf16[86,8,128]{2,1,0:T(8,128)(2,1)S(1)} %pack.1.refs_0_), channel_id=1, source_target_pairs={{0,2},{1,3},{2,0},{3,1},{4,6},{5,7},{6,4},{7,5},{8,10},{9,11},{10,... | collective-permute-start | bytes 528392 | tf_op jit(solution)/shard_map/ppermute | solution.py:456
  13.5 7.3 %collective-permute-start = (bf16[86,8,128]{2,1,0:T(8,128)(2,1)S(1)}, bf16[86,8,128]{2,1,0:T(8,128)(2,1)S(1)}, u32[]{:S(2)}, u32[]{:S(2)}) collective-permute-start(bf16[86,8,128]{2,1,0:T(8,128)(2,1)S(1)} %pack.1.refs_0_), channel_id=1, source_target_pairs={{0,3},{1,0},{2,1},{3,2},{4,7},{5,4},{6,5},{7,6},{8,11},{9,8},{10,9... | collective-permute-start | bytes 528392 | tf_op jit(solution)/shard_map/ppermute | solution.py:456
  15.5 16.2 %copy-start.2 = (bf16[86,8,128]{2,1,0:T(8,128)(2,1)}, bf16[86,8,128]{2,1,0:T(8,128)(2,1)S(1)}, u32[]{:S(2)}) copy-start(bf16[86,8,128]{2,1,0:T(8,128)(2,1)S(1)} %collective-permute-done.2.refs_1_) | copy-start | bytes 528388
  18.4 2.5 %copy-start.8 = (bf16[86,8,128]{2,1,0:T(8,128)(2,1)}, bf16[86,8,128]{2,1,0:T(8,128)(2,1)S(1)}, u32[]{:S(2)}) copy-start(bf16[86,8,128]{2,1,0:T(8,128)(2,1)S(1)} %collective-permute-done.1.refs_3_) | copy-start | bytes 528388
  18.4 11.7 %collective-permute-start.3 = (bf16[172,8,128]{2,1,0:T(8,128)(2,1)S(1)}, bf16[172,8,128]{2,1,0:T(8,128)(2,1)S(1)}, u32[]{:S(2)}, u32[]{:S(2)}) collective-permute-start(bf16[172,8,128]{2,1,0:T(8,128)(2,1)S(1)} %maximum_select_fusion), channel_id=1, source_target_pairs={{0,4},{1,5},{2,6},{3,7},{4,8},{5,9},{6,10},{7,11},{8,12},{9,13},{1... | collective-permute-start | bytes 1056776 | tf_op jit(solution)/shard_map/ppermute | solution.py:456
  20.9 0.7 copy-start.16
  21.6 9.8 %collective-permute-start.5 = (bf16[172,8,128]{2,1,0:T(8,128)(2,1)S(1)}, bf16[172,8,128]{2,1,0:T(8,128)(2,1)S(1)}, u32[]{:S(2)}, u32[]{:S(2)}) collective-permute-start(bf16[172,8,128]{2,1,0:T(8,128)(2,1)S(1)} %constant_dynamic-update-slice_fusion), channel_id=1, source_target_pairs={{0,28},{1,29},{2,30},{3,31},{4,0},{5,1},{6,2},{7,3},{8,4},{9,5},{1... | collective-permute-start | bytes 1056776 | tf_op jit(solution)/shard_map/ppermute | solution.py:456
  30.1 1.6 %copy-start.12 = (bf16[172,8,128]{2,1,0:T(8,128)(2,1)}, bf16[172,8,128]{2,1,0:T(8,128)(2,1)S(1)}, u32[]{:S(2)}) copy-start(bf16[172,8,128]{2,1,0:T(8,128)(2,1)S(1)} %collective-permute-done.3.refs_4_) | copy-start | bytes 1056772
  31.4 0.7 copy-start.4
  31.6 3.0 %copy-start.7 = (bf16[256,29,49]{0,2,1:T(8,128)(2,1)S(1)}, bf16[256,29,49]{0,2,1:T(8,128)(2,1)}, u32[]{:S(2)}) copy-start(bf16[256,29,49]{0,2,1:T(8,128)(2,1)} %copy.27) | copy-start | bytes 2182660
  31.7 3.0 %copy-start.10 = (bf16[48,6272]{1,0:T(8,128)(2,1)S(1)}, bf16[48,6272]{1,0:T(8,128)(2,1)}, u32[]{:S(2)}) copy-start(bf16[48,6272]{1,0:T(8,128)(2,1)} %node.3) | copy-start | bytes 1806340
  31.7 3.0 %copy-start.19 = (s32[192,1]{1,0:T(8,128)S(1)}, s32[192,1]{1,0:T(8,128)}, u32[]{:S(2)}) copy-start(s32[192,1]{1,0:T(8,128)} %copy.22.source) | copy-start | bytes 2308
  31.7 3.0 %copy-start.20 = (s32[192,1]{1,0:T(8,128)S(1)}, s32[192,1]{1,0:T(8,128)}, u32[]{:S(2)}) copy-start(s32[192,1]{1,0:T(8,128)} %copy.23.target) | copy-start | bytes 2308
  31.7 3.0 %copy-start.21 = (s32[192,1]{1,0:T(8,128)S(1)}, s32[192,1]{1,0:T(8,128)}, u32[]{:S(2)}) copy-start(s32[192,1]{1,0:T(8,128)} %copy.24.rotation) | copy-start | bytes 2308
  32.2 13.3 %collective-permute-start.7 = (bf16[344,8,128]{2,1,0:T(8,128)(2,1)S(1)}, bf16[344,8,128]{2,1,0:T(8,128)(2,1)S(1)}, u32[]{:S(2)}, u32[]{:S(2)}) collective-permute-start(bf16[344,8,128]{2,1,0:T(8,128)(2,1)S(1)} %pad_maximum_fusion.1), channel_id=1, source_target_pairs={{0,28},{1,29},{2,30},{3,31},{4,0},{5,1},{6,2},{7,3},{8,4},{9,5},{1... | collective-permute-start | bytes 2113544 | tf_op jit(solution)/shard_map/ppermute | solution.py:456
  34.6 11.5 %collective-permute-start.4 = (bf16[344,8,128]{2,1,0:T(8,128)(2,1)S(1)}, bf16[344,8,128]{2,1,0:T(8,128)(2,1)S(1)}, u32[]{:S(2)}, u32[]{:S(2)}) collective-permute-start(bf16[344,8,128]{2,1,0:T(8,128)(2,1)S(1)} %pad_maximum_fusion), channel_id=1, source_target_pairs={{0,4},{1,5},{2,6},{3,7},{4,8},{5,9},{6,10},{7,11},{8,12},{9,13},{1... | collective-permute-start | bytes 2113544 | tf_op jit(solution)/shard_map/ppermute | solution.py:456
  34.7 10.7 %copy-start.5 = (bf16[172,8,128]{2,1,0:T(8,128)(2,1)S(1)}, bf16[172,8,128]{2,1,0:T(8,128)(2,1)}, u32[]{:S(2)}) copy-start(bf16[172,8,128]{2,1,0:T(8,128)(2,1)} %copy-done.4) | copy-start | bytes 1056772
  44.0 1.5 %copy-start.14 = (bf16[512,256]{1,0:T(8,128)(2,1)}, bf16[512,256]{1,0:T(8,128)(2,1)S(1)}, u32[]{:S(2)}) copy-start(bf16[512,256]{1,0:T(8,128)(2,1)S(1)} %get-tuple-element.14.wig) | copy-start | bytes 786436
  44.0 18.2 %collective-permute-start.11 = (bf16[20,192,256]{2,1,0:T(8,128)(2,1)}, bf16[20,192,256]{2,1,0:T(8,128)(2,1)}, u32[]{:S(2)}, u32[]{:S(2)}) collective-permute-start(bf16[20,192,256]{2,1,0:T(8,128)(2,1)} %get-tuple-element.18), channel_id=1, source_target_pairs={{0,32},{32,0},{64,96},{96,64},{128,160},{160,128},{192,224},{224,1... | collective-permute-start | bytes 5898248 | tf_op jit(solution)/shard_map/ppermute | solution.py:527
  47.5 11.8 %collective-permute-start.6 = (bf16[344,8,128]{2,1,0:T(8,128)(2,1)}, bf16[344,8,128]{2,1,0:T(8,128)(2,1)}, u32[]{:S(2)}, u32[]{:S(2)}) collective-permute-start(bf16[344,8,128]{2,1,0:T(8,128)(2,1)} %get-tuple-element.27), channel_id=1, source_target_pairs={{0,4},{1,5},{2,6},{3,7},{4,8},{5,9},{6,10},{7,11},{8,12},{9,13},{1... | collective-permute-start | bytes 2113544 | tf_op jit(solution)/shard_map/ppermute | solution.py:456
  47.9 11.4 %collective-permute-start.8 = (bf16[344,8,128]{2,1,0:T(8,128)(2,1)}, bf16[344,8,128]{2,1,0:T(8,128)(2,1)}, u32[]{:S(2)}, u32[]{:S(2)}) collective-permute-start(bf16[344,8,128]{2,1,0:T(8,128)(2,1)} %get-tuple-element.26), channel_id=1, source_target_pairs={{0,28},{1,29},{2,30},{3,31},{4,0},{5,1},{6,2},{7,3},{8,4},{9,5},{1... | collective-permute-start | bytes 2113544 | tf_op jit(solution)/shard_map/ppermute | solution.py:456
  50.1 0.9 %copy-start.15 = (bf16[512,256]{1,0:T(8,128)(2,1)S(1)}, bf16[512,256]{1,0:T(8,128)(2,1)}, u32[]{:S(2)}) copy-start(bf16[512,256]{1,0:T(8,128)(2,1)} %copy-done.14) | copy-start | bytes 786436
  51.1 0.7 copy-start.29
  52.6 2.5 %copy-start = (bf16[11280,192]{1,0:T(8,128)(2,1)}, bf16[11280,192]{1,0:T(8,128)(2,1)S(1)}, u32[]{:S(2)}) copy-start(bf16[11280,192]{1,0:T(8,128)(2,1)S(1)} %ends_of.1.hot) | copy-start | bytes 12994564
  55.1 7.1 %copy-start.36 = (s32[2,32,2]{1,2,0:T(2,128)S(1)}, s32[2,32,2]{1,2,0:T(2,128)}, u32[]{:S(2)}) copy-start(s32[2,32,2]{1,2,0:T(2,128)} %constant.72.clone) | copy-start | bytes 1540
  55.1 7.1 %copy-start.3 = (bf16[86,8,128]{2,1,0:T(8,128)(2,1)S(1)}, bf16[86,8,128]{2,1,0:T(8,128)(2,1)}, u32[]{:S(2)}) copy-start(bf16[86,8,128]{2,1,0:T(8,128)(2,1)} %copy-done.2) | copy-start | bytes 528388
  55.1 7.1 %copy-start.6 = (bf16[172,8,128]{2,1,0:T(8,128)(2,1)S(1)}, bf16[172,8,128]{2,1,0:T(8,128)(2,1)}, u32[]{:S(2)}) copy-start(bf16[172,8,128]{2,1,0:T(8,128)(2,1)} %copy-done.4) | copy-start | bytes 1056772
  55.1 7.1 %copy-start.9 = (bf16[86,8,128]{2,1,0:T(8,128)(2,1)S(1)}, bf16[86,8,128]{2,1,0:T(8,128)(2,1)}, u32[]{:S(2)}) copy-start(bf16[86,8,128]{2,1,0:T(8,128)(2,1)} %copy-done.8) | copy-start | bytes 528388
  55.1 7.2 %copy-start.13 = (bf16[172,8,128]{2,1,0:T(8,128)(2,1)S(1)}, bf16[172,8,128]{2,1,0:T(8,128)(2,1)}, u32[]{:S(2)}) copy-start(bf16[172,8,128]{2,1,0:T(8,128)(2,1)} %copy-done.12) | copy-start | bytes 1056772
  55.1 7.2 %copy-start.17 = (bf16[86,8,128]{2,1,0:T(8,128)(2,1)S(1)}, bf16[86,8,128]{2,1,0:T(8,128)(2,1)}, u32[]{:S(2)}) copy-start(bf16[86,8,128]{2,1,0:T(8,128)(2,1)} %copy-done.16) | copy-start | bytes 528388
  59.3 13.3 %collective-permute-start.9 = (bf16[344,8,128]{2,1,0:T(8,128)(2,1)S(1)}, bf16[344,8,128]{2,1,0:T(8,128)(2,1)S(1)}, u32[]{:S(2)}, u32[]{:S(2)}) collective-permute-start(bf16[344,8,128]{2,1,0:T(8,128)(2,1)S(1)} %broadcast_select_fusion), channel_id=1, source_target_pairs={{0,4},{1,5},{2,6},{3,7},{4,8},{5,9},{6,10},{7,11},{8,12},{9,13},{1... | collective-permute-start | bytes 2113544 | tf_op jit(solution)/shard_map/ppermute | solution.py:456
  59.4 13.2 %collective-permute-start.10 = (bf16[344,8,128]{2,1,0:T(8,128)(2,1)}, bf16[344,8,128]{2,1,0:T(8,128)(2,1)S(1)}, u32[]{:S(2)}, u32[]{:S(2)}) collective-permute-start(bf16[344,8,128]{2,1,0:T(8,128)(2,1)} %collective-permute-done.8.refs_9_), channel_id=1, source_target_pairs={{0,28},{1,29},{2,30},{3,31},{4,0},{5,1},{6,2},{7,3},{8,4},{9,5},{1... | collective-permute-start | bytes 2113544 | tf_op jit(solution)/shard_map/ppermute | solution.py:456
  72.6 10.0 %copy-start.35 = (s32[48]{0:T(128)S(1)}, s32[48]{0:T(128)}, u32[]{:S(2)}) copy-start(s32[48]{0:T(128)} %param.29) | copy-start | bytes 580
  72.6 10.1 %copy-start.34 = (s32[2,15]{1,0:T(2,128)S(1)}, s32[2,15]{1,0:T(2,128)}, u32[]{:S(2)}) copy-start(s32[2,15]{1,0:T(2,128)} %constant.73.clone) | copy-start | bytes 364
  72.6 12.0 %copy-start.26 = (f32[5,128]{1,0:T(8,128)S(1)}, f32[5,128]{1,0:T(8,128)}, u32[]{:S(2)}) copy-start(f32[5,128]{1,0:T(8,128)} %head.1) | copy-start | bytes 7684
  72.6 12.0 %copy-start.30 = (s32[4]{0:T(128)S(1)}, s32[4]{0:T(128)}, u32[]{:S(2)}) copy-start(s32[4]{0:T(128)} %task.1) | copy-start | bytes 52
  76.9 7.7 %collective-permute-start.12 = (bf16[15,192,128]{2,1,0:T(8,128)(2,1)}, bf16[15,192,128]{2,1,0:T(8,128)(2,1)S(1)}, u32[]{:S(2)}, u32[]{:S(2)}) collective-permute-start(bf16[15,192,128]{2,1,0:T(8,128)(2,1)} %get-tuple-element.24), channel_id=1, source_target_pairs={{0,32},{32,0},{64,96},{96,64},{128,160},{160,128},{192,224},{224,1... | collective-permute-start | bytes 2211848 | tf_op jit(solution)/shard_map/ppermute | solution.py:531
  84.7 2.6 %copy-start.1 = (bf16[11280,192]{1,0:T(8,128)(2,1)S(1)}, bf16[11280,192]{1,0:T(8,128)(2,1)}, u32[]{:S(2)}) copy-start(bf16[11280,192]{1,0:T(8,128)(2,1)} %copy-done) | copy-start | bytes 12994564
  87.3 1.1 %copy-start.11 = (bf16[48,6272]{1,0:T(8,128)(2,1)S(1)}, bf16[48,6272]{1,0:T(8,128)(2,1)}, u32[]{:S(2)}) copy-start(bf16[48,6272]{1,0:T(8,128)(2,1)} %node.3) | copy-start | bytes 1806340

commit v4 on v3

--- a/solution.py
+++ b/solution.py
@@ -25,7 +25,7 @@
     ROWS[degree] += [17 + degree, 22 + degree]
 
 MADE = (
-    tuple(range(7, 19)) + (0, 1, 29),
+    tuple(range(7, 19)) + (0, 1),
     tuple(range(19, 29)) + (2, 3, 4, 5, 6),
 )
 
@@ -58,7 +58,7 @@
 
 
 def feature_kernel(
-    core, node, wig, source, target, rotation, filt, own, send, wc_out, x, xs, xt, wc, fz, fa, ff, sem
+    core, node, wig, source, target, rotation, filt, own, send, wc_out, node_out, x, xs, xt, wc, fz, fa, sem
 ):
     wc[...] = jnp.zeros_like(wc)
     for degree in range(7):
@@ -78,11 +78,11 @@
     d_all = lax.dot_general(
         hot_r, entries, (((1,), (1,)), ((), ())), preferred_element_type=F32
     ).astype(BF)
-    ff[:, :C] = filt[...]
-    ff[:, C:] = filt[...]
-    is_second = core[0]
-    base_one = is_second * 12
-    base_two = (1 - is_second) * 12
+    node_out[...] = node[:, :C]
+    slot_one = core[0]
+    slot_two = 1 - core[0]
+    for slot in range(2):
+        fa[slot, :EDGES, 12 * C : 13 * C] = filt[...]
     for degree in range(7):
         wide = (2 * degree + 1) * ATOMS
         at = degree * degree
@@ -96,23 +96,21 @@
             d = jnp.dot(d, spread, preferred_element_type=F32).astype(BF)
             one = jnp.dot(d * xs[:, :wide], coefs, preferred_element_type=F32).astype(BF)
             two = jnp.dot(d * xt[:, :wide], coefs, preferred_element_type=F32).astype(BF)
-            if r < 7:
-                ref, plane = fz, r
-            elif r < 19:
-                ref, plane = fa, base_one + (r - 7)
-            else:
-                q = r - 19
-                ref, plane = fa, base_two + (q // 5) * 6 + q % 5
-            ref[plane, :, :C] = one
-            ref[plane, :, C:] = two
+            for at_lane, value in ((0, one), (C, two)):
+                if r < 7:
+                    fz[:, r * 2 * C + at_lane : r * 2 * C + at_lane + C] = value
+                    continue
+                slot = slot_one if r < 19 else slot_two
+                sign, k = divmod(r - 7, 6) if r < 19 else divmod(r - 19, 5)
+                lanes = slice(k * 2 * C + at_lane, k * 2 * C + at_lane + C)
+                fa[slot, sign * EDGES : (sign + 1) * EDGES, lanes] = value
     copies = []
-    for place, out in ((0, own), (12, send)):
+    for slot, out in enumerate((own, send)):
         copies += [
-            pltpu.make_async_copy(fz, out.at[pl.ds(0, 7)], sem.at[len(copies)]),
+            pltpu.make_async_copy(fz, out.at[pl.ds(0, EDGES)], sem.at[2 * slot]),
             pltpu.make_async_copy(
-                fa.at[pl.ds(place, 12)], out.at[pl.ds(7, 12)], sem.at[len(copies) + 1]
+                fa.at[slot], out.at[pl.ds(EDGES, 2 * EDGES)], sem.at[2 * slot + 1]
             ),
-            pltpu.make_async_copy(ff, out.at[19], sem.at[len(copies) + 2]),
         ]
     for copy in copies:
         copy.start()
@@ -126,21 +124,21 @@
     return pl.pallas_call(
         feature_kernel,
         out_shape=(
-            jax.ShapeDtypeStruct((20, EDGES, 2 * C), BF),
-            jax.ShapeDtypeStruct((20, EDGES, 2 * C), BF),
+            jax.ShapeDtypeStruct((3 * EDGES, 14 * C), BF),
+            jax.ShapeDtypeStruct((3 * EDGES, 14 * C), BF),
             jax.ShapeDtypeStruct((4 * C, NROT), BF),
+            jax.ShapeDtypeStruct((ATOMS, C), BF),
         ),
         in_specs=[pl.BlockSpec(memory_space=SMEM)] + [vm] * 6,
-        out_specs=(anywhere, anywhere, vm),
+        out_specs=(anywhere, anywhere, vm, vm),
         scratch_shapes=[
             VMEM((COEF * ATOMS, C), BF),
             VMEM((EDGES, 13 * ATOMS), BF),
             VMEM((EDGES, 13 * ATOMS), BF),
             VMEM((4 * C, NROT), F32),
-            VMEM((7, EDGES, 2 * C), BF),
-            VMEM((24, EDGES, 2 * C), BF),
-            VMEM((EDGES, 2 * C), BF),
-            pltpu.SemaphoreType.DMA((6,)),
+            VMEM((EDGES, 14 * C), BF),
+            VMEM((2, 2 * EDGES, 14 * C), BF),
+            pltpu.SemaphoreType.DMA((4,)),
         ],
         compiler_params=pltpu.CompilerParams(vmem_limit_bytes=8 * 2**20),
         cost_estimate=pl.CostEstimate(flops=6 * 10**9, bytes_accessed=8 * 10**6, transcendentals=0),
@@ -148,8 +146,19 @@
     )(core, node, wig, source, target, rotation, filt)
 
 
-def pack_kernel(core, zero, one_real, one_imag, two_real, two_imag, out):
+def pack_kernel(core, *refs):
+    given, out, held, sem = refs[:5], refs[5], refs[6:11], refs[11]
+    zero, one_real, one_imag, two_real, two_imag = held
+
     def run(parts):
+        copies = []
+        for i in range(5):
+            if any(held[i] is part[0] for part in parts):
+                copies.append(pltpu.make_async_copy(given[i], held[i], sem.at[i]))
+        for copy in copies:
+            copy.start()
+        for copy in copies:
+            copy.wait()
         at = 0
         for ref, first, groups in parts:
             tiles = ref.shape[0] // 8
@@ -173,9 +182,11 @@
     return pl.pallas_call(
         pack_kernel,
         out_shape=jax.ShapeDtypeStruct((TILES, 8, C), BF),
-        in_specs=[pl.BlockSpec(memory_space=SMEM)] + [vm] * 5,
+        in_specs=[pl.BlockSpec(memory_space=SMEM)] + [pl.BlockSpec(memory_space=pltpu.HBM)] * 5,
         out_specs=vm,
-        compiler_params=pltpu.CompilerParams(vmem_limit_bytes=4 * 2**20),
+        scratch_shapes=[VMEM(w.shape, BF) for w in (zero, one_real, one_imag, two_real, two_imag)]
+        + [pltpu.SemaphoreType.DMA((5,))],
+        compiler_params=pltpu.CompilerParams(vmem_limit_bytes=60 * 2**20),
         name="pack",
     )(core, zero, one_real, one_imag, two_real, two_imag)
 
@@ -195,26 +206,17 @@
     return tiles.reshape(held.shape[0] * count * 8, C)
 
 
+def zero_features(own, got):
+    return jnp.concatenate((own[:EDGES, :], got[:EDGES, :]), axis=0)
+
+
+def order_features(own, got, deep):
+    return jnp.concatenate((own[EDGES:, :deep], got[EDGES:, :deep]), axis=0)
+
+
 def early_kernel(core, shard, *refs):
     blocks = refs[:10]
-    own, got, part, part_zero, late, late_zero, w_all, xz, xa, fsem = refs[10:]
-
-    def fetch_features(pieces):
-        copies = []
-
-        def add(src, dst):
-            copies.append(pltpu.make_async_copy(src, dst, fsem.at[len(copies)]))
-
-        for who, src in enumerate((own, got)):
-            for k in range(7):
-                add(src.at[k], xz.at[pl.ds(who * EDGES, EDGES), pl.ds(k * 2 * C, 2 * C)])
-            for sign in range(2):
-                for k in range(pieces):
-                    add(
-                        src.at[7 + sign * 6 + k],
-                        xa.at[pl.ds((sign * 2 + who) * EDGES, EDGES), pl.ds(k * 2 * C, 2 * C)],
-                    )
-        return copies
+    own, got, part, part_zero, late, late_zero, w_all = refs[10:]
 
     def chosen(rows, deep):
         lane = lax.broadcasted_iota(jnp.int32, (1, LATE * rows), 1)
@@ -225,11 +227,6 @@
         return (lax.broadcasted_iota(jnp.int32, (deep, 1), 0) == wanted).astype(F32).astype(BF)
 
     def run(pieces, tiles, zero_groups):
-        copies = fetch_features(pieces)
-        for copy in copies:
-            copy.start()
-        for copy in copies:
-            copy.wait()
         deep = pieces * 2 * C
         size = pieces * tiles
 
@@ -237,7 +234,7 @@
             w = jnp.concatenate(
                 (group_rows(w_all, 0, tiles, g), group_rows(w_all, size, tiles, g)), axis=1
             )
-            part[g] = jnp.dot(xa[:, :deep], w, preferred_element_type=F32)
+            part[g] = jnp.dot(order_features(own, got, deep), w, preferred_element_type=F32)
             return carry
 
         lax.fori_loop(0, pieces, column, 0)
@@ -246,13 +243,15 @@
             w = jnp.concatenate(
                 [group_rows(w_all, 2 * size, 7, g + i) for i in range(count)], axis=1
             )
-            part_zero[g // 2, :, : count * C] = jnp.dot(xz[...], w, preferred_element_type=F32)
+            part_zero[g // 2, :, : count * C] = jnp.dot(
+                zero_features(own, got), w, preferred_element_type=F32
+            )
         rows = tiles * 8
         late[:, : LATE * rows] = jnp.dot(
-            xa[:, :deep], chosen(rows, deep), preferred_element_type=F32
+            order_features(own, got, deep), chosen(rows, deep), preferred_element_type=F32
         ).astype(BF)
         late_zero[...] = jnp.dot(
-            xz[...], chosen(56, 14 * C), preferred_element_type=F32
+            zero_features(own, got), chosen(56, 14 * C), preferred_element_type=F32
         ).astype(BF)
 
     def place(block, index):
@@ -277,7 +276,6 @@
 
 def mix_early(core, shard, blocks, own, got):
     vm = pl.BlockSpec(memory_space=VMEM)
-    anywhere = pl.BlockSpec(memory_space=pl.ANY)
     smem = pl.BlockSpec(memory_space=SMEM)
     return pl.pallas_call(
         early_kernel,
@@ -287,38 +285,22 @@
             jax.ShapeDtypeStruct((4 * EDGES, LATE * 48), BF),
             jax.ShapeDtypeStruct((2 * EDGES, LATE * 56), BF),
         ),
-        in_specs=[smem, smem] + [vm] * 10 + [anywhere] * 2,
+        in_specs=[smem, smem] + [vm] * 12,
         out_specs=(vm,) * 4,
-        scratch_shapes=[
-            VMEM((32, TILES, 8, C), BF),
-            VMEM((2 * EDGES, 14 * C), BF),
-            VMEM((4 * EDGES, 12 * C), BF),
-            pltpu.SemaphoreType.DMA((38,)),
-        ],
+        scratch_shapes=[VMEM((32, TILES, 8, C), BF)],
         compiler_params=pltpu.CompilerParams(vmem_limit_bytes=20 * 2**20),
         cost_estimate=pl.CostEstimate(flops=4 * 10**9, bytes_accessed=12 * 10**6, transcendentals=0),
         name="mix_early",
     )(core, shard, *blocks, own, got)
 
 
-def late_kernel(core, up, down, part, part_zero, late, late_zero, own, got, mine, other, fl, fsem):
-    copies = [
-        pltpu.make_async_copy(src.at[19], fl.at[pl.ds(who * EDGES, EDGES)], fsem.at[who])
-        for who, src in enumerate((own, got))
-    ]
-    for copy in copies:
-        copy.start()
-    for copy in copies:
-        copy.wait()
-
-    def finish(plane, value, filters):
-        message = (value * filters).astype(BF)
-        mine[plane] = message[:EDGES]
-        other[plane] = message[EDGES:]
+def late_kernel(core, up, down, part, part_zero, late, late_zero, own, got, mine, other):
+    def finish(plane, own_value, got_value, filters):
+        mine[plane] = (own_value * filters[0]).astype(BF)
+        other[plane] = (got_value * filters[1]).astype(BF)
 
     def run(pieces, tiles, zero_groups):
-        filters = fl[:, :C].astype(F32)
-        half = 2 * EDGES
+        filters = [ref[EDGES : 2 * EDGES, 12 * C : 13 * C].astype(F32) for ref in (own, got)]
         size = pieces * tiles
 
         def rows_of(first, count, g):
@@ -331,8 +313,10 @@
             both = part[g] + jnp.dot(
                 late[:, : LATE * tiles * 8], w, preferred_element_type=F32
             )
-            finish(g, both[:half, :C] - both[half:, C:], filters)
-            finish(pieces + g, both[half:, :C] + both[:half, C:], filters)
+            real = [both[i * EDGES : (i + 1) * EDGES, :C] for i in range(4)]
+            imag = [both[i * EDGES : (i + 1) * EDGES, C:] for i in range(4)]
+            finish(g, real[0] - imag[1], real[2] - imag[3], filters)
+            finish(pieces + g, real[1] + imag[0], real[3] + imag[2], filters)
             return carry
 
         lax.fori_loop(0, pieces, column, 0)
@@ -343,21 +327,20 @@
                 late_zero[...], w, preferred_element_type=F32
             )
             for i in range(count):
-                finish(2 * pieces + g + i, total[:, i * C : (i + 1) * C], filters)
+                value = total[:, i * C : (i + 1) * C]
+                finish(2 * pieces + g + i, value[:EDGES], value[EDGES:], filters)
 
     by_core(core, run)
 
 
 def mix_late(core, up, down, part, part_zero, late, late_zero, own, got):
     vm = pl.BlockSpec(memory_space=VMEM)
-    anywhere = pl.BlockSpec(memory_space=pl.ANY)
     out = jax.ShapeDtypeStruct((15, EDGES, C), BF)
     return pl.pallas_call(
         late_kernel,
         out_shape=(out, out),
-        in_specs=[pl.BlockSpec(memory_space=SMEM)] + [vm] * 6 + [anywhere] * 2,
+        in_specs=[pl.BlockSpec(memory_space=SMEM)] + [vm] * 8,
         out_specs=(vm, vm),
-        scratch_shapes=[VMEM((2 * EDGES, 2 * C), BF), pltpu.SemaphoreType.DMA((2,))],
         compiler_params=pltpu.CompilerParams(vmem_limit_bytes=8 * 2**20),
         cost_estimate=pl.CostEstimate(flops=10**9, bytes_accessed=8 * 10**6, transcendentals=0),
         name="mix_late",
@@ -391,23 +374,22 @@
     )(wig, rotation, target, after)
 
 
-def back_kernel(
-    place_mine, place_got, task, mine, got, hot, node, struct, head, update, energy, m, first, sem
-):
-    copies = [pltpu.make_async_copy(node.at[:, pl.ds(0, C)], first, sem.at[30])]
-    for i in range(15):
-        copies.append(pltpu.make_async_copy(mine.at[i], m.at[place_mine[i]], sem.at[2 * i]))
-        copies.append(pltpu.make_async_copy(got.at[i], m.at[place_got[i]], sem.at[2 * i + 1]))
-    for copy in copies:
-        copy.start()
-    for copy in copies:
-        copy.wait()
+def back_kernel(core, task, mine, got, hot, node, struct, head, update, energy):
+    is_first = core[0] == 0
+
+    def message(r):
+        if r in MADE[0]:
+            i = MADE[0].index(r)
+            return jnp.where(is_first, mine[i], got[i])
+        i = MADE[1].index(r)
+        return jnp.where(is_first, got[i], mine[i])
+
     at = 0
     for degree in range(7):
         span = 2 * degree + 1
         total = None
         for r in ROWS[degree]:
-            term = jnp.dot(hot[at : at + span * ATOMS, :], m[r], preferred_element_type=F32)
+            term = jnp.dot(hot[at : at + span * ATOMS, :], message(r), preferred_element_type=F32)
             total = term if total is None else total + term
             at += span * ATOMS
         for place in range(span):
@@ -415,15 +397,14 @@
             j = degree * degree + place
             update[:, j * C : (j + 1) * C] = value.astype(BF)
             if j == 0:
-                scalar_part = first[...].astype(F32) + value
+                scalar_part = node[...].astype(F32) + value
     for s in range(4):
         member = jnp.where(struct[...] == s, scalar_part, 0.0) * head[pl.ds(task[s], 1), :]
         energy[s] = jnp.sum(member)
 
 
-def turn_back(place_mine, place_got, task, mine, got, hot, node, struct, head):
+def turn_back(core, task, mine, got, hot, node, struct, head):
     vm = pl.BlockSpec(memory_space=VMEM)
-    anywhere = pl.BlockSpec(memory_space=pl.ANY)
     smem = pl.BlockSpec(memory_space=SMEM)
     return pl.pallas_call(
         back_kernel,
@@ -431,17 +412,12 @@
             jax.ShapeDtypeStruct((ATOMS, COEF * C), BF),
             jax.ShapeDtypeStruct((4,), F32),
         ),
-        in_specs=[smem] * 3 + [anywhere] * 2 + [vm, anywhere, vm, vm],
+        in_specs=[smem] * 2 + [vm] * 6,
         out_specs=(vm, smem),
-        scratch_shapes=[
-            VMEM((30, EDGES, C), BF),
-            VMEM((ATOMS, C), BF),
-            pltpu.SemaphoreType.DMA((31,)),
-        ],
         compiler_params=pltpu.CompilerParams(vmem_limit_bytes=6 * 2**20),
         cost_estimate=pl.CostEstimate(flops=10**9, bytes_accessed=4 * 10**6, transcendentals=0),
         name="turn_back",
-    )(place_mine, place_got, task, mine, got, hot, node, struct, head)
+    )(core, task, mine, got, hot, node, struct, head)
 
 
 def exchange(value, sizes, steps_first, steps_second):
@@ -505,7 +481,7 @@
     s2p, s2m = forth(pick(s1p, p1)), aft(pick(s1m, p1))
     live = (jnp.arange(EDGES, dtype=jnp.int32) < edge_count[0])[:, None]
     filters = jnp.where(live, edge_filter, jnp.zeros_like(edge_filter))
-    own, send, entries = features(
+    own, send, entries, node_first = features(
         core_vec,
         node_embed,
         wigner.transpose(1, 2, 0),
@@ -514,8 +490,6 @@
         rotation.reshape(EDGES, 1),
         filters,
     )
-    hot = ends_of(entries, rotation.reshape(1, EDGES), target.reshape(1, EDGES), s1m)
-    s2p, s2m, hot = lax.optimization_barrier((s2p, s2m, hot))
     s3p, s3m = forth(pick(s2p, s1p)), aft(s2m)
 
     blocks = (b0, a1, a2, a3, p1p, p1m, s1p, s1m, s2p, s2m)
@@ -529,15 +503,14 @@
     held = (4, TILES, 8, C)
     mine, other = mix_late(core_vec, s3p.reshape(held), s3m.reshape(held), *parts, own, got)
     back = lax.ppermute(other, "mol", swap)
-    places = jnp.asarray(MADE, jnp.int32)
+    hot = ends_of(entries, rotation.reshape(1, EDGES), target.reshape(1, EDGES), mine)
     update, energy = turn_back(
-        places[core],
-        places[1 - core],
+        core_vec,
         struct_task,
         mine,
         back,
         hot,
-        node_embed,
+        node_first,
         atom_struct.reshape(ATOMS, 1),
         task_head,
     )

time: 94.5 us -> 83.3 us (0.88)
  local copies, waits for them, and re-layouts: 17.1 us -> 5.1 us
  waiting for transfers between devices: 14.9 us -> 18 us
  Pallas kernels: 30 us -> 28.4 us
  starting transfers between devices: 28.1 us -> 26.8 us
  other arithmetic: 1.96 us -> 2.91 us
    unnamed x76 -> x52, local copies, waits for them, and re-layouts: 14.6 us -> 2.63 us
    ppermute x11, waiting for transfers between devices: 13 us -> 16.9 us  [exchange(): return lax.ppermute(value, ('mol', 'task'), pairs)]
    pallas_call x1, Pallas kernels: 5.38 us -> 3.04 us  [turn_back(): pl.pallas_call(back_kernel, out_shape=(jax.ShapeDtypeStruct((ATOMS, COEF...]
    ppermute x1, starting transfers between devices: 5.66 us -> 3.76 us  [body(): back = lax.ppermute(other, 'mol', swap)]
    pallas_call x1, Pallas kernels: 0.03 us -> 1.71 us  [pack(): pl.pallas_call(pack_kernel, out_shape=jax.ShapeDtypeStruct((TILES, 8, C),...]
    pallas_call x1, Pallas kernels: 10.3 us -> 9.06 us  [mix_early(): pl.pallas_call(early_kernel, out_shape=(jax.ShapeDtypeStruct((6, 4 * EDGE...]
    select_n x4, other arithmetic: 1.71 us -> 2.66 us  [pick(): return jnp.where(first, a, b)]
  transfers between devices with their start and end apart: 13 -> 13, of which waited for: 7 -> 6; matrix products, arithmetic and copies ran while one was open for 6% -> 8% of each run, Pallas kernels for 22% -> 23%
where the time goes in v4:
time: 83.3 us; the launch traced here: 83 us
  Pallas kernels  28.4 us (34%)
  starting transfers between devices  26.8 us (32%)
  waiting for transfers between devices  18 us (22%)
  local copies, waits for them, and re-layouts  5.1 us (6%)
  other arithmetic  2.91 us (3%)
  between operations  1.83 us (2%)
    ppermute x11, starting transfers between devices, exchange(): return lax.ppermute(value, ('mol', 'task'), pairs)  21.3 us
    ppermute x11, waiting for transfers between devices, exchange(): return lax.ppermute(value, ('mol', 'task'), pairs)  16.9 us
    pallas_call x1, Pallas kernels, mix_early(): pl.pallas_call(early_kernel, out_shape=(jax.ShapeDtypeStruct((6, 4 * EDGE...  9.06 us
    pallas_call x1, Pallas kernels, features(): pl.pallas_call(feature_kernel, out_shape=(jax.ShapeDtypeStruct((3 * EDGES...  9.01 us
    pallas_call x1, Pallas kernels, mix_late(): pl.pallas_call(late_kernel, out_shape=(out, out), in_specs=[pl.BlockSpec(...  4.78 us
    ppermute x1, starting transfers between devices, body(): back = lax.ppermute(other, 'mol', swap)  3.76 us
    pallas_call x1, Pallas kernels, turn_back(): pl.pallas_call(back_kernel, out_shape=(jax.ShapeDtypeStruct((ATOMS, COEF...  3.04 us
    select_n x4, other arithmetic, pick(): return jnp.where(first, a, b)  2.66 us
  transfers between devices with their start and end apart: 13, of which 6 were waited for; matrix products, arithmetic and copies ran while one was open for 8% of the time, Pallas kernels for 23%

profile of v4, /device:TPU:1, one launch (start us, length us, event | category | flops | bytes accessed | tf_op | source)
XLA Modules:
  0.0 83.0 jit_solution(17074916054487312088)
XLA Ops:
  0.6 0.0 copy-start.20
  0.6 0.0 copy-start.22
  0.7 0.0 copy-start.16
  0.7 0.0 copy-start.17
  0.7 0.0 copy-start.21
  0.7 1.7 %pack.1.refs_0_ = bf16[86,8,128]{2,1,0:T(8,128)(2,1)} custom-call(s32[1]{0:T(128)} %bitcast.core, bf16[56,896]{1,0:T(8,128)(2,1)} %refs_0_.1, bf16[48,768]{1,0:T(8,128)(2,1)} %refs_1_.1, bf16[48,768]{1,0:T(8,128)(2,1)} %refs_2_.1, bf16[40,640]{1,0:T(8,128)(2,1)} %refs_3_.1, bf16[40,640]{1,0:T(8,128)(2,1)} %refs_4_.1), custom_call_target="tpu_custom_call" | custom-call | tf_op jit(solution)/shard_map/pack/pallas_call | solution.py:182
  2.4 0.0 copy-start
  2.4 2.5 %collective-permute-start.2 = (bf16[86,8,128]{2,1,0:T(8,128)(2,1)}, bf16[86,8,128]{2,1,0:T(8,128)(2,1)S(1)}, u32[]{:S(2)}, u32[]{:S(2)}) collective-permute-start(bf16[86,8,128]{2,1,0:T(8,128)(2,1)} %pack.1.refs_0_), channel_id=1, source_target_pairs={{0,1},{1,2},{2,3},{3,0},{4,5},{5,6},{6,7},{7,4},{8,9},{9,10},{10,1... | collective-permute-start | bytes 528392 | tf_op jit(solution)/shard_map/ppermute | solution.py:432
  5.0 6.0 %collective-permute-start.1 = (bf16[86,8,128]{2,1,0:T(8,128)(2,1)}, bf16[86,8,128]{2,1,0:T(8,128)(2,1)S(1)}, u32[]{:S(2)}, u32[]{:S(2)}) collective-permute-start(bf16[86,8,128]{2,1,0:T(8,128)(2,1)} %pack.1.refs_0_), channel_id=1, source_target_pairs={{0,2},{1,3},{2,0},{3,1},{4,6},{5,7},{6,4},{7,5},{8,10},{9,11},{10,... | collective-permute-start | bytes 528392 | tf_op jit(solution)/shard_map/ppermute | solution.py:432
  11.0 1.9 %collective-permute-start = (bf16[86,8,128]{2,1,0:T(8,128)(2,1)}, bf16[86,8,128]{2,1,0:T(8,128)(2,1)S(1)}, u32[]{:S(2)}, u32[]{:S(2)}) collective-permute-start(bf16[86,8,128]{2,1,0:T(8,128)(2,1)} %pack.1.refs_0_), channel_id=1, source_target_pairs={{0,3},{1,0},{2,1},{3,2},{4,7},{5,4},{6,5},{7,6},{8,11},{9,8},{10,9... | collective-permute-start | bytes 528392 | tf_op jit(solution)/shard_map/ppermute | solution.py:432
  12.9 0.0 collective-permute-done.2.refs_1_
  12.9 3.1 %collective-permute-done.1.refs_3_ = bf16[86,8,128]{2,1,0:T(8,128)(2,1)S(1)} collective-permute-done((bf16[86,8,128]{2,1,0:T(8,128)(2,1)}, bf16[86,8,128]{2,1,0:T(8,128)(2,1)S(1)}, u32[]{:S(2)}, u32[]{:S(2)}) %collective-permute-start.1) | collective-permute-done | bytes 176160 | tf_op jit(solution)/shard_map/ppermute | solution.py:432
  16.0 1.0 %maximum_select_fusion = bf16[172,8,128]{2,1,0:T(8,128)(2,1)S(1)} fusion(bf16[86,8,128]{2,1,0:T(8,128)(2,1)S(1)} %collective-permute-done.1.refs_3_, bf16[86,8,128]{2,1,0:T(8,128)(2,1)S(1)} %collective-permute-done.2.refs_1_, pred[]{:T(512)S(6)} %eq.9, bf16[86,8,128]{2,1,0:T(8,128)(2,1)} %pack.1.refs_0_), kind=kLoop, calls=%fused_computation.7 | loop fusion | flops 528384 | bytes 880641 | tf_op jit(solution)/shard_map/jit(_where)/select_n | solution.py:461
  17.1 0.1 collective-permute-start.3
  17.1 1.4 %collective-permute-done.refs_2_ = bf16[86,8,128]{2,1,0:T(8,128)(2,1)S(1)} collective-permute-done((bf16[86,8,128]{2,1,0:T(8,128)(2,1)}, bf16[86,8,128]{2,1,0:T(8,128)(2,1)S(1)}, u32[]{:S(2)}, u32[]{:S(2)}) %collective-permute-start) | collective-permute-done | bytes 176160 | tf_op jit(solution)/shard_map/ppermute | solution.py:432
  18.6 2.5 %collective-permute-start.5 = (bf16[172,8,128]{2,1,0:T(8,128)(2,1)S(1)}, bf16[172,8,128]{2,1,0:T(8,128)(2,1)S(1)}, u32[]{:S(2)}, u32[]{:S(2)}) collective-permute-start(bf16[172,8,128]{2,1,0:T(8,128)(2,1)S(1)} %constant_dynamic-update-slice_fusion), channel_id=1, source_target_pairs={{0,28},{1,29},{2,30},{3,31},{4,0},{5,1},{6,2},{7,3},{8,4},{9,5},{1... | collective-permute-start | bytes 1056776 | tf_op jit(solution)/shard_map/ppermute | solution.py:432
  21.1 1.3 %copy.26 = bf16[256,29,49]{0,2,1:T(8,128)(2,1)} copy(bf16[256,29,49]{0,1,2:T(8,128)(2,1)S(1)} %copy-done.20) | data formatting | bytes 1455104 | tf_op args[1]
  22.4 0.8 copy.21.source
  23.2 0.8 copy.22.target
  23.9 0.0 copy-done.17
  23.9 0.8 copy.23.rotation
  25.4 0.1 broadcast_select_fusion.6.filt
  25.5 3.2 %collective-permute-done.3.refs_4_ = bf16[172,8,128]{2,1,0:T(8,128)(2,1)S(1)} collective-permute-done((bf16[172,8,128]{2,1,0:T(8,128)(2,1)S(1)}, bf16[172,8,128]{2,1,0:T(8,128)(2,1)S(1)}, u32[]{:S(2)}, u32[]{:S(2)}) %collective-permute-start.3) | collective-permute-done | bytes 352288 | tf_op jit(solution)/shard_map/ppermute | solution.py:432
  28.7 0.1 collective-permute-done.5.refs_5_
  28.8 0.2 broadcast_select_fusion.3
  29.0 0.0 copy-done.2
  29.0 0.0 copy-done.10
  29.0 0.0 copy-start.1
  29.1 0.0 copy-start.12
  29.1 0.0 copy-start.13
  29.1 0.0 copy-start.14
  29.1 0.0 copy-start.19
  29.1 0.3 copy-done.6
  29.4 0.1 pad_maximum_fusion
  29.5 1.0 %collective-permute-start.4 = (bf16[344,8,128]{2,1,0:T(8,128)(2,1)S(1)}, bf16[344,8,128]{2,1,0:T(8,128)(2,1)S(1)}, u32[]{:S(2)}, u32[]{:S(2)}) collective-permute-start(bf16[344,8,128]{2,1,0:T(8,128)(2,1)S(1)} %pad_maximum_fusion), channel_id=1, source_target_pairs={{0,4},{1,5},{2,6},{3,7},{4,8},{5,9},{6,10},{7,11},{8,12},{9,13},{1... | collective-permute-start | bytes 2113544 | tf_op jit(solution)/shard_map/ppermute | solution.py:432
  30.5 0.1 pad_maximum_fusion.1
  30.5 1.8 %collective-permute-start.8 = (bf16[344,8,128]{2,1,0:T(8,128)(2,1)S(1)}, bf16[344,8,128]{2,1,0:T(8,128)(2,1)S(1)}, u32[]{:S(2)}, u32[]{:S(2)}) collective-permute-start(bf16[344,8,128]{2,1,0:T(8,128)(2,1)S(1)} %pad_maximum_fusion.1), channel_id=1, source_target_pairs={{0,28},{1,29},{2,30},{3,31},{4,0},{5,1},{6,2},{7,3},{8,4},{9,5},{1... | collective-permute-start | bytes 2113544 | tf_op jit(solution)/shard_map/ppermute | solution.py:432
  32.4 9.0 %features.1 = (bf16[576,1792]{1,0:T(8,128)(2,1)S(1)}, bf16[576,1792]{1,0:T(8,128)(2,1)}, bf16[512,256]{1,0:T(8,128)(2,1)S(1)}, bf16[48,128]{1,0:T(8,128)(2,1)S(1)}) custom-call(s32[1]{0:T(128)} %bitcast.core, bf16[48,6272]{1,0:T(8,128)(2,1)S(1)} %copy-done.19, bf16[29,49,256]{2,1,0:T(8,128)(2,1)S(1)} %bitcast.20, s32[192,1]{1,0:T(8,128)S(1)} %copy-done.12, ...), custom_call_target="tpu_custom_call" | custom-call | flops 6000000000 | bytes 8000000 | tf_op jit(solution)/shard_map/features/pallas_call | solution.py:124
  41.4 1.7 %collective-permute-start.11 = (bf16[576,1792]{1,0:T(8,128)(2,1)}, bf16[576,1792]{1,0:T(8,128)(2,1)}, u32[]{:S(2)}, u32[]{:S(2)}) collective-permute-start(bf16[576,1792]{1,0:T(8,128)(2,1)} %get-tuple-element.13), channel_id=1, source_target_pairs={{0,32},{32,0},{64,96},{96,64},{128,160},{160,128},{192,224},{224,1... | collective-permute-start | bytes 6193160 | tf_op jit(solution)/shard_map/ppermute | solution.py:501
  43.2 0.0 copy-start.24
  43.2 0.0 collective-permute-done.4.refs_6_
  43.3 0.0 collective-permute-done.8.refs_7_
  43.3 1.3 %broadcast_select_fusion = (bf16[344,8,128]{2,1,0:T(8,128)(2,1)}, bf16[344,8,128]{2,1,0:T(8,128)(2,1)}) fusion(bf16[344,8,128]{2,1,0:T(8,128)(2,1)S(1)} %collective-permute-done.8.refs_7_, bf16[344,8,128]{2,1,0:T(8,128)(2,1)S(1)} %constant_dynamic-update-slice_fusion.2, pred[]{:T(512)S(6)} %eq.9, bf16[344,8,128]{2,1,0:T(8,128)(2,1)S(1)} %collective-permute-done.4.refs_6_), kind=kLoop, calls=%fused_computation.3 | loop fusion | flops 704512 | bytes 3522561 | tf_op jit(solution)/shard_map/jit(_where)/select_n | solution.py:461
  44.6 0.9 %copy-done.4 = bf16[344,8,128]{2,1,0:T(8,128)(2,1)} copy-done((bf16[344,8,128]{2,1,0:T(8,128)(2,1)}, bf16[344,8,128]{2,1,0:T(8,128)(2,1)S(1)}, u32[]{:S(2)}) %copy-start.4) | copy-done | bytes 704536
  45.4 0.2 collective-permute-start.6
  45.6 2.5 %collective-permute-start.9 = (bf16[344,8,128]{2,1,0:T(8,128)(2,1)}, bf16[344,8,128]{2,1,0:T(8,128)(2,1)}, u32[]{:S(2)}, u32[]{:S(2)}) collective-permute-start(bf16[344,8,128]{2,1,0:T(8,128)(2,1)} %get-tuple-element.22), channel_id=1, source_target_pairs={{0,28},{1,29},{2,30},{3,31},{4,0},{5,1},{6,2},{7,3},{8,4},{9,5},{1... | collective-permute-start | bytes 2113544 | tf_op jit(solution)/shard_map/ppermute | solution.py:432
  48.1 9.1 %collective-permute-done.6.refs_8_ = bf16[344,8,128]{2,1,0:T(8,128)(2,1)} collective-permute-done((bf16[344,8,128]{2,1,0:T(8,128)(2,1)}, bf16[344,8,128]{2,1,0:T(8,128)(2,1)}, u32[]{:S(2)}, u32[]{:S(2)}) %collective-permute-start.6) | collective-permute-done | bytes 704544 | tf_op jit(solution)/shard_map/ppermute | solution.py:432
  57.2 0.1 broadcast_select_fusion.1
  57.3 0.1 collective-permute-start.7
  57.4 0.0 collective-permute-done.9.refs_9_
  57.4 2.7 %collective-permute-start.10 = (bf16[344,8,128]{2,1,0:T(8,128)(2,1)}, bf16[344,8,128]{2,1,0:T(8,128)(2,1)S(1)}, u32[]{:S(2)}, u32[]{:S(2)}) collective-permute-start(bf16[344,8,128]{2,1,0:T(8,128)(2,1)} %collective-permute-done.9.refs_9_), channel_id=1, source_target_pairs={{0,28},{1,29},{2,30},{3,31},{4,0},{5,1},{6,2},{7,3},{8,4},{9,5},{1... | collective-permute-start | bytes 2113544 | tf_op jit(solution)/shard_map/ppermute | solution.py:432
  60.1 0.0 collective-permute-done.11.refs_11_.got
  60.1 9.1 %mix_early.1 = (f32[6,768,256]{2,1,0:T(8,128)S(1)}, f32[3,384,256]{2,1,0:T(8,128)S(1)}, bf16[768,384]{1,0:T(8,128)(2,1)S(1)}, bf16[384,448]{1,0:T(8,128)(2,1)S(1)}) custom-call(s32[1]{0:T(128)} %bitcast.core, s32[32]{0:T(128)S(1)} %fusion.shard, bf16[86,8,128]{2,1,0:T(8,128)(2,1)S(1)} %copy-done, bf16[86,8,128]{2,1,0:T(8,128)(2,1)S(1)} %collective-permute-done.2.refs_1_, ...), custom_call_target="tpu_custom_call" | custom-call | flops 4000000000 | bytes 12000000 | tf_op jit(solution)/shard_map/mix_early/pallas_call | solution.py:280
  69.2 0.0 collective-permute-done.7
  69.2 0.0 collective-permute-done.10
  69.2 0.0 copy-start.23
  69.2 4.8 %mix_late.1 = (bf16[15,192,128]{2,1,0:T(8,128)(2,1)S(1)}, bf16[15,192,128]{2,1,0:T(8,128)(2,1)}) custom-call(s32[1]{0:T(128)} %bitcast.core, bf16[4,86,8,128]{3,2,1,0:T(8,128)(2,1)S(1)} %bitcast.21, bf16[4,86,8,128]{3,2,1,0:T(8,128)(2,1)S(1)} %bitcast.22, f32[6,768,256]{2,1,0:T(8,128)S(1)} %get-tuple-element.14.part, ...), custom_call_target="tpu_custom_call" | custom-call | flops 1000000000 | bytes 8000000 | tf_op jit(solution)/shard_map/mix_late/pallas_call | solution.py:339
  74.0 3.8 %collective-permute-start.12 = (bf16[15,192,128]{2,1,0:T(8,128)(2,1)}, bf16[15,192,128]{2,1,0:T(8,128)(2,1)S(1)}, u32[]{:S(2)}, u32[]{:S(2)}) collective-permute-start(bf16[15,192,128]{2,1,0:T(8,128)(2,1)} %get-tuple-element.19), channel_id=1, source_target_pairs={{0,32},{32,0},{64,96},{96,64},{128,160},{160,128},{192,224},{224,1... | collective-permute-start | bytes 2211848 | tf_op jit(solution)/shard_map/ppermute | solution.py:505
  77.8 0.1 copy.24.struct
  77.9 0.0 copy-start.18
  77.9 0.8 ends_of.1.hot
  78.7 1.1 %collective-permute-done.12.got = bf16[15,192,128]{2,1,0:T(8,128)(2,1)S(1)} collective-permute-done((bf16[15,192,128]{2,1,0:T(8,128)(2,1)}, bf16[15,192,128]{2,1,0:T(8,128)(2,1)S(1)}, u32[]{:S(2)}, u32[]{:S(2)}) %collective-permute-start.12) | collective-permute-done | bytes 737312 | tf_op jit(solution)/shard_map/ppermute | solution.py:505
  79.8 0.0 copy-done.18
  79.8 3.0 %turn_back.1 = (bf16[48,6272]{1,0:T(8,128)(2,1)}, f32[4]{0:T(128)}) custom-call(s32[1]{0:T(128)} %bitcast.core, s32[4]{0:T(128)S(1)} %copy-done.18, bf16[15,192,128]{2,1,0:T(8,128)(2,1)S(1)} %get-tuple-element.18.after.mine, bf16[15,192,128]{2,1,0:T(8,128)(2,1)S(1)} %collective-permute-done.12.got, bf16[11280,192]{1,0:T(8,128)(2,1)S(1)} %ends_of.1.hot, ...), custom_call_target="tpu_custom_call" | custom-call | flops 1000000000 | bytes 4000000 | tf_op jit(solution)/shard_map/turn_back/pallas_call | solution.py:409
  (36 shorter events, 0.2 us)
Async XLA Ops:
  0.6 20.4 %copy-start.20 = (bf16[256,29,49]{0,1,2:T(8,128)(2,1)S(1)}, bf16[256,29,49]{0,1,2:T(8,128)(2,1)}, u32[]{:S(2)}) copy-start(bf16[256,29,49]{0,1,2:T(8,128)(2,1)} %param.17) | copy-start | bytes 2182660
  0.6 21.7 %copy-start.22 = (s32[192]{0:T(256)S(1)}, s32[192]{0:T(256)}, u32[]{:S(2)}) copy-start(s32[192]{0:T(256)} %param.18) | copy-start | bytes 2308
  0.7 22.5 %copy-start.16 = (s32[192]{0:T(256)S(1)}, s32[192]{0:T(256)}, u32[]{:S(2)}) copy-start(s32[192]{0:T(256)} %param.19) | copy-start | bytes 2308
  0.7 23.3 %copy-start.17 = (s32[192]{0:T(256)S(1)}, s32[192]{0:T(256)}, u32[]{:S(2)}) copy-start(s32[192]{0:T(256)} %param.20) | copy-start | bytes 2308
  0.7 24.7 %copy-start.21 = (bf16[192,128]{1,0:T(8,128)(2,1)S(1)}, bf16[192,128]{1,0:T(8,128)(2,1)}, u32[]{:S(2)}) copy-start(bf16[192,128]{1,0:T(8,128)(2,1)} %param.21) | copy-start | bytes 147460
  2.4 26.4 %copy-start = (bf16[86,8,128]{2,1,0:T(8,128)(2,1)S(1)}, bf16[86,8,128]{2,1,0:T(8,128)(2,1)}, u32[]{:S(2)}) copy-start(bf16[86,8,128]{2,1,0:T(8,128)(2,1)} %pack.1.refs_0_) | copy-start | bytes 528388
  2.4 10.5 %collective-permute-start.2 = (bf16[86,8,128]{2,1,0:T(8,128)(2,1)}, bf16[86,8,128]{2,1,0:T(8,128)(2,1)S(1)}, u32[]{:S(2)}, u32[]{:S(2)}) collective-permute-start(bf16[86,8,128]{2,1,0:T(8,128)(2,1)} %pack.1.refs_0_), channel_id=1, source_target_pairs={{0,1},{1,2},{2,3},{3,0},{4,5},{5,6},{6,7},{7,4},{8,9},{9,10},{10,1... | collective-permute-start | bytes 528392 | tf_op jit(solution)/shard_map/ppermute | solution.py:432
  5.0 11.0 %collective-permute-start.1 = (bf16[86,8,128]{2,1,0:T(8,128)(2,1)}, bf16[86,8,128]{2,1,0:T(8,128)(2,1)S(1)}, u32[]{:S(2)}, u32[]{:S(2)}) collective-permute-start(bf16[86,8,128]{2,1,0:T(8,128)(2,1)} %pack.1.refs_0_), channel_id=1, source_target_pairs={{0,2},{1,3},{2,0},{3,1},{4,6},{5,7},{6,4},{7,5},{8,10},{9,11},{10,... | collective-permute-start | bytes 528392 | tf_op jit(solution)/shard_map/ppermute | solution.py:432
  11.0 7.6 %collective-permute-start = (bf16[86,8,128]{2,1,0:T(8,128)(2,1)}, bf16[86,8,128]{2,1,0:T(8,128)(2,1)S(1)}, u32[]{:S(2)}, u32[]{:S(2)}) collective-permute-start(bf16[86,8,128]{2,1,0:T(8,128)(2,1)} %pack.1.refs_0_), channel_id=1, source_target_pairs={{0,3},{1,0},{2,1},{3,2},{4,7},{5,4},{6,5},{7,6},{8,11},{9,8},{10,9... | collective-permute-start | bytes 528392 | tf_op jit(solution)/shard_map/ppermute | solution.py:432
  16.0 13.0 %copy-start.2 = (bf16[86,8,128]{2,1,0:T(8,128)(2,1)}, bf16[86,8,128]{2,1,0:T(8,128)(2,1)S(1)}, u32[]{:S(2)}) copy-start(bf16[86,8,128]{2,1,0:T(8,128)(2,1)S(1)} %collective-permute-done.1.refs_3_) | copy-start | bytes 528388
  17.1 11.6 %collective-permute-start.3 = (bf16[172,8,128]{2,1,0:T(8,128)(2,1)S(1)}, bf16[172,8,128]{2,1,0:T(8,128)(2,1)S(1)}, u32[]{:S(2)}, u32[]{:S(2)}) collective-permute-start(bf16[172,8,128]{2,1,0:T(8,128)(2,1)S(1)} %maximum_select_fusion), channel_id=1, source_target_pairs={{0,4},{1,5},{2,6},{3,7},{4,8},{5,9},{6,10},{7,11},{8,12},{9,13},{1... | collective-permute-start | bytes 1056776 | tf_op jit(solution)/shard_map/ppermute | solution.py:432
  18.5 10.5 %copy-start.10 = (bf16[86,8,128]{2,1,0:T(8,128)(2,1)}, bf16[86,8,128]{2,1,0:T(8,128)(2,1)S(1)}, u32[]{:S(2)}) copy-start(bf16[86,8,128]{2,1,0:T(8,128)(2,1)S(1)} %collective-permute-done.refs_2_) | copy-start | bytes 528388
  18.6 10.2 %collective-permute-start.5 = (bf16[172,8,128]{2,1,0:T(8,128)(2,1)S(1)}, bf16[172,8,128]{2,1,0:T(8,128)(2,1)S(1)}, u32[]{:S(2)}, u32[]{:S(2)}) collective-permute-start(bf16[172,8,128]{2,1,0:T(8,128)(2,1)S(1)} %constant_dynamic-update-slice_fusion), channel_id=1, source_target_pairs={{0,28},{1,29},{2,30},{3,31},{4,0},{5,1},{6,2},{7,3},{8,4},{9,5},{1... | collective-permute-start | bytes 1056776 | tf_op jit(solution)/shard_map/ppermute | solution.py:432
  28.7 0.7 copy-start.6
  29.0 3.3 %copy-start.1 = (bf16[256,29,49]{0,2,1:T(8,128)(2,1)S(1)}, bf16[256,29,49]{0,2,1:T(8,128)(2,1)}, u32[]{:S(2)}) copy-start(bf16[256,29,49]{0,2,1:T(8,128)(2,1)} %copy.26) | copy-start | bytes 2182660
  29.1 3.3 %copy-start.12 = (s32[192,1]{1,0:T(8,128)S(1)}, s32[192,1]{1,0:T(8,128)}, u32[]{:S(2)}) copy-start(s32[192,1]{1,0:T(8,128)} %copy.21.source) | copy-start | bytes 2308
  29.1 3.3 %copy-start.13 = (s32[192,1]{1,0:T(8,128)S(1)}, s32[192,1]{1,0:T(8,128)}, u32[]{:S(2)}) copy-start(s32[192,1]{1,0:T(8,128)} %copy.22.target) | copy-start | bytes 2308
  29.1 3.3 %copy-start.14 = (s32[192,1]{1,0:T(8,128)S(1)}, s32[192,1]{1,0:T(8,128)}, u32[]{:S(2)}) copy-start(s32[192,1]{1,0:T(8,128)} %copy.23.rotation) | copy-start | bytes 2308
  29.1 3.3 %copy-start.19 = (bf16[48,6272]{1,0:T(8,128)(2,1)S(1)}, bf16[48,6272]{1,0:T(8,128)(2,1)}, u32[]{:S(2)}) copy-start(bf16[48,6272]{1,0:T(8,128)(2,1)} %node.1) | copy-start | bytes 1806340
  29.5 13.8 %collective-permute-start.4 = (bf16[344,8,128]{2,1,0:T(8,128)(2,1)S(1)}, bf16[344,8,128]{2,1,0:T(8,128)(2,1)S(1)}, u32[]{:S(2)}, u32[]{:S(2)}) collective-permute-start(bf16[344,8,128]{2,1,0:T(8,128)(2,1)S(1)} %pad_maximum_fusion), channel_id=1, source_target_pairs={{0,4},{1,5},{2,6},{3,7},{4,8},{5,9},{6,10},{7,11},{8,12},{9,13},{1... | collective-permute-start | bytes 2113544 | tf_op jit(solution)/shard_map/ppermute | solution.py:432
  30.5 12.7 %collective-permute-start.8 = (bf16[344,8,128]{2,1,0:T(8,128)(2,1)S(1)}, bf16[344,8,128]{2,1,0:T(8,128)(2,1)S(1)}, u32[]{:S(2)}, u32[]{:S(2)}) collective-permute-start(bf16[344,8,128]{2,1,0:T(8,128)(2,1)S(1)} %pad_maximum_fusion.1), channel_id=1, source_target_pairs={{0,28},{1,29},{2,30},{3,31},{4,0},{5,1},{6,2},{7,3},{8,4},{9,5},{1... | collective-permute-start | bytes 2113544 | tf_op jit(solution)/shard_map/ppermute | solution.py:432
  41.4 1.8 %copy-start.8 = (bf16[512,256]{1,0:T(8,128)(2,1)}, bf16[512,256]{1,0:T(8,128)(2,1)S(1)}, u32[]{:S(2)}) copy-start(bf16[512,256]{1,0:T(8,128)(2,1)S(1)} %get-tuple-element.20.wig) | copy-start | bytes 786436
  41.4 18.6 %collective-permute-start.11 = (bf16[576,1792]{1,0:T(8,128)(2,1)}, bf16[576,1792]{1,0:T(8,128)(2,1)}, u32[]{:S(2)}, u32[]{:S(2)}) collective-permute-start(bf16[576,1792]{1,0:T(8,128)(2,1)} %get-tuple-element.13), channel_id=1, source_target_pairs={{0,32},{32,0},{64,96},{96,64},{128,160},{160,128},{192,224},{224,1... | collective-permute-start | bytes 6193160 | tf_op jit(solution)/shard_map/ppermute | solution.py:501
  43.2 16.8 %copy-start.24 = (s32[2,32,2]{1,2,0:T(2,128)S(1)}, s32[2,32,2]{1,2,0:T(2,128)}, u32[]{:S(2)}) copy-start(s32[2,32,2]{1,2,0:T(2,128)} %constant.68.clone) | copy-start | bytes 1540
  44.6 0.9 %copy-start.4 = (bf16[344,8,128]{2,1,0:T(8,128)(2,1)}, bf16[344,8,128]{2,1,0:T(8,128)(2,1)S(1)}, u32[]{:S(2)}) copy-start(bf16[344,8,128]{2,1,0:T(8,128)(2,1)S(1)} %collective-permute-done.8.refs_7_) | copy-start | bytes 2113540
  45.4 11.8 %collective-permute-start.6 = (bf16[344,8,128]{2,1,0:T(8,128)(2,1)}, bf16[344,8,128]{2,1,0:T(8,128)(2,1)}, u32[]{:S(2)}, u32[]{:S(2)}) collective-permute-start(bf16[344,8,128]{2,1,0:T(8,128)(2,1)} %get-tuple-element.23), channel_id=1, source_target_pairs={{0,4},{1,5},{2,6},{3,7},{4,8},{5,9},{6,10},{7,11},{8,12},{9,13},{1... | collective-permute-start | bytes 2113544 | tf_op jit(solution)/shard_map/ppermute | solution.py:432
  45.6 11.8 %collective-permute-start.9 = (bf16[344,8,128]{2,1,0:T(8,128)(2,1)}, bf16[344,8,128]{2,1,0:T(8,128)(2,1)}, u32[]{:S(2)}, u32[]{:S(2)}) collective-permute-start(bf16[344,8,128]{2,1,0:T(8,128)(2,1)} %get-tuple-element.22), channel_id=1, source_target_pairs={{0,28},{1,29},{2,30},{3,31},{4,0},{5,1},{6,2},{7,3},{8,4},{9,5},{1... | collective-permute-start | bytes 2113544 | tf_op jit(solution)/shard_map/ppermute | solution.py:432
  48.1 12.0 %copy-start.3 = (bf16[86,8,128]{2,1,0:T(8,128)(2,1)S(1)}, bf16[86,8,128]{2,1,0:T(8,128)(2,1)}, u32[]{:S(2)}) copy-start(bf16[86,8,128]{2,1,0:T(8,128)(2,1)} %copy-done.2) | copy-start | bytes 528388
  48.1 12.0 %copy-start.5 = (bf16[344,8,128]{2,1,0:T(8,128)(2,1)S(1)}, bf16[344,8,128]{2,1,0:T(8,128)(2,1)}, u32[]{:S(2)}) copy-start(bf16[344,8,128]{2,1,0:T(8,128)(2,1)} %copy-done.4) | copy-start | bytes 2113540
  48.1 12.0 %copy-start.7 = (bf16[172,8,128]{2,1,0:T(8,128)(2,1)S(1)}, bf16[172,8,128]{2,1,0:T(8,128)(2,1)}, u32[]{:S(2)}) copy-start(bf16[172,8,128]{2,1,0:T(8,128)(2,1)} %copy-done.6) | copy-start | bytes 1056772
  48.1 12.0 %copy-start.11 = (bf16[86,8,128]{2,1,0:T(8,128)(2,1)S(1)}, bf16[86,8,128]{2,1,0:T(8,128)(2,1)}, u32[]{:S(2)}) copy-start(bf16[86,8,128]{2,1,0:T(8,128)(2,1)} %copy-done.10) | copy-start | bytes 528388
  57.3 11.9 %collective-permute-start.7 = (bf16[344,8,128]{2,1,0:T(8,128)(2,1)S(1)}, bf16[344,8,128]{2,1,0:T(8,128)(2,1)S(1)}, u32[]{:S(2)}, u32[]{:S(2)}) collective-permute-start(bf16[344,8,128]{2,1,0:T(8,128)(2,1)S(1)} %broadcast_select_fusion.1), channel_id=1, source_target_pairs={{0,4},{1,5},{2,6},{3,7},{4,8},{5,9},{6,10},{7,11},{8,12},{9,13},{1... | collective-permute-start | bytes 2113544 | tf_op jit(solution)/shard_map/ppermute | solution.py:432
  57.4 11.8 %collective-permute-start.10 = (bf16[344,8,128]{2,1,0:T(8,128)(2,1)}, bf16[344,8,128]{2,1,0:T(8,128)(2,1)S(1)}, u32[]{:S(2)}, u32[]{:S(2)}) collective-permute-start(bf16[344,8,128]{2,1,0:T(8,128)(2,1)} %collective-permute-done.9.refs_9_), channel_id=1, source_target_pairs={{0,28},{1,29},{2,30},{3,31},{4,0},{5,1},{6,2},{7,3},{8,4},{9,5},{1... | collective-permute-start | bytes 2113544 | tf_op jit(solution)/shard_map/ppermute | solution.py:432
  69.2 8.6 %copy-start.23 = (s32[48]{0:T(128)S(1)}, s32[48]{0:T(128)}, u32[]{:S(2)}) copy-start(s32[48]{0:T(128)} %param.28) | copy-start | bytes 580
  69.2 8.7 %copy-start.9 = (bf16[512,256]{1,0:T(8,128)(2,1)S(1)}, bf16[512,256]{1,0:T(8,128)(2,1)}, u32[]{:S(2)}) copy-start(bf16[512,256]{1,0:T(8,128)(2,1)} %copy-done.8) | copy-start | bytes 786436
  74.0 5.8 %collective-permute-start.12 = (bf16[15,192,128]{2,1,0:T(8,128)(2,1)}, bf16[15,192,128]{2,1,0:T(8,128)(2,1)S(1)}, u32[]{:S(2)}, u32[]{:S(2)}) collective-permute-start(bf16[15,192,128]{2,1,0:T(8,128)(2,1)} %get-tuple-element.19), channel_id=1, source_target_pairs={{0,32},{32,0},{64,96},{96,64},{128,160},{160,128},{192,224},{224,1... | collective-permute-start | bytes 2211848 | tf_op jit(solution)/shard_map/ppermute | solution.py:505
  77.9 2.0 %copy-start.15 = (f32[5,128]{1,0:T(8,128)S(1)}, f32[5,128]{1,0:T(8,128)}, u32[]{:S(2)}) copy-start(f32[5,128]{1,0:T(8,128)} %head.1) | copy-start | bytes 7684
  77.9 2.0 %copy-start.18 = (s32[4]{0:T(128)S(1)}, s32[4]{0:T(128)}, u32[]{:S(2)}) copy-start(s32[4]{0:T(128)} %task.1) | copy-start | bytes 52

commit v5 on v4

--- a/solution.py
+++ b/solution.py
@@ -49,11 +49,9 @@
         first += moved(H1, -step, 0) + moved(H0, -step - 1, 0)
         first += moved(H0, step, 0) + moved(H1, step + 1, 0)
     second = [block for part in U for block in part]
-    for part in (0, 2):
-        for y in (-1, 1):
-            second += moved(U[part], 0, y) + moved(U[part + 1], 0, y)
-    for part in (0, 2):
-        second += moved(U[part], 0, 2) + moved(U[part + 1], 0, 2)
+    for step in (1, 2, 3):
+        second += moved(U[0], 0, -step) + moved(U[1], 0, -step)
+        second += moved(U[2], 0, step) + moved(U[3], 0, step)
     return first, second
 
 
@@ -319,7 +317,7 @@
             finish(pieces + g, real[1] + imag[0], real[3] + imag[2], filters)
             return carry
 
-        lax.fori_loop(0, pieces, column, 0)
+        lax.fori_loop(0, pieces, column, 0, unroll=True)
         for g in range(0, zero_groups, 2):
             count = min(2, zero_groups - g)
             w = jnp.concatenate([rows_of(2 * size, 7, g + i) for i in range(count)], axis=1)
@@ -475,10 +473,13 @@
 
     p1p = forth(pick(h0, jnp.concatenate((a1, a3))), (1, 0))
     p1m = aft(h1, (-1, 0))
-    s1p = forth(jnp.concatenate((pick(h1, h0), pick(p1p, h1))))
-    s1m = aft(jnp.concatenate((h0, pick(p1m, h1))))
-    p1 = jnp.concatenate((p1p, p1m))
-    s2p, s2m = forth(pick(s1p, p1)), aft(pick(s1m, p1))
+    def both(a, b):
+        return jnp.concatenate((a, b))
+
+    x1p = both(pick(h1, h0), pick(p1p, h1))
+    x1m = both(pick(h0, p1p), p1m)
+    s1p, s1m = forth(x1p), aft(x1m)
+
     live = (jnp.arange(EDGES, dtype=jnp.int32) < edge_count[0])[:, None]
     filters = jnp.where(live, edge_filter, jnp.zeros_like(edge_filter))
     own, send, entries, node_first = features(
@@ -490,7 +491,10 @@
         rotation.reshape(EDGES, 1),
         filters,
     )
-    s3p, s3m = forth(pick(s2p, s1p)), aft(s2m)
+
+    s1p, s1m, node_first = lax.optimization_barrier((s1p, s1m, node_first))
+    s2p, s2m = lax.optimization_barrier((forth(s1p), aft(s1m)))
+    s3p, s3m = forth(s2p), aft(s2m)
 
     blocks = (b0, a1, a2, a3, p1p, p1m, s1p, s1m, s2p, s2m)
     offsets_first, offsets_second = block_offsets()

time: 83.3 us -> 87.6 us (1.052)
  local copies, waits for them, and re-layouts: 5.1 us -> 9.7 us
  waiting for transfers between devices: 18 us -> 21.8 us
  starting transfers between devices: 26.8 us -> 24.1 us
  other arithmetic: 2.91 us -> 1.79 us
    unnamed x52 -> x42, local copies, waits for them, and re-layouts: 2.63 us -> 7.94 us
    ppermute x11, waiting for transfers between devices: 16.9 us -> 20.7 us  [exchange(): return lax.ppermute(value, ('mol', 'task'), pairs)]
    select_n x4 -> x2, other arithmetic: 2.66 us -> 0.13 us  [pick(): return jnp.where(first, a, b)]
    ppermute x11, starting transfers between devices: 21.3 us -> 19.4 us  [exchange(): return lax.ppermute(value, ('mol', 'task'), pairs)]
    select_n x1, other arithmetic: 0.09 us -> 1.51 us  [body(): filters = jnp.where(live, edge_filter, jnp.zeros_like(edge_filter))]
  transfers between devices with their start and end apart: 13 -> 13, of which waited for: 6 -> 4; matrix products, arithmetic and copies ran while one was open for 8% -> 6% of each run, Pallas kernels for 23% -> 22%
where the time goes in v5:
time: 87.6 us; the launch traced here: 87.1 us
  Pallas kernels  28 us (32%)
  starting transfers between devices  24.1 us (28%)
  waiting for transfers between devices  21.8 us (25%)
  local copies, waits for them, and re-layouts  9.7 us (11%)
  other arithmetic  1.79 us (2%)
  between operations  1.73 us (2%)
    ppermute x11, waiting for transfers between devices, exchange(): return lax.ppermute(value, ('mol', 'task'), pairs)  20.7 us
    ppermute x11, starting transfers between devices, exchange(): return lax.ppermute(value, ('mol', 'task'), pairs)  19.4 us
    pallas_call x1, Pallas kernels, mix_early(): pl.pallas_call(early_kernel, out_shape=(jax.ShapeDtypeStruct((6, 4 * EDGE...  9.45 us
    pallas_call x1, Pallas kernels, features(): pl.pallas_call(feature_kernel, out_shape=(jax.ShapeDtypeStruct((3 * EDGES...  8.99 us
    unnamed x42, local copies, waits for them, and re-layouts  7.94 us
    pallas_call x1, Pallas kernels, mix_late(): pl.pallas_call(late_kernel, out_shape=(out, out), in_specs=[pl.BlockSpec(...  4.06 us
    ppermute x1, starting transfers between devices, body(): back = lax.ppermute(other, 'mol', swap)  3.46 us
    pallas_call x1, Pallas kernels, turn_back(): pl.pallas_call(back_kernel, out_shape=(jax.ShapeDtypeStruct((ATOMS, COEF...  3.05 us
  transfers between devices with their start and end apart: 13, of which 4 were waited for; matrix products, arithmetic and copies ran while one was open for 6% of the time, Pallas kernels for 22%

profile of v5, /device:TPU:1, one launch (start us, length us, event | category | flops | bytes accessed | tf_op | source)
XLA Modules:
  0.0 87.1 jit_solution(5635316105744998)
XLA Ops:
  0.6 0.0 copy-start.17
  0.6 0.0 copy-start.13
  0.7 0.0 copy-start.14
  0.7 1.7 %pack.1.refs_0_ = bf16[86,8,128]{2,1,0:T(8,128)(2,1)} custom-call(s32[1]{0:T(128)} %bitcast.core, bf16[56,896]{1,0:T(8,128)(2,1)} %refs_0_.1, bf16[48,768]{1,0:T(8,128)(2,1)} %refs_1_.1, bf16[48,768]{1,0:T(8,128)(2,1)} %refs_2_.1, bf16[40,640]{1,0:T(8,128)(2,1)} %refs_3_.1, bf16[40,640]{1,0:T(8,128)(2,1)} %refs_4_.1), custom_call_target="tpu_custom_call" | custom-call | tf_op jit(solution)/shard_map/pack/pallas_call | solution.py:180
  2.3 0.0 copy-start
  2.4 7.8 %collective-permute-start.1 = (bf16[86,8,128]{2,1,0:T(8,128)(2,1)}, bf16[86,8,128]{2,1,0:T(8,128)(2,1)S(1)}, u32[]{:S(2)}, u32[]{:S(2)}) collective-permute-start(bf16[86,8,128]{2,1,0:T(8,128)(2,1)} %pack.1.refs_0_), channel_id=1, source_target_pairs={{0,2},{1,3},{2,0},{3,1},{4,6},{5,7},{6,4},{7,5},{8,10},{9,11},{10,... | collective-permute-start | bytes 528392 | tf_op jit(solution)/shard_map/ppermute | solution.py:430
  10.2 0.0 collective-permute-start
  10.2 1.5 %collective-permute-start.2 = (bf16[86,8,128]{2,1,0:T(8,128)(2,1)}, bf16[86,8,128]{2,1,0:T(8,128)(2,1)S(1)}, u32[]{:S(2)}, u32[]{:S(2)}) collective-permute-start(bf16[86,8,128]{2,1,0:T(8,128)(2,1)} %pack.1.refs_0_), channel_id=1, source_target_pairs={{0,1},{1,2},{2,3},{3,0},{4,5},{5,6},{6,7},{7,4},{8,9},{9,10},{10,1... | collective-permute-start | bytes 528392 | tf_op jit(solution)/shard_map/ppermute | solution.py:430
  12.3 1.5 %broadcast_select_fusion.3.filt = bf16[192,128]{1,0:T(8,128)(2,1)} fusion(bf16[192,128]{1,0:T(8,128)(2,1)} %param.21, pred[192]{0:T(512)(128)(4,1)S(1)} %iota_compare_fusion), kind=kLoop, calls=%fused_computation.8 | loop fusion | flops 24576 | bytes 98496 | tf_op jit(solution)/shard_map/jit(_where)/select_n | solution.py:484
  13.8 1.6 %copy.26 = bf16[256,29,49]{0,2,1:T(8,128)(2,1)S(1)} copy(bf16[256,29,49]{0,1,2:T(8,128)(2,1)} %param.17) | data formatting | bytes 1455104 | tf_op args[1]
  15.4 0.0 copy-done.17
  15.4 0.1 copy.21.source
  15.5 0.0 copy-done.13
  15.5 0.8 copy.22.target
  16.3 0.0 copy-done.14
  16.3 0.8 copy.23.rotation
  17.1 0.0 collective-permute-done.1.refs_3_
  17.1 0.0 collective-permute-done.2.refs_1_
  17.1 0.0 copy-done
  17.1 0.1 maximum_select_fusion
  17.1 0.8 collective-permute-start.3
  18.0 0.0 collective-permute-done.refs_2_
  18.0 2.1 %collective-permute-start.5 = (bf16[172,8,128]{2,1,0:T(8,128)(2,1)S(1)}, bf16[172,8,128]{2,1,0:T(8,128)(2,1)S(1)}, u32[]{:S(2)}, u32[]{:S(2)}) collective-permute-start(bf16[172,8,128]{2,1,0:T(8,128)(2,1)S(1)} %constant_dynamic-update-slice_fusion), channel_id=1, source_target_pairs={{0,28},{1,29},{2,30},{3,31},{4,0},{5,1},{6,2},{7,3},{8,4},{9,5},{1... | collective-permute-start | bytes 1056776 | tf_op jit(solution)/shard_map/ppermute | solution.py:430
  20.1 0.0 copy-done.7
  20.1 0.9 %copy-done.9 = s32[192,1]{1,0:T(8,128)S(1)} copy-done((s32[192,1]{1,0:T(8,128)S(1)}, s32[192,1]{1,0:T(8,128)}, u32[]{:S(2)}) %copy-start.9) | copy-done | bytes 792
  21.0 0.9 %copy-done.10 = s32[192,1]{1,0:T(8,128)S(1)} copy-done((s32[192,1]{1,0:T(8,128)S(1)}, s32[192,1]{1,0:T(8,128)}, u32[]{:S(2)}) %copy-start.10) | copy-done | bytes 792
  21.9 0.8 copy-done.11
  22.7 1.1 %copy-done.16 = bf16[48,6272]{1,0:T(8,128)(2,1)S(1)} copy-done((bf16[48,6272]{1,0:T(8,128)(2,1)S(1)}, bf16[48,6272]{1,0:T(8,128)(2,1)}, u32[]{:S(2)}) %copy-start.16) | copy-done | bytes 602136
  23.8 9.0 %features.1 = (bf16[576,1792]{1,0:T(8,128)(2,1)S(1)}, bf16[576,1792]{1,0:T(8,128)(2,1)}, bf16[512,256]{1,0:T(8,128)(2,1)S(1)}, bf16[48,128]{1,0:T(8,128)(2,1)S(1)}) custom-call(s32[1]{0:T(128)} %bitcast.core, bf16[48,6272]{1,0:T(8,128)(2,1)S(1)} %copy-done.16, bf16[29,49,256]{2,1,0:T(8,128)(2,1)S(1)} %bitcast.20, s32[192,1]{1,0:T(8,128)S(1)} %copy.21.source, ...), custom_call_target="tpu_custom_call" | custom-call | flops 6000000000 | bytes 8000000 | tf_op jit(solution)/shard_map/features/pallas_call | solution.py:122
  32.8 0.0 copy-start.5
  32.8 0.7 copy-done.5
  33.5 1.2 %collective-permute-start.11 = (bf16[576,1792]{1,0:T(8,128)(2,1)}, bf16[576,1792]{1,0:T(8,128)(2,1)}, u32[]{:S(2)}, u32[]{:S(2)}) collective-permute-start(bf16[576,1792]{1,0:T(8,128)(2,1)} %get-tuple-element.23), channel_id=1, source_target_pairs={{0,32},{32,0},{64,96},{96,64},{128,160},{160,128},{192,224},{224,1... | collective-permute-start | bytes 6193160 | tf_op jit(solution)/shard_map/ppermute | solution.py:505
  34.7 0.0 collective-permute-done.3.refs_4_
  34.7 0.1 broadcast_select_fusion
  34.8 0.0 collective-permute-done.5.refs_5_
  34.8 0.0 copy-start.3
  34.8 0.1 pad_maximum_fusion.1
  34.8 1.6 %collective-permute-start.6 = (bf16[344,8,128]{2,1,0:T(8,128)(2,1)S(1)}, bf16[344,8,128]{2,1,0:T(8,128)(2,1)}, u32[]{:S(2)}, u32[]{:S(2)}) collective-permute-start(bf16[344,8,128]{2,1,0:T(8,128)(2,1)S(1)} %pad_maximum_fusion.1), channel_id=1, source_target_pairs={{0,28},{1,29},{2,30},{3,31},{4,0},{5,1},{6,2},{7,3},{8,4},{9,5},{1... | collective-permute-start | bytes 2113544 | tf_op jit(solution)/shard_map/ppermute | solution.py:430
  36.4 0.1 pad_maximum_fusion
  36.5 0.3 collective-permute-start.4
  36.8 8.5 %collective-permute-done.6.refs_7_ = bf16[344,8,128]{2,1,0:T(8,128)(2,1)} collective-permute-done((bf16[344,8,128]{2,1,0:T(8,128)(2,1)S(1)}, bf16[344,8,128]{2,1,0:T(8,128)(2,1)}, u32[]{:S(2)}, u32[]{:S(2)}) %collective-permute-start.6) | collective-permute-done | bytes 704544 | tf_op jit(solution)/shard_map/ppermute | solution.py:430
  45.3 3.1 %collective-permute-done.4.refs_6_ = bf16[344,8,128]{2,1,0:T(8,128)(2,1)} collective-permute-done((bf16[344,8,128]{2,1,0:T(8,128)(2,1)S(1)}, bf16[344,8,128]{2,1,0:T(8,128)(2,1)}, u32[]{:S(2)}, u32[]{:S(2)}) %collective-permute-start.4) | collective-permute-done | bytes 704544 | tf_op jit(solution)/shard_map/ppermute | solution.py:430
  48.3 0.0 collective-permute-start.7
  48.3 2.7 %collective-permute-start.8 = (bf16[344,8,128]{2,1,0:T(8,128)(2,1)}, bf16[344,8,128]{2,1,0:T(8,128)(2,1)}, u32[]{:S(2)}, u32[]{:S(2)}) collective-permute-start(bf16[344,8,128]{2,1,0:T(8,128)(2,1)} %collective-permute-done.6.refs_7_), channel_id=1, source_target_pairs={{0,28},{1,29},{2,30},{3,31},{4,0},{5,1},{6,2},{7,3},{8,4},{9,5},{1... | collective-permute-start | bytes 2113544 | tf_op jit(solution)/shard_map/ppermute | solution.py:430
  51.0 9.1 %collective-permute-done.7.refs_8_ = bf16[344,8,128]{2,1,0:T(8,128)(2,1)} collective-permute-done((bf16[344,8,128]{2,1,0:T(8,128)(2,1)}, bf16[344,8,128]{2,1,0:T(8,128)(2,1)}, u32[]{:S(2)}, u32[]{:S(2)}) %collective-permute-start.7) | collective-permute-done | bytes 704544 | tf_op jit(solution)/shard_map/ppermute | solution.py:430
  60.1 0.0 collective-permute-done.8.refs_9_
  60.1 0.0 collective-permute-start.9
  60.1 2.7 %collective-permute-start.10 = (bf16[344,8,128]{2,1,0:T(8,128)(2,1)}, bf16[344,8,128]{2,1,0:T(8,128)(2,1)S(1)}, u32[]{:S(2)}, u32[]{:S(2)}) collective-permute-start(bf16[344,8,128]{2,1,0:T(8,128)(2,1)} %collective-permute-done.8.refs_9_), channel_id=1, source_target_pairs={{0,28},{1,29},{2,30},{3,31},{4,0},{5,1},{6,2},{7,3},{8,4},{9,5},{1... | collective-permute-start | bytes 2113544 | tf_op jit(solution)/shard_map/ppermute | solution.py:430
  62.8 0.0 collective-permute-done.11.refs_11_.got
  62.9 0.0 copy-start.2
  62.9 1.0 %copy-done.2 = bf16[172,8,128]{2,1,0:T(8,128)(2,1)S(1)} copy-done((bf16[172,8,128]{2,1,0:T(8,128)(2,1)S(1)}, bf16[172,8,128]{2,1,0:T(8,128)(2,1)}, u32[]{:S(2)}) %copy-start.2) | copy-done | bytes 352280
  63.8 1.0 %copy-done.4 = bf16[172,8,128]{2,1,0:T(8,128)(2,1)S(1)} copy-done((bf16[172,8,128]{2,1,0:T(8,128)(2,1)S(1)}, bf16[172,8,128]{2,1,0:T(8,128)(2,1)}, u32[]{:S(2)}) %copy-start.4) | copy-done | bytes 352280
  64.8 9.5 %mix_early.1 = (f32[6,768,256]{2,1,0:T(8,128)S(1)}, f32[3,384,256]{2,1,0:T(8,128)S(1)}, bf16[768,384]{1,0:T(8,128)(2,1)S(1)}, bf16[384,448]{1,0:T(8,128)(2,1)S(1)}) custom-call(s32[1]{0:T(128)} %bitcast.core, s32[32]{0:T(128)S(1)} %fusion.shard, bf16[86,8,128]{2,1,0:T(8,128)(2,1)S(1)} %copy-done, bf16[86,8,128]{2,1,0:T(8,128)(2,1)S(1)} %collective-permute-done.2.refs_1_, ...), custom_call_target="tpu_custom_call" | custom-call | flops 4000000000 | bytes 12000000 | tf_op jit(solution)/shard_map/mix_early/pallas_call | solution.py:278
  74.3 0.0 collective-permute-done.9
  74.3 0.0 collective-permute-done.10
  74.3 0.0 copy-start.18
  74.3 4.1 %mix_late.1 = (bf16[15,192,128]{2,1,0:T(8,128)(2,1)S(1)}, bf16[15,192,128]{2,1,0:T(8,128)(2,1)}) custom-call(s32[1]{0:T(128)} %bitcast.core, bf16[4,86,8,128]{3,2,1,0:T(8,128)(2,1)S(1)} %bitcast.21, bf16[4,86,8,128]{3,2,1,0:T(8,128)(2,1)S(1)} %bitcast.22, f32[6,768,256]{2,1,0:T(8,128)S(1)} %get-tuple-element.24.part, ...), custom_call_target="tpu_custom_call" | custom-call | flops 1000000000 | bytes 8000000 | tf_op jit(solution)/shard_map/mix_late/pallas_call | solution.py:337
  78.4 3.5 %collective-permute-start.12 = (bf16[15,192,128]{2,1,0:T(8,128)(2,1)}, bf16[15,192,128]{2,1,0:T(8,128)(2,1)S(1)}, u32[]{:S(2)}, u32[]{:S(2)}) collective-permute-start(bf16[15,192,128]{2,1,0:T(8,128)(2,1)} %get-tuple-element.29), channel_id=1, source_target_pairs={{0,32},{32,0},{64,96},{96,64},{128,160},{160,128},{192,224},{224,1... | collective-permute-start | bytes 2211848 | tf_op jit(solution)/shard_map/ppermute | solution.py:509
  81.8 0.1 copy.24.struct
  81.9 0.0 copy-start.15
  82.0 0.8 ends_of.1.hot
  82.8 1.1 %collective-permute-done.12.got = bf16[15,192,128]{2,1,0:T(8,128)(2,1)S(1)} collective-permute-done((bf16[15,192,128]{2,1,0:T(8,128)(2,1)}, bf16[15,192,128]{2,1,0:T(8,128)(2,1)S(1)}, u32[]{:S(2)}, u32[]{:S(2)}) %collective-permute-start.12) | collective-permute-done | bytes 737312 | tf_op jit(solution)/shard_map/ppermute | solution.py:509
  83.9 0.0 copy-done.15
  83.9 3.1 %turn_back.1 = (bf16[48,6272]{1,0:T(8,128)(2,1)}, f32[4]{0:T(128)}) custom-call(s32[1]{0:T(128)} %bitcast.core, s32[4]{0:T(128)S(1)} %copy-done.15, bf16[15,192,128]{2,1,0:T(8,128)(2,1)S(1)} %get-tuple-element.28.after.mine, bf16[15,192,128]{2,1,0:T(8,128)(2,1)S(1)} %collective-permute-done.12.got, bf16[11280,192]{1,0:T(8,128)(2,1)S(1)} %ends_of.1.hot, ...), custom_call_target="tpu_custom_call" | custom-call | flops 1000000000 | bytes 4000000 | tf_op jit(solution)/shard_map/turn_back/pallas_call | solution.py:407
  (23 shorter events, 0.1 us)
Async XLA Ops:
  0.6 14.7 %copy-start.17 = (s32[192]{0:T(256)S(1)}, s32[192]{0:T(256)}, u32[]{:S(2)}) copy-start(s32[192]{0:T(256)} %param.18) | copy-start | bytes 2308
  0.6 14.9 %copy-start.13 = (s32[192]{0:T(256)S(1)}, s32[192]{0:T(256)}, u32[]{:S(2)}) copy-start(s32[192]{0:T(256)} %param.19) | copy-start | bytes 2308
  0.7 15.6 %copy-start.14 = (s32[192]{0:T(256)S(1)}, s32[192]{0:T(256)}, u32[]{:S(2)}) copy-start(s32[192]{0:T(256)} %param.20) | copy-start | bytes 2308
  2.3 14.7 %copy-start = (bf16[86,8,128]{2,1,0:T(8,128)(2,1)S(1)}, bf16[86,8,128]{2,1,0:T(8,128)(2,1)}, u32[]{:S(2)}) copy-start(bf16[86,8,128]{2,1,0:T(8,128)(2,1)} %pack.1.refs_0_) | copy-start | bytes 528388
  2.4 14.7 %collective-permute-start.1 = (bf16[86,8,128]{2,1,0:T(8,128)(2,1)}, bf16[86,8,128]{2,1,0:T(8,128)(2,1)S(1)}, u32[]{:S(2)}, u32[]{:S(2)}) collective-permute-start(bf16[86,8,128]{2,1,0:T(8,128)(2,1)} %pack.1.refs_0_), channel_id=1, source_target_pairs={{0,2},{1,3},{2,0},{3,1},{4,6},{5,7},{6,4},{7,5},{8,10},{9,11},{10,... | collective-permute-start | bytes 528392 | tf_op jit(solution)/shard_map/ppermute | solution.py:430
  10.2 7.8 %collective-permute-start = (bf16[86,8,128]{2,1,0:T(8,128)(2,1)}, bf16[86,8,128]{2,1,0:T(8,128)(2,1)S(1)}, u32[]{:S(2)}, u32[]{:S(2)}) collective-permute-start(bf16[86,8,128]{2,1,0:T(8,128)(2,1)} %pack.1.refs_0_), channel_id=1, source_target_pairs={{0,3},{1,0},{2,1},{3,2},{4,7},{5,4},{6,5},{7,6},{8,11},{9,8},{10,9... | collective-permute-start | bytes 528392 | tf_op jit(solution)/shard_map/ppermute | solution.py:430
  10.2 6.9 %collective-permute-start.2 = (bf16[86,8,128]{2,1,0:T(8,128)(2,1)}, bf16[86,8,128]{2,1,0:T(8,128)(2,1)S(1)}, u32[]{:S(2)}, u32[]{:S(2)}) collective-permute-start(bf16[86,8,128]{2,1,0:T(8,128)(2,1)} %pack.1.refs_0_), channel_id=1, source_target_pairs={{0,1},{1,2},{2,3},{3,0},{4,5},{5,6},{6,7},{7,4},{8,9},{9,10},{10,1... | collective-permute-start | bytes 528392 | tf_op jit(solution)/shard_map/ppermute | solution.py:430
  17.1 17.5 %collective-permute-start.3 = (bf16[172,8,128]{2,1,0:T(8,128)(2,1)S(1)}, bf16[172,8,128]{2,1,0:T(8,128)(2,1)S(1)}, u32[]{:S(2)}, u32[]{:S(2)}) collective-permute-start(bf16[172,8,128]{2,1,0:T(8,128)(2,1)S(1)} %maximum_select_fusion), channel_id=1, source_target_pairs={{0,4},{1,5},{2,6},{3,7},{4,8},{5,9},{6,10},{7,11},{8,12},{9,13},{1... | collective-permute-start | bytes 1056776 | tf_op jit(solution)/shard_map/ppermute | solution.py:430
  18.0 2.2 %copy-start.7 = (bf16[86,8,128]{2,1,0:T(8,128)(2,1)}, bf16[86,8,128]{2,1,0:T(8,128)(2,1)S(1)}, u32[]{:S(2)}) copy-start(bf16[86,8,128]{2,1,0:T(8,128)(2,1)S(1)} %collective-permute-done.refs_2_) | copy-start | bytes 528388
  18.0 16.7 %collective-permute-start.5 = (bf16[172,8,128]{2,1,0:T(8,128)(2,1)S(1)}, bf16[172,8,128]{2,1,0:T(8,128)(2,1)S(1)}, u32[]{:S(2)}, u32[]{:S(2)}) collective-permute-start(bf16[172,8,128]{2,1,0:T(8,128)(2,1)S(1)} %constant_dynamic-update-slice_fusion), channel_id=1, source_target_pairs={{0,28},{1,29},{2,30},{3,31},{4,0},{5,1},{6,2},{7,3},{8,4},{9,5},{1... | collective-permute-start | bytes 1056776 | tf_op jit(solution)/shard_map/ppermute | solution.py:430
  20.1 0.9 %copy-start.9 = (s32[192,1]{1,0:T(8,128)S(1)}, s32[192,1]{1,0:T(8,128)}, u32[]{:S(2)}) copy-start(s32[192,1]{1,0:T(8,128)} %copy.22.target) | copy-start | bytes 2308
  21.0 0.9 %copy-start.10 = (s32[192,1]{1,0:T(8,128)S(1)}, s32[192,1]{1,0:T(8,128)}, u32[]{:S(2)}) copy-start(s32[192,1]{1,0:T(8,128)} %copy.23.rotation) | copy-start | bytes 2308
  21.9 0.8 copy-start.11
  22.7 1.1 %copy-start.16 = (bf16[48,6272]{1,0:T(8,128)(2,1)S(1)}, bf16[48,6272]{1,0:T(8,128)(2,1)}, u32[]{:S(2)}) copy-start(bf16[48,6272]{1,0:T(8,128)(2,1)} %node.1) | copy-start | bytes 1806340
  32.8 0.7 copy-start.5
  33.5 29.3 %copy-start.19 = (s32[2,32,2]{1,2,0:T(2,128)S(1)}, s32[2,32,2]{1,2,0:T(2,128)}, u32[]{:S(2)}) copy-start(s32[2,32,2]{1,2,0:T(2,128)} %constant.68.clone) | copy-start | bytes 1540
  33.5 29.3 %copy-start.8 = (bf16[86,8,128]{2,1,0:T(8,128)(2,1)S(1)}, bf16[86,8,128]{2,1,0:T(8,128)(2,1)}, u32[]{:S(2)}) copy-start(bf16[86,8,128]{2,1,0:T(8,128)(2,1)} %copy-done.7) | copy-start | bytes 528388
  33.5 29.3 %collective-permute-start.11 = (bf16[576,1792]{1,0:T(8,128)(2,1)}, bf16[576,1792]{1,0:T(8,128)(2,1)}, u32[]{:S(2)}, u32[]{:S(2)}) collective-permute-start(bf16[576,1792]{1,0:T(8,128)(2,1)} %get-tuple-element.23), channel_id=1, source_target_pairs={{0,32},{32,0},{64,96},{96,64},{128,160},{160,128},{192,224},{224,1... | collective-permute-start | bytes 6193160 | tf_op jit(solution)/shard_map/ppermute | solution.py:505
  34.7 1.8 %copy-start.1 = (bf16[172,8,128]{2,1,0:T(8,128)(2,1)}, bf16[172,8,128]{2,1,0:T(8,128)(2,1)S(1)}, u32[]{:S(2)}) copy-start(bf16[172,8,128]{2,1,0:T(8,128)(2,1)S(1)} %collective-permute-done.3.refs_4_) | copy-start | bytes 1056772
  34.8 2.0 %copy-start.3 = (bf16[172,8,128]{2,1,0:T(8,128)(2,1)}, bf16[172,8,128]{2,1,0:T(8,128)(2,1)S(1)}, u32[]{:S(2)}) copy-start(bf16[172,8,128]{2,1,0:T(8,128)(2,1)S(1)} %collective-permute-done.5.refs_5_) | copy-start | bytes 1056772
  34.8 10.4 %collective-permute-start.6 = (bf16[344,8,128]{2,1,0:T(8,128)(2,1)S(1)}, bf16[344,8,128]{2,1,0:T(8,128)(2,1)}, u32[]{:S(2)}, u32[]{:S(2)}) collective-permute-start(bf16[344,8,128]{2,1,0:T(8,128)(2,1)S(1)} %pad_maximum_fusion.1), channel_id=1, source_target_pairs={{0,28},{1,29},{2,30},{3,31},{4,0},{5,1},{6,2},{7,3},{8,4},{9,5},{1... | collective-permute-start | bytes 2113544 | tf_op jit(solution)/shard_map/ppermute | solution.py:430
  36.5 11.8 %collective-permute-start.4 = (bf16[344,8,128]{2,1,0:T(8,128)(2,1)S(1)}, bf16[344,8,128]{2,1,0:T(8,128)(2,1)}, u32[]{:S(2)}, u32[]{:S(2)}) collective-permute-start(bf16[344,8,128]{2,1,0:T(8,128)(2,1)S(1)} %pad_maximum_fusion), channel_id=1, source_target_pairs={{0,4},{1,5},{2,6},{3,7},{4,8},{5,9},{6,10},{7,11},{8,12},{9,13},{1... | collective-permute-start | bytes 2113544 | tf_op jit(solution)/shard_map/ppermute | solution.py:430
  48.3 11.8 %collective-permute-start.7 = (bf16[344,8,128]{2,1,0:T(8,128)(2,1)}, bf16[344,8,128]{2,1,0:T(8,128)(2,1)}, u32[]{:S(2)}, u32[]{:S(2)}) collective-permute-start(bf16[344,8,128]{2,1,0:T(8,128)(2,1)} %collective-permute-done.4.refs_6_), channel_id=1, source_target_pairs={{0,4},{1,5},{2,6},{3,7},{4,8},{5,9},{6,10},{7,11},{8,12},{9,13},{1... | collective-permute-start | bytes 2113544 | tf_op jit(solution)/shard_map/ppermute | solution.py:430
  48.3 11.8 %collective-permute-start.8 = (bf16[344,8,128]{2,1,0:T(8,128)(2,1)}, bf16[344,8,128]{2,1,0:T(8,128)(2,1)}, u32[]{:S(2)}, u32[]{:S(2)}) collective-permute-start(bf16[344,8,128]{2,1,0:T(8,128)(2,1)} %collective-permute-done.6.refs_7_), channel_id=1, source_target_pairs={{0,28},{1,29},{2,30},{3,31},{4,0},{5,1},{6,2},{7,3},{8,4},{9,5},{1... | collective-permute-start | bytes 2113544 | tf_op jit(solution)/shard_map/ppermute | solution.py:430
  60.1 14.2 %collective-permute-start.9 = (bf16[344,8,128]{2,1,0:T(8,128)(2,1)}, bf16[344,8,128]{2,1,0:T(8,128)(2,1)S(1)}, u32[]{:S(2)}, u32[]{:S(2)}) collective-permute-start(bf16[344,8,128]{2,1,0:T(8,128)(2,1)} %collective-permute-done.7.refs_8_), channel_id=1, source_target_pairs={{0,4},{1,5},{2,6},{3,7},{4,8},{5,9},{6,10},{7,11},{8,12},{9,13},{1... | collective-permute-start | bytes 2113544 | tf_op jit(solution)/shard_map/ppermute | solution.py:430
  60.1 14.2 %collective-permute-start.10 = (bf16[344,8,128]{2,1,0:T(8,128)(2,1)}, bf16[344,8,128]{2,1,0:T(8,128)(2,1)S(1)}, u32[]{:S(2)}, u32[]{:S(2)}) collective-permute-start(bf16[344,8,128]{2,1,0:T(8,128)(2,1)} %collective-permute-done.8.refs_9_), channel_id=1, source_target_pairs={{0,28},{1,29},{2,30},{3,31},{4,0},{5,1},{6,2},{7,3},{8,4},{9,5},{1... | collective-permute-start | bytes 2113544 | tf_op jit(solution)/shard_map/ppermute | solution.py:430
  62.9 1.0 %copy-start.2 = (bf16[172,8,128]{2,1,0:T(8,128)(2,1)S(1)}, bf16[172,8,128]{2,1,0:T(8,128)(2,1)}, u32[]{:S(2)}) copy-start(bf16[172,8,128]{2,1,0:T(8,128)(2,1)} %copy-done.1) | copy-start | bytes 1056772
  63.8 1.0 %copy-start.4 = (bf16[172,8,128]{2,1,0:T(8,128)(2,1)S(1)}, bf16[172,8,128]{2,1,0:T(8,128)(2,1)}, u32[]{:S(2)}) copy-start(bf16[172,8,128]{2,1,0:T(8,128)(2,1)} %copy-done.3) | copy-start | bytes 1056772
  74.3 7.5 %copy-start.18 = (s32[48]{0:T(128)S(1)}, s32[48]{0:T(128)}, u32[]{:S(2)}) copy-start(s32[48]{0:T(128)} %param.28) | copy-start | bytes 580
  74.3 7.6 %copy-start.6 = (bf16[512,256]{1,0:T(8,128)(2,1)S(1)}, bf16[512,256]{1,0:T(8,128)(2,1)}, u32[]{:S(2)}) copy-start(bf16[512,256]{1,0:T(8,128)(2,1)} %copy-done.5) | copy-start | bytes 786436
  78.4 5.5 %collective-permute-start.12 = (bf16[15,192,128]{2,1,0:T(8,128)(2,1)}, bf16[15,192,128]{2,1,0:T(8,128)(2,1)S(1)}, u32[]{:S(2)}, u32[]{:S(2)}) collective-permute-start(bf16[15,192,128]{2,1,0:T(8,128)(2,1)} %get-tuple-element.29), channel_id=1, source_target_pairs={{0,32},{32,0},{64,96},{96,64},{128,160},{160,128},{192,224},{224,1... | collective-permute-start | bytes 2211848 | tf_op jit(solution)/shard_map/ppermute | solution.py:509
  81.9 2.0 %copy-start.12 = (f32[5,128]{1,0:T(8,128)S(1)}, f32[5,128]{1,0:T(8,128)}, u32[]{:S(2)}) copy-start(f32[5,128]{1,0:T(8,128)} %head.1) | copy-start | bytes 7684
  81.9 2.0 %copy-start.15 = (s32[4]{0:T(128)S(1)}, s32[4]{0:T(128)}, u32[]{:S(2)}) copy-start(s32[4]{0:T(128)} %task.1) | copy-start | bytes 52

commit v6 on v5

--- a/solution.py
+++ b/solution.py
@@ -212,9 +212,8 @@
     return jnp.concatenate((own[EDGES:, :deep], got[EDGES:, :deep]), axis=0)
 
 
-def early_kernel(core, shard, *refs):
-    blocks = refs[:10]
-    own, got, part, part_zero, late, late_zero, w_all = refs[10:]
+def choose_kernel(core, shard, own, got, *refs):
+    late, late_zero = refs[6:]
 
     def chosen(rows, deep):
         lane = lax.broadcasted_iota(jnp.int32, (1, LATE * rows), 1)
@@ -223,6 +222,41 @@
             here = jnp.logical_and(lane >= i * rows, lane < (i + 1) * rows)
             wanted = jnp.where(here, lane + (shard[32 - LATE + i] - i) * rows, wanted)
         return (lax.broadcasted_iota(jnp.int32, (deep, 1), 0) == wanted).astype(F32).astype(BF)
+
+    def run(pieces, tiles, zero_groups):
+        del zero_groups
+        deep = pieces * 2 * C
+        rows = tiles * 8
+        late[:, : LATE * rows] = jnp.dot(
+            order_features(own, got, deep), chosen(rows, deep), preferred_element_type=F32
+        ).astype(BF)
+        late_zero[...] = jnp.dot(
+            zero_features(own, got), chosen(56, 14 * C), preferred_element_type=F32
+        ).astype(BF)
+
+    by_core(core, run)
+
+
+def choose(core, shard, own, got, blocks):
+    vm = pl.BlockSpec(memory_space=VMEM)
+    smem = pl.BlockSpec(memory_space=SMEM)
+    return pl.pallas_call(
+        choose_kernel,
+        out_shape=(
+            jax.ShapeDtypeStruct((4 * EDGES, LATE * 48), BF),
+            jax.ShapeDtypeStruct((2 * EDGES, LATE * 56), BF),
+        ),
+        in_specs=[smem, smem] + [vm] * 8,
+        out_specs=(vm, vm),
+        compiler_params=pltpu.CompilerParams(vmem_limit_bytes=8 * 2**20),
+        cost_estimate=pl.CostEstimate(flops=10**9, bytes_accessed=4 * 10**6, transcendentals=0),
+        name="choose",
+    )(core, shard, own, got, *blocks)
+
+
+def early_kernel(core, shard, *refs):
+    blocks = refs[:10]
+    own, got, part, part_zero, w_all = refs[10:]
 
     def run(pieces, tiles, zero_groups):
         deep = pieces * 2 * C
@@ -244,13 +278,6 @@
             part_zero[g // 2, :, : count * C] = jnp.dot(
                 zero_features(own, got), w, preferred_element_type=F32
             )
-        rows = tiles * 8
-        late[:, : LATE * rows] = jnp.dot(
-            order_features(own, got, deep), chosen(rows, deep), preferred_element_type=F32
-        ).astype(BF)
-        late_zero[...] = jnp.dot(
-            zero_features(own, got), chosen(56, 14 * C), preferred_element_type=F32
-        ).astype(BF)
 
     def place(block, index):
         def one(i, carry):
@@ -280,13 +307,11 @@
         out_shape=(
             jax.ShapeDtypeStruct((6, 4 * EDGES, 2 * C), F32),
             jax.ShapeDtypeStruct((3, 2 * EDGES, 2 * C), F32),
-            jax.ShapeDtypeStruct((4 * EDGES, LATE * 48), BF),
-            jax.ShapeDtypeStruct((2 * EDGES, LATE * 56), BF),
         ),
         in_specs=[smem, smem] + [vm] * 12,
-        out_specs=(vm,) * 4,
+        out_specs=(vm, vm),
         scratch_shapes=[VMEM((32, TILES, 8, C), BF)],
-        compiler_params=pltpu.CompilerParams(vmem_limit_bytes=20 * 2**20),
+        compiler_params=pltpu.CompilerParams(vmem_limit_bytes=16 * 2**20),
         cost_estimate=pl.CostEstimate(flops=4 * 10**9, bytes_accessed=12 * 10**6, transcendentals=0),
         name="mix_early",
     )(core, shard, *blocks, own, got)
@@ -492,20 +517,20 @@
         filters,
     )
 
-    s1p, s1m, node_first = lax.optimization_barrier((s1p, s1m, node_first))
-    s2p, s2m = lax.optimization_barrier((forth(s1p), aft(s1m)))
-    s3p, s3m = forth(s2p), aft(s2m)
-
-    blocks = (b0, a1, a2, a3, p1p, p1m, s1p, s1m, s2p, s2m)
+    s1p, s1m, send = lax.optimization_barrier((s1p, s1m, send))
     offsets_first, offsets_second = block_offsets()
     table = jnp.asarray((offsets_first, offsets_second), jnp.int32)[core]
     shard = ((z + table[:, 0]) % 8) * 4 + (y + table[:, 1]) % 4
 
     swap = [(i, i ^ 1) for i in range(8)]
     got = lax.ppermute(send, "mol", swap)
+    late, late_zero = choose(core_vec, shard, own, got, (b0, a1, a2, a3, p1p, p1m))
+    s2p, s2m, late = lax.optimization_barrier((forth(s1p), aft(s1m), late))
+    s3p, s3m = forth(s2p), aft(s2m)
+    blocks = (b0, a1, a2, a3, p1p, p1m, s1p, s1m, s2p, s2m)
     parts = mix_early(core_vec, shard, blocks, own, got)
     held = (4, TILES, 8, C)
-    mine, other = mix_late(core_vec, s3p.reshape(held), s3m.reshape(held), *parts, own, got)
+    mine, other = mix_late(core_vec, s3p.reshape(held), s3m.reshape(held), *parts, late, late_zero, own, got)
     back = lax.ppermute(other, "mol", swap)
     hot = ends_of(entries, rotation.reshape(1, EDGES), target.reshape(1, EDGES), mine)
     update, energy = turn_back(

time: 87.6 us -> 88.5 us (1.010)
  local copies, waits for them, and re-layouts: 9.7 us -> 5.67 us
  starting transfers between devices: 24.1 us -> 26.8 us
  Pallas kernels: 28 us -> 29.8 us
  waiting for transfers between devices: 21.8 us -> 23 us
    unnamed x42 -> x34, local copies, waits for them, and re-layouts: 7.94 us -> 3.24 us
    pallas_call x0 -> x1, Pallas kernels: none -> 3.5 us  [choose(): pl.pallas_call(choose_kernel, out_shape=(jax.ShapeDtypeStruct((4 * EDGES,...]
    ppermute x1, starting transfers between devices: 1.17 us -> 4.02 us  [body(): got = lax.ppermute(send, 'mol', swap)]
    pallas_call x1, Pallas kernels: 9.45 us -> 7.72 us  [mix_early(): pl.pallas_call(early_kernel, out_shape=(jax.ShapeDtypeStruct((6, 4 * EDGE...]
    select_n x1, other arithmetic: 1.51 us -> 0.09 us  [body(): filters = jnp.where(live, edge_filter, jnp.zeros_like(edge_filter))]
    ppermute x1, waiting for transfers between devices: 0.01 us -> 1.38 us  [body(): got = lax.ppermute(send, 'mol', swap)]
    select_n x2, other arithmetic: 0.13 us -> 1.07 us  [pick(): return jnp.where(first, a, b)]
    ppermute x1, starting transfers between devices: 3.46 us -> 2.52 us  [body(): back = lax.ppermute(other, 'mol', swap)]
  transfers between devices with their start and end apart: 13 -> 13, of which waited for: 4 -> 11; matrix products, arithmetic and copies ran while one was open for 6% -> 7% of each run, Pallas kernels for 22% -> 24%
where the time goes in v6:
time: 88.5 us; the launch traced here: 88.2 us
  Pallas kernels  29.8 us (34%)
  starting transfers between devices  26.8 us (30%)
  waiting for transfers between devices  23 us (26%)
  local copies, waits for them, and re-layouts  5.67 us (6%)
  between operations  1.7 us (2%)
  other arithmetic  1.31 us (1%)
    ppermute x11, waiting for transfers between devices, exchange(): return lax.ppermute(value, ('mol', 'task'), pairs)  20.5 us
    ppermute x11, starting transfers between devices, exchange(): return lax.ppermute(value, ('mol', 'task'), pairs)  20.2 us
    pallas_call x1, Pallas kernels, features(): pl.pallas_call(feature_kernel, out_shape=(jax.ShapeDtypeStruct((3 * EDGES...  8.98 us
    pallas_call x1, Pallas kernels, mix_early(): pl.pallas_call(early_kernel, out_shape=(jax.ShapeDtypeStruct((6, 4 * EDGE...  7.72 us
    pallas_call x1, Pallas kernels, mix_late(): pl.pallas_call(late_kernel, out_shape=(out, out), in_specs=[pl.BlockSpec(...  4.05 us
    ppermute x1, starting transfers between devices, body(): got = lax.ppermute(send, 'mol', swap)  4.02 us
    pallas_call x1, Pallas kernels, choose(): pl.pallas_call(choose_kernel, out_shape=(jax.ShapeDtypeStruct((4 * EDGES,...  3.5 us
    unnamed x34, local copies, waits for them, and re-layouts  3.24 us
  transfers between devices with their start and end apart: 13, of which 11 were waited for; matrix products, arithmetic and copies ran while one was open for 7% of the time, Pallas kernels for 24%

profile of v6, /device:TPU:1, one launch (start us, length us, event | category | flops | bytes accessed | tf_op | source)
XLA Modules:
  0.0 88.2 jit_solution(10838703119620172492)
XLA Ops:
  0.6 0.0 copy-start.13
  0.6 0.0 copy-start.8
  0.7 0.0 copy-start.9
  0.7 1.7 %pack.1.refs_0_ = bf16[86,8,128]{2,1,0:T(8,128)(2,1)} custom-call(s32[1]{0:T(128)} %bitcast.core, bf16[56,896]{1,0:T(8,128)(2,1)} %refs_0_.1, bf16[48,768]{1,0:T(8,128)(2,1)} %refs_1_.1, bf16[48,768]{1,0:T(8,128)(2,1)} %refs_2_.1, bf16[40,640]{1,0:T(8,128)(2,1)} %refs_3_.1, bf16[40,640]{1,0:T(8,128)(2,1)} %refs_4_.1), custom_call_target="tpu_custom_call" | custom-call | tf_op jit(solution)/shard_map/pack/pallas_call | solution.py:180
  2.3 0.0 copy-start
  2.4 7.8 %collective-permute-start.1 = (bf16[86,8,128]{2,1,0:T(8,128)(2,1)}, bf16[86,8,128]{2,1,0:T(8,128)(2,1)S(1)}, u32[]{:S(2)}, u32[]{:S(2)}) collective-permute-start(bf16[86,8,128]{2,1,0:T(8,128)(2,1)} %pack.1.refs_0_), channel_id=1, source_target_pairs={{0,2},{1,3},{2,0},{3,1},{4,6},{5,7},{6,4},{7,5},{8,10},{9,11},{10,... | collective-permute-start | bytes 528392 | tf_op jit(solution)/shard_map/ppermute | solution.py:455
  10.2 0.7 collective-permute-start.2
  10.9 1.9 %collective-permute-start = (bf16[86,8,128]{2,1,0:T(8,128)(2,1)}, bf16[86,8,128]{2,1,0:T(8,128)(2,1)S(1)}, u32[]{:S(2)}, u32[]{:S(2)}) collective-permute-start(bf16[86,8,128]{2,1,0:T(8,128)(2,1)} %pack.1.refs_0_), channel_id=1, source_target_pairs={{0,3},{1,0},{2,1},{3,2},{4,7},{5,4},{6,5},{7,6},{8,11},{9,8},{10,9... | collective-permute-start | bytes 528392 | tf_op jit(solution)/shard_map/ppermute | solution.py:455
  12.9 0.5 collective-permute-done.1.refs_3_
  13.3 3.0 %collective-permute-done.2.refs_1_ = bf16[86,8,128]{2,1,0:T(8,128)(2,1)S(1)} collective-permute-done((bf16[86,8,128]{2,1,0:T(8,128)(2,1)}, bf16[86,8,128]{2,1,0:T(8,128)(2,1)S(1)}, u32[]{:S(2)}, u32[]{:S(2)}) %collective-permute-start.2) | collective-permute-done | bytes 176160 | tf_op jit(solution)/shard_map/ppermute | solution.py:455
  16.4 1.0 %maximum_select_fusion = bf16[172,8,128]{2,1,0:T(8,128)(2,1)S(1)} fusion(bf16[86,8,128]{2,1,0:T(8,128)(2,1)S(1)} %collective-permute-done.1.refs_3_, bf16[86,8,128]{2,1,0:T(8,128)(2,1)S(1)} %collective-permute-done.2.refs_1_, pred[]{:T(512)S(6)} %eq.9, bf16[86,8,128]{2,1,0:T(8,128)(2,1)} %pack.1.refs_0_), kind=kLoop, calls=%fused_computation.4 | loop fusion | flops 528384 | bytes 880641 | tf_op jit(solution)/shard_map/jit(_where)/select_n | solution.py:484
  17.4 1.5 %collective-permute-start.3 = (bf16[172,8,128]{2,1,0:T(8,128)(2,1)S(1)}, bf16[172,8,128]{2,1,0:T(8,128)(2,1)S(1)}, u32[]{:S(2)}, u32[]{:S(2)}) collective-permute-start(bf16[172,8,128]{2,1,0:T(8,128)(2,1)S(1)} %maximum_select_fusion), channel_id=1, source_target_pairs={{0,4},{1,5},{2,6},{3,7},{4,8},{5,9},{6,10},{7,11},{8,12},{9,13},{1... | collective-permute-start | bytes 1056776 | tf_op jit(solution)/shard_map/ppermute | solution.py:455
  18.8 2.5 %copy.26 = bf16[256,29,49]{0,2,1:T(8,128)(2,1)} copy(bf16[256,29,49]{0,1,2:T(8,128)(2,1)} %param.17) | data formatting | bytes 1455104 | tf_op args[1]
  21.3 0.0 copy-done.13
  21.3 0.8 copy.21.source
  22.1 0.0 copy-done.8
  22.1 0.8 copy.22.target
  22.8 0.0 copy-done.9
  22.8 0.8 copy.23.rotation
  24.3 0.0 collective-permute-done.refs_2_
  24.3 1.4 %collective-permute-start.5 = (bf16[172,8,128]{2,1,0:T(8,128)(2,1)S(1)}, bf16[172,8,128]{2,1,0:T(8,128)(2,1)S(1)}, u32[]{:S(2)}, u32[]{:S(2)}) collective-permute-start(bf16[172,8,128]{2,1,0:T(8,128)(2,1)S(1)} %constant_dynamic-update-slice_fusion), channel_id=1, source_target_pairs={{0,28},{1,29},{2,30},{3,31},{4,0},{5,1},{6,2},{7,3},{8,4},{9,5},{1... | collective-permute-start | bytes 1056776 | tf_op jit(solution)/shard_map/ppermute | solution.py:455
  25.7 0.0 copy-start.4
  25.7 0.0 copy-start.5
  25.7 0.0 copy-start.6
  25.7 0.0 copy-start.11
  25.7 2.4 %collective-permute-done.3.refs_4_ = bf16[172,8,128]{2,1,0:T(8,128)(2,1)S(1)} collective-permute-done((bf16[172,8,128]{2,1,0:T(8,128)(2,1)S(1)}, bf16[172,8,128]{2,1,0:T(8,128)(2,1)S(1)}, u32[]{:S(2)}, u32[]{:S(2)}) %collective-permute-start.3) | collective-permute-done | bytes 352288 | tf_op jit(solution)/shard_map/ppermute | solution.py:455
  28.1 0.0 copy-done
  28.1 0.1 broadcast_select_fusion
  28.2 4.8 %collective-permute-done.5.refs_5_ = bf16[172,8,128]{2,1,0:T(8,128)(2,1)S(1)} collective-permute-done((bf16[172,8,128]{2,1,0:T(8,128)(2,1)S(1)}, bf16[172,8,128]{2,1,0:T(8,128)(2,1)S(1)}, u32[]{:S(2)}, u32[]{:S(2)}) %collective-permute-start.5) | collective-permute-done | bytes 352288 | tf_op jit(solution)/shard_map/ppermute | solution.py:455
  33.1 0.1 pad_maximum_fusion.1
  33.1 1.7 %collective-permute-start.6 = (bf16[344,8,128]{2,1,0:T(8,128)(2,1)S(1)}, bf16[344,8,128]{2,1,0:T(8,128)(2,1)}, u32[]{:S(2)}, u32[]{:S(2)}) collective-permute-start(bf16[344,8,128]{2,1,0:T(8,128)(2,1)S(1)} %pad_maximum_fusion.1), channel_id=1, source_target_pairs={{0,28},{1,29},{2,30},{3,31},{4,0},{5,1},{6,2},{7,3},{8,4},{9,5},{1... | collective-permute-start | bytes 2113544 | tf_op jit(solution)/shard_map/ppermute | solution.py:455
  34.8 0.1 pad_maximum_fusion
  34.9 0.2 collective-permute-start.4
  35.1 0.0 copy-done.12
  35.1 0.1 broadcast_select_fusion.3.filt
  35.2 0.0 copy-done.1
  35.2 0.0 copy-done.4
  35.2 0.0 copy-done.5
  35.2 0.0 copy-done.6
  35.3 0.0 copy-start.15
  35.3 9.0 %features.1 = (bf16[576,1792]{1,0:T(8,128)(2,1)S(1)}, bf16[576,1792]{1,0:T(8,128)(2,1)}, bf16[512,256]{1,0:T(8,128)(2,1)S(1)}, bf16[48,128]{1,0:T(8,128)(2,1)S(1)}) custom-call(s32[1]{0:T(128)} %bitcast.core, bf16[48,6272]{1,0:T(8,128)(2,1)S(1)} %copy-done.11, bf16[29,49,256]{2,1,0:T(8,128)(2,1)S(1)} %bitcast.20, s32[192,1]{1,0:T(8,128)S(1)} %copy-done.4, ...), custom_call_target="tpu_custom_call" | custom-call | flops 6000000000 | bytes 8000000 | tf_op jit(solution)/shard_map/features/pallas_call | solution.py:122
  44.3 0.0 copy-start.2
  44.3 0.7 copy-done.2
  45.0 0.0 collective-permute-done.6.refs_7_
  45.0 1.5 %collective-permute-done.4.refs_6_ = bf16[344,8,128]{2,1,0:T(8,128)(2,1)} collective-permute-done((bf16[344,8,128]{2,1,0:T(8,128)(2,1)S(1)}, bf16[344,8,128]{2,1,0:T(8,128)(2,1)}, u32[]{:S(2)}, u32[]{:S(2)}) %collective-permute-start.4) | collective-permute-done | bytes 704544 | tf_op jit(solution)/shard_map/ppermute | solution.py:455
  46.5 4.0 %collective-permute-start.9 = (bf16[576,1792]{1,0:T(8,128)(2,1)}, bf16[576,1792]{1,0:T(8,128)(2,1)}, u32[]{:S(2)}, u32[]{:S(2)}) collective-permute-start(bf16[576,1792]{1,0:T(8,128)(2,1)} %get-tuple-element.22), channel_id=1, source_target_pairs={{0,32},{32,0},{64,96},{96,64},{128,160},{160,128},{192,224},{224,1... | collective-permute-start | bytes 6193160 | tf_op jit(solution)/shard_map/ppermute | solution.py:526
  50.5 1.3 %collective-permute-start.7 = (bf16[344,8,128]{2,1,0:T(8,128)(2,1)}, bf16[344,8,128]{2,1,0:T(8,128)(2,1)}, u32[]{:S(2)}, u32[]{:S(2)}) collective-permute-start(bf16[344,8,128]{2,1,0:T(8,128)(2,1)} %collective-permute-done.4.refs_6_), channel_id=1, source_target_pairs={{0,4},{1,5},{2,6},{3,7},{4,8},{5,9},{6,10},{7,11},{8,12},{9,13},{1... | collective-permute-start | bytes 2113544 | tf_op jit(solution)/shard_map/ppermute | solution.py:455
  51.8 1.4 %collective-permute-start.8 = (bf16[344,8,128]{2,1,0:T(8,128)(2,1)}, bf16[344,8,128]{2,1,0:T(8,128)(2,1)}, u32[]{:S(2)}, u32[]{:S(2)}) collective-permute-start(bf16[344,8,128]{2,1,0:T(8,128)(2,1)} %collective-permute-done.6.refs_7_), channel_id=1, source_target_pairs={{0,28},{1,29},{2,30},{3,31},{4,0},{5,1},{6,2},{7,3},{8,4},{9,5},{1... | collective-permute-start | bytes 2113544 | tf_op jit(solution)/shard_map/ppermute | solution.py:455
  53.2 1.4 %collective-permute-done.9.got.refs_11_ = bf16[576,1792]{1,0:T(8,128)(2,1)} collective-permute-done((bf16[576,1792]{1,0:T(8,128)(2,1)}, bf16[576,1792]{1,0:T(8,128)(2,1)}, u32[]{:S(2)}, u32[]{:S(2)}) %collective-permute-start.9) | collective-permute-done | bytes 2064416 | tf_op jit(solution)/shard_map/ppermute | solution.py:526
  54.6 3.5 %choose.1 = (bf16[768,384]{1,0:T(8,128)(2,1)S(1)}, bf16[384,448]{1,0:T(8,128)(2,1)S(1)}) custom-call(s32[1]{0:T(128)} %bitcast.core, s32[32]{0:T(128)S(1)} %fusion.shard, bf16[576,1792]{1,0:T(8,128)(2,1)S(1)} %get-tuple-element.21.own.refs_10_, bf16[576,1792]{1,0:T(8,128)(2,1)} %collective-permute-done.9.got.refs_11_, bf16[86,8,128]{2,1,0:T(8,128)(2,1)S(1)} %copy-done, ...), custom_call_target="tpu_custom_call" | custom-call | flops 1000000000 | bytes 4000000 | tf_op jit(solution)/shard_map/choose/pallas_call | solution.py:243
  58.1 4.2 %collective-permute-done.7.refs_8_ = bf16[344,8,128]{2,1,0:T(8,128)(2,1)} collective-permute-done((bf16[344,8,128]{2,1,0:T(8,128)(2,1)}, bf16[344,8,128]{2,1,0:T(8,128)(2,1)}, u32[]{:S(2)}, u32[]{:S(2)}) %collective-permute-start.7) | collective-permute-done | bytes 704544 | tf_op jit(solution)/shard_map/ppermute | solution.py:455
  62.3 0.1 collective-permute-done.8.refs_9_
  62.4 2.3 %collective-permute-start.11 = (bf16[344,8,128]{2,1,0:T(8,128)(2,1)}, bf16[344,8,128]{2,1,0:T(8,128)(2,1)S(1)}, u32[]{:S(2)}, u32[]{:S(2)}) collective-permute-start(bf16[344,8,128]{2,1,0:T(8,128)(2,1)} %collective-permute-done.8.refs_9_), channel_id=1, source_target_pairs={{0,28},{1,29},{2,30},{3,31},{4,0},{5,1},{6,2},{7,3},{8,4},{9,5},{1... | collective-permute-start | bytes 2113544 | tf_op jit(solution)/shard_map/ppermute | solution.py:455
  64.7 0.0 collective-permute-start.10
  64.7 7.7 %mix_early.1 = (f32[6,768,256]{2,1,0:T(8,128)S(1)}, f32[3,384,256]{2,1,0:T(8,128)S(1)}) custom-call(s32[1]{0:T(128)} %bitcast.core, s32[32]{0:T(128)S(1)} %fusion.shard, bf16[86,8,128]{2,1,0:T(8,128)(2,1)S(1)} %copy-done, bf16[86,8,128]{2,1,0:T(8,128)(2,1)S(1)} %collective-permute-done.2.refs_1_, bf16[86,8,128]{2,1,0:T(8,128)(2,1)S(1)} %collective-permute-done.refs_2_, ...), custom_call_target="tpu_custom_call" | custom-call | flops 4000000000 | bytes 12000000 | tf_op jit(solution)/shard_map/mix_early/pallas_call | solution.py:305
  72.4 0.6 collective-permute-done.11
  73.1 3.3 %collective-permute-done.10 = bf16[344,8,128]{2,1,0:T(8,128)(2,1)S(1)} collective-permute-done((bf16[344,8,128]{2,1,0:T(8,128)(2,1)}, bf16[344,8,128]{2,1,0:T(8,128)(2,1)S(1)}, u32[]{:S(2)}, u32[]{:S(2)}) %collective-permute-start.10) | collective-permute-done | bytes 704544 | tf_op jit(solution)/shard_map/ppermute | solution.py:455
  76.4 4.0 %mix_late.1 = (bf16[15,192,128]{2,1,0:T(8,128)(2,1)S(1)}, bf16[15,192,128]{2,1,0:T(8,128)(2,1)}) custom-call(s32[1]{0:T(128)} %bitcast.core, bf16[4,86,8,128]{3,2,1,0:T(8,128)(2,1)S(1)} %bitcast.22, bf16[4,86,8,128]{3,2,1,0:T(8,128)(2,1)S(1)} %bitcast.21, f32[6,768,256]{2,1,0:T(8,128)S(1)} %get-tuple-element.26.part, ...), custom_call_target="tpu_custom_call" | custom-call | flops 1000000000 | bytes 8000000 | tf_op jit(solution)/shard_map/mix_late/pallas_call | solution.py:362
  80.4 2.5 %collective-permute-start.12 = (bf16[15,192,128]{2,1,0:T(8,128)(2,1)}, bf16[15,192,128]{2,1,0:T(8,128)(2,1)S(1)}, u32[]{:S(2)}, u32[]{:S(2)}) collective-permute-start(bf16[15,192,128]{2,1,0:T(8,128)(2,1)} %get-tuple-element.31), channel_id=1, source_target_pairs={{0,32},{32,0},{64,96},{96,64},{128,160},{160,128},{192,224},{224,1... | collective-permute-start | bytes 2211848 | tf_op jit(solution)/shard_map/ppermute | solution.py:534
  83.0 0.1 copy.24.struct
  83.1 0.0 copy-start.10
  83.1 0.8 ends_of.1.hot
  83.9 1.1 %collective-permute-done.12.got = bf16[15,192,128]{2,1,0:T(8,128)(2,1)S(1)} collective-permute-done((bf16[15,192,128]{2,1,0:T(8,128)(2,1)}, bf16[15,192,128]{2,1,0:T(8,128)(2,1)S(1)}, u32[]{:S(2)}, u32[]{:S(2)}) %collective-permute-start.12) | collective-permute-done | bytes 737312 | tf_op jit(solution)/shard_map/ppermute | solution.py:534
  85.0 3.1 %turn_back.1 = (bf16[48,6272]{1,0:T(8,128)(2,1)}, f32[4]{0:T(128)}) custom-call(s32[1]{0:T(128)} %bitcast.core, s32[4]{0:T(128)S(1)} %copy-done.10, bf16[15,192,128]{2,1,0:T(8,128)(2,1)S(1)} %get-tuple-element.30.after.mine, bf16[15,192,128]{2,1,0:T(8,128)(2,1)S(1)} %collective-permute-done.12.got, bf16[11280,192]{1,0:T(8,128)(2,1)S(1)} %ends_of.1.hot, ...), custom_call_target="tpu_custom_call" | custom-call | flops 1000000000 | bytes 4000000 | tf_op jit(solution)/shard_map/turn_back/pallas_call | solution.py:432
  (16 shorter events, 0.1 us)
Async XLA Ops:
  0.6 20.7 %copy-start.13 = (s32[192]{0:T(256)S(1)}, s32[192]{0:T(256)}, u32[]{:S(2)}) copy-start(s32[192]{0:T(256)} %param.18) | copy-start | bytes 2308
  0.6 21.4 %copy-start.8 = (s32[192]{0:T(256)S(1)}, s32[192]{0:T(256)}, u32[]{:S(2)}) copy-start(s32[192]{0:T(256)} %param.19) | copy-start | bytes 2308
  0.7 22.2 %copy-start.9 = (s32[192]{0:T(256)S(1)}, s32[192]{0:T(256)}, u32[]{:S(2)}) copy-start(s32[192]{0:T(256)} %param.20) | copy-start | bytes 2308
  2.3 25.8 %copy-start = (bf16[86,8,128]{2,1,0:T(8,128)(2,1)S(1)}, bf16[86,8,128]{2,1,0:T(8,128)(2,1)}, u32[]{:S(2)}) copy-start(bf16[86,8,128]{2,1,0:T(8,128)(2,1)} %pack.1.refs_0_) | copy-start | bytes 528388
  2.4 11.0 %collective-permute-start.1 = (bf16[86,8,128]{2,1,0:T(8,128)(2,1)}, bf16[86,8,128]{2,1,0:T(8,128)(2,1)S(1)}, u32[]{:S(2)}, u32[]{:S(2)}) collective-permute-start(bf16[86,8,128]{2,1,0:T(8,128)(2,1)} %pack.1.refs_0_), channel_id=1, source_target_pairs={{0,2},{1,3},{2,0},{3,1},{4,6},{5,7},{6,4},{7,5},{8,10},{9,11},{10,... | collective-permute-start | bytes 528392 | tf_op jit(solution)/shard_map/ppermute | solution.py:455
  10.2 6.2 %collective-permute-start.2 = (bf16[86,8,128]{2,1,0:T(8,128)(2,1)}, bf16[86,8,128]{2,1,0:T(8,128)(2,1)S(1)}, u32[]{:S(2)}, u32[]{:S(2)}) collective-permute-start(bf16[86,8,128]{2,1,0:T(8,128)(2,1)} %pack.1.refs_0_), channel_id=1, source_target_pairs={{0,1},{1,2},{2,3},{3,0},{4,5},{5,6},{6,7},{7,4},{8,9},{9,10},{10,1... | collective-permute-start | bytes 528392 | tf_op jit(solution)/shard_map/ppermute | solution.py:455
  10.9 13.3 %collective-permute-start = (bf16[86,8,128]{2,1,0:T(8,128)(2,1)}, bf16[86,8,128]{2,1,0:T(8,128)(2,1)S(1)}, u32[]{:S(2)}, u32[]{:S(2)}) collective-permute-start(bf16[86,8,128]{2,1,0:T(8,128)(2,1)} %pack.1.refs_0_), channel_id=1, source_target_pairs={{0,3},{1,0},{2,1},{3,2},{4,7},{5,4},{6,5},{7,6},{8,11},{9,8},{10,9... | collective-permute-start | bytes 528392 | tf_op jit(solution)/shard_map/ppermute | solution.py:455
  17.4 10.8 %collective-permute-start.3 = (bf16[172,8,128]{2,1,0:T(8,128)(2,1)S(1)}, bf16[172,8,128]{2,1,0:T(8,128)(2,1)S(1)}, u32[]{:S(2)}, u32[]{:S(2)}) collective-permute-start(bf16[172,8,128]{2,1,0:T(8,128)(2,1)S(1)} %maximum_select_fusion), channel_id=1, source_target_pairs={{0,4},{1,5},{2,6},{3,7},{4,8},{5,9},{6,10},{7,11},{8,12},{9,13},{1... | collective-permute-start | bytes 1056776 | tf_op jit(solution)/shard_map/ppermute | solution.py:455
  24.3 8.7 %collective-permute-start.5 = (bf16[172,8,128]{2,1,0:T(8,128)(2,1)S(1)}, bf16[172,8,128]{2,1,0:T(8,128)(2,1)S(1)}, u32[]{:S(2)}, u32[]{:S(2)}) collective-permute-start(bf16[172,8,128]{2,1,0:T(8,128)(2,1)S(1)} %constant_dynamic-update-slice_fusion), channel_id=1, source_target_pairs={{0,28},{1,29},{2,30},{3,31},{4,0},{5,1},{6,2},{7,3},{8,4},{9,5},{1... | collective-permute-start | bytes 1056776 | tf_op jit(solution)/shard_map/ppermute | solution.py:455
  25.7 9.4 %copy-start.12 = (bf16[192,128]{1,0:T(8,128)(2,1)S(1)}, bf16[192,128]{1,0:T(8,128)(2,1)}, u32[]{:S(2)}) copy-start(bf16[192,128]{1,0:T(8,128)(2,1)} %param.21) | copy-start | bytes 147460
  25.7 9.5 %copy-start.1 = (bf16[256,29,49]{0,2,1:T(8,128)(2,1)S(1)}, bf16[256,29,49]{0,2,1:T(8,128)(2,1)}, u32[]{:S(2)}) copy-start(bf16[256,29,49]{0,2,1:T(8,128)(2,1)} %copy.26) | copy-start | bytes 2182660
  25.7 9.5 %copy-start.4 = (s32[192,1]{1,0:T(8,128)S(1)}, s32[192,1]{1,0:T(8,128)}, u32[]{:S(2)}) copy-start(s32[192,1]{1,0:T(8,128)} %copy.21.source) | copy-start | bytes 2308
  25.7 9.5 %copy-start.5 = (s32[192,1]{1,0:T(8,128)S(1)}, s32[192,1]{1,0:T(8,128)}, u32[]{:S(2)}) copy-start(s32[192,1]{1,0:T(8,128)} %copy.22.target) | copy-start | bytes 2308
  25.7 9.5 %copy-start.6 = (s32[192,1]{1,0:T(8,128)S(1)}, s32[192,1]{1,0:T(8,128)}, u32[]{:S(2)}) copy-start(s32[192,1]{1,0:T(8,128)} %copy.23.rotation) | copy-start | bytes 2308
  25.7 9.5 %copy-start.11 = (bf16[48,6272]{1,0:T(8,128)(2,1)S(1)}, bf16[48,6272]{1,0:T(8,128)(2,1)}, u32[]{:S(2)}) copy-start(bf16[48,6272]{1,0:T(8,128)(2,1)} %node.1) | copy-start | bytes 1806340
  33.1 11.9 %collective-permute-start.6 = (bf16[344,8,128]{2,1,0:T(8,128)(2,1)S(1)}, bf16[344,8,128]{2,1,0:T(8,128)(2,1)}, u32[]{:S(2)}, u32[]{:S(2)}) collective-permute-start(bf16[344,8,128]{2,1,0:T(8,128)(2,1)S(1)} %pad_maximum_fusion.1), channel_id=1, source_target_pairs={{0,28},{1,29},{2,30},{3,31},{4,0},{5,1},{6,2},{7,3},{8,4},{9,5},{1... | collective-permute-start | bytes 2113544 | tf_op jit(solution)/shard_map/ppermute | solution.py:455
  34.9 11.7 %collective-permute-start.4 = (bf16[344,8,128]{2,1,0:T(8,128)(2,1)S(1)}, bf16[344,8,128]{2,1,0:T(8,128)(2,1)}, u32[]{:S(2)}, u32[]{:S(2)}) collective-permute-start(bf16[344,8,128]{2,1,0:T(8,128)(2,1)S(1)} %pad_maximum_fusion), channel_id=1, source_target_pairs={{0,4},{1,5},{2,6},{3,7},{4,8},{5,9},{6,10},{7,11},{8,12},{9,13},{1... | collective-permute-start | bytes 2113544 | tf_op jit(solution)/shard_map/ppermute | solution.py:455
  35.3 18.0 %copy-start.15 = (s32[2,32,2]{1,2,0:T(2,128)S(1)}, s32[2,32,2]{1,2,0:T(2,128)}, u32[]{:S(2)}) copy-start(s32[2,32,2]{1,2,0:T(2,128)} %constant.68.clone) | copy-start | bytes 1540
  44.3 0.7 copy-start.2
  46.5 8.1 %collective-permute-start.9 = (bf16[576,1792]{1,0:T(8,128)(2,1)}, bf16[576,1792]{1,0:T(8,128)(2,1)}, u32[]{:S(2)}, u32[]{:S(2)}) collective-permute-start(bf16[576,1792]{1,0:T(8,128)(2,1)} %get-tuple-element.22), channel_id=1, source_target_pairs={{0,32},{32,0},{64,96},{96,64},{128,160},{160,128},{192,224},{224,1... | collective-permute-start | bytes 6193160 | tf_op jit(solution)/shard_map/ppermute | solution.py:526
  50.5 11.8 %collective-permute-start.7 = (bf16[344,8,128]{2,1,0:T(8,128)(2,1)}, bf16[344,8,128]{2,1,0:T(8,128)(2,1)}, u32[]{:S(2)}, u32[]{:S(2)}) collective-permute-start(bf16[344,8,128]{2,1,0:T(8,128)(2,1)} %collective-permute-done.4.refs_6_), channel_id=1, source_target_pairs={{0,4},{1,5},{2,6},{3,7},{4,8},{5,9},{6,10},{7,11},{8,12},{9,13},{1... | collective-permute-start | bytes 2113544 | tf_op jit(solution)/shard_map/ppermute | solution.py:455
  51.8 10.6 %collective-permute-start.8 = (bf16[344,8,128]{2,1,0:T(8,128)(2,1)}, bf16[344,8,128]{2,1,0:T(8,128)(2,1)}, u32[]{:S(2)}, u32[]{:S(2)}) collective-permute-start(bf16[344,8,128]{2,1,0:T(8,128)(2,1)} %collective-permute-done.6.refs_7_), channel_id=1, source_target_pairs={{0,28},{1,29},{2,30},{3,31},{4,0},{5,1},{6,2},{7,3},{8,4},{9,5},{1... | collective-permute-start | bytes 2113544 | tf_op jit(solution)/shard_map/ppermute | solution.py:455
  62.4 10.7 %collective-permute-start.11 = (bf16[344,8,128]{2,1,0:T(8,128)(2,1)}, bf16[344,8,128]{2,1,0:T(8,128)(2,1)S(1)}, u32[]{:S(2)}, u32[]{:S(2)}) collective-permute-start(bf16[344,8,128]{2,1,0:T(8,128)(2,1)} %collective-permute-done.8.refs_9_), channel_id=1, source_target_pairs={{0,28},{1,29},{2,30},{3,31},{4,0},{5,1},{6,2},{7,3},{8,4},{9,5},{1... | collective-permute-start | bytes 2113544 | tf_op jit(solution)/shard_map/ppermute | solution.py:455
  64.7 11.7 %collective-permute-start.10 = (bf16[344,8,128]{2,1,0:T(8,128)(2,1)}, bf16[344,8,128]{2,1,0:T(8,128)(2,1)S(1)}, u32[]{:S(2)}, u32[]{:S(2)}) collective-permute-start(bf16[344,8,128]{2,1,0:T(8,128)(2,1)} %collective-permute-done.7.refs_8_), channel_id=1, source_target_pairs={{0,4},{1,5},{2,6},{3,7},{4,8},{5,9},{6,10},{7,11},{8,12},{9,13},{1... | collective-permute-start | bytes 2113544 | tf_op jit(solution)/shard_map/ppermute | solution.py:455
  76.4 6.6 %copy-start.14 = (s32[48]{0:T(128)S(1)}, s32[48]{0:T(128)}, u32[]{:S(2)}) copy-start(s32[48]{0:T(128)} %param.28) | copy-start | bytes 580
  76.4 6.7 %copy-start.3 = (bf16[512,256]{1,0:T(8,128)(2,1)S(1)}, bf16[512,256]{1,0:T(8,128)(2,1)}, u32[]{:S(2)}) copy-start(bf16[512,256]{1,0:T(8,128)(2,1)} %copy-done.2) | copy-start | bytes 786436
  80.4 4.6 %collective-permute-start.12 = (bf16[15,192,128]{2,1,0:T(8,128)(2,1)}, bf16[15,192,128]{2,1,0:T(8,128)(2,1)S(1)}, u32[]{:S(2)}, u32[]{:S(2)}) collective-permute-start(bf16[15,192,128]{2,1,0:T(8,128)(2,1)} %get-tuple-element.31), channel_id=1, source_target_pairs={{0,32},{32,0},{64,96},{96,64},{128,160},{160,128},{192,224},{224,1... | collective-permute-start | bytes 2211848 | tf_op jit(solution)/shard_map/ppermute | solution.py:534
  83.1 2.0 %copy-start.7 = (f32[5,128]{1,0:T(8,128)S(1)}, f32[5,128]{1,0:T(8,128)}, u32[]{:S(2)}) copy-start(f32[5,128]{1,0:T(8,128)} %head.1) | copy-start | bytes 7684
  83.1 2.0 %copy-start.10 = (s32[4]{0:T(128)S(1)}, s32[4]{0:T(128)}, u32[]{:S(2)}) copy-start(s32[4]{0:T(128)} %task.1) | copy-start | bytes 52

commit v7 on v6

--- a/solution.py
+++ b/solution.py
@@ -496,8 +496,8 @@
     def aft(value, second=(0, -1)):
         return exchange(value, sizes, (-1, 0), second)
 
-    p1p = forth(pick(h0, jnp.concatenate((a1, a3))), (1, 0))
-    p1m = aft(h1, (-1, 0))
+    q, h1 = lax.optimization_barrier((pick(h0, jnp.concatenate((a1, a3))), h1))
+    p1p, p1m = lax.optimization_barrier((forth(q, (1, 0)), aft(h1, (-1, 0))))
     def both(a, b):
         return jnp.concatenate((a, b))
 

time: 88.5 us -> 83.4 us (0.942)
  waiting for transfers between devices: 23 us -> 20.9 us
  starting transfers between devices: 26.8 us -> 25 us
  local copies, waits for them, and re-layouts: 5.67 us -> 4.46 us
    ppermute x1, starting transfers between devices: 4.02 us -> 1.73 us  [body(): got = lax.ppermute(send, 'mol', swap)]
    ppermute x11, waiting for transfers between devices: 20.5 us -> 18.4 us  [exchange(): return lax.ppermute(value, ('mol', 'task'), pairs)]
    unnamed x34 -> x35, local copies, waits for them, and re-layouts: 3.24 us -> 2.08 us
    select_n x2 -> x1, other arithmetic: 1.07 us -> 0.07 us  [pick(): return jnp.where(first, a, b)]
    concatenate x0 -> x1, other arithmetic: none -> 1 us  [body(): h1 = jnp.concatenate((a2, a3))]
  transfers between devices with their start and end apart: 13 -> 13, of which waited for: 11 -> 9; matrix products, arithmetic and copies ran while one was open for 7% -> 5% of each run, Pallas kernels for 24% -> 25%
where the time goes in v7:
time: 83.4 us; the launch traced here: 83.2 us
  Pallas kernels  29.8 us (36%)
  starting transfers between devices  25 us (30%)
  waiting for transfers between devices  20.9 us (25%)
  local copies, waits for them, and re-layouts  4.46 us (5%)
  between operations  1.72 us (2%)
  other arithmetic  1.31 us (2%)
    ppermute x11, starting transfers between devices, exchange(): return lax.ppermute(value, ('mol', 'task'), pairs)  20.7 us
    ppermute x11, waiting for transfers between devices, exchange(): return lax.ppermute(value, ('mol', 'task'), pairs)  18.4 us
    pallas_call x1, Pallas kernels, features(): pl.pallas_call(feature_kernel, out_shape=(jax.ShapeDtypeStruct((3 * EDGES...  8.99 us
    pallas_call x1, Pallas kernels, mix_early(): pl.pallas_call(early_kernel, out_shape=(jax.ShapeDtypeStruct((6, 4 * EDGE...  7.71 us
    pallas_call x1, Pallas kernels, mix_late(): pl.pallas_call(late_kernel, out_shape=(out, out), in_specs=[pl.BlockSpec(...  4.05 us
    pallas_call x1, Pallas kernels, choose(): pl.pallas_call(choose_kernel, out_shape=(jax.ShapeDtypeStruct((4 * EDGES,...  3.5 us
    pallas_call x1, Pallas kernels, turn_back(): pl.pallas_call(back_kernel, out_shape=(jax.ShapeDtypeStruct((ATOMS, COEF...  3.05 us
    ppermute x1, starting transfers between devices, body(): back = lax.ppermute(other, 'mol', swap)  2.53 us
  transfers between devices with their start and end apart: 13, of which 9 were waited for; matrix products, arithmetic and copies ran while one was open for 5% of the time, Pallas kernels for 25%

profile of v7, /device:TPU:1, one launch (start us, length us, event | category | flops | bytes accessed | tf_op | source)
XLA Modules:
  0.0 83.2 jit_solution(11604407477133468151)
XLA Ops:
  0.6 0.0 copy-start.12
  0.6 0.0 copy-start.14
  0.7 0.0 copy-start.8
  0.7 0.0 copy-start.9
  0.7 1.7 %pack.1.refs_0_ = bf16[86,8,128]{2,1,0:T(8,128)(2,1)} custom-call(s32[1]{0:T(128)} %bitcast.core, bf16[56,896]{1,0:T(8,128)(2,1)} %refs_0_.1, bf16[48,768]{1,0:T(8,128)(2,1)} %refs_1_.1, bf16[48,768]{1,0:T(8,128)(2,1)} %refs_2_.1, bf16[40,640]{1,0:T(8,128)(2,1)} %refs_3_.1, bf16[40,640]{1,0:T(8,128)(2,1)} %refs_4_.1), custom_call_target="tpu_custom_call" | custom-call | tf_op jit(solution)/shard_map/pack/pallas_call | solution.py:180
  2.4 0.0 copy-start
  2.4 2.5 %collective-permute-start = (bf16[86,8,128]{2,1,0:T(8,128)(2,1)}, bf16[86,8,128]{2,1,0:T(8,128)(2,1)S(1)}, u32[]{:S(2)}, u32[]{:S(2)}) collective-permute-start(bf16[86,8,128]{2,1,0:T(8,128)(2,1)} %pack.1.refs_0_), channel_id=1, source_target_pairs={{0,1},{1,2},{2,3},{3,0},{4,5},{5,6},{6,7},{7,4},{8,9},{9,10},{10,1... | collective-permute-start | bytes 528392 | tf_op jit(solution)/shard_map/ppermute | solution.py:455
  5.0 6.0 %collective-permute-start.1 = (bf16[86,8,128]{2,1,0:T(8,128)(2,1)}, bf16[86,8,128]{2,1,0:T(8,128)(2,1)S(1)}, u32[]{:S(2)}, u32[]{:S(2)}) collective-permute-start(bf16[86,8,128]{2,1,0:T(8,128)(2,1)} %pack.1.refs_0_), channel_id=1, source_target_pairs={{0,2},{1,3},{2,0},{3,1},{4,6},{5,7},{6,4},{7,5},{8,10},{9,11},{10,... | collective-permute-start | bytes 528392 | tf_op jit(solution)/shard_map/ppermute | solution.py:455
  11.0 1.9 %collective-permute-start.2 = (bf16[86,8,128]{2,1,0:T(8,128)(2,1)}, bf16[86,8,128]{2,1,0:T(8,128)(2,1)S(1)}, u32[]{:S(2)}, u32[]{:S(2)}) collective-permute-start(bf16[86,8,128]{2,1,0:T(8,128)(2,1)} %pack.1.refs_0_), channel_id=1, source_target_pairs={{0,3},{1,0},{2,1},{3,2},{4,7},{5,4},{6,5},{7,6},{8,11},{9,8},{10,9... | collective-permute-start | bytes 528392 | tf_op jit(solution)/shard_map/ppermute | solution.py:455
  12.9 0.0 collective-permute-done.refs_1_
  12.9 3.1 %collective-permute-done.1.refs_3_ = bf16[86,8,128]{2,1,0:T(8,128)(2,1)S(1)} collective-permute-done((bf16[86,8,128]{2,1,0:T(8,128)(2,1)}, bf16[86,8,128]{2,1,0:T(8,128)(2,1)S(1)}, u32[]{:S(2)}, u32[]{:S(2)}) %collective-permute-start.1) | collective-permute-done | bytes 176160 | tf_op jit(solution)/shard_map/ppermute | solution.py:455
  16.0 2.5 %collective-permute-done.2.refs_2_ = bf16[86,8,128]{2,1,0:T(8,128)(2,1)S(1)} collective-permute-done((bf16[86,8,128]{2,1,0:T(8,128)(2,1)}, bf16[86,8,128]{2,1,0:T(8,128)(2,1)S(1)}, u32[]{:S(2)}, u32[]{:S(2)}) %collective-permute-start.2) | collective-permute-done | bytes 176160 | tf_op jit(solution)/shard_map/ppermute | solution.py:455
  18.5 1.0 %pad_maximum_fusion.2 = (bf16[172,8,128]{2,1,0:T(8,128)(2,1)S(1)}, bf16[172,8,128]{2,1,0:T(8,128)(2,1)S(1)}) fusion(bf16[86,8,128]{2,1,0:T(8,128)(2,1)S(1)} %collective-permute-done.1.refs_3_, bf16[86,8,128]{2,1,0:T(8,128)(2,1)S(1)} %collective-permute-done.2.refs_2_, bf16[86,8,128]{2,1,0:T(8,128)(2,1)S(1)} %collective-permute-done.refs_1_, ...), kind=kLoop, calls=%fused_computation.3 | loop fusion | flops 704512 | bytes 1409025 | tf_op jit(solution)/shard_map/concatenate | solution.py:491
  19.5 0.3 collective-permute-start.3
  19.9 2.4 %collective-permute-start.4 = (bf16[172,8,128]{2,1,0:T(8,128)(2,1)S(1)}, bf16[172,8,128]{2,1,0:T(8,128)(2,1)S(1)}, u32[]{:S(2)}, u32[]{:S(2)}) collective-permute-start(bf16[172,8,128]{2,1,0:T(8,128)(2,1)S(1)} %get-tuple-element.22), channel_id=1, source_target_pairs={{0,28},{1,29},{2,30},{3,31},{4,0},{5,1},{6,2},{7,3},{8,4},{9,5},{1... | collective-permute-start | bytes 1056776 | tf_op jit(solution)/shard_map/ppermute | solution.py:455
  22.3 0.0 copy-done.12
  22.3 1.3 %copy.26 = bf16[256,29,49]{0,2,1:T(8,128)(2,1)} copy(bf16[256,29,49]{0,1,2:T(8,128)(2,1)S(1)} %copy-done.12) | data formatting | bytes 1455104 | tf_op args[1]
  23.6 0.0 copy-done.14
  23.6 0.8 copy.21.source
  24.4 0.0 copy-done.8
  24.4 0.8 copy.22.target
  25.1 0.0 copy-done.9
  25.1 0.8 copy.23.rotation
  26.6 0.0 copy-start.13
  26.6 0.0 copy-start.1
  26.6 0.0 copy-start.4
  26.6 0.0 copy-start.5
  26.6 0.0 copy-start.6
  26.6 0.0 copy-start.11
  26.6 2.9 %collective-permute-done.3.refs_4_ = bf16[172,8,128]{2,1,0:T(8,128)(2,1)S(1)} collective-permute-done((bf16[172,8,128]{2,1,0:T(8,128)(2,1)S(1)}, bf16[172,8,128]{2,1,0:T(8,128)(2,1)S(1)}, u32[]{:S(2)}, u32[]{:S(2)}) %collective-permute-start.3) | collective-permute-done | bytes 352288 | tf_op jit(solution)/shard_map/ppermute | solution.py:455
  29.5 0.0 collective-permute-done.4.refs_5_
  29.6 0.0 copy-done
  29.6 0.1 broadcast_select_fusion
  29.6 0.1 pad_maximum_fusion.1
  29.7 2.4 %collective-permute-start.6 = (bf16[344,8,128]{2,1,0:T(8,128)(2,1)S(1)}, bf16[344,8,128]{2,1,0:T(8,128)(2,1)}, u32[]{:S(2)}, u32[]{:S(2)}) collective-permute-start(bf16[344,8,128]{2,1,0:T(8,128)(2,1)S(1)} %pad_maximum_fusion.1), channel_id=1, source_target_pairs={{0,28},{1,29},{2,30},{3,31},{4,0},{5,1},{6,2},{7,3},{8,4},{9,5},{1... | collective-permute-start | bytes 2113544 | tf_op jit(solution)/shard_map/ppermute | solution.py:455
  32.1 0.1 pad_maximum_fusion
  32.1 0.1 collective-permute-start.5
  32.2 0.1 broadcast_select_fusion.3.filt
  32.4 0.0 copy-start.16
  32.4 9.0 %features.1 = (bf16[576,1792]{1,0:T(8,128)(2,1)S(1)}, bf16[576,1792]{1,0:T(8,128)(2,1)}, bf16[512,256]{1,0:T(8,128)(2,1)S(1)}, bf16[48,128]{1,0:T(8,128)(2,1)S(1)}) custom-call(s32[1]{0:T(128)} %bitcast.core, bf16[48,6272]{1,0:T(8,128)(2,1)S(1)} %copy-done.11, bf16[29,49,256]{2,1,0:T(8,128)(2,1)S(1)} %bitcast.20, s32[192,1]{1,0:T(8,128)S(1)} %copy-done.4, ...), custom_call_target="tpu_custom_call" | custom-call | flops 6000000000 | bytes 8000000 | tf_op jit(solution)/shard_map/features/pallas_call | solution.py:122
  41.4 0.0 copy-start.2
  41.4 0.7 copy-done.2
  42.1 0.0 collective-permute-done.6.refs_7_
  42.1 1.7 %collective-permute-done.5.refs_6_ = bf16[344,8,128]{2,1,0:T(8,128)(2,1)} collective-permute-done((bf16[344,8,128]{2,1,0:T(8,128)(2,1)S(1)}, bf16[344,8,128]{2,1,0:T(8,128)(2,1)}, u32[]{:S(2)}, u32[]{:S(2)}) %collective-permute-start.5) | collective-permute-done | bytes 704544 | tf_op jit(solution)/shard_map/ppermute | solution.py:455
  43.8 1.7 %collective-permute-start.9 = (bf16[576,1792]{1,0:T(8,128)(2,1)}, bf16[576,1792]{1,0:T(8,128)(2,1)}, u32[]{:S(2)}, u32[]{:S(2)}) collective-permute-start(bf16[576,1792]{1,0:T(8,128)(2,1)} %get-tuple-element.30), channel_id=1, source_target_pairs={{0,32},{32,0},{64,96},{96,64},{128,160},{160,128},{192,224},{224,1... | collective-permute-start | bytes 6193160 | tf_op jit(solution)/shard_map/ppermute | solution.py:526
  45.5 1.1 %collective-permute-start.7 = (bf16[344,8,128]{2,1,0:T(8,128)(2,1)}, bf16[344,8,128]{2,1,0:T(8,128)(2,1)}, u32[]{:S(2)}, u32[]{:S(2)}) collective-permute-start(bf16[344,8,128]{2,1,0:T(8,128)(2,1)} %collective-permute-done.5.refs_6_), channel_id=1, source_target_pairs={{0,4},{1,5},{2,6},{3,7},{4,8},{5,9},{6,10},{7,11},{8,12},{9,13},{1... | collective-permute-start | bytes 2113544 | tf_op jit(solution)/shard_map/ppermute | solution.py:455
  46.6 1.5 %collective-permute-start.8 = (bf16[344,8,128]{2,1,0:T(8,128)(2,1)}, bf16[344,8,128]{2,1,0:T(8,128)(2,1)}, u32[]{:S(2)}, u32[]{:S(2)}) collective-permute-start(bf16[344,8,128]{2,1,0:T(8,128)(2,1)} %collective-permute-done.6.refs_7_), channel_id=1, source_target_pairs={{0,28},{1,29},{2,30},{3,31},{4,0},{5,1},{6,2},{7,3},{8,4},{9,5},{1... | collective-permute-start | bytes 2113544 | tf_op jit(solution)/shard_map/ppermute | solution.py:455
  48.2 1.4 %collective-permute-done.9.got.refs_11_ = bf16[576,1792]{1,0:T(8,128)(2,1)} collective-permute-done((bf16[576,1792]{1,0:T(8,128)(2,1)}, bf16[576,1792]{1,0:T(8,128)(2,1)}, u32[]{:S(2)}, u32[]{:S(2)}) %collective-permute-start.9) | collective-permute-done | bytes 2064416 | tf_op jit(solution)/shard_map/ppermute | solution.py:526
  49.6 3.5 %choose.1 = (bf16[768,384]{1,0:T(8,128)(2,1)S(1)}, bf16[384,448]{1,0:T(8,128)(2,1)S(1)}) custom-call(s32[1]{0:T(128)} %bitcast.core, s32[32]{0:T(128)S(1)} %fusion.1.shard, bf16[576,1792]{1,0:T(8,128)(2,1)S(1)} %get-tuple-element.29.own.refs_10_, bf16[576,1792]{1,0:T(8,128)(2,1)} %collective-permute-done.9.got.refs_11_, bf16[86,8,128]{2,1,0:T(8,128)(2,1)S(1)} %copy-done, ...), custom_call_target="tpu_custom_call" | custom-call | flops 1000000000 | bytes 4000000 | tf_op jit(solution)/shard_map/choose/pallas_call | solution.py:243
  53.1 4.2 %collective-permute-done.7.refs_8_ = bf16[344,8,128]{2,1,0:T(8,128)(2,1)} collective-permute-done((bf16[344,8,128]{2,1,0:T(8,128)(2,1)}, bf16[344,8,128]{2,1,0:T(8,128)(2,1)}, u32[]{:S(2)}, u32[]{:S(2)}) %collective-permute-start.7) | collective-permute-done | bytes 704544 | tf_op jit(solution)/shard_map/ppermute | solution.py:455
  57.3 0.0 collective-permute-done.8.refs_9_
  57.3 2.4 %collective-permute-start.11 = (bf16[344,8,128]{2,1,0:T(8,128)(2,1)}, bf16[344,8,128]{2,1,0:T(8,128)(2,1)S(1)}, u32[]{:S(2)}, u32[]{:S(2)}) collective-permute-start(bf16[344,8,128]{2,1,0:T(8,128)(2,1)} %collective-permute-done.8.refs_9_), channel_id=1, source_target_pairs={{0,28},{1,29},{2,30},{3,31},{4,0},{5,1},{6,2},{7,3},{8,4},{9,5},{1... | collective-permute-start | bytes 2113544 | tf_op jit(solution)/shard_map/ppermute | solution.py:455
  59.7 0.0 collective-permute-start.10
  59.7 7.7 %mix_early.1 = (f32[6,768,256]{2,1,0:T(8,128)S(1)}, f32[3,384,256]{2,1,0:T(8,128)S(1)}) custom-call(s32[1]{0:T(128)} %bitcast.core, s32[32]{0:T(128)S(1)} %fusion.1.shard, bf16[86,8,128]{2,1,0:T(8,128)(2,1)S(1)} %copy-done, bf16[86,8,128]{2,1,0:T(8,128)(2,1)S(1)} %collective-permute-done.refs_1_, bf16[86,8,128]{2,1,0:T(8,128)(2,1)S(1)} %collective-permute-done.2.refs_2_, ...), custom_call_target="tpu_custom_call" | custom-call | flops 4000000000 | bytes 12000000 | tf_op jit(solution)/shard_map/mix_early/pallas_call | solution.py:305
  67.4 0.6 collective-permute-done.11
  68.0 3.3 %collective-permute-done.10 = bf16[344,8,128]{2,1,0:T(8,128)(2,1)S(1)} collective-permute-done((bf16[344,8,128]{2,1,0:T(8,128)(2,1)}, bf16[344,8,128]{2,1,0:T(8,128)(2,1)S(1)}, u32[]{:S(2)}, u32[]{:S(2)}) %collective-permute-start.10) | collective-permute-done | bytes 704544 | tf_op jit(solution)/shard_map/ppermute | solution.py:455
  71.4 4.0 %mix_late.1 = (bf16[15,192,128]{2,1,0:T(8,128)(2,1)S(1)}, bf16[15,192,128]{2,1,0:T(8,128)(2,1)}) custom-call(s32[1]{0:T(128)} %bitcast.core, bf16[4,86,8,128]{3,2,1,0:T(8,128)(2,1)S(1)} %bitcast.22, bf16[4,86,8,128]{3,2,1,0:T(8,128)(2,1)S(1)} %bitcast.21, f32[6,768,256]{2,1,0:T(8,128)S(1)} %get-tuple-element.34.part, ...), custom_call_target="tpu_custom_call" | custom-call | flops 1000000000 | bytes 8000000 | tf_op jit(solution)/shard_map/mix_late/pallas_call | solution.py:362
  75.4 2.5 %collective-permute-start.12 = (bf16[15,192,128]{2,1,0:T(8,128)(2,1)}, bf16[15,192,128]{2,1,0:T(8,128)(2,1)S(1)}, u32[]{:S(2)}, u32[]{:S(2)}) collective-permute-start(bf16[15,192,128]{2,1,0:T(8,128)(2,1)} %get-tuple-element.39), channel_id=1, source_target_pairs={{0,32},{32,0},{64,96},{96,64},{128,160},{160,128},{192,224},{224,1... | collective-permute-start | bytes 2211848 | tf_op jit(solution)/shard_map/ppermute | solution.py:534
  77.9 0.1 copy.24.struct
  78.0 0.0 copy-start.10
  78.0 0.8 ends_of.1.hot
  78.9 1.1 %collective-permute-done.12.got = bf16[15,192,128]{2,1,0:T(8,128)(2,1)S(1)} collective-permute-done((bf16[15,192,128]{2,1,0:T(8,128)(2,1)}, bf16[15,192,128]{2,1,0:T(8,128)(2,1)S(1)}, u32[]{:S(2)}, u32[]{:S(2)}) %collective-permute-start.12) | collective-permute-done | bytes 737312 | tf_op jit(solution)/shard_map/ppermute | solution.py:534
  80.0 0.0 copy-done.10
  80.0 3.1 %turn_back.1 = (bf16[48,6272]{1,0:T(8,128)(2,1)}, f32[4]{0:T(128)}) custom-call(s32[1]{0:T(128)} %bitcast.core, s32[4]{0:T(128)S(1)} %copy-done.10, bf16[15,192,128]{2,1,0:T(8,128)(2,1)S(1)} %get-tuple-element.38.after.mine, bf16[15,192,128]{2,1,0:T(8,128)(2,1)S(1)} %collective-permute-done.12.got, bf16[11280,192]{1,0:T(8,128)(2,1)S(1)} %ends_of.1.hot, ...), custom_call_target="tpu_custom_call" | custom-call | flops 1000000000 | bytes 4000000 | tf_op jit(solution)/shard_map/turn_back/pallas_call | solution.py:432
  (16 shorter events, 0.0 us)
Async XLA Ops:
  0.6 21.7 %copy-start.12 = (bf16[256,29,49]{0,1,2:T(8,128)(2,1)S(1)}, bf16[256,29,49]{0,1,2:T(8,128)(2,1)}, u32[]{:S(2)}) copy-start(bf16[256,29,49]{0,1,2:T(8,128)(2,1)} %param.17) | copy-start | bytes 2182660
  0.6 23.0 %copy-start.14 = (s32[192]{0:T(256)S(1)}, s32[192]{0:T(256)}, u32[]{:S(2)}) copy-start(s32[192]{0:T(256)} %param.18) | copy-start | bytes 2308
  0.7 23.7 %copy-start.8 = (s32[192]{0:T(256)S(1)}, s32[192]{0:T(256)}, u32[]{:S(2)}) copy-start(s32[192]{0:T(256)} %param.19) | copy-start | bytes 2308
  0.7 24.5 %copy-start.9 = (s32[192]{0:T(256)S(1)}, s32[192]{0:T(256)}, u32[]{:S(2)}) copy-start(s32[192]{0:T(256)} %param.20) | copy-start | bytes 2308
  2.4 27.1 %copy-start = (bf16[86,8,128]{2,1,0:T(8,128)(2,1)S(1)}, bf16[86,8,128]{2,1,0:T(8,128)(2,1)}, u32[]{:S(2)}) copy-start(bf16[86,8,128]{2,1,0:T(8,128)(2,1)} %pack.1.refs_0_) | copy-start | bytes 528388
  2.4 10.5 %collective-permute-start = (bf16[86,8,128]{2,1,0:T(8,128)(2,1)}, bf16[86,8,128]{2,1,0:T(8,128)(2,1)S(1)}, u32[]{:S(2)}, u32[]{:S(2)}) collective-permute-start(bf16[86,8,128]{2,1,0:T(8,128)(2,1)} %pack.1.refs_0_), channel_id=1, source_target_pairs={{0,1},{1,2},{2,3},{3,0},{4,5},{5,6},{6,7},{7,4},{8,9},{9,10},{10,1... | collective-permute-start | bytes 528392 | tf_op jit(solution)/shard_map/ppermute | solution.py:455
  5.0 11.0 %collective-permute-start.1 = (bf16[86,8,128]{2,1,0:T(8,128)(2,1)}, bf16[86,8,128]{2,1,0:T(8,128)(2,1)S(1)}, u32[]{:S(2)}, u32[]{:S(2)}) collective-permute-start(bf16[86,8,128]{2,1,0:T(8,128)(2,1)} %pack.1.refs_0_), channel_id=1, source_target_pairs={{0,2},{1,3},{2,0},{3,1},{4,6},{5,7},{6,4},{7,5},{8,10},{9,11},{10,... | collective-permute-start | bytes 528392 | tf_op jit(solution)/shard_map/ppermute | solution.py:455
  11.0 7.6 %collective-permute-start.2 = (bf16[86,8,128]{2,1,0:T(8,128)(2,1)}, bf16[86,8,128]{2,1,0:T(8,128)(2,1)S(1)}, u32[]{:S(2)}, u32[]{:S(2)}) collective-permute-start(bf16[86,8,128]{2,1,0:T(8,128)(2,1)} %pack.1.refs_0_), channel_id=1, source_target_pairs={{0,3},{1,0},{2,1},{3,2},{4,7},{5,4},{6,5},{7,6},{8,11},{9,8},{10,9... | collective-permute-start | bytes 528392 | tf_op jit(solution)/shard_map/ppermute | solution.py:455
  19.5 10.0 %collective-permute-start.3 = (bf16[172,8,128]{2,1,0:T(8,128)(2,1)S(1)}, bf16[172,8,128]{2,1,0:T(8,128)(2,1)S(1)}, u32[]{:S(2)}, u32[]{:S(2)}) collective-permute-start(bf16[172,8,128]{2,1,0:T(8,128)(2,1)S(1)} %get-tuple-element.23), channel_id=1, source_target_pairs={{0,4},{1,5},{2,6},{3,7},{4,8},{5,9},{6,10},{7,11},{8,12},{9,13},{1... | collective-permute-start | bytes 1056776 | tf_op jit(solution)/shard_map/ppermute | solution.py:455
  19.9 9.7 %collective-permute-start.4 = (bf16[172,8,128]{2,1,0:T(8,128)(2,1)S(1)}, bf16[172,8,128]{2,1,0:T(8,128)(2,1)S(1)}, u32[]{:S(2)}, u32[]{:S(2)}) collective-permute-start(bf16[172,8,128]{2,1,0:T(8,128)(2,1)S(1)} %get-tuple-element.22), channel_id=1, source_target_pairs={{0,28},{1,29},{2,30},{3,31},{4,0},{5,1},{6,2},{7,3},{8,4},{9,5},{1... | collective-permute-start | bytes 1056776 | tf_op jit(solution)/shard_map/ppermute | solution.py:455
  26.6 5.7 %copy-start.13 = (bf16[192,128]{1,0:T(8,128)(2,1)S(1)}, bf16[192,128]{1,0:T(8,128)(2,1)}, u32[]{:S(2)}) copy-start(bf16[192,128]{1,0:T(8,128)(2,1)} %param.21) | copy-start | bytes 147460
  26.6 5.8 %copy-start.1 = (bf16[256,29,49]{0,2,1:T(8,128)(2,1)S(1)}, bf16[256,29,49]{0,2,1:T(8,128)(2,1)}, u32[]{:S(2)}) copy-start(bf16[256,29,49]{0,2,1:T(8,128)(2,1)} %copy.26) | copy-start | bytes 2182660
  26.6 5.8 %copy-start.4 = (s32[192,1]{1,0:T(8,128)S(1)}, s32[192,1]{1,0:T(8,128)}, u32[]{:S(2)}) copy-start(s32[192,1]{1,0:T(8,128)} %copy.21.source) | copy-start | bytes 2308
  26.6 5.8 %copy-start.5 = (s32[192,1]{1,0:T(8,128)S(1)}, s32[192,1]{1,0:T(8,128)}, u32[]{:S(2)}) copy-start(s32[192,1]{1,0:T(8,128)} %copy.22.target) | copy-start | bytes 2308
  26.6 5.8 %copy-start.6 = (s32[192,1]{1,0:T(8,128)S(1)}, s32[192,1]{1,0:T(8,128)}, u32[]{:S(2)}) copy-start(s32[192,1]{1,0:T(8,128)} %copy.23.rotation) | copy-start | bytes 2308
  26.6 5.8 %copy-start.11 = (bf16[48,6272]{1,0:T(8,128)(2,1)S(1)}, bf16[48,6272]{1,0:T(8,128)(2,1)}, u32[]{:S(2)}) copy-start(bf16[48,6272]{1,0:T(8,128)(2,1)} %node.1) | copy-start | bytes 1806340
  29.7 12.4 %collective-permute-start.6 = (bf16[344,8,128]{2,1,0:T(8,128)(2,1)S(1)}, bf16[344,8,128]{2,1,0:T(8,128)(2,1)}, u32[]{:S(2)}, u32[]{:S(2)}) collective-permute-start(bf16[344,8,128]{2,1,0:T(8,128)(2,1)S(1)} %pad_maximum_fusion.1), channel_id=1, source_target_pairs={{0,28},{1,29},{2,30},{3,31},{4,0},{5,1},{6,2},{7,3},{8,4},{9,5},{1... | collective-permute-start | bytes 2113544 | tf_op jit(solution)/shard_map/ppermute | solution.py:455
  32.1 11.7 %collective-permute-start.5 = (bf16[344,8,128]{2,1,0:T(8,128)(2,1)S(1)}, bf16[344,8,128]{2,1,0:T(8,128)(2,1)}, u32[]{:S(2)}, u32[]{:S(2)}) collective-permute-start(bf16[344,8,128]{2,1,0:T(8,128)(2,1)S(1)} %pad_maximum_fusion), channel_id=1, source_target_pairs={{0,4},{1,5},{2,6},{3,7},{4,8},{5,9},{6,10},{7,11},{8,12},{9,13},{1... | collective-permute-start | bytes 2113544 | tf_op jit(solution)/shard_map/ppermute | solution.py:455
  32.4 15.8 %copy-start.16 = (s32[2,32,2]{1,2,0:T(2,128)S(1)}, s32[2,32,2]{1,2,0:T(2,128)}, u32[]{:S(2)}) copy-start(s32[2,32,2]{1,2,0:T(2,128)} %constant.68.clone) | copy-start | bytes 1540
  41.4 0.7 copy-start.2
  43.8 5.8 %collective-permute-start.9 = (bf16[576,1792]{1,0:T(8,128)(2,1)}, bf16[576,1792]{1,0:T(8,128)(2,1)}, u32[]{:S(2)}, u32[]{:S(2)}) collective-permute-start(bf16[576,1792]{1,0:T(8,128)(2,1)} %get-tuple-element.30), channel_id=1, source_target_pairs={{0,32},{32,0},{64,96},{96,64},{128,160},{160,128},{192,224},{224,1... | collective-permute-start | bytes 6193160 | tf_op jit(solution)/shard_map/ppermute | solution.py:526
  45.5 11.8 %collective-permute-start.7 = (bf16[344,8,128]{2,1,0:T(8,128)(2,1)}, bf16[344,8,128]{2,1,0:T(8,128)(2,1)}, u32[]{:S(2)}, u32[]{:S(2)}) collective-permute-start(bf16[344,8,128]{2,1,0:T(8,128)(2,1)} %collective-permute-done.5.refs_6_), channel_id=1, source_target_pairs={{0,4},{1,5},{2,6},{3,7},{4,8},{5,9},{6,10},{7,11},{8,12},{9,13},{1... | collective-permute-start | bytes 2113544 | tf_op jit(solution)/shard_map/ppermute | solution.py:455
  46.6 10.6 %collective-permute-start.8 = (bf16[344,8,128]{2,1,0:T(8,128)(2,1)}, bf16[344,8,128]{2,1,0:T(8,128)(2,1)}, u32[]{:S(2)}, u32[]{:S(2)}) collective-permute-start(bf16[344,8,128]{2,1,0:T(8,128)(2,1)} %collective-permute-done.6.refs_7_), channel_id=1, source_target_pairs={{0,28},{1,29},{2,30},{3,31},{4,0},{5,1},{6,2},{7,3},{8,4},{9,5},{1... | collective-permute-start | bytes 2113544 | tf_op jit(solution)/shard_map/ppermute | solution.py:455
  57.3 10.8 %collective-permute-start.11 = (bf16[344,8,128]{2,1,0:T(8,128)(2,1)}, bf16[344,8,128]{2,1,0:T(8,128)(2,1)S(1)}, u32[]{:S(2)}, u32[]{:S(2)}) collective-permute-start(bf16[344,8,128]{2,1,0:T(8,128)(2,1)} %collective-permute-done.8.refs_9_), channel_id=1, source_target_pairs={{0,28},{1,29},{2,30},{3,31},{4,0},{5,1},{6,2},{7,3},{8,4},{9,5},{1... | collective-permute-start | bytes 2113544 | tf_op jit(solution)/shard_map/ppermute | solution.py:455
  59.7 11.7 %collective-permute-start.10 = (bf16[344,8,128]{2,1,0:T(8,128)(2,1)}, bf16[344,8,128]{2,1,0:T(8,128)(2,1)S(1)}, u32[]{:S(2)}, u32[]{:S(2)}) collective-permute-start(bf16[344,8,128]{2,1,0:T(8,128)(2,1)} %collective-permute-done.7.refs_8_), channel_id=1, source_target_pairs={{0,4},{1,5},{2,6},{3,7},{4,8},{5,9},{6,10},{7,11},{8,12},{9,13},{1... | collective-permute-start | bytes 2113544 | tf_op jit(solution)/shard_map/ppermute | solution.py:455
  71.4 6.6 %copy-start.15 = (s32[48]{0:T(128)S(1)}, s32[48]{0:T(128)}, u32[]{:S(2)}) copy-start(s32[48]{0:T(128)} %param.28) | copy-start | bytes 580
  71.4 6.7 %copy-start.3 = (bf16[512,256]{1,0:T(8,128)(2,1)S(1)}, bf16[512,256]{1,0:T(8,128)(2,1)}, u32[]{:S(2)}) copy-start(bf16[512,256]{1,0:T(8,128)(2,1)} %copy-done.2) | copy-start | bytes 786436
  75.4 4.6 %collective-permute-start.12 = (bf16[15,192,128]{2,1,0:T(8,128)(2,1)}, bf16[15,192,128]{2,1,0:T(8,128)(2,1)S(1)}, u32[]{:S(2)}, u32[]{:S(2)}) collective-permute-start(bf16[15,192,128]{2,1,0:T(8,128)(2,1)} %get-tuple-element.39), channel_id=1, source_target_pairs={{0,32},{32,0},{64,96},{96,64},{128,160},{160,128},{192,224},{224,1... | collective-permute-start | bytes 2211848 | tf_op jit(solution)/shard_map/ppermute | solution.py:534
  78.0 2.0 %copy-start.7 = (f32[5,128]{1,0:T(8,128)S(1)}, f32[5,128]{1,0:T(8,128)}, u32[]{:S(2)}) copy-start(f32[5,128]{1,0:T(8,128)} %head.1) | copy-start | bytes 7684
  78.0 2.0 %copy-start.10 = (s32[4]{0:T(128)S(1)}, s32[4]{0:T(128)}, u32[]{:S(2)}) copy-start(s32[4]{0:T(128)} %task.1) | copy-start | bytes 52

commit v8 on v7

--- a/solution.py
+++ b/solution.py
@@ -503,6 +503,7 @@
 
     x1p = both(pick(h1, h0), pick(p1p, h1))
     x1m = both(pick(h0, p1p), p1m)
+    x1p, x1m = lax.optimization_barrier((x1p, x1m))
     s1p, s1m = forth(x1p), aft(x1m)
 
     live = (jnp.arange(EDGES, dtype=jnp.int32) < edge_count[0])[:, None]
@@ -526,7 +527,7 @@
     got = lax.ppermute(send, "mol", swap)
     late, late_zero = choose(core_vec, shard, own, got, (b0, a1, a2, a3, p1p, p1m))
     s2p, s2m, late = lax.optimization_barrier((forth(s1p), aft(s1m), late))
-    s3p, s3m = forth(s2p), aft(s2m)
+    s3p, s3m = lax.optimization_barrier((forth(s2p), aft(s2m)))
     blocks = (b0, a1, a2, a3, p1p, p1m, s1p, s1m, s2p, s2m)
     parts = mix_early(core_vec, shard, blocks, own, got)
     held = (4, TILES, 8, C)

time: 83.4 us -> 79 us (0.947)
  waiting for transfers between devices: 20.9 us -> 16.5 us
    ppermute x11, waiting for transfers between devices: 18.4 us -> 14 us  [exchange(): return lax.ppermute(value, ('mol', 'task'), pairs)]
    ppermute x1, starting transfers between devices: 1.73 us -> 0.57 us  [body(): got = lax.ppermute(send, 'mol', swap)]
  transfers between devices with their start and end apart: 13 -> 13, of which waited for: 9 -> 7; matrix products, arithmetic and copies ran while one was open for 5% -> 5% of each run, Pallas kernels for 25% -> 27%
where the time goes in v8:
time: 79 us; the launch traced here: 78.8 us
  Pallas kernels  29.9 us (38%)
  starting transfers between devices  25 us (32%)
  waiting for transfers between devices  16.5 us (21%)
  local copies, waits for them, and re-layouts  4.48 us (6%)
  between operations  1.71 us (2%)
  other arithmetic  1.31 us (2%)
    ppermute x11, starting transfers between devices, exchange(): return lax.ppermute(value, ('mol', 'task'), pairs)  21.4 us
    ppermute x11, waiting for transfers between devices, exchange(): return lax.ppermute(value, ('mol', 'task'), pairs)  14 us
    pallas_call x1, Pallas kernels, features(): pl.pallas_call(feature_kernel, out_shape=(jax.ShapeDtypeStruct((3 * EDGES...  9 us
    pallas_call x1, Pallas kernels, mix_early(): pl.pallas_call(early_kernel, out_shape=(jax.ShapeDtypeStruct((6, 4 * EDGE...  7.72 us
    pallas_call x1, Pallas kernels, mix_late(): pl.pallas_call(late_kernel, out_shape=(out, out), in_specs=[pl.BlockSpec(...  4.07 us
    pallas_call x1, Pallas kernels, choose(): pl.pallas_call(choose_kernel, out_shape=(jax.ShapeDtypeStruct((4 * EDGES,...  3.5 us
    pallas_call x1, Pallas kernels, turn_back(): pl.pallas_call(back_kernel, out_shape=(jax.ShapeDtypeStruct((ATOMS, COEF...  3.05 us
    ppermute x1, starting transfers between devices, body(): back = lax.ppermute(other, 'mol', swap)  3.03 us
  transfers between devices with their start and end apart: 13, of which 7 were waited for; matrix products, arithmetic and copies ran while one was open for 5% of the time, Pallas kernels for 27%

profile of v8, /device:TPU:1, one launch (start us, length us, event | category | flops | bytes accessed | tf_op | source)
XLA Modules:
  0.0 78.8 jit_solution(410917076962514611)
XLA Ops:
  0.6 0.0 copy-start.12
  0.6 0.0 copy-start.14
  0.7 0.0 copy-start.8
  0.7 0.0 copy-start.9
  0.7 1.7 %pack.1.refs_0_ = bf16[86,8,128]{2,1,0:T(8,128)(2,1)} custom-call(s32[1]{0:T(128)} %bitcast.core, bf16[56,896]{1,0:T(8,128)(2,1)} %refs_0_.1, bf16[48,768]{1,0:T(8,128)(2,1)} %refs_1_.1, bf16[48,768]{1,0:T(8,128)(2,1)} %refs_2_.1, bf16[40,640]{1,0:T(8,128)(2,1)} %refs_3_.1, bf16[40,640]{1,0:T(8,128)(2,1)} %refs_4_.1), custom_call_target="tpu_custom_call" | custom-call | tf_op jit(solution)/shard_map/pack/pallas_call | solution.py:180
  2.4 0.0 copy-start
  2.4 2.5 %collective-permute-start = (bf16[86,8,128]{2,1,0:T(8,128)(2,1)}, bf16[86,8,128]{2,1,0:T(8,128)(2,1)S(1)}, u32[]{:S(2)}, u32[]{:S(2)}) collective-permute-start(bf16[86,8,128]{2,1,0:T(8,128)(2,1)} %pack.1.refs_0_), channel_id=1, source_target_pairs={{0,1},{1,2},{2,3},{3,0},{4,5},{5,6},{6,7},{7,4},{8,9},{9,10},{10,1... | collective-permute-start | bytes 528392 | tf_op jit(solution)/shard_map/ppermute | solution.py:455
  5.0 6.0 %collective-permute-start.1 = (bf16[86,8,128]{2,1,0:T(8,128)(2,1)}, bf16[86,8,128]{2,1,0:T(8,128)(2,1)S(1)}, u32[]{:S(2)}, u32[]{:S(2)}) collective-permute-start(bf16[86,8,128]{2,1,0:T(8,128)(2,1)} %pack.1.refs_0_), channel_id=1, source_target_pairs={{0,2},{1,3},{2,0},{3,1},{4,6},{5,7},{6,4},{7,5},{8,10},{9,11},{10,... | collective-permute-start | bytes 528392 | tf_op jit(solution)/shard_map/ppermute | solution.py:455
  11.0 1.9 %collective-permute-start.2 = (bf16[86,8,128]{2,1,0:T(8,128)(2,1)}, bf16[86,8,128]{2,1,0:T(8,128)(2,1)S(1)}, u32[]{:S(2)}, u32[]{:S(2)}) collective-permute-start(bf16[86,8,128]{2,1,0:T(8,128)(2,1)} %pack.1.refs_0_), channel_id=1, source_target_pairs={{0,3},{1,0},{2,1},{3,2},{4,7},{5,4},{6,5},{7,6},{8,11},{9,8},{10,9... | collective-permute-start | bytes 528392 | tf_op jit(solution)/shard_map/ppermute | solution.py:455
  12.9 0.0 collective-permute-done.refs_1_
  12.9 3.1 %collective-permute-done.1.refs_3_ = bf16[86,8,128]{2,1,0:T(8,128)(2,1)S(1)} collective-permute-done((bf16[86,8,128]{2,1,0:T(8,128)(2,1)}, bf16[86,8,128]{2,1,0:T(8,128)(2,1)S(1)}, u32[]{:S(2)}, u32[]{:S(2)}) %collective-permute-start.1) | collective-permute-done | bytes 176160 | tf_op jit(solution)/shard_map/ppermute | solution.py:455
  16.0 2.5 %collective-permute-done.2.refs_2_ = bf16[86,8,128]{2,1,0:T(8,128)(2,1)S(1)} collective-permute-done((bf16[86,8,128]{2,1,0:T(8,128)(2,1)}, bf16[86,8,128]{2,1,0:T(8,128)(2,1)S(1)}, u32[]{:S(2)}, u32[]{:S(2)}) %collective-permute-start.2) | collective-permute-done | bytes 176160 | tf_op jit(solution)/shard_map/ppermute | solution.py:455
  18.5 1.0 %pad_maximum_fusion.2 = (bf16[172,8,128]{2,1,0:T(8,128)(2,1)S(1)}, bf16[172,8,128]{2,1,0:T(8,128)(2,1)S(1)}) fusion(bf16[86,8,128]{2,1,0:T(8,128)(2,1)S(1)} %collective-permute-done.1.refs_3_, bf16[86,8,128]{2,1,0:T(8,128)(2,1)S(1)} %collective-permute-done.2.refs_2_, bf16[86,8,128]{2,1,0:T(8,128)(2,1)S(1)} %collective-permute-done.refs_1_, ...), kind=kLoop, calls=%fused_computation.3 | loop fusion | flops 704512 | bytes 1409025 | tf_op jit(solution)/shard_map/concatenate | solution.py:491
  19.5 0.3 collective-permute-start.3
  19.9 2.4 %collective-permute-start.4 = (bf16[172,8,128]{2,1,0:T(8,128)(2,1)S(1)}, bf16[172,8,128]{2,1,0:T(8,128)(2,1)S(1)}, u32[]{:S(2)}, u32[]{:S(2)}) collective-permute-start(bf16[172,8,128]{2,1,0:T(8,128)(2,1)S(1)} %get-tuple-element.26), channel_id=1, source_target_pairs={{0,28},{1,29},{2,30},{3,31},{4,0},{5,1},{6,2},{7,3},{8,4},{9,5},{1... | collective-permute-start | bytes 1056776 | tf_op jit(solution)/shard_map/ppermute | solution.py:455
  22.3 0.0 copy-done.12
  22.3 1.3 %copy.26 = bf16[256,29,49]{0,2,1:T(8,128)(2,1)} copy(bf16[256,29,49]{0,1,2:T(8,128)(2,1)S(1)} %copy-done.12) | data formatting | bytes 1455104 | tf_op args[1]
  23.6 0.0 copy-done.14
  23.6 0.8 copy.21.source
  24.4 0.0 copy-done.8
  24.4 0.8 copy.22.target
  25.1 0.0 copy-done.9
  25.1 0.8 copy.23.rotation
  26.6 0.0 copy-start.13
  26.6 0.0 copy-start.1
  26.6 0.0 copy-start.4
  26.6 0.0 copy-start.5
  26.6 0.0 copy-start.6
  26.6 0.0 copy-start.11
  26.6 2.9 %collective-permute-done.3.refs_4_ = bf16[172,8,128]{2,1,0:T(8,128)(2,1)S(1)} collective-permute-done((bf16[172,8,128]{2,1,0:T(8,128)(2,1)S(1)}, bf16[172,8,128]{2,1,0:T(8,128)(2,1)S(1)}, u32[]{:S(2)}, u32[]{:S(2)}) %collective-permute-start.3) | collective-permute-done | bytes 352288 | tf_op jit(solution)/shard_map/ppermute | solution.py:455
  29.5 0.0 collective-permute-done.4.refs_5_
  29.6 0.0 copy-done
  29.6 0.1 broadcast_select_fusion
  29.6 0.1 pad_maximum_fusion
  29.8 1.3 %collective-permute-start.5 = (bf16[344,8,128]{2,1,0:T(8,128)(2,1)S(1)}, bf16[344,8,128]{2,1,0:T(8,128)(2,1)}, u32[]{:S(2)}, u32[]{:S(2)}) collective-permute-start(bf16[344,8,128]{2,1,0:T(8,128)(2,1)S(1)} %get-tuple-element.30), channel_id=1, source_target_pairs={{0,4},{1,5},{2,6},{3,7},{4,8},{5,9},{6,10},{7,11},{8,12},{9,13},{1... | collective-permute-start | bytes 2113544 | tf_op jit(solution)/shard_map/ppermute | solution.py:455
  31.1 1.5 %collective-permute-start.6 = (bf16[344,8,128]{2,1,0:T(8,128)(2,1)S(1)}, bf16[344,8,128]{2,1,0:T(8,128)(2,1)}, u32[]{:S(2)}, u32[]{:S(2)}) collective-permute-start(bf16[344,8,128]{2,1,0:T(8,128)(2,1)S(1)} %get-tuple-element.31), channel_id=1, source_target_pairs={{0,28},{1,29},{2,30},{3,31},{4,0},{5,1},{6,2},{7,3},{8,4},{9,5},{1... | collective-permute-start | bytes 2113544 | tf_op jit(solution)/shard_map/ppermute | solution.py:455
  32.5 0.1 broadcast_select_fusion.3.filt
  32.7 0.0 copy-start.16
  32.7 9.0 %features.1 = (bf16[576,1792]{1,0:T(8,128)(2,1)S(1)}, bf16[576,1792]{1,0:T(8,128)(2,1)}, bf16[512,256]{1,0:T(8,128)(2,1)S(1)}, bf16[48,128]{1,0:T(8,128)(2,1)S(1)}) custom-call(s32[1]{0:T(128)} %bitcast.core, bf16[48,6272]{1,0:T(8,128)(2,1)S(1)} %copy-done.11, bf16[29,49,256]{2,1,0:T(8,128)(2,1)S(1)} %bitcast.20, s32[192,1]{1,0:T(8,128)S(1)} %copy-done.4, ...), custom_call_target="tpu_custom_call" | custom-call | flops 6000000000 | bytes 8000000 | tf_op jit(solution)/shard_map/features/pallas_call | solution.py:122
  41.7 0.0 copy-start.2
  41.7 0.7 copy-done.2
  42.4 0.0 collective-permute-done.5.refs_6_
  42.4 0.0 collective-permute-done.6.refs_7_
  42.4 0.6 collective-permute-start.9
  43.0 1.1 %collective-permute-start.7 = (bf16[344,8,128]{2,1,0:T(8,128)(2,1)}, bf16[344,8,128]{2,1,0:T(8,128)(2,1)}, u32[]{:S(2)}, u32[]{:S(2)}) collective-permute-start(bf16[344,8,128]{2,1,0:T(8,128)(2,1)} %collective-permute-done.5.refs_6_), channel_id=1, source_target_pairs={{0,4},{1,5},{2,6},{3,7},{4,8},{5,9},{6,10},{7,11},{8,12},{9,13},{1... | collective-permute-start | bytes 2113544 | tf_op jit(solution)/shard_map/ppermute | solution.py:455
  44.1 1.5 %collective-permute-start.8 = (bf16[344,8,128]{2,1,0:T(8,128)(2,1)}, bf16[344,8,128]{2,1,0:T(8,128)(2,1)}, u32[]{:S(2)}, u32[]{:S(2)}) collective-permute-start(bf16[344,8,128]{2,1,0:T(8,128)(2,1)} %collective-permute-done.6.refs_7_), channel_id=1, source_target_pairs={{0,28},{1,29},{2,30},{3,31},{4,0},{5,1},{6,2},{7,3},{8,4},{9,5},{1... | collective-permute-start | bytes 2113544 | tf_op jit(solution)/shard_map/ppermute | solution.py:455
  45.6 0.0 copy-done.16
  45.7 1.4 %collective-permute-done.9.got.refs_11_ = bf16[576,1792]{1,0:T(8,128)(2,1)} collective-permute-done((bf16[576,1792]{1,0:T(8,128)(2,1)}, bf16[576,1792]{1,0:T(8,128)(2,1)}, u32[]{:S(2)}, u32[]{:S(2)}) %collective-permute-start.9) | collective-permute-done | bytes 2064416 | tf_op jit(solution)/shard_map/ppermute | solution.py:527
  47.1 3.5 %choose.1 = (bf16[768,384]{1,0:T(8,128)(2,1)S(1)}, bf16[384,448]{1,0:T(8,128)(2,1)S(1)}) custom-call(s32[1]{0:T(128)} %bitcast.core, s32[32]{0:T(128)S(1)} %fusion.1.shard, bf16[576,1792]{1,0:T(8,128)(2,1)S(1)} %get-tuple-element.35.own.refs_10_, bf16[576,1792]{1,0:T(8,128)(2,1)} %collective-permute-done.9.got.refs_11_, bf16[86,8,128]{2,1,0:T(8,128)(2,1)S(1)} %copy-done, ...), custom_call_target="tpu_custom_call" | custom-call | flops 1000000000 | bytes 4000000 | tf_op jit(solution)/shard_map/choose/pallas_call | solution.py:243
  50.6 4.2 %collective-permute-done.7.refs_8_ = bf16[344,8,128]{2,1,0:T(8,128)(2,1)} collective-permute-done((bf16[344,8,128]{2,1,0:T(8,128)(2,1)}, bf16[344,8,128]{2,1,0:T(8,128)(2,1)}, u32[]{:S(2)}, u32[]{:S(2)}) %collective-permute-start.7) | collective-permute-done | bytes 704544 | tf_op jit(solution)/shard_map/ppermute | solution.py:455
  54.8 0.0 collective-permute-done.8.refs_9_
  54.8 0.4 collective-permute-start.10
  55.1 2.3 %collective-permute-start.11 = (bf16[344,8,128]{2,1,0:T(8,128)(2,1)}, bf16[344,8,128]{2,1,0:T(8,128)(2,1)S(1)}, u32[]{:S(2)}, u32[]{:S(2)}) collective-permute-start(bf16[344,8,128]{2,1,0:T(8,128)(2,1)} %collective-permute-done.8.refs_9_), channel_id=1, source_target_pairs={{0,28},{1,29},{2,30},{3,31},{4,0},{5,1},{6,2},{7,3},{8,4},{9,5},{1... | collective-permute-start | bytes 2113544 | tf_op jit(solution)/shard_map/ppermute | solution.py:455
  57.4 7.7 %mix_early.1 = (f32[6,768,256]{2,1,0:T(8,128)S(1)}, f32[3,384,256]{2,1,0:T(8,128)S(1)}) custom-call(s32[1]{0:T(128)} %bitcast.core, s32[32]{0:T(128)S(1)} %fusion.1.shard, bf16[86,8,128]{2,1,0:T(8,128)(2,1)S(1)} %copy-done, bf16[86,8,128]{2,1,0:T(8,128)(2,1)S(1)} %collective-permute-done.refs_1_, bf16[86,8,128]{2,1,0:T(8,128)(2,1)S(1)} %collective-permute-done.2.refs_2_, ...), custom_call_target="tpu_custom_call" | custom-call | flops 4000000000 | bytes 12000000 | tf_op jit(solution)/shard_map/mix_early/pallas_call | solution.py:305
  65.2 1.3 %collective-permute-done.10 = bf16[344,8,128]{2,1,0:T(8,128)(2,1)S(1)} collective-permute-done((bf16[344,8,128]{2,1,0:T(8,128)(2,1)}, bf16[344,8,128]{2,1,0:T(8,128)(2,1)S(1)}, u32[]{:S(2)}, u32[]{:S(2)}) %collective-permute-start.10) | collective-permute-done | bytes 704544 | tf_op jit(solution)/shard_map/ppermute | solution.py:455
  66.4 0.0 collective-permute-done.11
  66.4 4.1 %mix_late.1 = (bf16[15,192,128]{2,1,0:T(8,128)(2,1)S(1)}, bf16[15,192,128]{2,1,0:T(8,128)(2,1)}) custom-call(s32[1]{0:T(128)} %bitcast.core, bf16[4,86,8,128]{3,2,1,0:T(8,128)(2,1)S(1)} %bitcast.21, bf16[4,86,8,128]{3,2,1,0:T(8,128)(2,1)S(1)} %bitcast.22, f32[6,768,256]{2,1,0:T(8,128)S(1)} %get-tuple-element.42.part, ...), custom_call_target="tpu_custom_call" | custom-call | flops 1000000000 | bytes 8000000 | tf_op jit(solution)/shard_map/mix_late/pallas_call | solution.py:362
  70.5 3.0 %collective-permute-start.12 = (bf16[15,192,128]{2,1,0:T(8,128)(2,1)}, bf16[15,192,128]{2,1,0:T(8,128)(2,1)S(1)}, u32[]{:S(2)}, u32[]{:S(2)}) collective-permute-start(bf16[15,192,128]{2,1,0:T(8,128)(2,1)} %get-tuple-element.47), channel_id=1, source_target_pairs={{0,32},{32,0},{64,96},{96,64},{128,160},{160,128},{192,224},{224,1... | collective-permute-start | bytes 2211848 | tf_op jit(solution)/shard_map/ppermute | solution.py:535
  73.5 0.1 copy.24.struct
  73.6 0.0 copy-start.10
  73.7 0.8 %ends_of.1.hot = bf16[11280,192]{1,0:T(8,128)(2,1)S(1)} custom-call(bf16[512,256]{1,0:T(8,128)(2,1)S(1)} %copy-done.3, s32[1,192]{1,0:T(1,128)S(1)} %bitcast.26, s32[1,192]{1,0:T(1,128)S(1)} %bitcast.24, bf16[15,192,128]{2,1,0:T(8,128)(2,1)S(1)} %get-tuple-element.46.after.mine), custom_call_target="tpu_custom_call" | custom-call | flops 100000000 | bytes 6000000 | tf_op jit(solution)/shard_map/ends_of/pallas_call | solution.py:389
  74.5 1.1 %collective-permute-done.12.got = bf16[15,192,128]{2,1,0:T(8,128)(2,1)S(1)} collective-permute-done((bf16[15,192,128]{2,1,0:T(8,128)(2,1)}, bf16[15,192,128]{2,1,0:T(8,128)(2,1)S(1)}, u32[]{:S(2)}, u32[]{:S(2)}) %collective-permute-start.12) | collective-permute-done | bytes 737312 | tf_op jit(solution)/shard_map/ppermute | solution.py:535
  75.6 0.0 copy-done.10
  75.6 3.1 %turn_back.1 = (bf16[48,6272]{1,0:T(8,128)(2,1)}, f32[4]{0:T(128)}) custom-call(s32[1]{0:T(128)} %bitcast.core, s32[4]{0:T(128)S(1)} %copy-done.10, bf16[15,192,128]{2,1,0:T(8,128)(2,1)S(1)} %get-tuple-element.46.after.mine, bf16[15,192,128]{2,1,0:T(8,128)(2,1)S(1)} %collective-permute-done.12.got, bf16[11280,192]{1,0:T(8,128)(2,1)S(1)} %ends_of.1.hot, ...), custom_call_target="tpu_custom_call" | custom-call | flops 1000000000 | bytes 4000000 | tf_op jit(solution)/shard_map/turn_back/pallas_call | solution.py:432
  (15 shorter events, 0.0 us)
Async XLA Ops:
  0.6 21.7 %copy-start.12 = (bf16[256,29,49]{0,1,2:T(8,128)(2,1)S(1)}, bf16[256,29,49]{0,1,2:T(8,128)(2,1)}, u32[]{:S(2)}) copy-start(bf16[256,29,49]{0,1,2:T(8,128)(2,1)} %param.17) | copy-start | bytes 2182660
  0.6 23.0 %copy-start.14 = (s32[192]{0:T(256)S(1)}, s32[192]{0:T(256)}, u32[]{:S(2)}) copy-start(s32[192]{0:T(256)} %param.18) | copy-start | bytes 2308
  0.7 23.7 %copy-start.8 = (s32[192]{0:T(256)S(1)}, s32[192]{0:T(256)}, u32[]{:S(2)}) copy-start(s32[192]{0:T(256)} %param.19) | copy-start | bytes 2308
  0.7 24.5 %copy-start.9 = (s32[192]{0:T(256)S(1)}, s32[192]{0:T(256)}, u32[]{:S(2)}) copy-start(s32[192]{0:T(256)} %param.20) | copy-start | bytes 2308
  2.4 27.1 %copy-start = (bf16[86,8,128]{2,1,0:T(8,128)(2,1)S(1)}, bf16[86,8,128]{2,1,0:T(8,128)(2,1)}, u32[]{:S(2)}) copy-start(bf16[86,8,128]{2,1,0:T(8,128)(2,1)} %pack.1.refs_0_) | copy-start | bytes 528388
  2.4 10.5 %collective-permute-start = (bf16[86,8,128]{2,1,0:T(8,128)(2,1)}, bf16[86,8,128]{2,1,0:T(8,128)(2,1)S(1)}, u32[]{:S(2)}, u32[]{:S(2)}) collective-permute-start(bf16[86,8,128]{2,1,0:T(8,128)(2,1)} %pack.1.refs_0_), channel_id=1, source_target_pairs={{0,1},{1,2},{2,3},{3,0},{4,5},{5,6},{6,7},{7,4},{8,9},{9,10},{10,1... | collective-permute-start | bytes 528392 | tf_op jit(solution)/shard_map/ppermute | solution.py:455
  5.0 11.0 %collective-permute-start.1 = (bf16[86,8,128]{2,1,0:T(8,128)(2,1)}, bf16[86,8,128]{2,1,0:T(8,128)(2,1)S(1)}, u32[]{:S(2)}, u32[]{:S(2)}) collective-permute-start(bf16[86,8,128]{2,1,0:T(8,128)(2,1)} %pack.1.refs_0_), channel_id=1, source_target_pairs={{0,2},{1,3},{2,0},{3,1},{4,6},{5,7},{6,4},{7,5},{8,10},{9,11},{10,... | collective-permute-start | bytes 528392 | tf_op jit(solution)/shard_map/ppermute | solution.py:455
  11.0 7.6 %collective-permute-start.2 = (bf16[86,8,128]{2,1,0:T(8,128)(2,1)}, bf16[86,8,128]{2,1,0:T(8,128)(2,1)S(1)}, u32[]{:S(2)}, u32[]{:S(2)}) collective-permute-start(bf16[86,8,128]{2,1,0:T(8,128)(2,1)} %pack.1.refs_0_), channel_id=1, source_target_pairs={{0,3},{1,0},{2,1},{3,2},{4,7},{5,4},{6,5},{7,6},{8,11},{9,8},{10,9... | collective-permute-start | bytes 528392 | tf_op jit(solution)/shard_map/ppermute | solution.py:455
  19.5 10.0 %collective-permute-start.3 = (bf16[172,8,128]{2,1,0:T(8,128)(2,1)S(1)}, bf16[172,8,128]{2,1,0:T(8,128)(2,1)S(1)}, u32[]{:S(2)}, u32[]{:S(2)}) collective-permute-start(bf16[172,8,128]{2,1,0:T(8,128)(2,1)S(1)} %get-tuple-element.27), channel_id=1, source_target_pairs={{0,4},{1,5},{2,6},{3,7},{4,8},{5,9},{6,10},{7,11},{8,12},{9,13},{1... | collective-permute-start | bytes 1056776 | tf_op jit(solution)/shard_map/ppermute | solution.py:455
  19.9 9.7 %collective-permute-start.4 = (bf16[172,8,128]{2,1,0:T(8,128)(2,1)S(1)}, bf16[172,8,128]{2,1,0:T(8,128)(2,1)S(1)}, u32[]{:S(2)}, u32[]{:S(2)}) collective-permute-start(bf16[172,8,128]{2,1,0:T(8,128)(2,1)S(1)} %get-tuple-element.26), channel_id=1, source_target_pairs={{0,28},{1,29},{2,30},{3,31},{4,0},{5,1},{6,2},{7,3},{8,4},{9,5},{1... | collective-permute-start | bytes 1056776 | tf_op jit(solution)/shard_map/ppermute | solution.py:455
  26.6 5.9 %copy-start.13 = (bf16[192,128]{1,0:T(8,128)(2,1)S(1)}, bf16[192,128]{1,0:T(8,128)(2,1)}, u32[]{:S(2)}) copy-start(bf16[192,128]{1,0:T(8,128)(2,1)} %param.21) | copy-start | bytes 147460
  26.6 6.0 %copy-start.1 = (bf16[256,29,49]{0,2,1:T(8,128)(2,1)S(1)}, bf16[256,29,49]{0,2,1:T(8,128)(2,1)}, u32[]{:S(2)}) copy-start(bf16[256,29,49]{0,2,1:T(8,128)(2,1)} %copy.26) | copy-start | bytes 2182660
  26.6 6.0 %copy-start.4 = (s32[192,1]{1,0:T(8,128)S(1)}, s32[192,1]{1,0:T(8,128)}, u32[]{:S(2)}) copy-start(s32[192,1]{1,0:T(8,128)} %copy.21.source) | copy-start | bytes 2308
  26.6 6.0 %copy-start.5 = (s32[192,1]{1,0:T(8,128)S(1)}, s32[192,1]{1,0:T(8,128)}, u32[]{:S(2)}) copy-start(s32[192,1]{1,0:T(8,128)} %copy.22.target) | copy-start | bytes 2308
  26.6 6.0 %copy-start.6 = (s32[192,1]{1,0:T(8,128)S(1)}, s32[192,1]{1,0:T(8,128)}, u32[]{:S(2)}) copy-start(s32[192,1]{1,0:T(8,128)} %copy.23.rotation) | copy-start | bytes 2308
  26.6 6.0 %copy-start.11 = (bf16[48,6272]{1,0:T(8,128)(2,1)S(1)}, bf16[48,6272]{1,0:T(8,128)(2,1)}, u32[]{:S(2)}) copy-start(bf16[48,6272]{1,0:T(8,128)(2,1)} %node.1) | copy-start | bytes 1806340
  29.8 12.6 %collective-permute-start.5 = (bf16[344,8,128]{2,1,0:T(8,128)(2,1)S(1)}, bf16[344,8,128]{2,1,0:T(8,128)(2,1)}, u32[]{:S(2)}, u32[]{:S(2)}) collective-permute-start(bf16[344,8,128]{2,1,0:T(8,128)(2,1)S(1)} %get-tuple-element.30), channel_id=1, source_target_pairs={{0,4},{1,5},{2,6},{3,7},{4,8},{5,9},{6,10},{7,11},{8,12},{9,13},{1... | collective-permute-start | bytes 2113544 | tf_op jit(solution)/shard_map/ppermute | solution.py:455
  31.1 11.3 %collective-permute-start.6 = (bf16[344,8,128]{2,1,0:T(8,128)(2,1)S(1)}, bf16[344,8,128]{2,1,0:T(8,128)(2,1)}, u32[]{:S(2)}, u32[]{:S(2)}) collective-permute-start(bf16[344,8,128]{2,1,0:T(8,128)(2,1)S(1)} %get-tuple-element.31), channel_id=1, source_target_pairs={{0,28},{1,29},{2,30},{3,31},{4,0},{5,1},{6,2},{7,3},{8,4},{9,5},{1... | collective-permute-start | bytes 2113544 | tf_op jit(solution)/shard_map/ppermute | solution.py:455
  32.7 13.0 %copy-start.16 = (s32[2,32,2]{1,2,0:T(2,128)S(1)}, s32[2,32,2]{1,2,0:T(2,128)}, u32[]{:S(2)}) copy-start(s32[2,32,2]{1,2,0:T(2,128)} %constant.68.clone) | copy-start | bytes 1540
  41.7 0.7 copy-start.2
  42.4 4.6 %collective-permute-start.9 = (bf16[576,1792]{1,0:T(8,128)(2,1)}, bf16[576,1792]{1,0:T(8,128)(2,1)}, u32[]{:S(2)}, u32[]{:S(2)}) collective-permute-start(bf16[576,1792]{1,0:T(8,128)(2,1)} %get-tuple-element.36), channel_id=1, source_target_pairs={{0,32},{32,0},{64,96},{96,64},{128,160},{160,128},{192,224},{224,1... | collective-permute-start | bytes 6193160 | tf_op jit(solution)/shard_map/ppermute | solution.py:527
  43.0 11.8 %collective-permute-start.7 = (bf16[344,8,128]{2,1,0:T(8,128)(2,1)}, bf16[344,8,128]{2,1,0:T(8,128)(2,1)}, u32[]{:S(2)}, u32[]{:S(2)}) collective-permute-start(bf16[344,8,128]{2,1,0:T(8,128)(2,1)} %collective-permute-done.5.refs_6_), channel_id=1, source_target_pairs={{0,4},{1,5},{2,6},{3,7},{4,8},{5,9},{6,10},{7,11},{8,12},{9,13},{1... | collective-permute-start | bytes 2113544 | tf_op jit(solution)/shard_map/ppermute | solution.py:455
  44.1 10.6 %collective-permute-start.8 = (bf16[344,8,128]{2,1,0:T(8,128)(2,1)}, bf16[344,8,128]{2,1,0:T(8,128)(2,1)}, u32[]{:S(2)}, u32[]{:S(2)}) collective-permute-start(bf16[344,8,128]{2,1,0:T(8,128)(2,1)} %collective-permute-done.6.refs_7_), channel_id=1, source_target_pairs={{0,28},{1,29},{2,30},{3,31},{4,0},{5,1},{6,2},{7,3},{8,4},{9,5},{1... | collective-permute-start | bytes 2113544 | tf_op jit(solution)/shard_map/ppermute | solution.py:455
  54.8 11.7 %collective-permute-start.10 = (bf16[344,8,128]{2,1,0:T(8,128)(2,1)}, bf16[344,8,128]{2,1,0:T(8,128)(2,1)S(1)}, u32[]{:S(2)}, u32[]{:S(2)}) collective-permute-start(bf16[344,8,128]{2,1,0:T(8,128)(2,1)} %collective-permute-done.7.refs_8_), channel_id=1, source_target_pairs={{0,4},{1,5},{2,6},{3,7},{4,8},{5,9},{6,10},{7,11},{8,12},{9,13},{1... | collective-permute-start | bytes 2113544 | tf_op jit(solution)/shard_map/ppermute | solution.py:455
  55.1 11.3 %collective-permute-start.11 = (bf16[344,8,128]{2,1,0:T(8,128)(2,1)}, bf16[344,8,128]{2,1,0:T(8,128)(2,1)S(1)}, u32[]{:S(2)}, u32[]{:S(2)}) collective-permute-start(bf16[344,8,128]{2,1,0:T(8,128)(2,1)} %collective-permute-done.8.refs_9_), channel_id=1, source_target_pairs={{0,28},{1,29},{2,30},{3,31},{4,0},{5,1},{6,2},{7,3},{8,4},{9,5},{1... | collective-permute-start | bytes 2113544 | tf_op jit(solution)/shard_map/ppermute | solution.py:455
  66.4 7.1 %copy-start.15 = (s32[48]{0:T(128)S(1)}, s32[48]{0:T(128)}, u32[]{:S(2)}) copy-start(s32[48]{0:T(128)} %param.28) | copy-start | bytes 580
  66.4 7.2 %copy-start.3 = (bf16[512,256]{1,0:T(8,128)(2,1)S(1)}, bf16[512,256]{1,0:T(8,128)(2,1)}, u32[]{:S(2)}) copy-start(bf16[512,256]{1,0:T(8,128)(2,1)} %copy-done.2) | copy-start | bytes 786436
  70.5 5.1 %collective-permute-start.12 = (bf16[15,192,128]{2,1,0:T(8,128)(2,1)}, bf16[15,192,128]{2,1,0:T(8,128)(2,1)S(1)}, u32[]{:S(2)}, u32[]{:S(2)}) collective-permute-start(bf16[15,192,128]{2,1,0:T(8,128)(2,1)} %get-tuple-element.47), channel_id=1, source_target_pairs={{0,32},{32,0},{64,96},{96,64},{128,160},{160,128},{192,224},{224,1... | collective-permute-start | bytes 2211848 | tf_op jit(solution)/shard_map/ppermute | solution.py:535
  73.6 2.0 %copy-start.7 = (f32[5,128]{1,0:T(8,128)S(1)}, f32[5,128]{1,0:T(8,128)}, u32[]{:S(2)}) copy-start(f32[5,128]{1,0:T(8,128)} %head.1) | copy-start | bytes 7684
  73.6 2.0 %copy-start.10 = (s32[4]{0:T(128)S(1)}, s32[4]{0:T(128)}, u32[]{:S(2)}) copy-start(s32[4]{0:T(128)} %task.1) | copy-start | bytes 52

commit v9 on v8

--- a/solution.py
+++ b/solution.py
@@ -484,9 +484,10 @@
         return jnp.where(first, a, b)
 
     b0 = pack(core_vec, w_zero, w_one_real, w_one_imag, w_two_real, w_two_imag)
+    a3 = exchange(b0, sizes, (0, 2), (4, 0))
     a1 = exchange(b0, sizes, (0, 1), (1, 0))
     a2 = exchange(b0, sizes, (0, -1), (-1, 0))
-    a3 = exchange(b0, sizes, (0, 2), (4, 0))
+    a3, a1, a2 = lax.optimization_barrier((a3, a1, a2))
     h0 = jnp.concatenate((b0, a1))
     h1 = jnp.concatenate((a2, a3))
 

time: 79 us -> 79.5 us (level)
    ppermute x11, starting transfers between devices: 21.4 us -> 22.2 us  [exchange(): return lax.ppermute(value, ('mol', 'task'), pairs)]
  transfers between devices with their start and end apart: 13 -> 13, of which waited for: 7 -> 8; matrix products, arithmetic and copies ran while one was open for 5% -> 5% of each run, Pallas kernels for 27% -> 27%
where the time goes in v9:
time: 79.5 us; the launch traced here: 79.3 us
  Pallas kernels  29.8 us (37%)
  starting transfers between devices  25.5 us (32%)
  waiting for transfers between devices  16.5 us (21%)
  local copies, waits for them, and re-layouts  4.48 us (6%)
  between operations  1.71 us (2%)
  other arithmetic  1.31 us (2%)
    ppermute x11, starting transfers between devices, exchange(): return lax.ppermute(value, ('mol', 'task'), pairs)  22.2 us
    ppermute x11, waiting for transfers between devices, exchange(): return lax.ppermute(value, ('mol', 'task'), pairs)  14.4 us
    pallas_call x1, Pallas kernels, features(): pl.pallas_call(feature_kernel, out_shape=(jax.ShapeDtypeStruct((3 * EDGES...  9 us
    pallas_call x1, Pallas kernels, mix_early(): pl.pallas_call(early_kernel, out_shape=(jax.ShapeDtypeStruct((6, 4 * EDGE...  7.71 us
    pallas_call x1, Pallas kernels, mix_late(): pl.pallas_call(late_kernel, out_shape=(out, out), in_specs=[pl.BlockSpec(...  4.06 us
    pallas_call x1, Pallas kernels, choose(): pl.pallas_call(choose_kernel, out_shape=(jax.ShapeDtypeStruct((4 * EDGES,...  3.5 us
    pallas_call x1, Pallas kernels, turn_back(): pl.pallas_call(back_kernel, out_shape=(jax.ShapeDtypeStruct((ATOMS, COEF...  3.05 us
    ppermute x1, starting transfers between devices, body(): back = lax.ppermute(other, 'mol', swap)  2.48 us
  transfers between devices with their start and end apart: 13, of which 8 were waited for; matrix products, arithmetic and copies ran while one was open for 5% of the time, Pallas kernels for 27%

profile of v9, /device:TPU:1, one launch (start us, length us, event | category | flops | bytes accessed | tf_op | source)
XLA Modules:
  0.0 79.3 jit_solution(12555050698533155250)
XLA Ops:
  0.6 0.0 copy-start.12
  0.6 0.0 copy-start.14
  0.7 0.0 copy-start.8
  0.7 0.0 copy-start.9
  0.7 1.7 %pack.1.refs_0_ = bf16[86,8,128]{2,1,0:T(8,128)(2,1)} custom-call(s32[1]{0:T(128)} %bitcast.core, bf16[56,896]{1,0:T(8,128)(2,1)} %refs_0_.1, bf16[48,768]{1,0:T(8,128)(2,1)} %refs_1_.1, bf16[48,768]{1,0:T(8,128)(2,1)} %refs_2_.1, bf16[40,640]{1,0:T(8,128)(2,1)} %refs_3_.1, bf16[40,640]{1,0:T(8,128)(2,1)} %refs_4_.1), custom_call_target="tpu_custom_call" | custom-call | tf_op jit(solution)/shard_map/pack/pallas_call | solution.py:180
  2.4 0.0 copy-start
  2.4 7.8 %collective-permute-start = (bf16[86,8,128]{2,1,0:T(8,128)(2,1)}, bf16[86,8,128]{2,1,0:T(8,128)(2,1)S(1)}, u32[]{:S(2)}, u32[]{:S(2)}) collective-permute-start(bf16[86,8,128]{2,1,0:T(8,128)(2,1)} %pack.1.refs_0_), channel_id=1, source_target_pairs={{0,2},{1,3},{2,0},{3,1},{4,6},{5,7},{6,4},{7,5},{8,10},{9,11},{10,... | collective-permute-start | bytes 528392 | tf_op jit(solution)/shard_map/ppermute | solution.py:455
  10.2 0.7 collective-permute-start.1
  11.0 1.9 %collective-permute-start.2 = (bf16[86,8,128]{2,1,0:T(8,128)(2,1)}, bf16[86,8,128]{2,1,0:T(8,128)(2,1)S(1)}, u32[]{:S(2)}, u32[]{:S(2)}) collective-permute-start(bf16[86,8,128]{2,1,0:T(8,128)(2,1)} %pack.1.refs_0_), channel_id=1, source_target_pairs={{0,3},{1,0},{2,1},{3,2},{4,7},{5,4},{6,5},{7,6},{8,11},{9,8},{10,9... | collective-permute-start | bytes 528392 | tf_op jit(solution)/shard_map/ppermute | solution.py:455
  12.9 0.5 collective-permute-done.refs_3_
  13.4 3.0 %collective-permute-done.1.refs_1_ = bf16[86,8,128]{2,1,0:T(8,128)(2,1)S(1)} collective-permute-done((bf16[86,8,128]{2,1,0:T(8,128)(2,1)}, bf16[86,8,128]{2,1,0:T(8,128)(2,1)S(1)}, u32[]{:S(2)}, u32[]{:S(2)}) %collective-permute-start.1) | collective-permute-done | bytes 176160 | tf_op jit(solution)/shard_map/ppermute | solution.py:455
  16.4 1.4 %collective-permute-done.2.refs_2_ = bf16[86,8,128]{2,1,0:T(8,128)(2,1)S(1)} collective-permute-done((bf16[86,8,128]{2,1,0:T(8,128)(2,1)}, bf16[86,8,128]{2,1,0:T(8,128)(2,1)S(1)}, u32[]{:S(2)}, u32[]{:S(2)}) %collective-permute-start.2) | collective-permute-done | bytes 176160 | tf_op jit(solution)/shard_map/ppermute | solution.py:455
  17.8 1.0 %pad_maximum_fusion.2 = (bf16[172,8,128]{2,1,0:T(8,128)(2,1)S(1)}, bf16[172,8,128]{2,1,0:T(8,128)(2,1)S(1)}) fusion(bf16[86,8,128]{2,1,0:T(8,128)(2,1)S(1)} %collective-permute-done.refs_3_, bf16[86,8,128]{2,1,0:T(8,128)(2,1)S(1)} %collective-permute-done.2.refs_2_, bf16[86,8,128]{2,1,0:T(8,128)(2,1)S(1)} %collective-permute-done.1.refs_1_, ...), kind=kLoop, calls=%fused_computation.3 | loop fusion | flops 704512 | bytes 1409025 | tf_op jit(solution)/shard_map/concatenate | solution.py:492
  18.8 0.1 collective-permute-start.3
  18.9 2.6 %collective-permute-start.4 = (bf16[172,8,128]{2,1,0:T(8,128)(2,1)S(1)}, bf16[172,8,128]{2,1,0:T(8,128)(2,1)S(1)}, u32[]{:S(2)}, u32[]{:S(2)}) collective-permute-start(bf16[172,8,128]{2,1,0:T(8,128)(2,1)S(1)} %get-tuple-element.32), channel_id=1, source_target_pairs={{0,28},{1,29},{2,30},{3,31},{4,0},{5,1},{6,2},{7,3},{8,4},{9,5},{1... | collective-permute-start | bytes 1056776 | tf_op jit(solution)/shard_map/ppermute | solution.py:455
  21.6 0.0 copy-done.12
  21.6 1.3 %copy.26 = bf16[256,29,49]{0,2,1:T(8,128)(2,1)} copy(bf16[256,29,49]{0,1,2:T(8,128)(2,1)S(1)} %copy-done.12) | data formatting | bytes 1455104 | tf_op args[1]
  22.9 0.0 copy-done.14
  22.9 0.8 copy.21.source
  23.7 0.0 copy-done.8
  23.7 0.8 copy.22.target
  24.4 0.0 copy-done.9
  24.4 0.8 copy.23.rotation
  25.9 0.0 copy-start.13
  25.9 0.0 copy-start.1
  25.9 0.0 copy-start.4
  25.9 0.0 copy-start.5
  25.9 0.0 copy-start.6
  25.9 0.0 copy-start.11
  25.9 3.6 %collective-permute-done.3.refs_4_ = bf16[172,8,128]{2,1,0:T(8,128)(2,1)S(1)} collective-permute-done((bf16[172,8,128]{2,1,0:T(8,128)(2,1)S(1)}, bf16[172,8,128]{2,1,0:T(8,128)(2,1)S(1)}, u32[]{:S(2)}, u32[]{:S(2)}) %collective-permute-start.3) | collective-permute-done | bytes 352288 | tf_op jit(solution)/shard_map/ppermute | solution.py:455
  29.5 0.0 collective-permute-done.4.refs_5_
  29.5 0.1 broadcast_select_fusion
  29.6 0.1 pad_maximum_fusion
  29.7 0.5 collective-permute-start.5
  30.2 2.6 %collective-permute-start.6 = (bf16[344,8,128]{2,1,0:T(8,128)(2,1)S(1)}, bf16[344,8,128]{2,1,0:T(8,128)(2,1)}, u32[]{:S(2)}, u32[]{:S(2)}) collective-permute-start(bf16[344,8,128]{2,1,0:T(8,128)(2,1)S(1)} %get-tuple-element.37), channel_id=1, source_target_pairs={{0,28},{1,29},{2,30},{3,31},{4,0},{5,1},{6,2},{7,3},{8,4},{9,5},{1... | collective-permute-start | bytes 2113544 | tf_op jit(solution)/shard_map/ppermute | solution.py:455
  32.9 0.1 broadcast_select_fusion.3.filt
  33.0 0.0 copy-start.16
  33.0 9.0 %features.1 = (bf16[576,1792]{1,0:T(8,128)(2,1)S(1)}, bf16[576,1792]{1,0:T(8,128)(2,1)}, bf16[512,256]{1,0:T(8,128)(2,1)S(1)}, bf16[48,128]{1,0:T(8,128)(2,1)S(1)}) custom-call(s32[1]{0:T(128)} %bitcast.core, bf16[48,6272]{1,0:T(8,128)(2,1)S(1)} %copy-done.11, bf16[29,49,256]{2,1,0:T(8,128)(2,1)S(1)} %bitcast.20, s32[192,1]{1,0:T(8,128)S(1)} %copy-done.4, ...), custom_call_target="tpu_custom_call" | custom-call | flops 6000000000 | bytes 8000000 | tf_op jit(solution)/shard_map/features/pallas_call | solution.py:122
  42.0 0.0 copy-start.2
  42.0 0.7 copy-done.2
  42.7 0.0 collective-permute-done.5.refs_6_
  42.7 0.0 collective-permute-done.6.refs_7_
  42.7 0.8 %collective-permute-start.9 = (bf16[576,1792]{1,0:T(8,128)(2,1)}, bf16[576,1792]{1,0:T(8,128)(2,1)}, u32[]{:S(2)}, u32[]{:S(2)}) collective-permute-start(bf16[576,1792]{1,0:T(8,128)(2,1)} %get-tuple-element.42), channel_id=1, source_target_pairs={{0,32},{32,0},{64,96},{96,64},{128,160},{160,128},{192,224},{224,1... | collective-permute-start | bytes 6193160 | tf_op jit(solution)/shard_map/ppermute | solution.py:528
  43.6 0.0 collective-permute-start.7
  43.6 3.2 %collective-permute-start.8 = (bf16[344,8,128]{2,1,0:T(8,128)(2,1)}, bf16[344,8,128]{2,1,0:T(8,128)(2,1)}, u32[]{:S(2)}, u32[]{:S(2)}) collective-permute-start(bf16[344,8,128]{2,1,0:T(8,128)(2,1)} %collective-permute-done.6.refs_7_), channel_id=1, source_target_pairs={{0,28},{1,29},{2,30},{3,31},{4,0},{5,1},{6,2},{7,3},{8,4},{9,5},{1... | collective-permute-start | bytes 2113544 | tf_op jit(solution)/shard_map/ppermute | solution.py:455
  46.7 0.0 copy-done.16
  46.7 0.9 %collective-permute-done.9.got.refs_11_ = bf16[576,1792]{1,0:T(8,128)(2,1)} collective-permute-done((bf16[576,1792]{1,0:T(8,128)(2,1)}, bf16[576,1792]{1,0:T(8,128)(2,1)}, u32[]{:S(2)}, u32[]{:S(2)}) %collective-permute-start.9) | collective-permute-done | bytes 2064416 | tf_op jit(solution)/shard_map/ppermute | solution.py:528
  47.6 3.5 %choose.1 = (bf16[768,384]{1,0:T(8,128)(2,1)S(1)}, bf16[384,448]{1,0:T(8,128)(2,1)S(1)}) custom-call(s32[1]{0:T(128)} %bitcast.core, s32[32]{0:T(128)S(1)} %fusion.1.shard, bf16[576,1792]{1,0:T(8,128)(2,1)S(1)} %get-tuple-element.41.own.refs_10_, bf16[576,1792]{1,0:T(8,128)(2,1)} %collective-permute-done.9.got.refs_11_, bf16[86,8,128]{2,1,0:T(8,128)(2,1)S(1)} %copy-done, ...), custom_call_target="tpu_custom_call" | custom-call | flops 1000000000 | bytes 4000000 | tf_op jit(solution)/shard_map/choose/pallas_call | solution.py:243
  51.2 4.7 %collective-permute-done.7.refs_8_ = bf16[344,8,128]{2,1,0:T(8,128)(2,1)} collective-permute-done((bf16[344,8,128]{2,1,0:T(8,128)(2,1)}, bf16[344,8,128]{2,1,0:T(8,128)(2,1)}, u32[]{:S(2)}, u32[]{:S(2)}) %collective-permute-start.7) | collective-permute-done | bytes 704544 | tf_op jit(solution)/shard_map/ppermute | solution.py:455
  55.8 0.0 collective-permute-done.8.refs_9_
  55.8 0.9 %collective-permute-start.10 = (bf16[344,8,128]{2,1,0:T(8,128)(2,1)}, bf16[344,8,128]{2,1,0:T(8,128)(2,1)S(1)}, u32[]{:S(2)}, u32[]{:S(2)}) collective-permute-start(bf16[344,8,128]{2,1,0:T(8,128)(2,1)} %collective-permute-done.7.refs_8_), channel_id=1, source_target_pairs={{0,4},{1,5},{2,6},{3,7},{4,8},{5,9},{6,10},{7,11},{8,12},{9,13},{1... | collective-permute-start | bytes 2113544 | tf_op jit(solution)/shard_map/ppermute | solution.py:455
  56.7 1.8 %collective-permute-start.11 = (bf16[344,8,128]{2,1,0:T(8,128)(2,1)}, bf16[344,8,128]{2,1,0:T(8,128)(2,1)S(1)}, u32[]{:S(2)}, u32[]{:S(2)}) collective-permute-start(bf16[344,8,128]{2,1,0:T(8,128)(2,1)} %collective-permute-done.8.refs_9_), channel_id=1, source_target_pairs={{0,28},{1,29},{2,30},{3,31},{4,0},{5,1},{6,2},{7,3},{8,4},{9,5},{1... | collective-permute-start | bytes 2113544 | tf_op jit(solution)/shard_map/ppermute | solution.py:455
  58.5 7.7 %mix_early.1 = (f32[6,768,256]{2,1,0:T(8,128)S(1)}, f32[3,384,256]{2,1,0:T(8,128)S(1)}) custom-call(s32[1]{0:T(128)} %bitcast.core, s32[32]{0:T(128)S(1)} %fusion.1.shard, bf16[86,8,128]{2,1,0:T(8,128)(2,1)S(1)} %copy-done, bf16[86,8,128]{2,1,0:T(8,128)(2,1)S(1)} %collective-permute-done.1.refs_1_, bf16[86,8,128]{2,1,0:T(8,128)(2,1)S(1)} %collective-permute-done.2.refs_2_, ...), custom_call_target="tpu_custom_call" | custom-call | flops 4000000000 | bytes 12000000 | tf_op jit(solution)/shard_map/mix_early/pallas_call | solution.py:305
  66.2 1.3 %collective-permute-done.10 = bf16[344,8,128]{2,1,0:T(8,128)(2,1)S(1)} collective-permute-done((bf16[344,8,128]{2,1,0:T(8,128)(2,1)}, bf16[344,8,128]{2,1,0:T(8,128)(2,1)S(1)}, u32[]{:S(2)}, u32[]{:S(2)}) %collective-permute-start.10) | collective-permute-done | bytes 704544 | tf_op jit(solution)/shard_map/ppermute | solution.py:455
  67.5 0.0 collective-permute-done.11
  67.5 4.1 %mix_late.1 = (bf16[15,192,128]{2,1,0:T(8,128)(2,1)S(1)}, bf16[15,192,128]{2,1,0:T(8,128)(2,1)}) custom-call(s32[1]{0:T(128)} %bitcast.core, bf16[4,86,8,128]{3,2,1,0:T(8,128)(2,1)S(1)} %bitcast.21, bf16[4,86,8,128]{3,2,1,0:T(8,128)(2,1)S(1)} %bitcast.22, f32[6,768,256]{2,1,0:T(8,128)S(1)} %get-tuple-element.48.part, ...), custom_call_target="tpu_custom_call" | custom-call | flops 1000000000 | bytes 8000000 | tf_op jit(solution)/shard_map/mix_late/pallas_call | solution.py:362
  71.6 2.5 %collective-permute-start.12 = (bf16[15,192,128]{2,1,0:T(8,128)(2,1)}, bf16[15,192,128]{2,1,0:T(8,128)(2,1)S(1)}, u32[]{:S(2)}, u32[]{:S(2)}) collective-permute-start(bf16[15,192,128]{2,1,0:T(8,128)(2,1)} %get-tuple-element.53), channel_id=1, source_target_pairs={{0,32},{32,0},{64,96},{96,64},{128,160},{160,128},{192,224},{224,1... | collective-permute-start | bytes 2211848 | tf_op jit(solution)/shard_map/ppermute | solution.py:536
  74.1 0.0 copy-done.15
  74.1 0.1 copy.24.struct
  74.2 0.0 copy-start.10
  74.2 0.8 %ends_of.1.hot = bf16[11280,192]{1,0:T(8,128)(2,1)S(1)} custom-call(bf16[512,256]{1,0:T(8,128)(2,1)S(1)} %copy-done.3, s32[1,192]{1,0:T(1,128)S(1)} %bitcast.26, s32[1,192]{1,0:T(1,128)S(1)} %bitcast.24, bf16[15,192,128]{2,1,0:T(8,128)(2,1)S(1)} %get-tuple-element.52.after.mine), custom_call_target="tpu_custom_call" | custom-call | flops 100000000 | bytes 6000000 | tf_op jit(solution)/shard_map/ends_of/pallas_call | solution.py:389
  75.0 1.1 %collective-permute-done.12.got = bf16[15,192,128]{2,1,0:T(8,128)(2,1)S(1)} collective-permute-done((bf16[15,192,128]{2,1,0:T(8,128)(2,1)}, bf16[15,192,128]{2,1,0:T(8,128)(2,1)S(1)}, u32[]{:S(2)}, u32[]{:S(2)}) %collective-permute-start.12) | collective-permute-done | bytes 737312 | tf_op jit(solution)/shard_map/ppermute | solution.py:536
  76.1 0.0 copy-done.10
  76.1 3.1 %turn_back.1 = (bf16[48,6272]{1,0:T(8,128)(2,1)}, f32[4]{0:T(128)}) custom-call(s32[1]{0:T(128)} %bitcast.core, s32[4]{0:T(128)S(1)} %copy-done.10, bf16[15,192,128]{2,1,0:T(8,128)(2,1)S(1)} %get-tuple-element.52.after.mine, bf16[15,192,128]{2,1,0:T(8,128)(2,1)S(1)} %collective-permute-done.12.got, bf16[11280,192]{1,0:T(8,128)(2,1)S(1)} %ends_of.1.hot, ...), custom_call_target="tpu_custom_call" | custom-call | flops 1000000000 | bytes 4000000 | tf_op jit(solution)/shard_map/turn_back/pallas_call | solution.py:432
  (15 shorter events, 0.0 us)
Async XLA Ops:
  0.6 20.9 %copy-start.12 = (bf16[256,29,49]{0,1,2:T(8,128)(2,1)S(1)}, bf16[256,29,49]{0,1,2:T(8,128)(2,1)}, u32[]{:S(2)}) copy-start(bf16[256,29,49]{0,1,2:T(8,128)(2,1)} %param.17) | copy-start | bytes 2182660
  0.6 22.2 %copy-start.14 = (s32[192]{0:T(256)S(1)}, s32[192]{0:T(256)}, u32[]{:S(2)}) copy-start(s32[192]{0:T(256)} %param.18) | copy-start | bytes 2308
  0.7 23.0 %copy-start.8 = (s32[192]{0:T(256)S(1)}, s32[192]{0:T(256)}, u32[]{:S(2)}) copy-start(s32[192]{0:T(256)} %param.19) | copy-start | bytes 2308
  0.7 23.8 %copy-start.9 = (s32[192]{0:T(256)S(1)}, s32[192]{0:T(256)}, u32[]{:S(2)}) copy-start(s32[192]{0:T(256)} %param.20) | copy-start | bytes 2308
  2.4 27.1 %copy-start = (bf16[86,8,128]{2,1,0:T(8,128)(2,1)S(1)}, bf16[86,8,128]{2,1,0:T(8,128)(2,1)}, u32[]{:S(2)}) copy-start(bf16[86,8,128]{2,1,0:T(8,128)(2,1)} %pack.1.refs_0_) | copy-start | bytes 528388
  2.4 11.0 %collective-permute-start = (bf16[86,8,128]{2,1,0:T(8,128)(2,1)}, bf16[86,8,128]{2,1,0:T(8,128)(2,1)S(1)}, u32[]{:S(2)}, u32[]{:S(2)}) collective-permute-start(bf16[86,8,128]{2,1,0:T(8,128)(2,1)} %pack.1.refs_0_), channel_id=1, source_target_pairs={{0,2},{1,3},{2,0},{3,1},{4,6},{5,7},{6,4},{7,5},{8,10},{9,11},{10,... | collective-permute-start | bytes 528392 | tf_op jit(solution)/shard_map/ppermute | solution.py:455
  10.2 6.2 %collective-permute-start.1 = (bf16[86,8,128]{2,1,0:T(8,128)(2,1)}, bf16[86,8,128]{2,1,0:T(8,128)(2,1)S(1)}, u32[]{:S(2)}, u32[]{:S(2)}) collective-permute-start(bf16[86,8,128]{2,1,0:T(8,128)(2,1)} %pack.1.refs_0_), channel_id=1, source_target_pairs={{0,1},{1,2},{2,3},{3,0},{4,5},{5,6},{6,7},{7,4},{8,9},{9,10},{10,1... | collective-permute-start | bytes 528392 | tf_op jit(solution)/shard_map/ppermute | solution.py:455
  11.0 6.8 %collective-permute-start.2 = (bf16[86,8,128]{2,1,0:T(8,128)(2,1)}, bf16[86,8,128]{2,1,0:T(8,128)(2,1)S(1)}, u32[]{:S(2)}, u32[]{:S(2)}) collective-permute-start(bf16[86,8,128]{2,1,0:T(8,128)(2,1)} %pack.1.refs_0_), channel_id=1, source_target_pairs={{0,3},{1,0},{2,1},{3,2},{4,7},{5,4},{6,5},{7,6},{8,11},{9,8},{10,9... | collective-permute-start | bytes 528392 | tf_op jit(solution)/shard_map/ppermute | solution.py:455
  18.8 10.7 %collective-permute-start.3 = (bf16[172,8,128]{2,1,0:T(8,128)(2,1)S(1)}, bf16[172,8,128]{2,1,0:T(8,128)(2,1)S(1)}, u32[]{:S(2)}, u32[]{:S(2)}) collective-permute-start(bf16[172,8,128]{2,1,0:T(8,128)(2,1)S(1)} %get-tuple-element.33), channel_id=1, source_target_pairs={{0,4},{1,5},{2,6},{3,7},{4,8},{5,9},{6,10},{7,11},{8,12},{9,13},{1... | collective-permute-start | bytes 1056776 | tf_op jit(solution)/shard_map/ppermute | solution.py:455
  18.9 10.6 %collective-permute-start.4 = (bf16[172,8,128]{2,1,0:T(8,128)(2,1)S(1)}, bf16[172,8,128]{2,1,0:T(8,128)(2,1)S(1)}, u32[]{:S(2)}, u32[]{:S(2)}) collective-permute-start(bf16[172,8,128]{2,1,0:T(8,128)(2,1)S(1)} %get-tuple-element.32), channel_id=1, source_target_pairs={{0,28},{1,29},{2,30},{3,31},{4,0},{5,1},{6,2},{7,3},{8,4},{9,5},{1... | collective-permute-start | bytes 1056776 | tf_op jit(solution)/shard_map/ppermute | solution.py:455
  25.9 7.0 %copy-start.13 = (bf16[192,128]{1,0:T(8,128)(2,1)S(1)}, bf16[192,128]{1,0:T(8,128)(2,1)}, u32[]{:S(2)}) copy-start(bf16[192,128]{1,0:T(8,128)(2,1)} %param.21) | copy-start | bytes 147460
  25.9 7.1 %copy-start.1 = (bf16[256,29,49]{0,2,1:T(8,128)(2,1)S(1)}, bf16[256,29,49]{0,2,1:T(8,128)(2,1)}, u32[]{:S(2)}) copy-start(bf16[256,29,49]{0,2,1:T(8,128)(2,1)} %copy.26) | copy-start | bytes 2182660
  25.9 7.1 %copy-start.4 = (s32[192,1]{1,0:T(8,128)S(1)}, s32[192,1]{1,0:T(8,128)}, u32[]{:S(2)}) copy-start(s32[192,1]{1,0:T(8,128)} %copy.21.source) | copy-start | bytes 2308
  25.9 7.1 %copy-start.5 = (s32[192,1]{1,0:T(8,128)S(1)}, s32[192,1]{1,0:T(8,128)}, u32[]{:S(2)}) copy-start(s32[192,1]{1,0:T(8,128)} %copy.22.target) | copy-start | bytes 2308
  25.9 7.1 %copy-start.6 = (s32[192,1]{1,0:T(8,128)S(1)}, s32[192,1]{1,0:T(8,128)}, u32[]{:S(2)}) copy-start(s32[192,1]{1,0:T(8,128)} %copy.23.rotation) | copy-start | bytes 2308
  25.9 7.1 %copy-start.11 = (bf16[48,6272]{1,0:T(8,128)(2,1)S(1)}, bf16[48,6272]{1,0:T(8,128)(2,1)}, u32[]{:S(2)}) copy-start(bf16[48,6272]{1,0:T(8,128)(2,1)} %node.1) | copy-start | bytes 1806340
  29.7 13.0 %collective-permute-start.5 = (bf16[344,8,128]{2,1,0:T(8,128)(2,1)S(1)}, bf16[344,8,128]{2,1,0:T(8,128)(2,1)}, u32[]{:S(2)}, u32[]{:S(2)}) collective-permute-start(bf16[344,8,128]{2,1,0:T(8,128)(2,1)S(1)} %get-tuple-element.36), channel_id=1, source_target_pairs={{0,4},{1,5},{2,6},{3,7},{4,8},{5,9},{6,10},{7,11},{8,12},{9,13},{1... | collective-permute-start | bytes 2113544 | tf_op jit(solution)/shard_map/ppermute | solution.py:455
  30.2 12.5 %collective-permute-start.6 = (bf16[344,8,128]{2,1,0:T(8,128)(2,1)S(1)}, bf16[344,8,128]{2,1,0:T(8,128)(2,1)}, u32[]{:S(2)}, u32[]{:S(2)}) collective-permute-start(bf16[344,8,128]{2,1,0:T(8,128)(2,1)S(1)} %get-tuple-element.37), channel_id=1, source_target_pairs={{0,28},{1,29},{2,30},{3,31},{4,0},{5,1},{6,2},{7,3},{8,4},{9,5},{1... | collective-permute-start | bytes 2113544 | tf_op jit(solution)/shard_map/ppermute | solution.py:455
  33.0 13.7 %copy-start.16 = (s32[2,32,2]{1,2,0:T(2,128)S(1)}, s32[2,32,2]{1,2,0:T(2,128)}, u32[]{:S(2)}) copy-start(s32[2,32,2]{1,2,0:T(2,128)} %constant.68.clone) | copy-start | bytes 1540
  42.0 0.7 copy-start.2
  42.7 4.9 %collective-permute-start.9 = (bf16[576,1792]{1,0:T(8,128)(2,1)}, bf16[576,1792]{1,0:T(8,128)(2,1)}, u32[]{:S(2)}, u32[]{:S(2)}) collective-permute-start(bf16[576,1792]{1,0:T(8,128)(2,1)} %get-tuple-element.42), channel_id=1, source_target_pairs={{0,32},{32,0},{64,96},{96,64},{128,160},{160,128},{192,224},{224,1... | collective-permute-start | bytes 6193160 | tf_op jit(solution)/shard_map/ppermute | solution.py:528
  43.6 12.3 %collective-permute-start.7 = (bf16[344,8,128]{2,1,0:T(8,128)(2,1)}, bf16[344,8,128]{2,1,0:T(8,128)(2,1)}, u32[]{:S(2)}, u32[]{:S(2)}) collective-permute-start(bf16[344,8,128]{2,1,0:T(8,128)(2,1)} %collective-permute-done.5.refs_6_), channel_id=1, source_target_pairs={{0,4},{1,5},{2,6},{3,7},{4,8},{5,9},{6,10},{7,11},{8,12},{9,13},{1... | collective-permute-start | bytes 2113544 | tf_op jit(solution)/shard_map/ppermute | solution.py:455
  43.6 12.3 %collective-permute-start.8 = (bf16[344,8,128]{2,1,0:T(8,128)(2,1)}, bf16[344,8,128]{2,1,0:T(8,128)(2,1)}, u32[]{:S(2)}, u32[]{:S(2)}) collective-permute-start(bf16[344,8,128]{2,1,0:T(8,128)(2,1)} %collective-permute-done.6.refs_7_), channel_id=1, source_target_pairs={{0,28},{1,29},{2,30},{3,31},{4,0},{5,1},{6,2},{7,3},{8,4},{9,5},{1... | collective-permute-start | bytes 2113544 | tf_op jit(solution)/shard_map/ppermute | solution.py:455
  55.8 11.7 %collective-permute-start.10 = (bf16[344,8,128]{2,1,0:T(8,128)(2,1)}, bf16[344,8,128]{2,1,0:T(8,128)(2,1)S(1)}, u32[]{:S(2)}, u32[]{:S(2)}) collective-permute-start(bf16[344,8,128]{2,1,0:T(8,128)(2,1)} %collective-permute-done.7.refs_8_), channel_id=1, source_target_pairs={{0,4},{1,5},{2,6},{3,7},{4,8},{5,9},{6,10},{7,11},{8,12},{9,13},{1... | collective-permute-start | bytes 2113544 | tf_op jit(solution)/shard_map/ppermute | solution.py:455
  56.7 10.8 %collective-permute-start.11 = (bf16[344,8,128]{2,1,0:T(8,128)(2,1)}, bf16[344,8,128]{2,1,0:T(8,128)(2,1)S(1)}, u32[]{:S(2)}, u32[]{:S(2)}) collective-permute-start(bf16[344,8,128]{2,1,0:T(8,128)(2,1)} %collective-permute-done.8.refs_9_), channel_id=1, source_target_pairs={{0,28},{1,29},{2,30},{3,31},{4,0},{5,1},{6,2},{7,3},{8,4},{9,5},{1... | collective-permute-start | bytes 2113544 | tf_op jit(solution)/shard_map/ppermute | solution.py:455
  67.5 6.5 %copy-start.15 = (s32[48]{0:T(128)S(1)}, s32[48]{0:T(128)}, u32[]{:S(2)}) copy-start(s32[48]{0:T(128)} %param.28) | copy-start | bytes 580
  67.5 6.6 %copy-start.3 = (bf16[512,256]{1,0:T(8,128)(2,1)S(1)}, bf16[512,256]{1,0:T(8,128)(2,1)}, u32[]{:S(2)}) copy-start(bf16[512,256]{1,0:T(8,128)(2,1)} %copy-done.2) | copy-start | bytes 786436
  71.6 4.5 %collective-permute-start.12 = (bf16[15,192,128]{2,1,0:T(8,128)(2,1)}, bf16[15,192,128]{2,1,0:T(8,128)(2,1)S(1)}, u32[]{:S(2)}, u32[]{:S(2)}) collective-permute-start(bf16[15,192,128]{2,1,0:T(8,128)(2,1)} %get-tuple-element.53), channel_id=1, source_target_pairs={{0,32},{32,0},{64,96},{96,64},{128,160},{160,128},{192,224},{224,1... | collective-permute-start | bytes 2211848 | tf_op jit(solution)/shard_map/ppermute | solution.py:536
  74.2 2.0 %copy-start.7 = (f32[5,128]{1,0:T(8,128)S(1)}, f32[5,128]{1,0:T(8,128)}, u32[]{:S(2)}) copy-start(f32[5,128]{1,0:T(8,128)} %head.1) | copy-start | bytes 7684
  74.2 2.0 %copy-start.10 = (s32[4]{0:T(128)S(1)}, s32[4]{0:T(128)}, u32[]{:S(2)}) copy-start(s32[4]{0:T(128)} %task.1) | copy-start | bytes 52
